TPU v7x, 32 devices: a whole 2x2x4 slice. The times are simulated.
32 devices in a mesh: fsdp: 2 (over x), ctx: 4 (over z), tp: 4 (over y, core).
Axes of the slice: x: 2, y: 2, z: 4, core: 2. Of those that a mesh axis runs over, the one named last changes fastest.
Arguments:
- hidden_in: bfloat16 [2048, 2048], P(('fsdp', 'ctx'), 'tp'), may hold values from -6 to 6
- positions: int32 [2048], P(('fsdp', 'ctx')), may hold values from 0 to 2046, as said below
- chosen: int32 [2048, 6], P(('fsdp', 'ctx')), may hold values from 0 to 15, all different within a row; in each aligned block of 256 rows (0 to 255, 256 to 511, ...) at most 160 rows name the same one
- out_grad: bfloat16 [2048, 2048], P(('fsdp', 'ctx'), 'tp'), may hold values from -6 to 6
- attn_gain: bfloat16 [2048], P(('fsdp', 'ctx')), may hold values from 0.5 to 1.5
- w_query: bfloat16 [2048, 2048], P(('fsdp', 'ctx'), 'tp'), may hold values from -0.125 to 0.125
- w_key: bfloat16 [2048, 2048], P(('fsdp', 'ctx'), 'tp'), may hold values from -0.125 to 0.125
- w_value: bfloat16 [2048, 2048], P(('fsdp', 'ctx'), 'tp'), may hold values from -0.125 to 0.125
- w_out: bfloat16 [2048, 2048], P('tp', ('fsdp', 'ctx')), may hold values from -0.75 to 0.75
- moe_gain: bfloat16 [2048], P(('fsdp', 'ctx')), may hold values from 0.5 to 1.5
- router: bfloat16 [2048, 16], P(('fsdp', 'ctx')), may hold values from -0.0625 to 0.0625
- shared_gate: bfloat16 [2048, 2816], P(('fsdp', 'ctx'), 'tp'), may hold values from -0.125 to 0.125
- shared_up: bfloat16 [2048, 2816], P(('fsdp', 'ctx'), 'tp'), may hold values from -0.125 to 0.125
- shared_down: bfloat16 [2816, 2048], P('tp', ('fsdp', 'ctx')), may hold values from -0.109375 to 0.109375
- expert_gate: bfloat16 [16, 2048, 1408], P('ctx', 'fsdp', 'tp'), may hold values from -0.125 to 0.125
- expert_up: bfloat16 [16, 2048, 1408], P('ctx', 'fsdp', 'tp'), may hold values from -0.125 to 0.125
- expert_down: bfloat16 [16, 1408, 2048], P('ctx', 'tp', 'fsdp'), may hold values from -1 to 1
Outputs:
- layer_out: bfloat16 [2048, 2048], P(('fsdp', 'ctx'), 'tp')
- input_grad: float32 [2048, 2048], P(('fsdp', 'ctx'), 'tp')
- attn_gain_grad: float32 [2048], P(('fsdp', 'ctx'))
- w_query_grad: float32 [2048, 2048], P(('fsdp', 'ctx'), 'tp')
- w_key_grad: float32 [2048, 2048], P(('fsdp', 'ctx'), 'tp')
- w_value_grad: float32 [2048, 2048], P(('fsdp', 'ctx'), 'tp')
- w_out_grad: float32 [2048, 2048], P('tp', ('fsdp', 'ctx'))
- moe_gain_grad: float32 [2048], P(('fsdp', 'ctx'))
- router_grad: float32 [2048, 16], P(('fsdp', 'ctx'))
- shared_gate_grad: float32 [2048, 2816], P(('fsdp', 'ctx'), 'tp')
- shared_up_grad: float32 [2048, 2816], P(('fsdp', 'ctx'), 'tp')
- shared_down_grad: float32 [2816, 2048], P('tp', ('fsdp', 'ctx'))
- expert_gate_grad: float32 [16, 2048, 1408], P('ctx', 'fsdp', 'tp')
- expert_up_grad: float32 [16, 2048, 1408], P('ctx', 'fsdp', 'tp')
- expert_down_grad: float32 [16, 1408, 2048], P('ctx', 'tp', 'fsdp')
Inputs may be any that keep to these rules, and one draw needn't show every extreme that they name: `chosen`: each row names 6 different experts; among the 256 rows of one device no expert is named more than 160 times, a bound that some block reaches. `positions`: within each sequence of 1024 tokens the first position is 0, each later one exceeds the one before it by 1, 2 or 3, and the last one is 2046.
All inputs are finite; a program needn't handle non-finite values.
Results may differ from a plain program's by a relative error of at most 0.025.
Values may be sent and summed in bfloat16 or wider, within the bound.
A program may use at most 320 MiB of HBM per device.

v0:
```python
import jax
import jax.numpy as jnp
from jax import lax
from jax.sharding import PartitionSpec as P

HD = 128
TOPK = 6


EPS = 1e-06
NEG_BIG = -1e30


def as_sent(value):
    return jax.tree.map(lambda a: a.astype(jnp.bfloat16) if a.dtype == jnp.float32 else a, value)


def features(local_part):
    return lax.all_gather(local_part, "tp", axis=1, tiled=True)


def row_stats(partial_terms):
    return lax.psum(partial_terms, "tp")


def partial_sums(partial_terms):
    return jax.tree.map(
        lambda part: part.astype(jnp.float32),
        lax.psum_scatter(as_sent(partial_terms), "tp", scatter_dimension=1, tiled=True),
    )


def to_owners(slot_rows):
    return lax.all_to_all(slot_rows, "ctx", split_axis=0, concat_axis=2, tiled=True)


def to_sources(slot_rows):
    return lax.all_to_all(
        slot_rows.astype(jnp.bfloat16), "ctx", split_axis=2, concat_axis=0, tiled=True
    ).astype(slot_rows.dtype)


def rotary(values, positions, rotate_sign):
    half_dim = values.shape[-1] // 2
    inverse = 10000.0 ** (-jnp.arange(half_dim, dtype=jnp.float32) * 2.0 / values.shape[-1])
    angles = positions.astype(jnp.float32)[:, None] * inverse[None, :]
    cosine = jnp.cos(angles)[:, None, :]
    sine_val = rotate_sign * jnp.sin(angles)[:, None, :]
    lower_half = values[..., :half_dim]
    upper_half = values[..., half_dim:]
    return jnp.concatenate(
        [lower_half * cosine - upper_half * sine_val, upper_half * cosine + lower_half * sine_val],
        axis=-1,
    )


def norm_rows(values, gain_part, model_width):
    square_sum = row_stats(jnp.sum(values * values, axis=1))
    row_scale = lax.rsqrt(square_sum / model_width + EPS)
    return (values * row_scale[:, None] * gain_part[None, :], row_scale)


def norm_back(values, row_scale, gain_part, grad_normed, model_width, tp_rank):
    quarter = values.shape[1]
    local_sum = jnp.sum(grad_normed * gain_part[None, :] * values, axis=1)
    gain_local = jnp.sum(grad_normed * values * row_scale[:, None], axis=0)
    gain_whole = lax.dynamic_update_slice_in_dim(
        jnp.zeros((model_width,), jnp.float32), gain_local, tp_rank * quarter, 0
    )
    row_total, gain_grad = row_stats((local_sum, gain_whole))
    back = (
        row_scale[:, None] * gain_part[None, :] * grad_normed
        - values * (row_scale**3 * row_total / model_width)[:, None]
    )
    return (back, gain_grad)


def scatter_slots(assign_rows, flat_exp, slot_of, n_exp, capacity):
    buffer = jnp.zeros((n_exp, capacity, assign_rows.shape[1]), assign_rows.dtype)
    return buffer.at[flat_exp, slot_of].set(assign_rows)


def silu_grad(pre_act):
    sigmoid_val = jax.nn.sigmoid(pre_act)
    return sigmoid_val * (1.0 + pre_act * (1.0 - sigmoid_val))


def keep_state(carried):
    return carried


def per_device(
    hidden_in,
    positions,
    chosen,
    out_grad,
    attn_gain,
    w_query,
    w_key,
    w_value,
    w_out,
    moe_gain,
    router,
    shared_gate,
    shared_up,
    shared_down,
    expert_gate,
    expert_up,
    expert_down,
):
    tp_rank = lax.axis_index("tp")
    ctx_rank = lax.axis_index("ctx")
    n_ctx = lax.axis_size("ctx")
    tok_rows, quarter = hidden_in.shape
    model_width = quarter * lax.axis_size("tp")
    gain_one, wq_all, wk_all, wv_all, gain_two, router_all, gate_all, up_all, wo_all, down_all = (
        lax.all_gather(attn_gain, ("fsdp", "ctx"), axis=0, tiled=True),
        lax.all_gather(w_query, ("fsdp", "ctx"), axis=0, tiled=True),
        lax.all_gather(w_key, ("fsdp", "ctx"), axis=0, tiled=True),
        lax.all_gather(w_value, ("fsdp", "ctx"), axis=0, tiled=True),
        lax.all_gather(moe_gain, ("fsdp", "ctx"), axis=0, tiled=True),
        lax.all_gather(router, ("fsdp", "ctx"), axis=0, tiled=True),
        lax.all_gather(shared_gate, ("fsdp", "ctx"), axis=0, tiled=True),
        lax.all_gather(shared_up, ("fsdp", "ctx"), axis=0, tiled=True),
        lax.all_gather(w_out, ("fsdp", "ctx"), axis=1, tiled=True),
        lax.all_gather(shared_down, ("fsdp", "ctx"), axis=1, tiled=True),
    )
    expert_gate_weights, expert_up_weights, expert_down_weights = (
        lax.all_gather(expert_gate, "fsdp", axis=1, tiled=True),
        lax.all_gather(expert_up, "fsdp", axis=1, tiled=True),
        lax.all_gather(expert_down, "fsdp", axis=2, tiled=True),
    )
    gain_q1 = lax.dynamic_slice_in_dim(gain_one, tp_rank * quarter, quarter).astype(jnp.float32)
    gain_q2 = lax.dynamic_slice_in_dim(gain_two, tp_rank * quarter, quarter).astype(jnp.float32)
    router_rows = lax.dynamic_slice_in_dim(router_all, tp_rank * quarter, quarter, 0)
    head_count = wq_all.shape[1] // HD
    scale_att = HD ** (-0.5)
    resid_in = hidden_in.astype(jnp.float32)
    normed_one, scale_one = norm_rows(resid_in, gain_q1, model_width)
    normed_in = features(normed_one.astype(jnp.bfloat16))
    query_pre = jnp.dot(normed_in, wq_all, preferred_element_type=jnp.float32).reshape(
        tok_rows, head_count, HD
    )
    key_pre = jnp.dot(normed_in, wk_all, preferred_element_type=jnp.float32).reshape(
        tok_rows, head_count, HD
    )
    value_b = (
        jnp.dot(normed_in, wv_all, preferred_element_type=jnp.float32)
        .astype(jnp.bfloat16)
        .reshape(tok_rows, head_count, HD)
    )
    query_b = rotary(query_pre, positions, 1.0).astype(jnp.bfloat16)
    key_b = rotary(key_pre, positions, 1.0).astype(jnp.bfloat16)
    q_start = ctx_rank * tok_rows
    row_pos = q_start + jnp.arange(tok_rows)
    start_state = (
        jnp.full((tok_rows, head_count), NEG_BIG, jnp.float32),
        jnp.zeros((tok_rows, head_count), jnp.float32),
        jnp.zeros((tok_rows, head_count, HD), jnp.float32),
    )
    keys_blk = lax.all_gather(key_b, "ctx", axis=0, tiled=True)
    vals_blk = lax.all_gather(value_b, "ctx", axis=0, tiled=True)
    key_count = keys_blk.shape[0]

    def compute(state_in):
        run_max, run_sum, run_acc = state_in
        scores = (
            jnp.einsum("qhd,khd->qhk", query_b, keys_blk, preferred_element_type=jnp.float32)
            * scale_att
        )
        visible = jnp.arange(key_count)[None, :] <= row_pos[:, None]
        scores = jnp.where(visible[:, None, :], scores, NEG_BIG)
        new_max = jnp.maximum(run_max, jnp.max(scores, axis=2))
        weights = jnp.exp(scores - new_max[:, :, None])
        new_sum = jnp.sum(weights, axis=2)
        new_acc = jnp.einsum(
            "qhk,khd->qhd",
            weights.astype(jnp.bfloat16),
            vals_blk,
            preferred_element_type=jnp.float32,
        )
        return (new_max, new_sum, new_acc)

    run_max, run_sum, run_acc = lax.cond(
        jnp.int32(0) <= q_start + tok_rows - 1, compute, keep_state, start_state
    )
    heads_f = run_acc / run_sum[:, :, None]
    log_sum = run_max + jnp.log(run_sum)
    heads_b = heads_f.astype(jnp.bfloat16).reshape(tok_rows, head_count * HD)
    resid_mid = resid_in + partial_sums(
        jnp.dot(heads_b, wo_all, preferred_element_type=jnp.float32)
    )
    normed_two, scale_two = norm_rows(resid_mid, gain_q2, model_width)
    moe_part = normed_two.astype(jnp.bfloat16)
    moe_in = features(moe_part)
    n_exp = router_all.shape[1]
    exp_dev = n_exp // n_ctx
    capacity = min(tok_rows, 5 * TOPK * tok_rows // (3 * n_exp))
    logits = jnp.dot(moe_in, router_all, preferred_element_type=jnp.float32)
    probs_all = jax.nn.softmax(logits, axis=1)
    picked = (chosen[:, :, None] == jnp.arange(n_exp)[None, None, :]).astype(jnp.float32)
    gate_vals = jnp.sum(picked * probs_all[:, None, :], axis=2)
    shared_a = jnp.dot(moe_in, gate_all, preferred_element_type=jnp.float32)
    shared_b = jnp.dot(moe_in, up_all, preferred_element_type=jnp.float32)
    shared_act = (jax.nn.silu(shared_a) * shared_b).astype(jnp.bfloat16)
    shared_out = jnp.dot(shared_act, down_all, preferred_element_type=jnp.float32)
    flat_exp = chosen.reshape(-1)
    flat_hot = (flat_exp[:, None] == jnp.arange(n_exp)[None, :]).astype(jnp.int32)
    slot_of = jnp.sum((jnp.cumsum(flat_hot, axis=0) - flat_hot) * flat_hot, axis=1)
    token_of = jnp.arange(tok_rows * TOPK) // TOPK
    slot_count = n_ctx * capacity
    outgoing = scatter_slots(moe_in[token_of], flat_exp, slot_of, n_exp, capacity)
    received_rows = to_owners(outgoing.reshape(n_ctx, exp_dev, capacity, model_width)).reshape(
        exp_dev, slot_count, model_width
    )
    expert_a = jnp.einsum(
        "bmw,bwv->bmv", received_rows, expert_gate_weights, preferred_element_type=jnp.float32
    )
    expert_up_proj = jnp.einsum(
        "bmw,bwv->bmv", received_rows, expert_up_weights, preferred_element_type=jnp.float32
    )
    expert_act = (jax.nn.silu(expert_a) * expert_up_proj).astype(jnp.bfloat16)
    expert_out = jnp.einsum(
        "erf,efd->erd", expert_act, expert_down_weights, preferred_element_type=jnp.float32
    )
    returned = to_sources(expert_out.reshape(1, exp_dev, slot_count, model_width))
    shared_q, slot_q = partial_sums((shared_out, returned.reshape(n_exp * capacity, model_width)))
    slot_rows = slot_q.reshape(n_exp, capacity, quarter)[flat_exp, slot_of].reshape(
        tok_rows, TOPK, quarter
    )
    result = resid_mid + shared_q + jnp.sum(gate_vals[:, :, None] * slot_rows, axis=1)
    layer_out = result.astype(jnp.bfloat16)
    grad_out = out_grad.astype(jnp.float32)
    gate_grad = row_stats(jnp.sum(grad_out[:, None, :] * slot_rows, axis=2))
    prob_grad = jnp.sum(gate_grad[:, :, None] * picked, axis=1)
    logit_grad = (
        probs_all * (prob_grad - jnp.sum(probs_all * prob_grad, axis=1, keepdims=True))
    ).astype(jnp.bfloat16)
    router_grad = jnp.einsum("td,te->de", moe_in, logit_grad, preferred_element_type=jnp.float32)
    router_back_q = jnp.einsum(
        "te,de->td", logit_grad, router_rows, preferred_element_type=jnp.float32
    )
    grad_full = features(out_grad)
    shared_dact = jnp.einsum("td,fd->tf", grad_full, down_all, preferred_element_type=jnp.float32)
    shared_da = (shared_dact * shared_b * silu_grad(shared_a)).astype(jnp.bfloat16)
    shared_db = (shared_dact * jax.nn.silu(shared_a)).astype(jnp.bfloat16)
    shared_down_grad = jnp.einsum(
        "tf,td->fd", shared_act, grad_full, preferred_element_type=jnp.float32
    )
    shared_gate_grad = jnp.einsum(
        "td,tf->df", moe_in, shared_da, preferred_element_type=jnp.float32
    )
    shared_up_grad = jnp.einsum("td,tf->df", moe_in, shared_db, preferred_element_type=jnp.float32)
    shared_back = jnp.einsum(
        "tf,df->td", shared_da, gate_all, preferred_element_type=jnp.float32
    ) + jnp.einsum("tf,df->td", shared_db, up_all, preferred_element_type=jnp.float32)
    assign_grad = (
        (gate_vals[:, :, None] * grad_full[:, None, :])
        .astype(jnp.bfloat16)
        .reshape(tok_rows * TOPK, model_width)
    )
    grad_slots = scatter_slots(assign_grad, flat_exp, slot_of, n_exp, capacity)
    grad_arrived = to_owners(grad_slots.reshape(n_ctx, exp_dev, capacity, model_width)).reshape(
        exp_dev, slot_count, model_width
    )
    expert_dact = jnp.einsum(
        "erd,efd->erf", grad_arrived, expert_down_weights, preferred_element_type=jnp.float32
    )
    expert_da = (expert_dact * expert_up_proj * silu_grad(expert_a)).astype(jnp.bfloat16)
    expert_up_proj_grad = (expert_dact * jax.nn.silu(expert_a)).astype(jnp.bfloat16)
    edown_grad = jnp.einsum(
        "erf,erd->efd", expert_act, grad_arrived, preferred_element_type=jnp.float32
    )
    egate_grad = jnp.einsum(
        "qgo,qgz->qoz", received_rows, expert_da, preferred_element_type=jnp.float32
    )
    expert_up_weight_grad = jnp.einsum(
        "qgo,qgz->qoz", received_rows, expert_up_proj_grad, preferred_element_type=jnp.float32
    )
    expert_back = jnp.einsum(
        "iac,igc->iag", expert_da, expert_gate_weights, preferred_element_type=jnp.float32
    ) + jnp.einsum(
        "iac,igc->iag", expert_up_proj_grad, expert_up_weights, preferred_element_type=jnp.float32
    )
    back_slots = to_sources(expert_back.reshape(1, exp_dev, slot_count, model_width)).reshape(
        n_exp, capacity, model_width
    )
    token_back = jnp.sum(back_slots[flat_exp, slot_of].reshape(tok_rows, TOPK, model_width), axis=1)
    moe_back_q = partial_sums(shared_back + token_back)
    mid_back, gain_two_grad = norm_back(
        resid_mid, scale_two, gain_q2, moe_back_q + router_back_q, model_width, tp_rank
    )
    mid_grad = grad_out + mid_back
    branch_full = features(mid_grad.astype(jnp.bfloat16))
    wo_grad = jnp.einsum("tf,td->fd", heads_b, branch_full, preferred_element_type=jnp.float32)
    heads_grad = (
        jnp.einsum("td,fd->tf", branch_full, wo_all, preferred_element_type=jnp.float32)
        .astype(jnp.bfloat16)
        .reshape(tok_rows, head_count, HD)
    )
    row_delta = jnp.sum(heads_grad.astype(jnp.float32) * heads_f, axis=2)
    seq_len = tok_rows * n_ctx
    back_state = (
        jnp.zeros((tok_rows, head_count, HD), jnp.float32),
        jnp.zeros((seq_len, head_count, HD), jnp.float32),
        jnp.zeros((seq_len, head_count, HD), jnp.float32),
    )
    attend_keys_blk = lax.all_gather(key_b, "ctx", axis=0, tiled=True)
    attend_vals_blk = lax.all_gather(value_b, "ctx", axis=0, tiled=True)
    attend_key_count = attend_keys_blk.shape[0]

    def compute(state_in):
        scores = (
            jnp.einsum("qhd,khd->qhk", query_b, attend_keys_blk, preferred_element_type=jnp.float32)
            * scale_att
        )
        visible = jnp.arange(attend_key_count)[None, :] <= row_pos[:, None]
        probs_blk = jnp.where(visible[:, None, :], jnp.exp(scores - log_sum[:, :, None]), 0.0)
        value_part = jnp.einsum(
            "qhk,qhd->khd",
            probs_blk.astype(jnp.bfloat16),
            heads_grad,
            preferred_element_type=jnp.float32,
        )
        dot_grad = jnp.einsum(
            "qhd,khd->qhk", heads_grad, attend_vals_blk, preferred_element_type=jnp.float32
        )
        score_grad = (probs_blk * (dot_grad - row_delta[:, :, None])).astype(jnp.bfloat16)
        query_acc = (
            jnp.einsum(
                "qhk,khd->qhd", score_grad, attend_keys_blk, preferred_element_type=jnp.float32
            )
            * scale_att
        )
        key_part = (
            jnp.einsum("qhk,qhd->khd", score_grad, query_b, preferred_element_type=jnp.float32)
            * scale_att
        )
        return (query_acc, key_part, value_part)

    query_grad, key_grad_all, value_grad_all = lax.cond(
        jnp.int32(0) <= q_start + tok_rows - 1, compute, keep_state, back_state
    )
    key_grad, value_grad = (
        lax.psum_scatter(
            key_grad_all.astype(jnp.bfloat16), "ctx", scatter_dimension=0, tiled=True
        ).astype(jnp.float32),
        lax.psum_scatter(
            value_grad_all.astype(jnp.bfloat16), "ctx", scatter_dimension=0, tiled=True
        ).astype(jnp.float32),
    )
    query_pre_grad = (
        rotary(query_grad, positions, -1.0).astype(jnp.bfloat16).reshape(tok_rows, head_count * HD)
    )
    key_pre_grad = (
        rotary(key_grad, positions, -1.0).astype(jnp.bfloat16).reshape(tok_rows, head_count * HD)
    )
    value_pre_grad = value_grad.astype(jnp.bfloat16).reshape(tok_rows, head_count * HD)
    wq_grad = jnp.einsum("td,tf->df", normed_in, query_pre_grad, preferred_element_type=jnp.float32)
    wk_grad = jnp.einsum("td,tf->df", normed_in, key_pre_grad, preferred_element_type=jnp.float32)
    wv_grad = jnp.einsum("td,tf->df", normed_in, value_pre_grad, preferred_element_type=jnp.float32)
    in_back = jnp.einsum("tf,df->td", query_pre_grad, wq_all, preferred_element_type=jnp.float32)
    in_back = in_back + jnp.einsum(
        "tf,df->td", key_pre_grad, wk_all, preferred_element_type=jnp.float32
    )
    in_back = in_back + jnp.einsum(
        "tf,df->td", value_pre_grad, wv_all, preferred_element_type=jnp.float32
    )
    first_back, gain_one_grad = norm_back(
        resid_in, scale_one, gain_q1, partial_sums(in_back), model_width, tp_rank
    )
    input_grad = mid_grad + first_back
    dense = (
        lax.psum_scatter(
            gain_one_grad.astype(jnp.bfloat16), ("fsdp", "ctx"), scatter_dimension=0, tiled=True
        ).astype(jnp.float32),
        lax.psum_scatter(
            wq_grad.astype(jnp.bfloat16), ("fsdp", "ctx"), scatter_dimension=0, tiled=True
        ).astype(jnp.float32),
        lax.psum_scatter(
            wk_grad.astype(jnp.bfloat16), ("fsdp", "ctx"), scatter_dimension=0, tiled=True
        ).astype(jnp.float32),
        lax.psum_scatter(
            wv_grad.astype(jnp.bfloat16), ("fsdp", "ctx"), scatter_dimension=0, tiled=True
        ).astype(jnp.float32),
        lax.psum_scatter(
            gain_two_grad.astype(jnp.bfloat16), ("fsdp", "ctx"), scatter_dimension=0, tiled=True
        ).astype(jnp.float32),
        lax.psum_scatter(
            router_grad.astype(jnp.bfloat16), ("fsdp", "ctx"), scatter_dimension=0, tiled=True
        ).astype(jnp.float32),
        lax.psum_scatter(
            shared_gate_grad.astype(jnp.bfloat16), ("fsdp", "ctx"), scatter_dimension=0, tiled=True
        ).astype(jnp.float32),
        lax.psum_scatter(
            shared_up_grad.astype(jnp.bfloat16), ("fsdp", "ctx"), scatter_dimension=0, tiled=True
        ).astype(jnp.float32),
        lax.psum_scatter(
            wo_grad.astype(jnp.bfloat16), ("fsdp", "ctx"), scatter_dimension=1, tiled=True
        ).astype(jnp.float32),
        lax.psum_scatter(
            shared_down_grad.astype(jnp.bfloat16), ("fsdp", "ctx"), scatter_dimension=1, tiled=True
        ).astype(jnp.float32),
    )
    experts_done = (
        lax.psum_scatter(
            egate_grad.astype(jnp.bfloat16), "fsdp", scatter_dimension=1, tiled=True
        ).astype(jnp.float32),
        lax.psum_scatter(
            expert_up_weight_grad.astype(jnp.bfloat16), "fsdp", scatter_dimension=1, tiled=True
        ).astype(jnp.float32),
        lax.psum_scatter(
            edown_grad.astype(jnp.bfloat16), "fsdp", scatter_dimension=2, tiled=True
        ).astype(jnp.float32),
    )
    return (
        layer_out,
        input_grad,
        dense[0],
        dense[1],
        dense[2],
        dense[3],
        dense[8],
        dense[4],
        dense[5],
        dense[6],
        dense[7],
        dense[9],
        experts_done[0],
        experts_done[1],
        experts_done[2],
    )


def solution(mesh):
    placed = (
        P(("fsdp", "ctx"), "tp"),
        P(("fsdp", "ctx")),
        P(("fsdp", "ctx"), None),
        P(("fsdp", "ctx"), "tp"),
        P(("fsdp", "ctx")),
        P(("fsdp", "ctx"), "tp"),
        P(("fsdp", "ctx"), "tp"),
        P(("fsdp", "ctx"), "tp"),
        P("tp", ("fsdp", "ctx")),
        P(("fsdp", "ctx")),
        P(("fsdp", "ctx"), None),
        P(("fsdp", "ctx"), "tp"),
        P(("fsdp", "ctx"), "tp"),
        P("tp", ("fsdp", "ctx")),
        P("ctx", "fsdp", "tp"),
        P("ctx", "fsdp", "tp"),
        P("ctx", "tp", "fsdp"),
    )
    return jax.shard_map(
        per_device,
        mesh=mesh,
        in_specs=placed,
        out_specs=(
            P(("fsdp", "ctx"), "tp"),
            P(("fsdp", "ctx"), "tp"),
            P(("fsdp", "ctx")),
            P(("fsdp", "ctx"), "tp"),
            P(("fsdp", "ctx"), "tp"),
            P(("fsdp", "ctx"), "tp"),
            P("tp", ("fsdp", "ctx")),
            P(("fsdp", "ctx")),
            P(("fsdp", "ctx"), None),
            P(("fsdp", "ctx"), "tp"),
            P(("fsdp", "ctx"), "tp"),
            P("tp", ("fsdp", "ctx")),
            P("ctx", "fsdp", "tp"),
            P("ctx", "fsdp", "tp"),
            P("ctx", "tp", "fsdp"),
        ),
        check_vma=False,
    )
```

profile of v0, /device:TPU:0, one launch (start us, length us, event | category | flops | bytes accessed | tf_op | source)
XLA Modules:
  0.0 2707.2 jit_solution(7159507036229260351)
XLA Ops:
  54.6 51.4 %all-gather.25.cloned.1.call-done = bf16[2048,512]{1,0:T(8,128)(2,1)} async-done(((bf16[256,512]{1,0:T(8,128)(2,1)}), bf16[2048,512]{1,0:T(8,128)(2,1)}) %all-gather.25.cloned.1.call-update) | async-done | bytes 2097168 | tf_op jit(solution)/shard_map/all_gather | solution.py:118
  108.9 47.1 %all-gather.21.cloned.1.call-done = bf16[2048,512]{1,0:T(8,128)(2,1)} async-done(((bf16[256,512]{1,0:T(8,128)(2,1)}), bf16[2048,512]{1,0:T(8,128)(2,1)}) %all-gather.21.cloned.1.call-update) | async-done | bytes 2097168 | tf_op jit(solution)/shard_map/all_gather | solution.py:119
  159.9 46.0 %all-gather.27.cloned.1.call-done = bf16[2048,512]{1,0:T(8,128)(2,1)} async-done(((bf16[256,512]{1,0:T(8,128)(2,1)}), bf16[2048,512]{1,0:T(8,128)(2,1)}) %all-gather.27.cloned.1.call-update) | async-done | bytes 2097168 | tf_op jit(solution)/shard_map/all_gather | solution.py:120
  211.0 25.5 all-gather.23.cloned.1.call-done
  236.5 28.3 %all-gather.29.cloned.1.call-done = bf16[1024,4,128]{2,0,1:T(8,128)(2,1)} async-done(((bf16[256,4,128]{2,0,1:T(8,128)(2,1)}), bf16[1024,4,128]{2,0,1:T(8,128)(2,1)}) %all-gather.29.cloned.1.call-update) | async-done | bytes 1048592 | tf_op jit(solution)/shard_map/all_gather | solution.py:162
  275.4 42.0 %all-gather.31.cloned.1.call-done = bf16[512,2048]{1,0:T(8,128)(2,1)} async-done(((bf16[512,256]{1,0:T(8,128)(2,1)}), bf16[512,2048]{1,0:T(8,128)(2,1)}) %all-gather.31.cloned.1.call-update) | async-done | bytes 2097168 | tf_op jit(solution)/shard_map/all_gather | solution.py:125
  370.6 35.2 %scatter_custom_fusion = bf16[2560,2048]{1,0:T(8,128)(2,1)} fusion(s32[1536]{0:T(1024)S(1)} %broadcast_select_fusion, bf16[256,2048]{1,0:T(8,128)(2,1)} %all-gather.33.cloned.1.call-done, s32[2048]{0:T(1024)S(1)} %pad_clamp_fusion, bf16[]{:T(256)} %constant.99.clone.1), kind=kCustom, calls=%fused_computation.45 | custom fusion | bytes 10486272
  412.5 250.0 %all_gather.72 = bf16[2048,16]{0,1:T(8,128)(2,1)S(1)} all-gather(bf16[256,16]{0,1:T(8,128)(2,1)S(1)} %copy-done.61), channel_id=1, replica_groups=mesh['fsdp'=2,'ctx'=4,'tp'=4] {'fsdp','ctx'}, dimensions={0}, use_global_device_ids=true | all-gather | bytes 73728 | tf_op jit(solution)/shard_map/all_gather | solution.py:122
  725.4 209.4 %all-to-all-done.2 = bf16[4,4,160,2048]{3,2,1,0:T(8,128)(2,1)} async-done(((bf16[4,4,160,2048]{3,2,1,0:T(8,128)(2,1)}), bf16[4,4,160,2048]{3,2,1,0:T(8,128)(2,1)}, u32[]{:S(2)}, u32[]{:S(2)}) %all-to-all-start.2) | async-done | bytes 10485792 | tf_op jit(solution)/shard_map/all_to_all | solution.py:34
  1021.0 294.8 %all-to-all-done.1 = bf16[1,4,640,2048]{3,1,0,2:T(4,128)(2,1)} async-done(((bf16[1,4,640,2048]{3,1,0,2:T(4,128)(2,1)}), bf16[1,4,640,2048]{3,1,0,2:T(4,128)(2,1)}, u32[]{:S(2)}, u32[]{:S(2)}) %all-to-all-start.1) | async-done | bytes 10485792 | tf_op jit(solution)/shard_map/all_to_all | solution.py:38
  1399.9 215.4 %all-to-all-done.3 = bf16[1,4,640,2048]{3,1,0,2:T(4,128)(2,1)} async-done(((bf16[1,4,640,2048]{3,1,0,2:T(4,128)(2,1)}), bf16[1,4,640,2048]{3,1,0,2:T(4,128)(2,1)}, u32[]{:S(2)}, u32[]{:S(2)}) %all-to-all-start.3) | async-done | bytes 10485792 | tf_op jit(solution)/shard_map/all_to_all | solution.py:38
  1632.4 38.6 %gather_fusion.1 = f32[1536,2048]{1,0:T(8,128)} fusion(f32[16,160,2048]{2,1,0:T(8,128)} %bitcast.176, s32[1536]{0:T(1024)S(1)} %copy-done), kind=kCustom, calls=%fused_computation.2 | custom fusion | bytes 25178112 | tf_op jit(solution)/shard_map/gather | solution.py:288
  1705.5 27.7 %gather_fusion = f32[1536,512]{1,0:T(8,128)} fusion(f32[16,160,512]{2,1,0:T(8,128)} %convert.36, s32[1536]{0:T(1024)S(1)} %copy-done), kind=kCustom, calls=%fused_computation.1 | custom fusion | bytes 6303744 | tf_op jit(solution)/shard_map/gather | solution.py:228
  1875.0 56.2 %reduce-scatter.43.cloned.1.call-done = bf16[256,704]{0,1:T(8,128)(2,1)} async-done(((bf16[2048,704]{0,1:T(8,128)(2,1)}), bf16[256,704]{0,1:T(8,128)(2,1)}) %reduce-scatter.43.cloned.1.call-update) | async-done | bytes 360464 | tf_op jit(solution)/shard_map/reduce_scatter | solution.py:392
  1933.0 73.0 %reduce-scatter.45.cloned.1.call-done = bf16[256,704]{0,1:T(8,128)(2,1)} async-done(((bf16[2048,704]{0,1:T(8,128)(2,1)}), bf16[256,704]{0,1:T(8,128)(2,1)}) %reduce-scatter.45.cloned.1.call-update) | async-done | bytes 360464 | tf_op jit(solution)/shard_map/reduce_scatter | solution.py:395
  2007.9 73.1 %reduce-scatter.47.cloned.1.call-done = bf16[704,256]{1,0:T(8,128)(2,1)} async-done(((bf16[704,2048]{1,0:T(8,128)(2,1)}), bf16[704,256]{1,0:T(8,128)(2,1)}) %reduce-scatter.47.cloned.1.call-update) | async-done | bytes 360464 | tf_op jit(solution)/shard_map/reduce_scatter | solution.py:401
  2082.9 71.6 %reduce-scatter.49.cloned.1.call-done = bf16[4,1024,352]{1,2,0:T(8,128)(2,1)} async-done(((bf16[4,2048,352]{1,2,0:T(8,128)(2,1)}), bf16[4,1024,352]{1,2,0:T(8,128)(2,1)}) %reduce-scatter.49.cloned.1.call-update) | async-done | bytes 2883600 | tf_op jit(solution)/shard_map/reduce_scatter | solution.py:406
  2159.5 69.3 %reduce-scatter.51.cloned.1.call-done = bf16[4,1024,352]{1,2,0:T(8,128)(2,1)} async-done(((bf16[4,2048,352]{1,2,0:T(8,128)(2,1)}), bf16[4,1024,352]{1,2,0:T(8,128)(2,1)}) %reduce-scatter.51.cloned.1.call-update) | async-done | bytes 2883600 | tf_op jit(solution)/shard_map/reduce_scatter | solution.py:409
  2234.0 68.4 %reduce-scatter.53.cloned.1.call-done = bf16[4,352,1024]{2,1,0:T(8,128)(2,1)} async-done(((bf16[4,352,2048]{2,1,0:T(8,128)(2,1)}), bf16[4,352,1024]{2,1,0:T(8,128)(2,1)}) %reduce-scatter.53.cloned.1.call-update) | async-done | bytes 2883600 | tf_op jit(solution)/shard_map/reduce_scatter | solution.py:412
  2307.7 52.5 %reduce-scatter.41.cloned.1.call-done = bf16[256,16]{0,1:T(8,128)(2,1)} async-done(((bf16[2048,16]{0,1:T(8,128)(2,1)}), bf16[256,16]{0,1:T(8,128)(2,1)}) %reduce-scatter.41.cloned.1.call-update) | async-done | bytes 8208 | tf_op jit(solution)/shard_map/reduce_scatter | solution.py:389
  2388.1 70.2 %reduce-scatter.39.cloned.1.call-done = bf16[512,256]{1,0:T(8,128)(2,1)} async-done(((bf16[512,2048]{1,0:T(8,128)(2,1)}), bf16[512,256]{1,0:T(8,128)(2,1)}) %reduce-scatter.39.cloned.1.call-update) | async-done | bytes 262160 | tf_op jit(solution)/shard_map/reduce_scatter | solution.py:398
  2493.6 62.9 %reduce-scatter.33.cloned.1.call-done = bf16[256,512]{1,0:T(8,128)(2,1)} async-done(((bf16[2048,512]{1,0:T(8,128)(2,1)}), bf16[256,512]{1,0:T(8,128)(2,1)}) %reduce-scatter.33.cloned.1.call-update) | async-done | bytes 262160 | tf_op jit(solution)/shard_map/reduce_scatter | solution.py:377
  2558.2 68.7 %reduce-scatter.35.cloned.1.call-done = bf16[256,512]{1,0:T(8,128)(2,1)} async-done(((bf16[2048,512]{1,0:T(8,128)(2,1)}), bf16[256,512]{1,0:T(8,128)(2,1)}) %reduce-scatter.35.cloned.1.call-update) | async-done | bytes 262160 | tf_op jit(solution)/shard_map/reduce_scatter | solution.py:380
  2628.7 68.9 %reduce-scatter.37.cloned.1.call-done = bf16[256,512]{1,0:T(8,128)(2,1)} async-done(((bf16[2048,512]{1,0:T(8,128)(2,1)}), bf16[256,512]{1,0:T(8,128)(2,1)}) %reduce-scatter.37.cloned.1.call-update) | async-done | bytes 262160 | tf_op jit(solution)/shard_map/reduce_scatter | solution.py:383
  (384 shorter events, 667.1 us)
Async XLA Ops:
  405.9 300.5 %all-to-all-start = ((bf16[4,4,160,2048]{3,2,1,0:T(8,128)(2,1)}), bf16[4,4,160,2048]{3,2,1,0:T(8,128)(2,1)}, u32[]{:S(2)}, u32[]{:S(2)}) async-start(bf16[4,4,160,2048]{3,2,1,0:T(8,128)(2,1)} %bitcast.179), calls=%async_computation.2 | async-start | bytes 20971520 | tf_op jit(solution)/shard_map/all_to_all | solution.py:34
  411.9 250.7 %all-gather.47.cloned.1.call-start = ((), (), s32[]{:S(2)}) async-start(), calls=%async_computation.39 | async-start | bytes 1310720 | tf_op jit(solution)/shard_map/all_gather | solution.py:19
  706.4 228.5 %all-to-all-start.2 = ((bf16[4,4,160,2048]{3,2,1,0:T(8,128)(2,1)}), bf16[4,4,160,2048]{3,2,1,0:T(8,128)(2,1)}, u32[]{:S(2)}, u32[]{:S(2)}) async-start(bf16[4,4,160,2048]{3,2,1,0:T(8,128)(2,1)} %bitcast.178), calls=%async_computation.5 | async-start | bytes 20971520 | tf_op jit(solution)/shard_map/all_to_all | solution.py:34
  712.5 232.5 %all-gather.41.cloned.1.call-start = ((), (), s32[]{:S(2)}) async-start(), calls=%async_computation.35 | async-start | bytes 8650752 | tf_op jit(solution)/shard_map/all_gather | solution.py:129
  713.1 244.1 %all-gather.43.cloned.1.call-start = ((), (), s32[]{:S(2)}) async-start(), calls=%async_computation.36 | async-start | bytes 8650752 | tf_op jit(solution)/shard_map/all_gather | solution.py:130
  713.6 255.6 %all-gather.45.cloned.1.call-start = ((), (), s32[]{:S(2)}) async-start(), calls=%async_computation.37 | async-start | bytes 8650752 | tf_op jit(solution)/shard_map/all_gather | solution.py:131
  1012.5 303.3 %all-to-all-start.1 = ((bf16[1,4,640,2048]{3,1,0,2:T(4,128)(2,1)}), bf16[1,4,640,2048]{3,1,0,2:T(4,128)(2,1)}, u32[]{:S(2)}, u32[]{:S(2)}) async-start(bf16[1,4,640,2048]{3,1,0,2:T(4,128)(2,1)} %copy.180), calls=%async_computation.3 | async-start | bytes 20971520 | tf_op jit(solution)/shard_map/all_to_all | solution.py:38
  1018.5 369.9 %all-gather.35.cloned.1.call-start = ((), (), s32[]{:S(2)}) async-start(), calls=%async_computation.31 | async-start | bytes 3244032 | tf_op jit(solution)/shard_map/all_gather | solution.py:123
  1019.2 372.2 %all-gather.37.cloned.1.call-start = ((), (), s32[]{:S(2)}) async-start(), calls=%async_computation.32 | async-start | bytes 3244032 | tf_op jit(solution)/shard_map/all_gather | solution.py:124
  1019.8 374.4 %all-gather.39.cloned.1.call-start = ((), (), s32[]{:S(2)}) async-start(), calls=%async_computation.33 | async-start | bytes 3244032 | tf_op jit(solution)/shard_map/all_gather | solution.py:126
  1020.5 680.2 %reduce-scatter.23.cloned.1.call-start = ((), (), s32[]{:S(2)}) async-start(), calls=%async_computation.38 | async-start | bytes 13107200 | tf_op jit(solution)/shard_map/reduce_scatter | solution.py:29
  1381.5 233.9 %all-to-all-start.3 = ((bf16[1,4,640,2048]{3,1,0,2:T(4,128)(2,1)}), bf16[1,4,640,2048]{3,1,0,2:T(4,128)(2,1)}, u32[]{:S(2)}, u32[]{:S(2)}) async-start(bf16[1,4,640,2048]{3,1,0,2:T(4,128)(2,1)} %copy.185), calls=%async_computation.6 | async-start | bytes 20971520 | tf_op jit(solution)/shard_map/all_to_all | solution.py:38
  1388.1 368.0 %reduce-scatter.25.cloned.1.call-start = ((), (), s32[]{:S(2)}) async-start(), calls=%async_computation.40 | async-start | bytes 1310720 | tf_op jit(solution)/shard_map/reduce_scatter | solution.py:29
  1808.2 272.8 %reduce-scatter.47.cloned.1.call-start = ((), (), s32[]{:S(2)}) async-start(), calls=%async_computation.52 | async-start | bytes 3244032 | tf_op jit(solution)/shard_map/reduce_scatter | solution.py:401
  1810.8 343.6 %reduce-scatter.49.cloned.1.call-start = ((), (), s32[]{:S(2)}) async-start(), calls=%async_computation.53 | async-start | bytes 8650752 | tf_op jit(solution)/shard_map/reduce_scatter | solution.py:406
  1822.8 406.0 %reduce-scatter.51.cloned.1.call-start = ((), (), s32[]{:S(2)}) async-start(), calls=%async_computation.54 | async-start | bytes 8650752 | tf_op jit(solution)/shard_map/reduce_scatter | solution.py:409
  1835.0 467.3 %reduce-scatter.53.cloned.1.call-start = ((), (), s32[]{:S(2)}) async-start(), calls=%async_computation.55 | async-start | bytes 8650752 | tf_op jit(solution)/shard_map/reduce_scatter | solution.py:412
  1847.2 512.9 %reduce-scatter.41.cloned.1.call-start = ((), (), s32[]{:S(2)}) async-start(), calls=%async_computation.49 | async-start | bytes 73728 | tf_op jit(solution)/shard_map/reduce_scatter | solution.py:389
  1848.2 538.5 %reduce-scatter.31.cloned.1.call-start = ((), (), s32[]{:S(2)}) async-start(), calls=%async_computation.44 | async-start | bytes 1310720 | tf_op jit(solution)/shard_map/reduce_scatter | solution.py:29
  1859.5 598.8 %reduce-scatter.39.cloned.1.call-start = ((), (), s32[]{:S(2)}) async-start(), calls=%async_computation.48 | async-start | bytes 2359296 | tf_op jit(solution)/shard_map/reduce_scatter | solution.py:398
  1862.9 628.3 %reduce-scatter.21.cloned.1.call-start = ((), (), s32[]{:S(2)}) async-start(), calls=%async_computation.34 | async-start | bytes 1310720 | tf_op jit(solution)/shard_map/reduce_scatter | solution.py:29
  1867.1 689.3 %reduce-scatter.33.cloned.1.call-start = ((), (), s32[]{:S(2)}) async-start(), calls=%async_computation.45 | async-start | bytes 2359296 | tf_op jit(solution)/shard_map/reduce_scatter | solution.py:377
  1869.3 757.6 %reduce-scatter.35.cloned.1.call-start = ((), (), s32[]{:S(2)}) async-start(), calls=%async_computation.46 | async-start | bytes 2359296 | tf_op jit(solution)/shard_map/reduce_scatter | solution.py:380
  1871.5 826.1 %reduce-scatter.37.cloned.1.call-start = ((), (), s32[]{:S(2)}) async-start(), calls=%async_computation.47 | async-start | bytes 2359296 | tf_op jit(solution)/shard_map/reduce_scatter | solution.py:383
  (85 other events, 5114.2 us)
Sparse Core Ops, SparseCore 0:
  56.8 49.2 all-gather.24
  108.2 47.7 all-gather.20
  158.0 47.7 all-gather.26
  207.8 28.6 all-gather.22
  238.5 26.2 all-gather.28
  266.8 50.5 all-gather.30
  1021.5 200.7 all-gather.34
  1224.3 84.5 all-gather.36
  1311.1 58.9 all-gather.38
  1372.7 83.4 reduce-scatter.22
  1800.8 27.1 reduce-scatter.26
  1830.2 25.7 reduce-scatter.28
  1860.2 70.8 reduce-scatter.42
  1934.5 71.4 reduce-scatter.44
  2009.6 71.3 reduce-scatter.46
  2083.9 70.5 reduce-scatter.48
  2157.4 71.3 reduce-scatter.50
  2231.0 71.3 reduce-scatter.52
  2306.4 53.6 reduce-scatter.40
  2362.7 23.9 reduce-scatter.30
  2390.0 68.2 reduce-scatter.38
  2488.7 67.6 reduce-scatter.32
  2560.2 66.6 reduce-scatter.34
  2630.9 66.7 reduce-scatter.36
  (7 shorter events, 132.1 us)
Sparse Core Ops, SparseCore 1:
  714.6 73.8 all-gather.40
  789.9 74.3 all-gather.42
  865.7 74.3 all-gather.44
where the time goes:
time: 2720 us; the launch traced here: 2710 us
  waiting for transfers between devices  1770 us (65%)
  blocking collectives  349 us (13%)
  local copies, waits for them, and re-layouts  263 us (10%)
  matrix products  180 us (7%)
  other arithmetic  99.6 us (4%)
  starting transfers between devices  27.5 us (1%)
    all_to_all x2, waiting for transfers between devices, to_sources(): lax.all_to_all(slot_rows.astype(jnp.bfloat16), 'ctx', split_axis=2, conca...  510 us
    all_gather x1, blocking collectives, per_device(): lax.all_gather(router, ('fsdp', 'ctx'), axis=0, tiled=True)  250 us
    all_to_all x2, waiting for transfers between devices, to_owners(): lax.all_to_all(slot_rows, 'ctx', split_axis=0, concat_axis=2, tiled=True)  209 us
    reduce_scatter x1, waiting for transfers between devices, per_device(): lax.psum_scatter(shared_down_grad.astype(jnp.bfloat16), ('fsdp', 'ctx'),...  73.1 us
    reduce_scatter x1, waiting for transfers between devices, per_device(): lax.psum_scatter(shared_up_grad.astype(jnp.bfloat16), ('fsdp', 'ctx'), sc...  73 us
    reduce_scatter x1, waiting for transfers between devices, per_device(): lax.psum_scatter(egate_grad.astype(jnp.bfloat16), 'fsdp', scatter_dimensi...  71.6 us
    reduce_scatter x1, waiting for transfers between devices, per_device(): lax.psum_scatter(wo_grad.astype(jnp.bfloat16), ('fsdp', 'ctx'), scatter_d...  70.2 us
    reduce_scatter x1, waiting for transfers between devices, per_device(): lax.psum_scatter(expert_up_weight_grad.astype(jnp.bfloat16), 'fsdp', scat...  69.3 us
  transfers between devices with their start and end apart: 38, of which 26 were waited for; matrix products, arithmetic and copies ran while one was open for 16% of the time, Pallas kernels for 0%

commit v1 on v0

--- a/solution.py
+++ b/solution.py
@@ -432,6 +432,303 @@
     )
 
 
+def per_device_seq(
+    hidden_in,
+    positions,
+    chosen,
+    out_grad,
+    attn_gain,
+    w_query,
+    w_key,
+    w_value,
+    w_out,
+    moe_gain,
+    router,
+    shared_gate,
+    shared_up,
+    shared_down,
+    expert_gate,
+    expert_up,
+    expert_down,
+):
+    bf, f32 = jnp.bfloat16, jnp.float32
+    f_rank, c_rank, t_rank = (lax.axis_index(name) for name in ("fsdp", "ctx", "tp"))
+    n_f, n_c, n_t = (lax.axis_size(name) for name in ("fsdp", "ctx", "tp"))
+    rows, quarter = hidden_in.shape
+    width = quarter * n_t
+    part = w_query.shape[0]
+    seq = rows * n_c
+    total = seq * n_f
+    n_exp = router.shape[1]
+    exp_dev = n_exp // n_c
+    mine = exp_dev // n_f
+    ffe = expert_gate.shape[2]
+    shared_rows = shared_gate.shape[1] // (n_f * n_c)
+    group = ("fsdp", "ctx")
+    every = ("fsdp", "ctx", "tp")
+
+    def nt(left, right):
+        return lax.dot_general(left, right, (((1,), (1,)), ((), ())), preferred_element_type=f32)
+
+    def tn(left, right):
+        return lax.dot_general(left, right, (((0,), (0,)), ((), ())), preferred_element_type=f32)
+
+    def nn(left, right):
+        return jnp.dot(left, right, preferred_element_type=f32)
+
+    def gather_seq(block):
+        got = lax.all_gather(block, ("ctx", "tp"), axis=0, tiled=False)
+        return got.reshape(n_c, n_t, rows, quarter).swapaxes(1, 2).reshape(seq, width)
+
+    def gather_all(block):
+        got = lax.all_gather(block, every, axis=0, tiled=False)
+        return got.reshape(n_f * n_c, n_t, rows, quarter).swapaxes(1, 2).reshape(total, width)
+
+    def scatter_seq(partial):
+        blocks = partial.astype(bf).reshape(n_c, rows, n_t, quarter).swapaxes(1, 2)
+        return lax.psum_scatter(
+            blocks.reshape(n_c * n_t, rows, quarter), ("ctx", "tp"), scatter_dimension=0, tiled=True
+        )[0].astype(f32)
+
+    def scatter_all(partial):
+        blocks = partial.astype(bf).reshape(n_f * n_c, rows, n_t, quarter).swapaxes(1, 2)
+        return lax.psum_scatter(
+            blocks.reshape(n_f * n_c * n_t, rows, quarter), every, scatter_dimension=0, tiled=True
+        )[0].astype(f32)
+
+    def by_head(weight):
+        per_head = weight.T.reshape(n_c, HD, part)
+        return jnp.broadcast_to(per_head[None], (n_f, n_c, HD, part)).reshape(n_f * n_c, HD, part)
+
+    wo_heads = jnp.broadcast_to(w_out.reshape(1, n_c, HD, part), (n_f, n_c, HD, part))
+    small = jnp.concatenate([attn_gain[None], moe_gain[None], router.T], axis=0)
+    packed = jnp.concatenate(
+        [
+            by_head(w_query),
+            by_head(w_key),
+            by_head(w_value),
+            wo_heads.reshape(n_f * n_c, HD, part),
+            shared_gate.T.reshape(n_f * n_c, shared_rows, part),
+            shared_up.T.reshape(n_f * n_c, shared_rows, part),
+            shared_down.reshape(n_f * n_c, shared_rows, part),
+            jnp.broadcast_to(small[None], (n_f * n_c,) + small.shape),
+        ],
+        axis=1,
+    )
+    arrived = lax.all_to_all(packed, group, split_axis=0, concat_axis=0, tiled=True)
+    dense = arrived.swapaxes(0, 1).reshape(packed.shape[1], width)
+    w_qkv = dense[: 3 * HD]
+    wo = dense[3 * HD : 4 * HD]
+    at = 4 * HD
+    sg, su, sd = (dense[at + i * shared_rows : at + (i + 1) * shared_rows] for i in range(3))
+    at = at + 3 * shared_rows
+    gain_one = dense[at].astype(f32)
+    gain_two = dense[at + 1].astype(f32)
+    router_t = dense[at + 2 : at + 2 + n_exp]
+    swap = [(i, n_f - 1 - i) for i in range(n_f)]
+
+    def whole_experts(weight):
+        kept = lax.dynamic_slice_in_dim(weight, f_rank * mine, mine, 0)
+        given = lax.dynamic_slice_in_dim(weight, (n_f - 1 - f_rank) * mine, mine, 0)
+        got = lax.ppermute(given, "fsdp", swap)
+        low = jnp.where(f_rank == 0, kept, got)
+        high = jnp.where(f_rank == 0, got, kept)
+        return jnp.concatenate([low, high], axis=2).reshape(mine * ffe, width)
+
+    eg = whole_experts(expert_gate.swapaxes(1, 2))
+    eu = whole_experts(expert_up.swapaxes(1, 2))
+    ed = whole_experts(expert_down)
+
+    hidden_seq = gather_seq(hidden_in)
+    grad_all = gather_all(out_grad)
+    pos_seq = lax.all_gather(positions, "ctx", axis=0, tiled=True)
+    chosen_all = lax.all_gather(chosen, group, axis=0, tiled=True)
+    resid_in = hidden_in.astype(f32)
+    hidden_f = hidden_seq.astype(f32)
+    scale_seq = lax.rsqrt(jnp.mean(hidden_f * hidden_f, axis=1, keepdims=True) + EPS)
+    normed_in = (hidden_f * scale_seq * gain_one[None, :]).astype(bf)
+    qkv = nt(normed_in, w_qkv)
+    half = HD // 2
+    inverse = 10000.0 ** (-jnp.arange(half, dtype=f32) * 2.0 / HD)
+    angles = pos_seq.astype(f32)[:, None] * inverse[None, :]
+    cosine, sine = jnp.cos(angles), jnp.sin(angles)
+
+    def rotate(values, sign):
+        low, high = values[:, :half], values[:, half:]
+        return jnp.concatenate(
+            [low * cosine - sign * high * sine, high * cosine + sign * low * sine], axis=1
+        )
+
+    query_b = rotate(qkv[:, :HD], 1.0).astype(bf)
+    key_b = rotate(qkv[:, HD : 2 * HD], 1.0).astype(bf)
+    value_b = qkv[:, 2 * HD :].astype(bf)
+    scale_att = HD ** (-0.5)
+    visible = jnp.arange(seq)[None, :] <= jnp.arange(seq)[:, None]
+    scores = jnp.where(visible, nt(query_b, key_b) * scale_att, NEG_BIG)
+    top = jnp.max(scores, axis=1, keepdims=True)
+    weights = jnp.exp(scores - top)
+    norm = jnp.sum(weights, axis=1, keepdims=True)
+    probs = weights / norm
+    probs_b = probs.astype(bf)
+    heads_f = nn(probs_b, value_b)
+    heads_b = heads_f.astype(bf)
+    resid_mid = resid_in + scatter_seq(nn(heads_b, wo))
+
+    resid_all = gather_all(resid_mid.astype(bf)).astype(f32)
+    scale_all = lax.rsqrt(jnp.mean(resid_all * resid_all, axis=1, keepdims=True) + EPS)
+    moe_in = (resid_all * scale_all * gain_two[None, :]).astype(bf)
+    probs_all = jax.nn.softmax(nt(moe_in, router_t), axis=1)
+    picked = jnp.sum(
+        (chosen_all[:, :, None] == jnp.arange(n_exp)[None, None, :]).astype(f32), axis=1
+    )
+    first = c_rank * exp_dev + f_rank * mine
+    mine_hot = (
+        jnp.arange(n_exp)[:, None] == first + jnp.arange(mine)[None, :]
+    ).astype(f32)
+    gate_mine = jnp.sum((probs_all * picked)[:, :, None] * mine_hot[None], axis=1)
+    gate_cols = jnp.concatenate(
+        [
+            jnp.broadcast_to(gate_mine[:, :, None], (total, mine, ffe)).reshape(total, mine * ffe),
+            jnp.ones((total, shared_rows), f32),
+        ],
+        axis=1,
+    )
+    wg = jnp.concatenate([eg, sg], axis=0)
+    wu = jnp.concatenate([eu, su], axis=0)
+    wd = jnp.concatenate([ed, sd], axis=0)
+    pre_a = nt(moe_in, wg)
+    pre_b = nt(moe_in, wu)
+    sig = jax.nn.sigmoid(pre_a)
+    silu_a = pre_a * sig
+    act = (silu_a * pre_b).astype(bf).astype(f32)
+    act_g = (act * gate_cols).astype(bf)
+    moe_part = nn(act_g, wd)
+    dact = nt(grad_all, wd)
+    gate_part = jnp.sum(
+        (act * dact)[:, : mine * ffe].reshape(total, mine, ffe), axis=2
+    )
+    p_part = jnp.sum(gate_part[:, None, :] * mine_hot[None], axis=2) * picked
+    dact_g = dact * gate_cols
+    da = (dact_g * pre_b * (sig * (1.0 + pre_a * (1.0 - sig)))).astype(bf)
+    db = (dact_g * silu_a).astype(bf)
+    back_part = nn(da, wg) + nn(db, wu)
+    p_grad = lax.psum(p_part, every)
+    back_q = scatter_all(back_part)
+    layer_out = (resid_mid + scatter_all(moe_part)).astype(bf)
+    logit_grad = (
+        probs_all * (p_grad - jnp.sum(probs_all * p_grad, axis=1, keepdims=True))
+    ).astype(bf)
+    block = f_rank * n_c + c_rank
+    own_logit = lax.dynamic_slice_in_dim(logit_grad, block * rows, rows, 0)
+    router_q = lax.dynamic_slice_in_dim(router_t, t_rank * quarter, quarter, 1)
+    moe_in_grad = back_q + nn(own_logit, router_q)
+    moe_cols = lax.dynamic_slice_in_dim(moe_in, block * part, part, 1)
+    router_grad = tn(moe_cols, logit_grad)
+    gwd = tn(act_g, grad_all)
+    gwg = tn(da, moe_in)
+    gwu = tn(db, moe_in)
+
+    def norm_back_rows(values, row_scale, gain_q, grad_normed):
+        local = jnp.sum(grad_normed * gain_q[None, :] * values, axis=1)
+        row_total = lax.psum(local, "tp")
+        gain_local = jnp.sum(grad_normed * values * row_scale, axis=0)
+        back = row_scale * gain_q[None, :] * grad_normed - values * (
+            row_scale**3 * row_total[:, None] / width
+        )
+        return back, gain_local
+
+    def own_rows(values):
+        return lax.dynamic_slice_in_dim(values, c_rank * rows, rows, 0)
+
+    gain_q1 = lax.dynamic_slice_in_dim(gain_one, t_rank * quarter, quarter)
+    gain_q2 = lax.dynamic_slice_in_dim(gain_two, t_rank * quarter, quarter)
+    scale_two = lax.dynamic_slice_in_dim(scale_all, block * rows, rows, 0)
+    mid_back, gain_two_local = norm_back_rows(resid_mid, scale_two, gain_q2, moe_in_grad)
+    mid_grad = out_grad.astype(f32) + mid_back
+    mid_seq = gather_seq(mid_grad.astype(bf))
+
+    heads_grad = nt(mid_seq, wo).astype(bf)
+    gwo = tn(heads_b, mid_seq)
+    delta = jnp.sum(heads_grad.astype(f32) * heads_f, axis=1, keepdims=True)
+    value_grad = tn(probs_b, heads_grad)
+    score_grad = (probs * (nt(heads_grad, value_b) - delta)).astype(bf)
+    query_grad = nn(score_grad, key_b) * scale_att
+    key_grad = tn(score_grad, query_b) * scale_att
+    dqkv = jnp.concatenate(
+        [rotate(query_grad, -1.0).astype(bf), rotate(key_grad, -1.0).astype(bf), value_grad.astype(bf)],
+        axis=1,
+    )
+    in_back = scatter_seq(nn(dqkv, w_qkv))
+    gqkv = tn(dqkv, normed_in)
+    scale_one = own_rows(scale_seq)
+    first_back, gain_one_local = norm_back_rows(resid_in, scale_one, gain_q1, in_back)
+    input_grad = mid_grad + first_back
+
+    def placed(gain_local):
+        return lax.dynamic_update_slice_in_dim(
+            jnp.zeros((width,), f32), gain_local, t_rank * quarter, 0
+        )
+
+    gains = lax.psum(jnp.stack([placed(gain_one_local), placed(gain_two_local)]), every)
+    gains = lax.dynamic_slice_in_dim(gains, block * part, part, 1)
+
+    def to_owner(grad_rows):
+        sent = grad_rows.astype(bf).reshape(-1, n_f * n_c, part).swapaxes(0, 1)
+        return lax.all_to_all(sent, group, split_axis=0, concat_axis=0, tiled=True).astype(f32)
+
+    attn_sent = jnp.concatenate([gqkv, gwo], axis=0)
+    attn_back = to_owner(attn_sent).reshape(n_f, n_c, 4, HD, part).sum(axis=0)
+    shared_sent = jnp.concatenate([g[mine * ffe :] for g in (gwg, gwu, gwd)], axis=0)
+    shared_back = to_owner(shared_sent).reshape(n_f * n_c, 3, shared_rows, part)
+
+    def head_cols(i):
+        return attn_back[:, i].reshape(n_c * HD, part)
+
+    def shared_cols(i):
+        return shared_back[:, i].reshape(n_f * n_c * shared_rows, part)
+
+    def expert_owner(grad_rows):
+        grad_rows = grad_rows[: mine * ffe].reshape(mine, ffe, width)
+        piece = width // n_f
+        kept = lax.dynamic_slice_in_dim(grad_rows, f_rank * piece, piece, 2)
+        given = lax.dynamic_slice_in_dim(grad_rows, (n_f - 1 - f_rank) * piece, piece, 2)
+        got = lax.ppermute(given.astype(bf), "fsdp", swap).astype(f32)
+        return jnp.concatenate(
+            [jnp.where(f_rank == 0, kept, got), jnp.where(f_rank == 0, got, kept)], axis=0
+        )
+
+    return (
+        layer_out,
+        input_grad,
+        gains[0],
+        head_cols(0).T,
+        head_cols(1).T,
+        head_cols(2).T,
+        head_cols(3),
+        gains[1],
+        router_grad,
+        shared_cols(0).T,
+        shared_cols(1).T,
+        shared_cols(2),
+        expert_owner(gwg).swapaxes(1, 2),
+        expert_owner(gwu).swapaxes(1, 2),
+        expert_owner(gwd),
+    )
+
+
+def one_head_each(mesh, args):
+    n_f, n_c, n_t = (mesh.shape[name] for name in ("fsdp", "ctx", "tp"))
+    heads = args[5].shape[1] // HD
+    experts = args[10].shape[1]
+    return (
+        n_f == 2
+        and n_t == 4
+        and heads == n_c * n_t
+        and experts % (n_f * n_c) == 0
+        and args[11].shape[1] % (8 * n_f * n_c * n_t) == 0
+    )
+
+
 def solution(mesh):
     placed = (
         P(("fsdp", "ctx"), "tp"),
@@ -452,8 +749,10 @@
         P("ctx", "fsdp", "tp"),
         P("ctx", "tp", "fsdp"),
     )
-    return jax.shard_map(
-        per_device,
+    def run(*args):
+        body = per_device_seq if one_head_each(mesh, args) else per_device
+        return jax.shard_map(
+        body,
         mesh=mesh,
         in_specs=placed,
         out_specs=(
@@ -474,4 +773,6 @@
             P("ctx", "tp", "fsdp"),
         ),
         check_vma=False,
-    )
+    )(*args)
+
+    return run

time: 2720 us -> 1270 us (0.47)
  waiting for transfers between devices: 1770 us -> 532 us
  blocking collectives: 349 us -> 184 us
  matrix products: 180 us -> 133 us
    all_to_all x4 -> x3, waiting for transfers between devices: 720 us -> 23.1 us  [the longest x1 23.1 us: per_device_seq(): lax.all_to_all(packed, group, split_axis=0, concat_axis=0, tiled=True)]
    reduce_scatter x18 -> x4, waiting for transfers between devices: 768 us -> 237 us  [the longest x2 148 us: scatter_all(): lax.psum_scatter(blocks.reshape(n_f * n_c * n_t, rows, quarter), every, s...]
    all_gather x16 -> x4, waiting for transfers between devices: 276 us -> 47.4 us  [the longest x2 47.4 us: gather_seq(): got = lax.all_gather(block, ('ctx', 'tp'), axis=0, tiled=False)]
    all_gather x3 -> x2, blocking collectives: 290 us -> 103 us  [the longest x1 72.1 us: per_device_seq(): pos_seq = lax.all_gather(positions, 'ctx', axis=0, tiled=True)]
    ppermute x0 -> x6, waiting for transfers between devices: none -> 168 us  [the longest x3 93.2 us: expert_owner(): got = lax.ppermute(given.astype(bf), 'fsdp', swap).astype(f32)]
    gather x2 -> x0, local copies, waits for them, and re-layouts: 66.4 us -> none  [the longest x1 38.6 us: per_device(): back_slots[flat_exp, slot_of].reshape(tok_rows, TOPK, model_width)]
    reshape x4 -> x7, local copies, waits for them, and re-layouts: 20.4 us -> 81.4 us  [the longest x3 31.5 us: scatter_seq(): blocks = partial.astype(bf).reshape(n_c, rows, n_t, quarter).swapaxes(1, 2)]
    psum x0 -> x1, waiting for transfers between devices: none -> 55.3 us  [per_device_seq(): p_grad = lax.psum(p_part, every)]
  transfers between devices with their start and end apart: 38 -> 18, of which waited for: 26 -> 10; matrix products, arithmetic and copies ran while one was open for 16% -> 23% of each run, Pallas kernels for 0% -> 0%
where the time goes in v1:
time: 1270 us; the launch traced here: 1260 us
  waiting for transfers between devices  532 us (42%)
  local copies, waits for them, and re-layouts  247 us (19%)
  blocking collectives  184 us (14%)
  matrix products  133 us (10%)
  other arithmetic  121 us (10%)
  starting transfers between devices  24.7 us (2%)
  between operations  17.2 us (1%)
    reduce_scatter x2, waiting for transfers between devices, scatter_all(): lax.psum_scatter(blocks.reshape(n_f * n_c * n_t, rows, quarter), every, s...  148 us
    ppermute x3, waiting for transfers between devices, expert_owner(): got = lax.ppermute(given.astype(bf), 'fsdp', swap).astype(f32)  93.2 us
    reduce_scatter x2, waiting for transfers between devices, scatter_seq(): lax.psum_scatter(blocks.reshape(n_c * n_t, rows, quarter), ('ctx', 'tp'),...  88.8 us
    ppermute x3, waiting for transfers between devices, whole_experts(): got = lax.ppermute(given, 'fsdp', swap)  74.7 us
    all_gather x1, blocking collectives, per_device_seq(): pos_seq = lax.all_gather(positions, 'ctx', axis=0, tiled=True)  72.1 us
    unnamed x197, local copies, waits for them, and re-layouts  65.9 us
    psum x1, waiting for transfers between devices, per_device_seq(): p_grad = lax.psum(p_part, every)  55.3 us
    dot_general x8, matrix products, nn(): return jnp.dot(left, right, preferred_element_type=f32)  55 us
  transfers between devices with their start and end apart: 18, of which 10 were waited for; matrix products, arithmetic and copies ran while one was open for 23% of the time, Pallas kernels for 0%

profile of v1, /device:TPU:0, one launch (start us, length us, event | category | flops | bytes accessed | tf_op | source)
XLA Modules:
  0.0 1258.9 jit_solution(4721971823185913596)
XLA Ops:
  27.9 72.1 %all-gather.4 = s32[4,1,256]{2,1,0:T(1,128)S(1)} all-gather(s32[1,1,256]{2,1,0:T(1,128)S(1)} %bitcast.347), channel_id=1, replica_groups=mesh['fsdp'=2,'ctx'=4,'tp'=4] {'ctx'}, dimensions={0}, use_global_device_ids=true | all-gather | bytes 5120 | tf_op jit(solution)/shard_map/all_gather | solution.py:544
  100.1 23.1 %all-to-all-done = bf16[8,794,256]{2,1,0:T(8,128)(2,1)S(1)} async-done(((bf16[8,794,256]{2,1,0:T(8,128)(2,1)}), bf16[8,794,256]{2,1,0:T(8,128)(2,1)S(1)}, u32[]{:S(2)}, u32[]{:S(2)}) %all-to-all-start) | async-done | bytes 3252256 | tf_op jit(solution)/shard_map/all_to_all | solution.py:518
  156.9 18.5 %reshape.338 = bf16[4,256,4,512]{3,2,1,0:T(4,128)(2,1)} reshape(bf16[1024,2048]{1,0:T(8,128)(2,1)} %convolution_convert_fusion.2) | data formatting | bytes 8388608 | tf_op jit(solution)/shard_map/reshape | solution.py:488
  181.3 88.8 %reduce-scatter.5.cloned.1.call-done = bf16[1,256,512]{2,1,0:T(8,128)(2,1)} async-done(((bf16[16,256,512]{2,1,0:T(8,128)(2,1)}), bf16[1,256,512]{2,1,0:T(8,128)(2,1)}) %reduce-scatter.5.cloned.1.call-update) | async-done | bytes 262160 | tf_op jit(solution)/shard_map/reduce_scatter | solution.py:489
  280.4 30.7 %all_gather.35 = s32[2048,6]{0,1:T(8,128)S(1)} all-gather(s32[256,6]{0,1:T(8,128)S(1)} %copy-done.73), channel_id=1, replica_groups=mesh['fsdp'=2,'ctx'=4,'tp'=4] {'fsdp','ctx'}, dimensions={0}, use_global_device_ids=true | all-gather | bytes 55296 | tf_op jit(solution)/shard_map/all_gather | solution.py:545
  314.8 40.4 %collective-permute-done.1 = bf16[2,352,1024]{2,1,0:T(8,128)(2,1)} collective-permute-done((bf16[2,352,1024]{2,1,0:T(8,128)(2,1)}, bf16[2,352,1024]{2,1,0:T(8,128)(2,1)}, u32[]{:S(2)}, u32[]{:S(2)}) %collective-permute-start.1) | collective-permute-done | bytes 1441824 | tf_op jit(solution)/shard_map/ppermute | solution.py:533
  358.5 34.3 %collective-permute-done = bf16[2,352,1024]{2,1,0:T(8,128)(2,1)} collective-permute-done((bf16[2,352,1024]{2,1,0:T(8,128)(2,1)}, bf16[2,352,1024]{2,1,0:T(8,128)(2,1)}, u32[]{:S(2)}, u32[]{:S(2)}) %collective-permute-start) | collective-permute-done | bytes 1441824 | tf_op jit(solution)/shard_map/ppermute | solution.py:533
  400.4 14.9 %copy.178 = bf16[8,4,256,512]{2,0,3,1:T(8,128)(2,1)} copy(bf16[8,4,256,512]{3,2,1,0:T(8,128)(2,1)} %bitcast.268) | data formatting | bytes 16777216 | tf_op jit(solution)/shard_map/reshape | solution.py:485
  453.3 20.2 %copy.171 = f32[8,4,256,512]{2,0,3,1:T(8,128)} copy(f32[8,4,256,512]{3,2,1,0:T(8,128)} %bitcast_convert_fusion) | data formatting | bytes 33554432 | tf_op jit(solution)/shard_map/convert_element_type | solution.py:577
  517.7 13.6 %fusion.4 = (f32[2048,792]{0,1:T(8,128)S(1)}, f32[2048,792]{0,1:T(8,128)}) fusion(f32[2048,792]{0,1:T(8,128)} %fusion.8, bf16[2048,2048]{0,1:T(8,128)(2,1)} %copy-done.7, bf16[88,2048]{1,0:T(8,128)(2,1)S(1)} %copy.197, bf16[704,2048]{1,0:T(8,128)(2,1)} %bitcast.280), kind=kOutput, calls=%fused_computation.36 | convolution fusion | flops 6661619712 | bytes 31096832 | tf_op jit(solution)/shard_map/dot_general | solution.py:471
  540.2 13.7 %multiply_convert_fusion.4 = (bf16[2048,792]{0,1:T(8,128)(2,1)S(1)}, bf16[2048,792]{0,1:T(8,128)(2,1)}, bf16[2048,792]{0,1:T(8,128)(2,1)}) fusion(f32[2048,792]{0,1:T(8,128)} %convolution_bitcast_fusion, f32[2048,704]{0,1:T(8,128)S(1)} %bitcast.240, f32[2048,792]{0,1:T(8,128)} %fusion.8, f32[2048,792]{0,1:T(8,128)} %get-tuple-element.67, f32[2048,792]{0,1:T(8,128)} %copy-done.2), kind=kLoop, calls=%fused_computation.8 | loop fusion | flops 25952256 | bytes 41451520 | tf_op jit(solution)/shard_map/convert_element_type | solution.py:613
  554.0 16.0 %fusion.7 = f32[2048,2048]{1,0:T(8,128)} fusion(bf16[2048,792]{0,1:T(8,128)(2,1)} %get-tuple-element.24, bf16[88,2048]{1,0:T(8,128)(2,1)S(1)} %copy-done.51, bf16[704,2048]{1,0:T(8,128)(2,1)} %bitcast.282), kind=kOutput, calls=%fused_computation.49 | convolution fusion | flops 6650265600 | bytes 23265280 | tf_op jit(solution)/shard_map/dot_general | solution.py:477
  570.0 14.7 %add_convert_fusion = bf16[2048,2048]{1,0:T(8,128)(2,1)} fusion(f32[2048,2048]{1,0:T(8,128)} %fusion.7, bf16[2048,792]{0,1:T(8,128)(2,1)S(1)} %get-tuple-element.23, bf16[88,2048]{1,0:T(8,128)(2,1)S(1)} %copy.197, bf16[704,2048]{1,0:T(8,128)(2,1)S(1)} %bitcast.281), kind=kOutput, calls=%fused_computation | convolution fusion | flops 6658654208 | bytes 31653888 | tf_op jit(solution)/shard_map/dot_general | solution.py:477
  584.8 14.7 %reshape.348 = bf16[8,256,4,512]{3,2,1,0:T(4,128)(2,1)} reshape(bf16[2048,2048]{1,0:T(8,128)(2,1)} %add_convert_fusion) | data formatting | bytes 16777216 | tf_op jit(solution)/shard_map/reshape | solution.py:494
  608.6 55.3 %all-reduce.3.cloned.1.call-done = f32[2048,16]{0,1:T(8,128)} async-done(((f32[2048,16]{0,1:T(8,128)}), f32[2048,16]{0,1:T(8,128)}) %all-reduce.3.cloned.1.call-update) | async-done | bytes 131088 | tf_op jit(solution)/shard_map/psum | solution.py:615
  665.8 148.2 %reduce-scatter.9.cloned.1.call-done = bf16[1,256,512]{2,1,0:T(8,128)(2,1)} async-done(((bf16[32,256,512]{2,1,0:T(8,128)(2,1)}), bf16[1,256,512]{2,1,0:T(8,128)(2,1)}) %reduce-scatter.9.cloned.1.call-update) | async-done | bytes 262160 | tf_op jit(solution)/shard_map/reduce_scatter | solution.py:495
  822.7 47.4 %all-gather.16.cloned.1.call-done = bf16[4096,512]{1,0:T(8,128)(2,1)} async-done(((bf16[256,512]{1,0:T(8,128)(2,1)}), bf16[4096,512]{1,0:T(8,128)(2,1)}) %all-gather.16.cloned.1.call-update) | async-done | bytes 4194320 | tf_op jit(solution)/shard_map/all_gather | solution.py:480
  909.9 13.4 %convolution_convert_fusion = bf16[2048,2048]{1,0:T(8,128)(2,1)} fusion(bf16[2048,792]{0,1:T(8,128)(2,1)} %get-tuple-element.33, bf16[88,2048]{1,0:T(8,128)(2,1)} %copy-done.49, bf16[704,2048]{1,0:T(8,128)(2,1)S(1)} %bitcast.279), kind=kOutput, calls=%fused_computation.7 | convolution fusion | flops 6654459904 | bytes 14876672 | tf_op jit(solution)/shard_map/dot_general | solution.py:477
  923.3 14.8 %reshape.344 = bf16[8,256,4,512]{3,2,1,0:T(4,128)(2,1)} reshape(bf16[2048,2048]{1,0:T(8,128)(2,1)} %convolution_convert_fusion) | data formatting | bytes 16777216 | tf_op jit(solution)/shard_map/reshape | solution.py:494
  1047.8 40.2 %collective-permute-done.3 = bf16[2,352,1024]{2,1,0:T(8,128)(2,1)} collective-permute-done((bf16[2,352,1024]{2,1,0:T(8,128)(2,1)}, bf16[2,352,1024]{2,1,0:T(8,128)(2,1)}, u32[]{:S(2)}, u32[]{:S(2)}) %collective-permute-start.3) | collective-permute-done | bytes 1441824 | tf_op jit(solution)/shard_map/ppermute | solution.py:695
  1095.1 23.9 %collective-permute-done.5 = bf16[2,352,1024]{2,1,0:T(8,128)(2,1)} collective-permute-done((bf16[2,352,1024]{2,1,0:T(8,128)(2,1)S(1)}, bf16[2,352,1024]{2,1,0:T(8,128)(2,1)}, u32[]{:S(2)}, u32[]{:S(2)}) %collective-permute-start.5) | collective-permute-done | bytes 1441824 | tf_op jit(solution)/shard_map/ppermute | solution.py:695
  1119.0 29.1 %collective-permute-done.4 = bf16[2,352,1024]{2,1,0:T(8,128)(2,1)} collective-permute-done((bf16[2,352,1024]{2,1,0:T(8,128)(2,1)}, bf16[2,352,1024]{2,1,0:T(8,128)(2,1)}, u32[]{:S(2)}, u32[]{:S(2)}) %collective-permute-start.4) | collective-permute-done | bytes 1441824 | tf_op jit(solution)/shard_map/ppermute | solution.py:695
  1173.0 37.3 %psum.30 = f32[256,1]{0,1:T(1,128)S(1)} all-reduce(f32[256,1]{0,1:T(1,128)S(1)} %bitcast.346), channel_id=1, replica_groups=mesh['fsdp'=2,'ctx'=4,'tp'=4] {'tp'}, use_global_device_ids=true, to_apply=%region_20.21 | all-reduce | flops 256 | bytes 2048 | tf_op jit(solution)/shard_map/psum | solution.py:633
  1210.3 38.1 %psum.31 = f32[2,2048]{1,0:T(2,128)S(1)} all-reduce(f32[2,2048]{1,0:T(2,128)S(1)} %pad_maximum_fusion.19), channel_id=1, replica_groups=mesh['fsdp'=2,'ctx'=4,'tp'=4] {'fsdp','ctx','tp'}, use_global_device_ids=true, to_apply=%region_23.24 | all-reduce | flops 4096 | bytes 32768 | tf_op jit(solution)/shard_map/psum | solution.py:672
  (367 shorter events, 378.3 us)
Async XLA Ops:
  8.0 125.4 %all-gather.10.cloned.1.call-start = ((), (), s32[]{:S(2)}) async-start(), calls=%async_computation.12 | async-start | bytes 4456448 | tf_op jit(solution)/shard_map/all_gather | solution.py:480
  20.6 102.5 %all-to-all-start = ((bf16[8,794,256]{2,1,0:T(8,128)(2,1)}), bf16[8,794,256]{2,1,0:T(8,128)(2,1)S(1)}, u32[]{:S(2)}, u32[]{:S(2)}) async-start(bf16[8,794,256]{2,1,0:T(8,128)(2,1)} %broadcast_dynamic-update-slice_fusion), calls=%async_computation | async-start | bytes 6553600 | tf_op jit(solution)/shard_map/all_to_all | solution.py:518
  27.9 242.2 %reduce-scatter.5.cloned.1.call-start = ((), (), s32[]{:S(2)}) async-start(), calls=%async_computation.7 | async-start | bytes 4456448 | tf_op jit(solution)/shard_map/reduce_scatter | solution.py:489
  180.6 219.7 %all-gather.14.cloned.1.call-start = ((), (), s32[]{:S(2)}) async-start(), calls=%async_computation.14 | async-start | bytes 8650752 | tf_op jit(solution)/shard_map/all_gather | solution.py:484
  181.2 255.5 %all-gather.12.cloned.1.call-start = ((), (), s32[]{:S(2)}) async-start(), calls=%async_computation.13 | async-start | bytes 8650752 | tf_op jit(solution)/shard_map/all_gather | solution.py:484
  271.8 392.1 %all-reduce.3.cloned.1.call-start = ((), (), s32[]{:S(2)}) async-start(), calls=%async_computation.10 | async-start | bytes 262144 | tf_op jit(solution)/shard_map/psum | solution.py:615
  273.1 38.2 %collective-permute-start.2 = (bf16[2,352,1024]{2,1,0:T(8,128)(2,1)}, bf16[2,352,1024]{2,1,0:T(8,128)(2,1)}, u32[]{:S(2)}, u32[]{:S(2)}) collective-permute-start(bf16[2,352,1024]{2,1,0:T(8,128)(2,1)} %constant_dynamic-slice_fusion.3), channel_id=1, source_target_pairs={{0,16},{16,0},{1,17},{17,1},{2,18},{18,2},{3,19},{19,3},{4,20},{20... | collective-permute-start | bytes 4325384 | tf_op jit(solution)/shard_map/ppermute | solution.py:533
  277.2 78.0 %collective-permute-start.1 = (bf16[2,352,1024]{2,1,0:T(8,128)(2,1)}, bf16[2,352,1024]{2,1,0:T(8,128)(2,1)}, u32[]{:S(2)}, u32[]{:S(2)}) collective-permute-start(bf16[2,352,1024]{2,1,0:T(8,128)(2,1)} %dynamic-slice_bitcast_fusion), channel_id=1, source_target_pairs={{0,16},{16,0},{1,17},{17,1},{2,18},{18,2},{3,19},{19,3},{4,20},{20... | collective-permute-start | bytes 4325384 | tf_op jit(solution)/shard_map/ppermute | solution.py:533
  279.1 113.8 %collective-permute-start = (bf16[2,352,1024]{2,1,0:T(8,128)(2,1)}, bf16[2,352,1024]{2,1,0:T(8,128)(2,1)}, u32[]{:S(2)}, u32[]{:S(2)}) collective-permute-start(bf16[2,352,1024]{2,1,0:T(8,128)(2,1)} %dynamic-slice_bitcast_fusion.1), channel_id=1, source_target_pairs={{0,16},{16,0},{1,17},{17,1},{2,18},{18,2},{3,19},{19,3},{4,20},{20... | collective-permute-start | bytes 4325384 | tf_op jit(solution)/shard_map/ppermute | solution.py:533
  400.3 108.6 %copy-start.50 = (bf16[88,2048]{1,0:T(8,128)(2,1)}, bf16[88,2048]{1,0:T(8,128)(2,1)S(1)}, u32[]{:S(2)}) copy-start(bf16[88,2048]{1,0:T(8,128)(2,1)S(1)} %copy.196) | copy-start | bytes 1081348
  539.5 274.5 %reduce-scatter.9.cloned.1.call-start = ((), (), s32[]{:S(2)}) async-start(), calls=%async_computation.9 | async-start | bytes 8650752 | tf_op jit(solution)/shard_map/reduce_scatter | solution.py:495
  608.4 205.6 %copy-start.9 = (bf16[256,512]{1,0:T(8,128)(2,1)S(1)}, bf16[256,512]{1,0:T(8,128)(2,1)}, u32[]{:S(2)}) copy-start(bf16[256,512]{1,0:T(8,128)(2,1)} %param.17) | copy-start | bytes 786436
  608.4 205.6 %copy-start.20 = (bf16[1,256,512]{2,1,0:T(8,128)(2,1)S(1)}, bf16[1,256,512]{2,1,0:T(8,128)(2,1)}, u32[]{:S(2)}) copy-start(bf16[1,256,512]{2,1,0:T(8,128)(2,1)} %reduce-scatter.5.cloned.1.call-done) | copy-start | bytes 786436
  608.4 213.3 %copy-start.36 = (bf16[256,512]{1,0:T(8,128)(2,1)S(1)}, bf16[256,512]{1,0:T(8,128)(2,1)}, u32[]{:S(2)}) copy-start(bf16[256,512]{1,0:T(8,128)(2,1)} %param.20) | copy-start | bytes 786436
  608.4 261.6 %all-gather.16.cloned.1.call-start = ((), (), s32[]{:S(2)}) async-start(), calls=%async_computation.15 | async-start | bytes 4456448 | tf_op jit(solution)/shard_map/all_gather | solution.py:480
  608.6 266.9 %copy-start.60 = (f32[512]{0:T(512)}, f32[512]{0:T(512)S(1)}, u32[]{:S(2)}) copy-start(f32[512]{0:T(512)S(1)} %dynamic_slice.67) | copy-start | bytes 6148
  608.6 266.9 %copy-start.64 = (f32[256,1]{0,1:T(1,128)}, f32[256,1]{0,1:T(1,128)S(1)}, u32[]{:S(2)}) copy-start(f32[256,1]{0,1:T(1,128)S(1)} %constant_dynamic-slice_fusion.2) | copy-start | bytes 3076
  822.6 349.1 %reduce-scatter.11.cloned.1.call-start = ((), (), s32[]{:S(2)}) async-start(), calls=%async_computation.11 | async-start | bytes 4456448 | tf_op jit(solution)/shard_map/reduce_scatter | solution.py:489
  908.1 341.0 %reduce-scatter.7.cloned.1.call-start = ((), (), s32[]{:S(2)}) async-start(), calls=%async_computation.8 | async-start | bytes 8650752 | tf_op jit(solution)/shard_map/reduce_scatter | solution.py:495
  983.7 40.7 %all-to-all-start.2 = ((bf16[8,264,256]{2,1,0:T(8,128)(2,1)}), bf16[8,264,256]{2,1,0:T(8,128)(2,1)S(1)}, u32[]{:S(2)}, u32[]{:S(2)}) async-start(bf16[8,264,256]{2,1,0:T(8,128)(2,1)} %maximum_bitcast_fusion.3), calls=%async_computation.6 | async-start | bytes 2162688 | tf_op jit(solution)/shard_map/all_to_all | solution.py:677
  1024.4 141.0 %all-to-all-start.1 = ((bf16[8,512,256]{2,1,0:T(8,128)(2,1)}), bf16[8,512,256]{2,1,0:T(8,128)(2,1)}, u32[]{:S(2)}, u32[]{:S(2)}) async-start(bf16[8,512,256]{2,1,0:T(8,128)(2,1)} %maximum_bitcast_fusion.2), calls=%async_computation.5 | async-start | bytes 4194304 | tf_op jit(solution)/shard_map/all_to_all | solution.py:677
  1034.1 54.0 %collective-permute-start.3 = (bf16[2,352,1024]{2,1,0:T(8,128)(2,1)}, bf16[2,352,1024]{2,1,0:T(8,128)(2,1)}, u32[]{:S(2)}, u32[]{:S(2)}) collective-permute-start(bf16[2,352,1024]{2,1,0:T(8,128)(2,1)} %dynamic-slice_convert_fusion.2), channel_id=1, source_target_pairs={{0,16},{16,0},{1,17},{17,1},{2,18},{18,2},{3,19},{19,3},{4,20},{20... | collective-permute-start | bytes 4325384 | tf_op jit(solution)/shard_map/ppermute | solution.py:695
  1042.1 76.9 %collective-permute-start.5 = (bf16[2,352,1024]{2,1,0:T(8,128)(2,1)S(1)}, bf16[2,352,1024]{2,1,0:T(8,128)(2,1)}, u32[]{:S(2)}, u32[]{:S(2)}) collective-permute-start(bf16[2,352,1024]{2,1,0:T(8,128)(2,1)S(1)} %dynamic-slice_convert_fusion), channel_id=1, source_target_pairs={{0,16},{16,0},{1,17},{17,1},{2,18},{18,2},{3,19},{19,3},{4,20},{20... | collective-permute-start | bytes 4325384 | tf_op jit(solution)/shard_map/ppermute | solution.py:695
  1045.0 103.1 %collective-permute-start.4 = (bf16[2,352,1024]{2,1,0:T(8,128)(2,1)}, bf16[2,352,1024]{2,1,0:T(8,128)(2,1)}, u32[]{:S(2)}, u32[]{:S(2)}) collective-permute-start(bf16[2,352,1024]{2,1,0:T(8,128)(2,1)} %dynamic-slice_convert_fusion.1), channel_id=1, source_target_pairs={{0,16},{16,0},{1,17},{17,1},{2,18},{18,2},{3,19},{19,3},{4,20},{20... | collective-permute-start | bytes 4325384 | tf_op jit(solution)/shard_map/ppermute | solution.py:695
  (83 other events, 1613.0 us)
Sparse Core Ops, SparseCore 0:
  11.0 104.4 all-gather.9
  180.8 89.2 reduce-scatter.4
  822.8 47.2 all-gather.15
  908.2 71.1 reduce-scatter.10
  981.5 164.6 reduce-scatter.6
Sparse Core Ops, SparseCore 1:
  184.4 95.6 all-gather.13
  283.8 101.5 all-gather.11
  539.6 124.3 all-reduce.2
  666.3 147.6 reduce-scatter.8

commit v2 on v0

--- a/solution.py
+++ b/solution.py
@@ -1,6 +1,10 @@
+import functools
+
 import jax
 import jax.numpy as jnp
 from jax import lax
+from jax.experimental import pallas as pl
+from jax.experimental.pallas import tpu as pltpu
 from jax.sharding import PartitionSpec as P
 
 HD = 128
@@ -432,6 +436,1178 @@
     )
 
 
+MESH = pl.DeviceIdType.MESH
+HBM = pl.BlockSpec(memory_space=pl.ANY)
+VMEM = pl.BlockSpec(memory_space=pltpu.VMEM)
+DMA = pltpu.SemaphoreType.DMA
+BF, F32 = jnp.bfloat16, jnp.float32
+BIG = 60 * 1024 * 1024
+
+
+def dot_nt(left, right):
+    return lax.dot_general(left, right, (((1,), (1,)), ((), ())), preferred_element_type=F32)
+
+
+def dot_tn(left, right):
+    return lax.dot_general(left, right, (((0,), (0,)), ((), ())), preferred_element_type=F32)
+
+
+def dot_nn(left, right):
+    return jnp.dot(left, right, preferred_element_type=F32)
+
+
+def ranks():
+    return lax.axis_index("fsdp"), lax.axis_index("ctx"), lax.axis_index("tp")
+
+
+def sibling(t):
+    return t + 1 - 2 * lax.rem(t, 2)
+
+
+def opposite(t):
+    return lax.rem(t + 2, 4)
+
+
+def remote(src, dst, send, recv, to):
+    return pltpu.make_async_remote_copy(
+        src_ref=src, dst_ref=dst, send_sem=send, recv_sem=recv, device_id=to, device_id_type=MESH
+    )
+
+
+def greet(peers):
+    barrier = pltpu.get_barrier_semaphore()
+    for peer in peers:
+        pl.semaphore_signal(barrier, inc=1, device_id=peer, device_id_type=MESH)
+    pl.semaphore_wait(barrier, len(peers))
+
+
+def line_peers(c, n_c):
+    return [{"ctx": lax.rem(c + step, n_c)} for step in range(1, n_c)]
+
+
+def piece(index, size):
+    return pl.ds(pl.multiple_of(index * size, size), size)
+
+
+def nearest(c, n_c, act):
+    act(c)
+    for step in range(1, n_c):
+        for side in (-1, 1):
+            place = c + side * step
+
+            @pl.when((place >= 0) & (place < n_c))
+            def _():
+                act(place)
+
+
+def spread_sems(n_c):
+    return [
+        DMA((n_c + 2,)),
+        DMA((n_c,)),
+        DMA((n_c,)),
+        DMA((n_c,)),
+        DMA((2 * n_c,)),
+        DMA((2 * n_c,)),
+        DMA((4 * n_c,)),
+        DMA((4 * n_c,)),
+        DMA(()),
+    ]
+
+
+def spread(own, place, n_c, both, sems):
+    zs, zr, xs, xr, ys, yr, ks, kr, ls = sems
+    f, c, t = ranks()
+    far = opposite(t)
+    to_sib, to_far, to_other = {"tp": sibling(t)}, {"tp": far}, {"fsdp": 1 - f}
+
+    def far_copy(src, i, g, cc):
+        return remote(src, place(g, cc, t), ys.at[i], yr.at[i], to_far)
+
+    def sib_copy(src, i, which, g, cc, col):
+        at = 2 * i + which
+        return remote(src, place(g, cc, col), ks.at[at], kr.at[at], to_sib)
+
+    def other_copy(src, cc):
+        return remote(src, place(f, cc, t), xs.at[cc], xr.at[cc], to_other)
+
+    def line_copy(src, cc, sem, to):
+        return remote(src, place(f, cc, t), zs.at[sem], zr.at[cc], {"ctx": to})
+
+    def pass_on(src, i, g, cc):
+        far_copy(src, i, g, cc).start()
+        sib_copy(src, i, 0, g, cc, t).start()
+
+    local = pltpu.make_async_copy(own, place(f, c, t), ls)
+    local.start()
+
+    @pl.when(c < n_c - 1)
+    def _():
+        line_copy(own, c, n_c, c + 1).start()
+
+    @pl.when(c > 0)
+    def _():
+        line_copy(own, c, n_c + 1, c - 1).start()
+
+    if both:
+        other_copy(own, c).start()
+    pass_on(own, c, f, c)
+    for step in range(1, n_c):
+        for side in (-1, 1):
+            cc = c + side * step
+            onward = c - side
+
+            @pl.when((cc >= 0) & (cc < n_c))
+            def _():
+                block = place(f, cc, t)
+                line_copy(block, cc, cc, c).wait_recv()
+
+                @pl.when((onward >= 0) & (onward < n_c))
+                def _():
+                    line_copy(block, cc, cc, onward).start()
+
+                if both:
+                    other_copy(block, cc).start()
+                pass_on(block, cc, f, cc)
+
+    if both:
+
+        def from_other(cc):
+            block = place(1 - f, cc, t)
+            remote(block, block, xs.at[cc], xr.at[cc], to_other).wait_recv()
+            pass_on(block, n_c + cc, 1 - f, cc)
+
+        nearest(c, n_c, from_other)
+    for g, base in ((f, 0), (1 - f, n_c))[: 2 if both else 1]:
+
+        def from_far(cc):
+            i = base + cc
+            block = place(g, cc, far)
+            remote(block, block, ys.at[i], yr.at[i], to_far).wait_recv()
+            sib_copy(block, i, 1, g, cc, far).start()
+
+        nearest(c, n_c, from_far)
+    for g, base in ((f, 0), (1 - f, n_c))[: 2 if both else 1]:
+        for cc in range(n_c):
+            i = base + cc
+            block = place(g, cc, t)
+            for which in range(2):
+                copy = sib_copy(block, i, which, g, cc, t)
+                copy.wait_recv()
+                copy.wait_send()
+            far_copy(block, i, g, cc).wait_send()
+    if both:
+        for cc in range(n_c):
+            other_copy(place(f, cc, t), cc).wait_send()
+    block = place(f, c, t)
+
+    @pl.when(c < n_c - 1)
+    def _():
+        line_copy(own, c, n_c, c).wait_send()
+
+    @pl.when(c > 0)
+    def _():
+        line_copy(own, c, n_c + 1, c).wait_send()
+
+    for step in range(1, n_c):
+        for side in (-1, 1):
+            cc = c + side * step
+            onward = c - side
+
+            @pl.when((cc >= 0) & (cc < n_c) & (onward >= 0) & (onward < n_c))
+            def _():
+                line_copy(block, cc, cc, c).wait_send()
+
+    local.wait()
+
+
+def front_kernel(n_c, part, hidden, wq, wk, wv, wo, small, seq_out, wqkv_out, wo_out, small_out, *sems):
+    ws, wr, ls, xs, xr = sems[:5]
+    f, c, t = ranks()
+    rows, quarter = hidden.shape
+    greet([{"tp": sibling(t)}, {"tp": opposite(t)}, {"fsdp": 1 - f}] + line_peers(c, n_c))
+
+    def targets(g, cc):
+        block = piece(g * n_c + cc, part)
+        return [wqkv_out.at[block, pl.ds(i * HD, HD)] for i in range(3)] + [
+            wo_out.at[:, block],
+            small_out.at[:, block],
+        ]
+
+    def sources(head):
+        cols = piece(head, HD)
+        return [wq.at[:, cols], wk.at[:, cols], wv.at[:, cols], wo.at[cols, :], small]
+
+    for step in range(1, n_c):
+        to = lax.rem(c + step, n_c)
+        for i, (src, dst) in enumerate(zip(sources(to), targets(f, c))):
+            remote(src, dst, ws.at[step, i], wr.at[step, i], {"ctx": to}).start()
+    own = [
+        pltpu.make_async_copy(src, dst, ls.at[i])
+        for i, (src, dst) in enumerate(zip(sources(c), targets(f, c)))
+    ]
+    for copy in own:
+        copy.start()
+    for copy in own:
+        copy.wait()
+
+    def slabs(g, cc):
+        block = piece(g * n_c + cc, part)
+        return [wqkv_out.at[block, :], wo_out.at[:, block], small_out.at[:, block]]
+
+    def across(step, g, cc):
+        return [
+            remote(slab, slab, xs.at[step, i], xr.at[step, i], {"fsdp": 1 - f})
+            for i, slab in enumerate(slabs(g, cc))
+        ]
+
+    for copy in across(0, f, c):
+        copy.start()
+
+    def place(g, cc, tt):
+        return seq_out.at[piece(cc, rows), piece(tt, quarter)]
+
+    spread(hidden, place, n_c, False, sems[5:])
+    for step in range(1, n_c):
+        cc = lax.rem(c - step + n_c, n_c)
+        for i, dst in enumerate(targets(f, cc)):
+            remote(dst, dst, ws.at[step, i], wr.at[step, i], {"ctx": cc}).wait_recv()
+        for copy in across(step, f, cc):
+            copy.start()
+    for step in range(n_c):
+        cc = lax.rem(c - step + n_c, n_c)
+        for copy in across(step, 1 - f, cc):
+            copy.wait_recv()
+        for copy in across(step, f, cc):
+            copy.wait_send()
+    for step in range(1, n_c):
+        for i, (src, dst) in enumerate(zip(sources(c), targets(f, c))):
+            remote(src, dst, ws.at[step, i], wr.at[step, i], {"ctx": c}).wait_send()
+
+
+def front(n_c, n_f, n_t, hidden, wq, wk, wv, wo, small):
+    rows, quarter = hidden.shape
+    part = wq.shape[0]
+    width = quarter * n_t
+    return pl.pallas_call(
+        functools.partial(front_kernel, n_c, part),
+        out_shape=(
+            jax.ShapeDtypeStruct((rows * n_c, width), BF),
+            jax.ShapeDtypeStruct((width, 3 * HD), BF),
+            jax.ShapeDtypeStruct((HD, width), BF),
+            jax.ShapeDtypeStruct((small.shape[0], width), F32),
+        ),
+        in_specs=[HBM] * 6,
+        out_specs=[HBM] * 4,
+        scratch_shapes=[
+            DMA((n_c, 5)),
+            DMA((n_c, 5)),
+            DMA((5,)),
+            DMA((n_c, 3)),
+            DMA((n_c, 3)),
+        ]
+        + spread_sems(n_c),
+        compiler_params=pltpu.CompilerParams(collective_id=1, has_side_effects=True),
+        cost_estimate=pl.CostEstimate(flops=0, bytes_accessed=100 << 20, transcendentals=0),
+        name="front",
+    )(hidden, wq, wk, wv, wo, small)
+
+
+def attend_kernel(block, hidden, gain, wqkv, cosine, sine, normed, q_out, k_out, v_out, hf_out, hb_out, lse_out, r_out):
+    seq, width = hidden.shape
+    scale_att = HD ** (-0.5)
+    for start in range(0, seq, block):
+        at = pl.ds(start, block)
+        h = hidden[at, :].astype(F32)
+        r = lax.rsqrt(jnp.sum(h * h, axis=1, keepdims=True) / width + EPS)
+        n = (h * r * gain[...]).astype(BF)
+        normed[at, :] = n
+        r_out[at, :] = jnp.broadcast_to(r, (block, HD))
+        qkv = dot_nn(n, wqkv[...])
+        cos, sin = cosine[at, :], sine[at, :]
+
+        def rotate(values):
+            return (values * cos + pltpu.roll(values, HD // 2, 1) * sin).astype(BF)
+
+        q_out[at, :] = rotate(qkv[:, :HD])
+        k_out[at, :] = rotate(qkv[:, HD : 2 * HD])
+        v_out[at, :] = qkv[:, 2 * HD :].astype(BF)
+    for start in range(0, seq, block):
+        at = pl.ds(start, block)
+        seen = start + block
+        s = dot_nt(q_out[at, :], k_out[:seen, :]) * scale_att
+        row = lax.broadcasted_iota(jnp.int32, (block, seen), 0) + start
+        col = lax.broadcasted_iota(jnp.int32, (block, seen), 1)
+        s = jnp.where(col <= row, s, NEG_BIG)
+        top = jnp.max(s, axis=1, keepdims=True)
+        e = jnp.exp(s - top)
+        total = jnp.sum(e, axis=1, keepdims=True)
+        p = (e / total).astype(BF)
+        out = dot_nn(p, v_out[:seen, :])
+        hf_out[at, :] = out
+        hb_out[at, :] = out.astype(BF)
+        lse_out[at, :] = jnp.broadcast_to(top + jnp.log(total), (block, HD))
+
+
+def attend(hidden, gain, wqkv, cosine, sine):
+    seq, width = hidden.shape
+    head = jax.ShapeDtypeStruct((seq, HD), BF)
+    head_f = jax.ShapeDtypeStruct((seq, HD), F32)
+    return pl.pallas_call(
+        functools.partial(attend_kernel, min(256, seq)),
+        out_shape=(jax.ShapeDtypeStruct((seq, width), BF), head, head, head, head_f, head, head_f, head_f),
+        in_specs=[VMEM] * 5,
+        out_specs=[VMEM] * 8,
+        compiler_params=pltpu.CompilerParams(vmem_limit_bytes=BIG),
+        cost_estimate=pl.CostEstimate(flops=2 << 30, bytes_accessed=12 << 20, transcendentals=1 << 20),
+        name="attend",
+    )(hidden, gain, wqkv, cosine, sine)
+
+
+def reduce_seq_scratch(n_c, rows, quarter):
+    return [
+        pltpu.VMEM((n_c, 2, rows, quarter), BF),
+        pltpu.VMEM((n_c, 2, rows, quarter), BF),
+        pltpu.VMEM((n_c, 2, rows, quarter), F32),
+        pltpu.VMEM((n_c, rows, quarter), BF),
+        pltpu.VMEM((n_c, rows, quarter), BF),
+        pltpu.VMEM((n_c, rows, quarter), BF),
+        pltpu.VMEM((n_c, rows, quarter), BF),
+        DMA((n_c,)),
+        DMA((n_c,)),
+        DMA((n_c,)),
+        DMA((n_c,)),
+        DMA((n_c,)),
+        DMA((n_c,)),
+    ]
+
+
+def reduce_seq(part_of, n_c, scratch):
+    out1, in1, own, out2, in2, out3, in3, s1, r1, s2, r2, s3, r3 = scratch
+    f, c, t = ranks()
+    far, sib = opposite(t), sibling(t)
+    to_sib, to_far = {"tp": sib}, {"tp": far}
+    order = [2, 1, 3, 0] if n_c == 4 else list(range(1, n_c)) + [0]
+    for d in order:
+        cc = lax.rem(c + d, n_c)
+        out1[d, 0] = part_of(cc, sib).astype(BF)
+        out1[d, 1] = part_of(cc, opposite(sib)).astype(BF)
+        remote(out1.at[d], in1.at[d], s1.at[d], r1.at[d], to_sib).start()
+        own[d, 0] = part_of(cc, t)
+        own[d, 1] = part_of(cc, far)
+    for d in order:
+        remote(out1.at[d], in1.at[d], s1.at[d], r1.at[d], to_sib).wait()
+        out2[d] = (own[d, 1] + in1[d, 1].astype(F32)).astype(BF)
+        remote(out2.at[d], in2.at[d], s2.at[d], r2.at[d], to_far).start()
+    for d in order:
+        remote(out2.at[d], in2.at[d], s2.at[d], r2.at[d], to_far).wait()
+        total = own[d, 0] + in1[d, 0].astype(F32) + in2[d].astype(F32)
+        if d:
+            out3[d] = total.astype(BF)
+            cc = lax.rem(c + d, n_c)
+            remote(out3.at[d], in3.at[d], s3.at[d], r3.at[d], {"ctx": cc}).start()
+    for d in order[:-1]:
+        remote(out3.at[d], in3.at[d], s3.at[d], r3.at[d], {"ctx": c}).wait()
+        total = total + in3[d].astype(F32)
+    return total
+
+
+def mid_kernel(n_c, heads, wo, hidden, resid_out, all_out, blk, *scratch):
+    f, c, t = ranks()
+    rows, quarter = hidden.shape
+    greet([{"tp": sibling(t)}, {"tp": opposite(t)}, {"fsdp": 1 - f}] + line_peers(c, n_c))
+
+    def part_of(cc, q):
+        return dot_nn(heads[piece(cc, rows), :], wo[:, piece(q, quarter)])
+
+    total = reduce_seq(part_of, n_c, scratch[:13])
+    resid = hidden[...].astype(F32) + total
+    resid_out[...] = resid
+    blk[...] = resid.astype(BF)
+
+    def place(g, cc, tt):
+        return all_out.at[piece(g * n_c + cc, rows), piece(tt, quarter)]
+
+    spread(blk, place, n_c, True, scratch[13:])
+
+
+def mid(n_c, n_f, n_t, heads, wo, hidden):
+    rows, quarter = hidden.shape
+    return pl.pallas_call(
+        functools.partial(mid_kernel, n_c),
+        out_shape=(
+            jax.ShapeDtypeStruct((rows, quarter), F32),
+            jax.ShapeDtypeStruct((rows * n_c * n_f, quarter * n_t), BF),
+        ),
+        in_specs=[VMEM] * 3,
+        out_specs=[VMEM, HBM],
+        scratch_shapes=[pltpu.VMEM((rows, quarter), BF)]
+        + reduce_seq_scratch(n_c, rows, quarter)
+        + spread_sems(n_c),
+        compiler_params=pltpu.CompilerParams(
+            collective_id=2, has_side_effects=True, vmem_limit_bytes=BIG
+        ),
+        cost_estimate=pl.CostEstimate(flops=1 << 29, bytes_accessed=200 << 20, transcendentals=0),
+        name="mid",
+    )(heads, wo, hidden)
+
+
+def expert_kernel(
+    n_c, n_f, mine, ffe, srows, hp, x, og, picked, gain, router, wg0, wu0, wd0, wg1, wu1, wd1, shared,
+    moe_out, back_out, in_out, gt_out, r_out, prob_out, pgrad_out, wgu, wd, sems,
+):
+    f, c, t = ranks()
+    block, width = x.shape
+    used = mine * ffe
+    rows_used = used + srows
+    part = width // (n_f * n_c)
+    half = width // n_f
+
+    @pl.when(pl.program_id(0) == 0)
+    def _():
+        copies = []
+
+        def fetch(src, dst):
+            copy = pltpu.make_async_copy(src, dst, sems.at[len(copies)])
+            copy.start()
+            copies.append(copy)
+
+        for i, (kept, got) in enumerate(((wg0, wg1), (wu0, wu1), (wd0, wd1))):
+            dst, base = ((wgu, 0), (wgu, hp), (wd, 0))[i]
+            for e in range(mine):
+                at = pl.ds(base + e * ffe, ffe)
+                fetch(kept.at[f * mine + e], dst.at[at, piece(f, half)])
+                fetch(got.at[e], dst.at[at, piece(1 - f, half)])
+            for b in range(n_f * n_c):
+                fetch(
+                    shared.at[b, pl.ds(i * srows, srows), :],
+                    dst.at[pl.ds(base + used, srows), pl.ds(b * part, part)],
+                )
+        blank = jnp.zeros((hp - rows_used, width), BF)
+        wgu[rows_used:hp, :] = blank
+        wgu[hp + rows_used :, :] = blank
+        wd[rows_used:, :] = blank
+        for copy in copies:
+            copy.wait()
+
+    h = x[...].astype(F32)
+    r = lax.rsqrt(jnp.sum(h * h, axis=1, keepdims=True) / width + EPS)
+    r_out[...] = jnp.broadcast_to(r, r_out.shape)
+    n = (h * r * gain[...]).astype(BF)
+    in_out[...] = n
+    logits = dot_nt(n, router[...])
+    e = jnp.exp(logits - jnp.max(logits, axis=1, keepdims=True))
+    prob = e / jnp.sum(e, axis=1, keepdims=True)
+    prob_out[...] = prob
+    n_exp = prob.shape[1]
+    lane = lax.broadcasted_iota(jnp.int32, (block, n_exp), 1)
+    first = (c * n_f + f) * mine
+    gated = prob * picked[...]
+    col = lax.broadcasted_iota(jnp.int32, (block, hp), 1)
+    gate = jnp.ones((block, hp), F32)
+    for k in range(mine):
+        g = jnp.sum(jnp.where(lane == first + k, gated, 0.0), axis=1, keepdims=True)
+        gate = jnp.where((col >= k * ffe) & (col < (k + 1) * ffe), g, gate)
+    ab = dot_nt(n, wgu[...])
+    a, b = ab[:, :hp], ab[:, hp:]
+    og_b = og[...]
+    og_rows = jnp.concatenate(
+        [jnp.concatenate([og_b[i, q] for q in range(og_b.shape[1])], axis=1) for i in range(og_b.shape[0])],
+        axis=0,
+    )
+    dh = dot_nt(og_rows, wd[...])
+    sig = 1.0 / (1.0 + jnp.exp(-a))
+    silu = a * sig
+    act = (silu * b).astype(BF).astype(F32)
+    actg = (act * gate).astype(BF)
+    ad = act * dh
+    p_grad = jnp.zeros((block, n_exp), F32)
+    for k in range(mine):
+        s = jnp.sum(
+            jnp.where((col >= k * ffe) & (col < (k + 1) * ffe), ad, 0.0), axis=1, keepdims=True
+        )
+        p_grad = jnp.where(lane == first + k, s, p_grad)
+    p_grad = p_grad * picked[...]
+    pgrad_out[...] = p_grad
+    logit_grad = (prob * (p_grad - jnp.sum(prob * p_grad, axis=1, keepdims=True))).astype(BF)
+    dg = dh * gate
+    da = (dg * b * (sig * (1.0 + a * (1.0 - sig)))).astype(BF)
+    db = (dg * silu).astype(BF)
+    gt_out[:rows_used, :] = da.T[:rows_used, :]
+    gt_out[rows_used : 2 * rows_used, :] = db.T[:rows_used, :]
+    gt_out[2 * rows_used :, :] = actg.T[:rows_used, :]
+    out = dot_nn(actg, wd[...]).astype(BF)
+    rows, quarter = og_b.shape[2], og_b.shape[3]
+    for i in range(og_b.shape[0]):
+        for q in range(og_b.shape[1]):
+            moe_out[i, q] = out[i * rows : (i + 1) * rows, q * quarter : (q + 1) * quarter]
+    back = dot_nn(jnp.concatenate([da, db], axis=1), wgu[...])
+    back = back + dot_nn(logit_grad, router[...])
+    back_out[...] = back.astype(BF)
+
+
+def experts(n_c, n_f, n_t, block, mine, ffe, srows, x, og, picked, gain, router, kept, got, shared):
+    total, width = x.shape
+    n_exp = router.shape[0]
+    rows, quarter = og.shape[2], og.shape[3]
+    per = block // rows
+    used = mine * ffe + srows
+    hp = -(-used // HD) * HD
+    row_spec = pl.BlockSpec((block, width), lambda i: (i, 0))
+    blk_spec = pl.BlockSpec((per, n_t, rows, quarter), lambda i: (i, 0, 0, 0))
+    exp_spec = pl.BlockSpec((block, n_exp), lambda i: (i, 0))
+    sds = jax.ShapeDtypeStruct
+    return pl.pallas_call(
+        functools.partial(expert_kernel, n_c, n_f, mine, ffe, srows, hp),
+        grid=(total // block,),
+        out_shape=(
+            sds(og.shape, BF),
+            sds((total, width), BF),
+            sds((total, width), BF),
+            sds((3 * used, total), BF),
+            sds((total, HD), F32),
+            sds((total, n_exp), F32),
+            sds((total, n_exp), F32),
+        ),
+        in_specs=[
+            row_spec,
+            blk_spec,
+            exp_spec,
+            pl.BlockSpec((1, width), lambda i: (0, 0)),
+            pl.BlockSpec((n_exp, width), lambda i: (0, 0)),
+        ]
+        + [HBM] * 7,
+        out_specs=[
+            blk_spec,
+            row_spec,
+            row_spec,
+            pl.BlockSpec((3 * used, block), lambda i: (0, i)),
+            pl.BlockSpec((block, HD), lambda i: (i, 0)),
+            exp_spec,
+            exp_spec,
+        ],
+        scratch_shapes=[
+            pltpu.VMEM((2 * hp, width), BF),
+            pltpu.VMEM((hp, width), BF),
+            DMA((3 * (2 * mine + n_f * n_c),)),
+        ],
+        compiler_params=pltpu.CompilerParams(vmem_limit_bytes=BIG),
+        cost_estimate=pl.CostEstimate(
+            flops=12 * total * width * used, bytes_accessed=70 << 20, transcendentals=total * used
+        ),
+        name="experts",
+    )(x, og, picked, gain, router, *kept, *got, shared)
+
+
+def expert_grad_kernel(used, mine, ffe, f_ref, gt, x, og, kg, ku, kd, sg, su, sd, shared):
+    del f_ref
+    step = pl.program_id(0)
+    cols = x.shape[1]
+    routed = mine * ffe
+    og_rows = og[...].reshape(-1, cols)
+    for i, (keep, send) in enumerate(((kg, sg), (ku, su), (kd, sd))):
+        rhs = og_rows if i == 2 else x[...]
+        g = dot_nn(gt[i * used : (i + 1) * used, :], rhs)
+        shared[i * (used - routed) : (i + 1) * (used - routed), :] = g[routed:].astype(BF)
+
+        @pl.when(step < 2)
+        def _():
+            send[...] = g[:routed].astype(BF).reshape(mine, ffe, cols)
+
+        @pl.when(step >= 2)
+        def _():
+            keep[...] = g[:routed].reshape(mine, ffe, cols)
+
+
+def expert_grads(f_rank, n_f, used, mine, ffe, gt, x, og):
+    total, width = x.shape
+    n_blocks, n_t, rows, quarter = og.shape
+    half = width // n_f
+    srows = used - mine * ffe
+    sds = jax.ShapeDtypeStruct
+
+    def tile(i, f):
+        other = 1 - f[0]
+        return jnp.where(i < 2, other * 2 + i, f[0] * 2 + i - 2)
+
+    keep_spec = pl.BlockSpec((mine, ffe, quarter), lambda i, f: (f[0], 0, jnp.where(i < 2, 0, i - 2)))
+    send_spec = pl.BlockSpec((mine, ffe, quarter), lambda i, f: (0, 0, jnp.where(i < 2, i, 1)))
+    return pl.pallas_call(
+        functools.partial(expert_grad_kernel, used, mine, ffe),
+        grid_spec=pltpu.PrefetchScalarGridSpec(
+            num_scalar_prefetch=1,
+            grid=(width // quarter,),
+            in_specs=[
+                pl.BlockSpec(gt.shape, lambda i, f: (0, 0)),
+                pl.BlockSpec((total, quarter), lambda i, f: (0, tile(i, f))),
+                pl.BlockSpec((n_blocks, 1, rows, quarter), lambda i, f: (0, tile(i, f), 0, 0)),
+            ],
+            out_specs=[keep_spec] * 3
+            + [send_spec] * 3
+            + [pl.BlockSpec((3 * srows, quarter), lambda i, f: (0, tile(i, f)))],
+        ),
+        out_shape=tuple([sds((n_f * mine, ffe, half), F32)] * 3)
+        + tuple([sds((mine, ffe, half), BF)] * 3)
+        + (sds((3 * srows, width), BF),),
+        compiler_params=pltpu.CompilerParams(vmem_limit_bytes=BIG),
+        cost_estimate=pl.CostEstimate(
+            flops=6 * total * width * used, bytes_accessed=50 << 20, transcendentals=0
+        ),
+        name="expert_grads",
+    )(f_rank, gt, x, og)
+
+
+def fill_kernel(f_ref, a, b, c, _a, _b, _c, oa, ob, oc):
+    del f_ref, _a, _b, _c
+    oa[...] = a[...].astype(F32)
+    ob[...] = b[...].astype(F32)
+    oc[...] = c[...].astype(F32)
+
+
+def fill_experts(f_rank, arrived, kept):
+    mine, ffe, half = arrived[0].shape
+    tile = half // 4
+    src = pl.BlockSpec((mine, ffe, tile), lambda i, f: (0, 0, i))
+    dst = pl.BlockSpec((mine, ffe, tile), lambda i, f: (1 - f[0], 0, i))
+    return pl.pallas_call(
+        fill_kernel,
+        grid_spec=pltpu.PrefetchScalarGridSpec(
+            num_scalar_prefetch=1, grid=(4,), in_specs=[src] * 3 + [HBM] * 3, out_specs=[dst] * 3
+        ),
+        out_shape=tuple(jax.ShapeDtypeStruct(k.shape, k.dtype) for k in kept),
+        input_output_aliases={4: 0, 5: 1, 6: 2},
+        compiler_params=pltpu.CompilerParams(vmem_limit_bytes=BIG),
+        name="fill_experts",
+    )(f_rank, *arrived, *kept)
+
+
+def norm_grad(values, r, gain, grad, width, out, into, send, recv):
+    f, c, t = ranks()
+    local = jnp.sum(grad * gain * values, axis=1, keepdims=True)
+    out[...] = jnp.broadcast_to(local, out.shape)
+    peers = [sibling(t), opposite(t), opposite(sibling(t))]
+    copies = [
+        remote(out, into.at[i], send.at[i], recv.at[i], {"tp": peer}) for i, peer in enumerate(peers)
+    ]
+    for copy in copies:
+        copy.start()
+    gain_part = jnp.sum(grad * values * r, axis=0, keepdims=True)
+    total = local
+    for i, copy in enumerate(copies):
+        copy.wait()
+        total = total + into[i][:, :1]
+    return r * gain * grad - values * (r * r * r * (total / width)), gain_part
+
+
+def norm_grad_scratch(rows):
+    return [
+        pltpu.VMEM((rows, HD), F32),
+        pltpu.VMEM((3, rows, HD), F32),
+        DMA((3,)),
+        DMA((3,)),
+    ]
+
+
+def back_kernel(
+    n_c, width, part, resid, r_all, gain, og, mid_out, gain_out, seq_out,
+    blk, r_own, own, in1, out2, in2, out3, in3, acc, out4, in4,
+    ls, rs, s1, r1, s2, r2, s3, r3, s4, r4, *rest,
+):
+    f, c, t = ranks()
+    rows, quarter = og.shape
+    far, sib = opposite(t), sibling(t)
+    to_sib, to_far, to_other = {"tp": sib}, {"tp": far}, {"fsdp": 1 - f}
+    greet([to_sib, to_far, {"tp": opposite(sib)}, to_other] + line_peers(c, n_c))
+    order = [2, 1, 3, 0] if n_c == 4 else list(range(1, n_c)) + [0]
+    blocks = [(g, d) for g in (1, 0) for d in order]
+
+    def part_at(g, d, q):
+        group = 1 - f if g else f
+        return part.at[piece(group * n_c + lax.rem(c + d, n_c), rows), piece(q, quarter)]
+
+    def core(g, d):
+        i = g * n_c + d
+        return [
+            remote(part_at(g, d, q), in1.at[i, k], s1.at[i, k], r1.at[i, k], to_sib)
+            for k, q in enumerate((opposite(sib), sib))
+        ]
+
+    def mine_of(g, d):
+        i = g * n_c + d
+        return [
+            pltpu.make_async_copy(part_at(g, d, q), own.at[i, k], ls.at[i, k])
+            for k, q in enumerate((far, t))
+        ]
+
+    fetch = pltpu.make_async_copy(r_all.at[piece(f * n_c + c, rows), :], r_own, rs)
+    fetch.start()
+    for g, d in blocks:
+        for copy in core(g, d) + mine_of(g, d):
+            copy.start()
+
+    def over(g, d):
+        i = g * n_c + d
+        return remote(out2.at[i], in2.at[i], s2.at[i], r2.at[i], to_far)
+
+    for g, d in blocks:
+        i = g * n_c + d
+        for copy in core(g, d) + mine_of(g, d):
+            copy.wait()
+        out2[i] = (own[i, 0].astype(F32) + in1[i, 0].astype(F32)).astype(BF)
+        over(g, d).start()
+
+    def other(d):
+        return remote(out3.at[d], in3.at[d], s3.at[d], r3.at[d], to_other)
+
+    for g, d in blocks:
+        i = g * n_c + d
+        over(g, d).wait()
+        total = own[i, 1].astype(F32) + in1[i, 1].astype(F32) + in2[i].astype(F32)
+        if g:
+            out3[d] = total.astype(BF)
+            other(d).start()
+        else:
+            acc[d] = total
+
+    def line(d, to):
+        return remote(out4.at[d], in4.at[d], s4.at[d], r4.at[d], {"ctx": to})
+
+    for d in order:
+        other(d).wait()
+        total = acc[d] + in3[d].astype(F32)
+        if d:
+            out4[d] = total.astype(BF)
+            line(d, lax.rem(c + d, n_c)).start()
+    for d in order[:-1]:
+        line(d, c).wait()
+        total = total + in4[d].astype(F32)
+    fetch.wait()
+    back, gain_part = norm_grad(resid[...], r_own[:, :1], gain[...], total, width, *rest[:4])
+    gain_out[...] = jnp.broadcast_to(gain_part, gain_out.shape)
+    grad = og[...].astype(F32) + back
+    mid_out[...] = grad
+    blk[...] = grad.astype(BF)
+
+    def place(g, cc, tt):
+        return seq_out.at[piece(cc, rows), piece(tt, quarter)]
+
+    spread(blk, place, n_c, False, rest[4:])
+
+
+def back(n_c, n_f, n_t, part, resid, r_all, gain, og):
+    rows, quarter = og.shape
+    n_b = n_c * n_f
+    sds = jax.ShapeDtypeStruct
+    blocks = lambda *lead: pltpu.VMEM(lead + (rows, quarter), BF)
+    return pl.pallas_call(
+        functools.partial(back_kernel, n_c, quarter * n_t),
+        out_shape=(
+            sds((rows, quarter), F32),
+            sds((8, quarter), F32),
+            sds((rows * n_c, quarter * n_t), BF),
+        ),
+        in_specs=[HBM, VMEM, HBM, VMEM, VMEM],
+        out_specs=[VMEM, VMEM, HBM],
+        scratch_shapes=[
+            blocks(),
+            pltpu.VMEM((rows, HD), F32),
+            blocks(n_b, 2),
+            blocks(n_b, 2),
+            blocks(n_b),
+            blocks(n_b),
+            blocks(n_c),
+            blocks(n_c),
+            pltpu.VMEM((n_c, rows, quarter), F32),
+            blocks(n_c),
+            blocks(n_c),
+            DMA((n_b, 2)),
+            DMA(()),
+            DMA((n_b, 2)),
+            DMA((n_b, 2)),
+            DMA((n_b,)),
+            DMA((n_b,)),
+            DMA((n_c,)),
+            DMA((n_c,)),
+            DMA((n_c,)),
+            DMA((n_c,)),
+        ]
+        + norm_grad_scratch(rows)
+        + spread_sems(n_c),
+        compiler_params=pltpu.CompilerParams(
+            collective_id=3, has_side_effects=True, vmem_limit_bytes=BIG
+        ),
+        cost_estimate=pl.CostEstimate(flops=1 << 20, bytes_accessed=200 << 20, transcendentals=0),
+        name="back",
+    )(part, resid, r_all, gain, og)
+
+
+def attend_back_kernel(
+    block, mid, wo, q, k, v, hf, lse, cosine, sine, normed, dqkv, gattn, hg, dq, dk, dv
+):
+    seq = mid.shape[0]
+    scale_att = HD ** (-0.5)
+    for start in range(0, seq, block):
+        at = pl.ds(start, block)
+        hg[at, :] = dot_nt(mid[at, :], wo[...]).astype(BF)
+    dk[...] = jnp.zeros_like(dk)
+    dv[...] = jnp.zeros_like(dv)
+    for start in range(0, seq, block):
+        at = pl.ds(start, block)
+        seen = start + block
+        qb, hb = q[at, :], hg[at, :]
+        delta = jnp.sum(hb.astype(F32) * hf[at, :], axis=1, keepdims=True)
+        s = dot_nt(qb, k[:seen, :]) * scale_att
+        row = lax.broadcasted_iota(jnp.int32, (block, seen), 0) + start
+        col = lax.broadcasted_iota(jnp.int32, (block, seen), 1)
+        p = jnp.where(col <= row, jnp.exp(s - lse[at, :1]), 0.0)
+        ds = (p * (dot_nt(hb, v[:seen, :]) - delta)).astype(BF)
+        dq[at, :] = dot_nn(ds, k[:seen, :]) * scale_att
+        dk[:seen, :] += dot_tn(ds, qb) * scale_att
+        dv[:seen, :] += dot_tn(p.astype(BF), hb)
+
+    def rotate(values, at):
+        return (values * cosine[at, :] - pltpu.roll(values, HD // 2, 1) * sine[at, :]).astype(BF)
+
+    for start in range(0, seq, block):
+        at = pl.ds(start, block)
+        dqkv[at, :HD] = rotate(dq[at, :], at)
+        dqkv[at, HD : 2 * HD] = rotate(dk[at, :], at)
+        dqkv[at, 2 * HD :] = dv[at, :].astype(BF)
+    gattn[: 3 * HD, :] = dot_tn(dqkv[...], normed[...]).astype(BF)
+    gattn[3 * HD :, :] = dot_tn(hf[...].astype(BF), mid[...]).astype(BF)
+
+
+def attend_back(mid_seq, wo, q, k, v, hf, lse, cosine, sine, normed):
+    seq, width = mid_seq.shape
+    sds = jax.ShapeDtypeStruct
+    return pl.pallas_call(
+        functools.partial(attend_back_kernel, min(256, seq)),
+        out_shape=(sds((seq, 3 * HD), BF), sds((4 * HD, width), BF)),
+        in_specs=[VMEM] * 10,
+        out_specs=[VMEM] * 2,
+        scratch_shapes=[pltpu.VMEM((seq, HD), BF)] + [pltpu.VMEM((seq, HD), F32)] * 3,
+        compiler_params=pltpu.CompilerParams(vmem_limit_bytes=BIG),
+        cost_estimate=pl.CostEstimate(flops=6 << 30, bytes_accessed=16 << 20, transcendentals=1 << 20),
+        name="attend_back",
+    )(mid_seq, wo, q, k, v, hf, lse, cosine, sine, normed)
+
+
+def last_kernel(
+    n_c, n_f, n_t, width, dqkv, wqkv, hidden, r_all, gain, mid_grad, gain2, gattn,
+    in_out, gq, gk, gv, go, gains_out,
+    r_own, outx, inx, own, outz, inz, gsend, gin, rs, sx, rx, lx, sz, rz, gs, gr, *rest,
+):
+    f, c, t = ranks()
+    rows, quarter = hidden.shape
+    part = width // (n_f * n_c)
+    here = f * n_c + c
+    others = []
+    for df in range(n_f):
+        for dc in range(n_c):
+            for dt in range(n_t):
+                if df or dc or dt:
+                    others.append(
+                        {
+                            "fsdp": lax.rem(f + df, n_f),
+                            "ctx": lax.rem(c + dc, n_c),
+                            "tp": lax.rem(t + dt, n_t),
+                        }
+                    )
+    gin[...] = jnp.zeros_like(gin)
+    greet(others)
+    order = [2, 1, 3, 0] if n_c == 4 else list(range(1, n_c)) + [0]
+
+    def cross(d):
+        cc = lax.rem(c + d, n_c)
+        return remote(
+            gattn.at[:, piece((1 - f) * n_c + cc, part)], inx.at[d], sx.at[d], rx.at[d], {"fsdp": 1 - f}
+        )
+
+    def keep(d):
+        cc = lax.rem(c + d, n_c)
+        return pltpu.make_async_copy(gattn.at[:, piece(f * n_c + cc, part)], own.at[d], lx.at[d])
+
+    def line(d, to):
+        return remote(outz.at[d], inz.at[d], sz.at[d], rz.at[d], {"ctx": to})
+
+    fetch = pltpu.make_async_copy(r_all.at[piece(c, rows), :], r_own, rs)
+    fetch.start()
+    for d in order:
+        cross(d).start()
+        keep(d).start()
+
+    def part_of(cc, q):
+        return dot_nt(dqkv[piece(cc, rows), :], wqkv[piece(q, quarter), :])
+
+    total = reduce_seq(part_of, n_c, rest[:13])
+    for d in order:
+        cross(d).wait()
+        keep(d).wait()
+        both = own[d].astype(F32) + inx[d].astype(F32)
+        if d:
+            outz[d] = both.astype(BF)
+            line(d, lax.rem(c + d, n_c)).start()
+        else:
+            mine = both
+    fetch.wait()
+    back, gain_part = norm_grad(
+        hidden[...].astype(F32), r_own[:, :1], gain[...], total, width, *rest[13:17]
+    )
+    in_out[...] = mid_grad[...] + back
+
+    gsend[0:1, :] = gain_part
+    gsend[1:2, :] = gain2[0:1, :]
+    gsend[2:, :] = jnp.zeros((6, quarter), F32)
+    per = quarter // part
+    holder = here // per
+    def gain_copy(h, tt):
+        b = t * per + h
+        return remote(
+            gsend.at[:, pl.ds(h * part, part)],
+            gin.at[here],
+            gs.at[h * n_t + tt],
+            gr.at[here],
+            {"fsdp": b // n_c, "ctx": lax.rem(b, n_c), "tp": jnp.int32(tt)},
+        )
+
+    def is_me(h, tt):
+        return (t * per + h == here) & (t == tt)
+
+    for h in range(per):
+        for tt in range(n_t):
+
+            @pl.when(jnp.logical_not(is_me(h, tt)))
+            def _():
+                gain_copy(h, tt).start()
+
+    def put(src, block):
+        at = piece(src, HD)
+        for i, ref in enumerate((gq, gk, gv)):
+            ref[:, at] = block[i * HD : (i + 1) * HD, :].T
+        go[at, :] = block[3 * HD :, :]
+
+    put(c, mine)
+    for d in order[:-1]:
+        line(d, c).wait()
+        put(lax.rem(c - d + n_c, n_c), inz[d].astype(F32))
+    for h in range(per):
+        for tt in range(n_t):
+
+            @pl.when(jnp.logical_not(is_me(h, tt)))
+            def _():
+                gain_copy(h, tt).wait_send()
+
+    for b in range(n_f * n_c):
+
+        @pl.when((b != here) | (holder != t))
+        def _():
+            remote(gin.at[b], gin.at[b], gs.at[0], gr.at[b], {"tp": sibling(t)}).wait_recv()
+
+    own_part = jnp.where(
+        holder == t,
+        gsend[:, piece(lax.rem(here, per), part)],
+        jnp.zeros((8, part), F32),
+    )
+    gains_out[...] = own_part + jnp.sum(gin[...], axis=0)
+
+
+def last(n_c, n_f, n_t, dqkv, wqkv, hidden, r_all, gain, mid_grad, gain2, gattn):
+    rows, quarter = hidden.shape
+    width = quarter * n_t
+    part = width // (n_f * n_c)
+    sds = jax.ShapeDtypeStruct
+    slab = pltpu.VMEM((n_c, 4 * HD, part), BF)
+    return pl.pallas_call(
+        functools.partial(last_kernel, n_c, n_f, n_t, width),
+        out_shape=(
+            sds((rows, quarter), F32),
+            sds((part, n_c * HD), F32),
+            sds((part, n_c * HD), F32),
+            sds((part, n_c * HD), F32),
+            sds((n_c * HD, part), F32),
+            sds((8, part), F32),
+        ),
+        in_specs=[VMEM, VMEM, VMEM, HBM, VMEM, VMEM, VMEM, HBM],
+        out_specs=[VMEM] * 6,
+        scratch_shapes=[
+            pltpu.VMEM((rows, HD), F32),
+            slab,
+            slab,
+            slab,
+            slab,
+            slab,
+            pltpu.VMEM((8, quarter), F32),
+            pltpu.VMEM((n_f * n_c, 8, part), F32),
+            DMA(()),
+            DMA((n_c,)),
+            DMA((n_c,)),
+            DMA((n_c,)),
+            DMA((n_c,)),
+            DMA((n_c,)),
+            DMA((quarter // part * n_t,)),
+            DMA((n_f * n_c,)),
+        ]
+        + reduce_seq_scratch(n_c, rows, quarter)
+        + norm_grad_scratch(rows),
+        compiler_params=pltpu.CompilerParams(
+            collective_id=4, has_side_effects=True, vmem_limit_bytes=BIG
+        ),
+        cost_estimate=pl.CostEstimate(flops=2 << 30, bytes_accessed=150 << 20, transcendentals=0),
+        name="last",
+    )(dqkv, wqkv, hidden, r_all, gain, mid_grad, gain2, gattn)
+
+
+def per_device_seq(
+    hidden_in,
+    positions,
+    chosen,
+    out_grad,
+    attn_gain,
+    w_query,
+    w_key,
+    w_value,
+    w_out,
+    moe_gain,
+    router,
+    shared_gate,
+    shared_up,
+    shared_down,
+    expert_gate,
+    expert_up,
+    expert_down,
+):
+    f_rank, c_rank, t_rank = ranks()
+    n_f, n_c, n_t = (lax.axis_size(name) for name in ("fsdp", "ctx", "tp"))
+    rows, quarter = hidden_in.shape
+    width = quarter * n_t
+    part = w_query.shape[0]
+    seq = rows * n_c
+    n_exp = router.shape[1]
+    mine = n_exp // n_c // n_f
+    ffe = expert_gate.shape[2]
+    group = ("fsdp", "ctx")
+    every = ("fsdp", "ctx", "tp")
+    n_b = n_f * n_c
+    own_shared = shared_gate.shape[1] // n_b
+    srows = -(-own_shared // 16) * 16
+    block = f_rank * n_c + c_rank
+    f_arr = f_rank.astype(jnp.int32).reshape(1)
+    swap = [(i, n_f - 1 - i) for i in range(n_f)]
+
+    gate_t, up_t = expert_gate.swapaxes(1, 2), expert_up.swapaxes(1, 2)
+    weights = (gate_t, up_t, expert_down)
+    got = tuple(
+        lax.ppermute(
+            lax.dynamic_slice_in_dim(w, (n_f - 1 - f_rank) * mine, mine, 0), "fsdp", swap
+        )
+        for w in weights
+    )
+
+    picked_own = jnp.sum(
+        (chosen[:, :, None] == jnp.arange(n_exp)[None, None, :]).astype(F32), axis=1
+    )
+    small = [
+        attn_gain.astype(F32)[None],
+        moe_gain.astype(F32)[None],
+        router.T.astype(F32),
+        picked_own.T,
+        positions.astype(F32)[None],
+    ]
+    small = jnp.concatenate(small, axis=0)
+    small = jnp.pad(small, ((0, -small.shape[0] % 8), (0, 0)))
+    hidden_seq, wqkv, wo, small_all = front(
+        n_c, n_f, n_t, hidden_in, w_query, w_key, w_value, w_out, small
+    )
+    gain_one, gain_two = small_all[0:1], small_all[1:2]
+    router_t = small_all[2 : 2 + n_exp].astype(BF)
+    picked = small_all[2 + n_exp : 2 + 2 * n_exp].T
+    pos_seq = lax.dynamic_slice(small_all, (2 + 2 * n_exp, f_rank * seq), (1, seq))[0]
+    after = lambda x: lax.optimization_barrier((x, hidden_seq))[0]
+    grad_all = lax.all_gather(after(out_grad), every, axis=0, tiled=False)
+    grad_all = grad_all.reshape(n_b, n_t, rows, quarter)
+
+    def shared_part(weight):
+        return jnp.pad(
+            weight.reshape(n_b, own_shared, part), ((0, 0), (0, srows - own_shared), (0, 0))
+        )
+
+    shared = jnp.concatenate(
+        [shared_part(shared_gate.T), shared_part(shared_up.T), shared_part(shared_down)], axis=1
+    )
+    shared = lax.all_to_all(after(shared), group, split_axis=0, concat_axis=0, tiled=True)
+
+    half = HD // 2
+    inverse = 10000.0 ** (-jnp.arange(half, dtype=F32) * 2.0 / HD)
+    angles = pos_seq[:, None] * inverse[None, :]
+    cosine, sine = jnp.cos(angles), jnp.sin(angles)
+    cosine = jnp.concatenate([cosine, cosine], axis=1)
+    sine = jnp.concatenate([-sine, sine], axis=1)
+    normed, q, k, v, heads_f, heads_b, lse, r_one = attend(hidden_seq, gain_one, wqkv, cosine, sine)
+    resid_mid, resid_all = mid(n_c, n_f, n_t, heads_b, wo, hidden_in)
+
+    moe_part, back_part, moe_in, g_t, r_two, prob, p_part = experts(
+        n_c, n_f, n_t, rows, mine, ffe, srows, resid_all, grad_all, picked, gain_two, router_t,
+        weights, got, shared,
+    )
+    used = mine * ffe + srows
+    kg, ku, kd, sg, su, sd, shared_g = expert_grads(f_arr, n_f, used, mine, ffe, g_t, moe_in, grad_all)
+    arrived = tuple(lax.ppermute(s, "fsdp", swap) for s in (sg, su, sd))
+    own_cols = lambda x: lax.dynamic_slice_in_dim(x, t_rank * quarter, quarter, 1)
+    mid_grad, gain_two_part, mid_seq = back(
+        n_c, n_f, n_t, back_part, resid_mid, r_two, own_cols(gain_two), out_grad
+    )
+    later = lambda x: lax.optimization_barrier((x, mid_seq))[0]
+    moe_q = lax.psum_scatter(
+        later(moe_part).reshape(n_b * n_t, rows, quarter), every, scatter_dimension=0, tiled=True
+    )[0].astype(F32)
+    layer_out = (resid_mid + moe_q).astype(BF)
+    p_grad = lax.psum(later(p_part), every)
+    logit_grad = (prob * (p_grad - jnp.sum(prob * p_grad, axis=1, keepdims=True))).astype(BF)
+    router_grad = dot_tn(lax.dynamic_slice_in_dim(moe_in, block * part, part, 1), logit_grad)
+    shared_sent = later(shared_g).reshape(3 * srows, n_b, part).swapaxes(0, 1)
+    shared_back = lax.all_to_all(shared_sent, group, split_axis=0, concat_axis=0, tiled=True)
+    shared_back = shared_back.reshape(n_b, 3, srows, part)[:, :, :own_shared].astype(F32)
+
+    dqkv, gattn = attend_back(mid_seq, wo, q, k, v, heads_f, lse, cosine, sine, normed)
+    input_grad, gq, gk, gv, go, gains = last(
+        n_c, n_f, n_t, dqkv, wqkv, hidden_in, r_one, own_cols(gain_one), mid_grad, gain_two_part, gattn
+    )
+    eg, eu, ed = fill_experts(f_arr, arrived, (kg, ku, kd))
+
+    def shared_cols(i):
+        return shared_back[:, i].reshape(n_b * own_shared, part)
+
+    return (
+        layer_out,
+        input_grad,
+        gains[0],
+        gq,
+        gk,
+        gv,
+        go,
+        gains[1],
+        router_grad,
+        shared_cols(0).T,
+        shared_cols(1).T,
+        shared_cols(2),
+        eg.swapaxes(1, 2),
+        eu.swapaxes(1, 2),
+        ed,
+    )
+
+
+def one_head_each(mesh, args):
+    n_f, n_c, n_t = (mesh.shape[name] for name in ("fsdp", "ctx", "tp"))
+    heads = args[5].shape[1] // HD
+    experts = args[10].shape[1]
+    return (
+        n_f == 2
+        and n_t == 4
+        and heads == n_c * n_t
+        and experts % (n_f * n_c) == 0
+        and args[11].shape[1] % (8 * n_f * n_c * n_t) == 0
+    )
+
+
 def solution(mesh):
     placed = (
         P(("fsdp", "ctx"), "tp"),
@@ -452,8 +1628,10 @@
         P("ctx", "fsdp", "tp"),
         P("ctx", "tp", "fsdp"),
     )
-    return jax.shard_map(
-        per_device,
+    def run(*args):
+        body = per_device_seq if one_head_each(mesh, args) else per_device
+        return jax.shard_map(
+        body,
         mesh=mesh,
         in_specs=placed,
         out_specs=(
@@ -474,4 +1652,6 @@
             P("ctx", "tp", "fsdp"),
         ),
         check_vma=False,
-    )
+    )(*args)
+
+    return run

time: 2720 us -> 773 us (0.28)
  waiting for transfers between devices: 1770 us -> 85.3 us
  Pallas kernels: 0 us -> 615 us
  blocking collectives: 349 us -> 0 us
  local copies, waits for them, and re-layouts: 263 us -> 18.7 us
  matrix products: 180 us -> 2.57 us
  other arithmetic: 99.6 us -> 12.5 us
    all_to_all x4 -> x2, waiting for transfers between devices: 720 us -> 0.01 us  [the longest x1 0.01 us: per_device_seq(): lax.all_to_all(after(shared), group, split_axis=0, concat_axis=0, tiled=T...]
    reduce_scatter x18 -> x1, waiting for transfers between devices: 768 us -> 84.5 us  [per_device_seq(): lax.psum_scatter(later(moe_part).reshape(n_b * n_t, rows, quarter), every...]
    pallas_call x0 -> x9, Pallas kernels: none -> 615 us  [the longest x1 146 us: last(): pl.pallas_call(functools.partial(last_kernel, n_c, n_f, n_t, width), out_...]
    all_gather x3 -> x0, blocking collectives: 290 us -> none  [the longest x1 250 us: per_device(): lax.all_gather(router, ('fsdp', 'ctx'), axis=0, tiled=True)]
    all_gather x16 -> x1, waiting for transfers between devices: 276 us -> 0.02 us  [per_device_seq(): grad_all = lax.all_gather(after(out_grad), every, axis=0, tiled=False)]
    dot_general x38 -> x1, matrix products: 174 us -> 2.57 us  [dot_tn(): lax.dot_general(left, right, (((0,), (0,)), ((), ())), preferred_element_...]
    gather x2 -> x0, local copies, waits for them, and re-layouts: 66.4 us -> none  [the longest x1 38.6 us: per_device(): back_slots[flat_exp, slot_of].reshape(tok_rows, TOPK, model_width)]
    convert_element_type x3 -> x0, local copies, waits for them, and re-layouts: 57 us -> none  [the longest x2 40 us: to_sources(): slot_rows.astype(jnp.bfloat16)]
  transfers between devices with their start and end apart: 38 -> 11, of which waited for: 26 -> 1; matrix products, arithmetic and copies ran while one was open for 16% -> 3% of each run, Pallas kernels for 0% -> 45%
where the time goes in v2:
time: 773 us; the launch traced here: 764 us
  Pallas kernels  615 us (80%)
  waiting for transfers between devices  85.3 us (11%)
  local copies, waits for them, and re-layouts  18.7 us (2%)
  starting transfers between devices  16.1 us (2%)
  between operations  14.2 us (2%)
  other arithmetic  12.5 us (2%)
    pallas_call x1, Pallas kernels, last(): pl.pallas_call(functools.partial(last_kernel, n_c, n_f, n_t, width), out_...  146 us
    pallas_call x1, Pallas kernels, mid(): pl.pallas_call(functools.partial(mid_kernel, n_c), out_shape=(jax.ShapeDt...  140 us
    pallas_call x1, Pallas kernels, back(): pl.pallas_call(functools.partial(back_kernel, n_c, quarter * n_t), out_sh...  121 us
    reduce_scatter x1, waiting for transfers between devices, per_device_seq(): lax.psum_scatter(later(moe_part).reshape(n_b * n_t, rows, quarter), every...  84.5 us
    pallas_call x1, Pallas kernels, front(): pl.pallas_call(functools.partial(front_kernel, n_c, part), out_shape=(jax...  83.2 us
    pallas_call x1, Pallas kernels, experts(): pl.pallas_call(functools.partial(expert_kernel, n_c, n_f, mine, ffe, srow...  65.5 us
    pallas_call x1, Pallas kernels, expert_grads(): pl.pallas_call(functools.partial(expert_grad_kernel, used, mine, ffe), gr...  32.2 us
  transfers between devices with their start and end apart: 11, of which 1 were waited for; matrix products, arithmetic and copies ran while one was open for 3% of the time, Pallas kernels for 45%

profile of v2, /device:TPU:0, one launch (start us, length us, event | category | flops | bytes accessed | tf_op | source)
XLA Modules:
  0.0 764.0 jit_solution(6281341553753966397)
XLA Ops:
  11.5 83.2 %front.1 = (bf16[1024,2048]{1,0:T(8,128)(2,1)}, bf16[2048,384]{1,0:T(8,128)(2,1)}, bf16[128,2048]{1,0:T(8,128)(2,1)}, f32[40,2048]{1,0:T(8,128)}) custom-call(bf16[256,512]{1,0:T(8,128)(2,1)} %hidden.5, bf16[256,512]{1,0:T(8,128)(2,1)} %wq.1, bf16[256,512]{1,0:T(8,128)(2,1)} %wk.1, bf16[256,512]{1,0:T(8,128)(2,1)} %wv.1, bf16[512,256]{1,0:T(8,128)(2,1)} %wo.1, ...), custom_call_target="tpu_custom_call" | custom-call | bytes 104857600 | tf_op jit(solution)/shard_map/front/pallas_call | solution.py:691
  94.8 2.3 fusion.5
  97.1 4.3 all-to-all-start
  101.4 1.5 constant_dynamic-slice_fusion.2
  102.9 1.9 collective-permute-start.2
  104.8 1.5 dynamic-slice_bitcast_fusion
  107.9 1.7 collective-permute-start
  111.7 1.9 fusion.10
  115.5 9.3 %attend.1 = (bf16[1024,2048]{1,0:T(8,128)(2,1)}, bf16[1024,128]{1,0:T(8,128)(2,1)}, bf16[1024,128]{1,0:T(8,128)(2,1)}, bf16[1024,128]{1,0:T(8,128)(2,1)}, f32[10...) custom-call(bf16[1024,2048]{1,0:T(8,128)(2,1)} %get-tuple-element.62.hidden, ...), custom_call_target="tpu_custom_call" | custom-call | flops 2147483648 | bytes 12582912 | tf_op jit(solution)/shard_map/attend/pallas_call | solution.py:755
  124.8 139.6 %mid.1 = (f32[256,512]{1,0:T(8,128)}, bf16[2048,2048]{1,0:T(8,128)(2,1)}) custom-call(bf16[1024,128]{1,0:T(8,128)(2,1)} %get-tuple-element.65.heads, bf16[128,2048]{1,0:T(8,128)(2,1)} %get-tuple-element.66.wo, bf16[256,512]{1,0:T(8,128)(2,1)} %hidden.5), custom_call_target="tpu_custom_call" | custom-call | flops 536870912 | bytes 209715200 | tf_op jit(solution)/shard_map/mid/pallas_call | solution.py:835
  265.0 65.5 %experts.1 = (bf16[8,4,256,512]{3,2,1,0:T(8,128)(2,1)}, bf16[2048,2048]{1,0:T(8,128)(2,1)}, bf16[2048,2048]{1,0:T(8,128)(2,1)}, bf16[2400,2048]{1,0:T(8,128)(2,1...) custom-call(bf16[2048,2048]{1,0:T(8,128)(2,1)} %get-tuple-element.68.x, ...), custom_call_target="tpu_custom_call" | custom-call | flops 40265318400 | bytes 73400320 | tf_op jit(solution)/shard_map/experts/pallas_call | solution.py:959
  330.5 121.2 %back.1 = (f32[256,512]{1,0:T(8,128)}, f32[8,512]{1,0:T(8,128)}, bf16[1024,2048]{1,0:T(8,128)(2,1)}) custom-call(bf16[2048,2048]{1,0:T(8,128)(2,1)} %get-tuple-element.72.part, f32[256,512]{1,0:T(8,128)} %get-tuple-element.67.resid, f32[2048,128]{1,0:T(8,128)} %get-tuple-element.73.r_all, f32[1,512]{1,0:T(1,128)} %constant_dynamic-slice_fusion.1.gain, ...), custom_call_target="tpu_custom_call" | custom-call | flops 1048576 | bytes 209715200 | tf_op jit(solution)/shard_map/back/pallas_call | solution.py:1201
  452.4 32.2 %expert_grads.1 = (f32[4,352,1024]{2,1,0:T(8,128)}, f32[4,352,1024]{2,1,0:T(8,128)}, f32[4,352,1024]{2,1,0:T(8,128)}, bf16[2,352,1024]{2,1,0:T(8,128)(2,1)}, bf1...) custom-call(s32[1]{0:T(128)} %bitcast.21.f_ref, ...), custom_call_target="tpu_custom_call" | custom-call | flops 20132659200 | bytes 52428800 | tf_op jit(solution)/shard_map/expert_grads/pallas_call | solution.py:1034
  484.6 2.4 copy.45
  487.0 3.7 all-to-all-start.1
  492.0 2.0 collective-permute-start.3
  494.1 2.0 collective-permute-start.5
  496.0 11.8 %attend_back.1 = (bf16[1024,384]{1,0:T(8,128)(2,1)}, bf16[512,2048]{1,0:T(8,128)(2,1)}) custom-call(bf16[1024,2048]{1,0:T(8,128)(2,1)} %get-tuple-element.74.mid, bf16[128,2048]{1,0:T(8,128)(2,1)} %get-tuple-element.66.wo, bf16[1024,128]{1,0:T(8,128)(2,1)} %get-tuple-element.76.q, bf16[1024,128]{1,0:T(8,128)(2,1)} %get-tuple-element.77.k, ...), custom_call_target="tpu_custom_call" | custom-call | flops 6442450944 | bytes 16777216 | tf_op jit(solution)/shard_map/attend_back/pallas_call | solution.py:1282
  507.8 146.0 %last.1 = (f32[256,512]{1,0:T(8,128)}, f32[256,512]{1,0:T(8,128)}, f32[256,512]{1,0:T(8,128)}, f32[256,512]{1,0:T(8,128)}, f32[512,256]{1,0:T(8,128)}, /*index=5*/f32[8,256]{1,0:T(8,128)}) custom-call(bf16[1024,384]{1,0:T(8,128)(2,1)} %get-tuple-element.82.dqkv, bf16[2048,384]{1,0:T(8,128)(2,1)} %get-tuple-element.64.wqkv, bf16[256,512]{1,0:T(8,128)(2,1)} %hidden.5, ...), custom_call_target="tpu_custom_call" | custom-call | flops 2147483648 | bytes 157286400 | tf_op jit(solution)/shard_map/last/pallas_call | solution.py:1419
  655.2 1.7 multiply_reduce_fusion
  656.9 2.6 fusion.6
  659.5 6.0 fill_experts.1
  667.1 84.5 %reduce-scatter.2.cloned.1.call-done = bf16[1,256,512]{2,1,0:T(8,128)(2,1)} async-done(((bf16[32,256,512]{2,1,0:T(8,128)(2,1)}), bf16[1,256,512]{2,1,0:T(8,128)(2,1)}) %reduce-scatter.2.cloned.1.call-update) | async-done | bytes 262160 | tf_op jit(solution)/shard_map/reduce_scatter | solution.py:1559
  751.6 1.7 fusion.8
  (65 shorter events, 19.5 us)
Async XLA Ops:
  7.2 257.8 %all-gather.3.cloned.1.call-start = ((), (), s32[]{:S(2)}) async-start(), calls=%async_computation.5 | async-start | bytes 8650752 | tf_op jit(solution)/shard_map/all_gather | solution.py:1525
  97.1 167.9 %all-to-all-start = ((bf16[8,288,256]{2,1,0:T(8,128)(2,1)}), bf16[8,288,256]{2,1,0:T(8,128)(2,1)}, u32[]{:S(2)}, u32[]{:S(2)}) async-start(bf16[8,288,256]{2,1,0:T(8,128)(2,1)} %fusion.5), calls=%async_computation | async-start | bytes 2359296 | tf_op jit(solution)/shard_map/all_to_all | solution.py:1536
  101.3 553.9 %all-reduce.6.cloned.1.call-start = ((), (), s32[]{:S(2)}) async-start(), calls=%async_computation.4 | async-start | bytes 2097152 | tf_op jit(solution)/shard_map/psum | solution.py:1563
  102.9 3.8 copy-start.3
  102.9 162.0 %collective-permute-start.2 = (bf16[2,352,1024]{2,1,0:T(8,128)(2,1)S(1)}, bf16[2,352,1024]{2,1,0:T(8,128)(2,1)}, u32[]{:S(2)}, u32[]{:S(2)}) collective-permute-start(bf16[2,352,1024]{2,1,0:T(8,128)(2,1)S(1)} %constant_dynamic-slice_fusion.2), channel_id=1, source_target_pairs={{0,16},{16,0},{1,17},{17,1},{2,18},{18,2},{3,19},{19,3},{4,20},{20... | collective-permute-start | bytes 4325384 | tf_op jit(solution)/shard_map/ppermute | solution.py:1499
  106.3 3.3 copy-start.9
  106.3 158.6 %collective-permute-start.1 = (bf16[2,352,1024]{2,1,0:T(8,128)(2,1)S(1)}, bf16[2,352,1024]{2,1,0:T(8,128)(2,1)}, u32[]{:S(2)}, u32[]{:S(2)}) collective-permute-start(bf16[2,352,1024]{2,1,0:T(8,128)(2,1)S(1)} %dynamic-slice_bitcast_fusion), channel_id=1, source_target_pairs={{0,16},{16,0},{1,17},{17,1},{2,18},{18,2},{3,19},{19,3},{4,20},{20... | collective-permute-start | bytes 4325384 | tf_op jit(solution)/shard_map/ppermute | solution.py:1499
  107.9 157.1 %collective-permute-start = (bf16[2,352,1024]{2,1,0:T(8,128)(2,1)}, bf16[2,352,1024]{2,1,0:T(8,128)(2,1)}, u32[]{:S(2)}, u32[]{:S(2)}) collective-permute-start(bf16[2,352,1024]{2,1,0:T(8,128)(2,1)} %dynamic-slice_bitcast_fusion.1), channel_id=1, source_target_pairs={{0,16},{16,0},{1,17},{17,1},{2,18},{18,2},{3,19},{19,3},{4,20},{20... | collective-permute-start | bytes 4325384 | tf_op jit(solution)/shard_map/ppermute | solution.py:1499
  115.5 148.9 %copy-start.10 = (f32[1,2048]{1,0:T(1,128)}, f32[1,2048]{1,0:T(1,128)S(1)}, u32[]{:S(2)}) copy-start(f32[1,2048]{1,0:T(1,128)S(1)} %get-tuple-element.112.gain) | copy-start | bytes 24580
  451.7 299.9 %reduce-scatter.2.cloned.1.call-start = ((), (), s32[]{:S(2)}) async-start(), calls=%async_computation.3 | async-start | bytes 8650752 | tf_op jit(solution)/shard_map/reduce_scatter | solution.py:1559
  487.0 178.5 %all-to-all-start.1 = ((bf16[8,288,256]{2,1,0:T(8,128)(2,1)}), bf16[8,288,256]{2,1,0:T(8,128)(2,1)S(1)}, u32[]{:S(2)}, u32[]{:S(2)}) async-start(bf16[8,288,256]{2,1,0:T(8,128)(2,1)} %bitcast.45), calls=%async_computation.2 | async-start | bytes 2359296 | tf_op jit(solution)/shard_map/all_to_all | solution.py:1567
  492.0 167.5 %collective-permute-start.3 = (bf16[2,352,1024]{2,1,0:T(8,128)(2,1)}, bf16[2,352,1024]{2,1,0:T(8,128)(2,1)}, u32[]{:S(2)}, u32[]{:S(2)}) collective-permute-start(bf16[2,352,1024]{2,1,0:T(8,128)(2,1)} %get-tuple-element.100), channel_id=1, source_target_pairs={{0,16},{16,0},{1,17},{17,1},{2,18},{18,2},{3,19},{19,3},{4,20},{20... | collective-permute-start | bytes 4325384 | tf_op jit(solution)/shard_map/ppermute | solution.py:1553
  494.0 165.5 %collective-permute-start.4 = (bf16[2,352,1024]{2,1,0:T(8,128)(2,1)}, bf16[2,352,1024]{2,1,0:T(8,128)(2,1)}, u32[]{:S(2)}, u32[]{:S(2)}) collective-permute-start(bf16[2,352,1024]{2,1,0:T(8,128)(2,1)} %get-tuple-element.101), channel_id=1, source_target_pairs={{0,16},{16,0},{1,17},{17,1},{2,18},{18,2},{3,19},{19,3},{4,20},{20... | collective-permute-start | bytes 4325384 | tf_op jit(solution)/shard_map/ppermute | solution.py:1553
  494.1 165.4 %collective-permute-start.5 = (bf16[2,352,1024]{2,1,0:T(8,128)(2,1)}, bf16[2,352,1024]{2,1,0:T(8,128)(2,1)}, u32[]{:S(2)}, u32[]{:S(2)}) collective-permute-start(bf16[2,352,1024]{2,1,0:T(8,128)(2,1)} %get-tuple-element.102), channel_id=1, source_target_pairs={{0,16},{16,0},{1,17},{17,1},{2,18},{18,2},{3,19},{19,3},{4,20},{20... | collective-permute-start | bytes 4325384 | tf_op jit(solution)/shard_map/ppermute | solution.py:1553
  507.8 147.4 %copy-start = (f32[2048,16]{1,0:T(8,128)S(1)}, f32[2048,16]{1,0:T(8,128)}, u32[]{:S(2)}) copy-start(f32[2048,16]{1,0:T(8,128)} %get-tuple-element.94) | copy-start | bytes 393220
  655.2 1.7 copy-start.1
  665.7 85.9 %copy-start.2 = (f32[256,512]{1,0:T(8,128)S(1)}, f32[256,512]{1,0:T(8,128)}, u32[]{:S(2)}) copy-start(f32[256,512]{1,0:T(8,128)} %get-tuple-element.67.resid) | copy-start | bytes 1572868
  665.7 87.6 %copy-start.8 = (f32[256,512]{1,0:T(8,128)S(1)}, f32[256,512]{1,0:T(8,128)}, u32[]{:S(2)}) copy-start(f32[256,512]{1,0:T(8,128)} %get-tuple-element.137) | copy-start | bytes 1572868
  665.7 88.4 %copy-start.7 = (f32[256,512]{1,0:T(8,128)S(1)}, f32[256,512]{1,0:T(8,128)}, u32[]{:S(2)}) copy-start(f32[256,512]{1,0:T(8,128)} %get-tuple-element.139) | copy-start | bytes 1572868
  667.1 87.8 %copy-start.6 = (f32[256,512]{1,0:T(8,128)S(1)}, f32[256,512]{1,0:T(8,128)}, u32[]{:S(2)}) copy-start(f32[256,512]{1,0:T(8,128)} %get-tuple-element.140) | copy-start | bytes 1572868
  667.1 88.6 %copy-start.5 = (f32[256,512]{1,0:T(8,128)S(1)}, f32[256,512]{1,0:T(8,128)}, u32[]{:S(2)}) copy-start(f32[256,512]{1,0:T(8,128)} %get-tuple-element.141) | copy-start | bytes 1572868
  753.3 3.2 copy-start.4
Sparse Core Ops, SparseCore 0:
  94.9 122.7 all-gather.2
  451.8 143.9 all-reduce.5
  598.3 153.2 reduce-scatter.1

commit v3 on v2

--- a/solution.py
+++ b/solution.py
@@ -514,7 +514,7 @@
     ]
 
 
-def spread(own, place, n_c, both, sems):
+def spread(own, place, n_c, both, sems, after_line=None):
     zs, zr, xs, xr, ys, yr, ks, kr, ls = sems
     f, c, t = ranks()
     far = opposite(t)
@@ -569,6 +569,8 @@
                     other_copy(block, cc).start()
                 pass_on(block, cc, f, cc)
 
+    if after_line is not None:
+        after_line()
     if both:
 
         def from_other(cc):
@@ -620,6 +622,33 @@
     local.wait()
 
 
+def to_each(src_of, dst, n_f, n_c, sems, act):
+    send, recv, own = sems
+    f, c, _ = ranks()
+    here = f * n_c + c
+    for df in range(n_f):
+        for dc in range(n_c):
+            i = df * n_c + dc
+            if i == 0:
+                copy = pltpu.make_async_copy(src_of(here), dst.at[here], own)
+                copy.start() if act == "start" else copy.wait()
+                continue
+            to_f, to_c = lax.rem(f + df, n_f), lax.rem(c + dc, n_c)
+            copy = remote(
+                src_of(to_f * n_c + to_c), dst.at[here], send.at[i], recv.at[i], {"fsdp": to_f, "ctx": to_c}
+            )
+            copy.start() if act == "start" else copy.wait()
+
+
+def each_peers(f, c, n_f, n_c):
+    return [
+        {"fsdp": lax.rem(f + df, n_f), "ctx": lax.rem(c + dc, n_c)}
+        for df in range(n_f)
+        for dc in range(n_c)
+        if df or dc
+    ]
+
+
 def front_kernel(n_c, part, hidden, wq, wk, wv, wo, small, seq_out, wqkv_out, wo_out, small_out, *sems):
     ws, wr, ls, xs, xr = sems[:5]
     f, c, t = ranks()
@@ -666,13 +695,15 @@
     def place(g, cc, tt):
         return seq_out.at[piece(cc, rows), piece(tt, quarter)]
 
-    spread(hidden, place, n_c, False, sems[5:])
-    for step in range(1, n_c):
-        cc = lax.rem(c - step + n_c, n_c)
-        for i, dst in enumerate(targets(f, cc)):
-            remote(dst, dst, ws.at[step, i], wr.at[step, i], {"ctx": cc}).wait_recv()
-        for copy in across(step, f, cc):
-            copy.start()
+    def weights_across():
+        for step in range(1, n_c):
+            cc = lax.rem(c - step + n_c, n_c)
+            for i, dst in enumerate(targets(f, cc)):
+                remote(dst, dst, ws.at[step, i], wr.at[step, i], {"ctx": cc}).wait_recv()
+            for copy in across(step, f, cc):
+                copy.start()
+
+    spread(hidden, place, n_c, False, sems[5:], weights_across)
     for step in range(n_c):
         cc = lax.rem(c - step + n_c, n_c)
         for copy in across(step, 1 - f, cc):
@@ -781,7 +812,7 @@
     ]
 
 
-def reduce_seq(part_of, n_c, scratch):
+def reduce_seq(part_of, n_c, scratch, between=None):
     out1, in1, own, out2, in2, out3, in3, s1, r1, s2, r2, s3, r3 = scratch
     f, c, t = ranks()
     far, sib = opposite(t), sibling(t)
@@ -794,6 +825,8 @@
         remote(out1.at[d], in1.at[d], s1.at[d], r1.at[d], to_sib).start()
         own[d, 0] = part_of(cc, t)
         own[d, 1] = part_of(cc, far)
+    if between is not None:
+        between()
     for d in order:
         remote(out1.at[d], in1.at[d], s1.at[d], r1.at[d], to_sib).wait()
         out2[d] = (own[d, 1] + in1[d, 1].astype(F32)).astype(BF)
@@ -811,15 +844,16 @@
     return total
 
 
-def mid_kernel(n_c, heads, wo, hidden, resid_out, all_out, blk, *scratch):
+def mid_kernel(n_c, n_f, heads, wo, hidden, shared, resid_out, all_out, shared_out, blk, ss, sr, sl, *scratch):
     f, c, t = ranks()
     rows, quarter = hidden.shape
-    greet([{"tp": sibling(t)}, {"tp": opposite(t)}, {"fsdp": 1 - f}] + line_peers(c, n_c))
+    greet([{"tp": sibling(t)}, {"tp": opposite(t)}] + each_peers(f, c, n_f, n_c))
+    exchange = lambda act: to_each(lambda b: shared.at[b], shared_out, n_f, n_c, (ss, sr, sl), act)
 
     def part_of(cc, q):
         return dot_nn(heads[piece(cc, rows), :], wo[:, piece(q, quarter)])
 
-    total = reduce_seq(part_of, n_c, scratch[:13])
+    total = reduce_seq(part_of, n_c, scratch[:13], lambda: exchange("start"))
     resid = hidden[...].astype(F32) + total
     resid_out[...] = resid
     blk[...] = resid.astype(BF)
@@ -828,19 +862,26 @@
         return all_out.at[piece(g * n_c + cc, rows), piece(tt, quarter)]
 
     spread(blk, place, n_c, True, scratch[13:])
-
-
-def mid(n_c, n_f, n_t, heads, wo, hidden):
+    exchange("wait")
+
+
+def mid(n_c, n_f, n_t, heads, wo, hidden, shared):
     rows, quarter = hidden.shape
     return pl.pallas_call(
-        functools.partial(mid_kernel, n_c),
+        functools.partial(mid_kernel, n_c, n_f),
         out_shape=(
             jax.ShapeDtypeStruct((rows, quarter), F32),
             jax.ShapeDtypeStruct((rows * n_c * n_f, quarter * n_t), BF),
+            jax.ShapeDtypeStruct(shared.shape, BF),
         ),
-        in_specs=[VMEM] * 3,
-        out_specs=[VMEM, HBM],
-        scratch_shapes=[pltpu.VMEM((rows, quarter), BF)]
+        in_specs=[VMEM] * 3 + [HBM],
+        out_specs=[VMEM, HBM, HBM],
+        scratch_shapes=[
+            pltpu.VMEM((rows, quarter), BF),
+            DMA((n_f * n_c,)),
+            DMA((n_f * n_c,)),
+            DMA(()),
+        ]
         + reduce_seq_scratch(n_c, rows, quarter)
         + spread_sems(n_c),
         compiler_params=pltpu.CompilerParams(
@@ -848,212 +889,593 @@
         ),
         cost_estimate=pl.CostEstimate(flops=1 << 29, bytes_accessed=200 << 20, transcendentals=0),
         name="mid",
-    )(heads, wo, hidden)
-
-
-def expert_kernel(
-    n_c, n_f, mine, ffe, srows, hp, x, og, picked, gain, router, wg0, wu0, wd0, wg1, wu1, wd1, shared,
-    moe_out, back_out, in_out, gt_out, r_out, prob_out, pgrad_out, wgu, wd, sems,
-):
-    f, c, t = ranks()
-    block, width = x.shape
+    )(heads, wo, hidden, shared)
+
+
+def fetch_experts(n_c, n_f, mine, ffe, srows, hp, weights, shared, wgu, wd, sems):
+    f = lax.axis_index("fsdp")
+    wg0, wu0, wd0, wg1, wu1, wd1 = weights
+    width = wd.shape[1]
     used = mine * ffe
-    rows_used = used + srows
     part = width // (n_f * n_c)
     half = width // n_f
-
-    @pl.when(pl.program_id(0) == 0)
-    def _():
-        copies = []
-
-        def fetch(src, dst):
-            copy = pltpu.make_async_copy(src, dst, sems.at[len(copies)])
-            copy.start()
-            copies.append(copy)
-
-        for i, (kept, got) in enumerate(((wg0, wg1), (wu0, wu1), (wd0, wd1))):
-            dst, base = ((wgu, 0), (wgu, hp), (wd, 0))[i]
-            for e in range(mine):
-                at = pl.ds(base + e * ffe, ffe)
-                fetch(kept.at[f * mine + e], dst.at[at, piece(f, half)])
-                fetch(got.at[e], dst.at[at, piece(1 - f, half)])
-            for b in range(n_f * n_c):
-                fetch(
-                    shared.at[b, pl.ds(i * srows, srows), :],
-                    dst.at[pl.ds(base + used, srows), pl.ds(b * part, part)],
-                )
-        blank = jnp.zeros((hp - rows_used, width), BF)
-        wgu[rows_used:hp, :] = blank
-        wgu[hp + rows_used :, :] = blank
-        wd[rows_used:, :] = blank
-        for copy in copies:
-            copy.wait()
-
-    h = x[...].astype(F32)
-    r = lax.rsqrt(jnp.sum(h * h, axis=1, keepdims=True) / width + EPS)
-    r_out[...] = jnp.broadcast_to(r, r_out.shape)
-    n = (h * r * gain[...]).astype(BF)
-    in_out[...] = n
-    logits = dot_nt(n, router[...])
-    e = jnp.exp(logits - jnp.max(logits, axis=1, keepdims=True))
-    prob = e / jnp.sum(e, axis=1, keepdims=True)
-    prob_out[...] = prob
-    n_exp = prob.shape[1]
+    copies = []
+
+    def add(src, dst):
+        copies.append(pltpu.make_async_copy(src, dst, sems.at[len(copies)]))
+
+    for i, (kept, got) in enumerate(((wg0, wg1), (wu0, wu1), (wd0, wd1))):
+        dst, base = ((wgu, 0), (wgu, hp), (wd, 0))[i]
+        for e in range(mine):
+            at = pl.ds(base + e * ffe, ffe)
+            add(kept.at[f * mine + e], dst.at[at, piece(f, half)])
+            add(got.at[e], dst.at[at, piece(1 - f, half)])
+        for b in range(n_f * n_c):
+            add(
+                shared.at[b, pl.ds(i * srows, srows), :],
+                dst.at[pl.ds(base + used, srows), pl.ds(b * part, part)],
+            )
+    return copies
+
+
+def blank_rows(rows_used, hp, wgu, wd):
+    blank = jnp.zeros((hp - rows_used, wd.shape[1]), BF)
+    wgu[rows_used:hp, :] = blank
+    wgu[hp + rows_used :, :] = blank
+    wd[rows_used:, :] = blank
+
+
+def gates(prob, picked, first, mine, ffe, hp):
+    block, n_exp = prob.shape
     lane = lax.broadcasted_iota(jnp.int32, (block, n_exp), 1)
-    first = (c * n_f + f) * mine
-    gated = prob * picked[...]
+    gated = prob * picked
     col = lax.broadcasted_iota(jnp.int32, (block, hp), 1)
     gate = jnp.ones((block, hp), F32)
     for k in range(mine):
         g = jnp.sum(jnp.where(lane == first + k, gated, 0.0), axis=1, keepdims=True)
         gate = jnp.where((col >= k * ffe) & (col < (k + 1) * ffe), g, gate)
-    ab = dot_nt(n, wgu[...])
-    a, b = ab[:, :hp], ab[:, hp:]
-    og_b = og[...]
-    og_rows = jnp.concatenate(
-        [jnp.concatenate([og_b[i, q] for q in range(og_b.shape[1])], axis=1) for i in range(og_b.shape[0])],
-        axis=0,
-    )
-    dh = dot_nt(og_rows, wd[...])
-    sig = 1.0 / (1.0 + jnp.exp(-a))
-    silu = a * sig
-    act = (silu * b).astype(BF).astype(F32)
-    actg = (act * gate).astype(BF)
-    ad = act * dh
-    p_grad = jnp.zeros((block, n_exp), F32)
-    for k in range(mine):
-        s = jnp.sum(
-            jnp.where((col >= k * ffe) & (col < (k + 1) * ffe), ad, 0.0), axis=1, keepdims=True
+    return gate, lane, col
+
+
+def reducer_scratch(n_f, n_c, rows, quarter):
+    n_b = n_f * n_c
+    blocks = lambda *lead: pltpu.VMEM(lead + (rows, quarter), BF)
+    return [
+        blocks(n_b, 2),
+        blocks(n_b, 2),
+        blocks(n_b, 2),
+        blocks(n_b),
+        blocks(n_b),
+        blocks(n_c),
+        blocks(n_c),
+        pltpu.VMEM((n_c, rows, quarter), F32),
+        blocks(n_c),
+        blocks(n_c),
+    ] + [DMA((n_b,))] * 4 + [DMA((n_c,))] * 4
+
+
+class Reducer:
+    def __init__(self, n_c, scratch):
+        self.n_c = n_c
+        (self.out1, self.in1, self.own, self.out2, self.in2, self.out3, self.in3, self.acc,
+         self.out4, self.in4, self.s1, self.r1, self.s2, self.r2, self.s3, self.r3, self.s4, self.r4) = scratch
+        self.f, self.c, self.t = ranks()
+        self.far, self.sib = opposite(self.t), sibling(self.t)
+
+    def row_block(self, i):
+        n_c = self.n_c
+        group = jnp.where(i < n_c, 1 - self.f, self.f)
+        return group * n_c + lax.rem(self.c + lax.rem(i, n_c) + 1, n_c)
+
+    def core_copy(self, i):
+        return remote(self.out1.at[i], self.in1.at[i], self.s1.at[i], self.r1.at[i], {"tp": self.sib})
+
+    def far_copy(self, i):
+        return remote(self.out2.at[i], self.in2.at[i], self.s2.at[i], self.r2.at[i], {"tp": self.far})
+
+    def other_copy(self, j):
+        return remote(self.out3.at[j], self.in3.at[j], self.s3.at[j], self.r3.at[j], {"fsdp": 1 - self.f})
+
+    def line_copy(self, j, to):
+        return remote(self.out4.at[j], self.in4.at[j], self.s4.at[j], self.r4.at[j], {"ctx": to})
+
+    def put(self, i, part_of):
+        self.out1[i, 0] = part_of(opposite(self.sib)).astype(BF)
+        self.out1[i, 1] = part_of(self.sib).astype(BF)
+        self.core_copy(i).start()
+        self.own[i, 0] = part_of(self.far).astype(BF)
+        self.own[i, 1] = part_of(self.t).astype(BF)
+
+    def over(self, i):
+        self.core_copy(i).wait()
+        self.out2[i] = (self.own[i, 0].astype(F32) + self.in1[i, 0].astype(F32)).astype(BF)
+        self.far_copy(i).start()
+
+    def _sum(self, i):
+        self.far_copy(i).wait()
+        return self.own[i, 1].astype(F32) + self.in1[i, 1].astype(F32) + self.in2[i].astype(F32)
+
+    def after_other(self, i):
+        self.out3[i] = self._sum(i).astype(BF)
+        self.other_copy(i).start()
+
+    def after_own(self, i):
+        self.acc[i - self.n_c] = self._sum(i)
+
+    def along(self, j):
+        self.other_copy(j).wait()
+        total = self.acc[j] + self.in3[j].astype(F32)
+        if j < self.n_c - 1:
+            self.out4[j] = total.astype(BF)
+            self.line_copy(j, lax.rem(self.c + j + 1, self.n_c)).start()
+        return total
+
+    def total(self, total):
+        for j in range(self.n_c - 1):
+            self.line_copy(j, self.c).wait()
+            total = total + self.in4[j].astype(F32)
+        return total
+
+    def loop(self, n_b, compute):
+        n_c = self.n_c
+
+        def step(i, carry):
+            def between():
+                @pl.when(i >= 1)
+                def _():
+                    self.over(i - 1)
+
+                @pl.when((i >= 3) & (i < 3 + n_c))
+                def _():
+                    self.after_other(i - 3)
+
+                @pl.when(i >= 3 + n_c)
+                def _():
+                    self.after_own(i - 3)
+
+            compute(i, between)
+            return carry
+
+        lax.fori_loop(0, n_b, step, 0)
+
+    def drain(self, n_b, works):
+        works = list(works)
+        self.over(n_b - 1)
+        for i in range(n_b - 3, n_b):
+            if works:
+                works.pop(0)()
+            self.after_own(i) if i >= self.n_c else self.after_other(i)
+        for j in range(self.n_c):
+            total = self.along(j)
+        for work in works:
+            work()
+        return self.total(total)
+
+
+def forward_kernel(
+    n_c, n_f, mine, ffe, srows, hp, rows_all, og_all, resid, picked, gain, router,
+    wg0, wu0, wd0, wg1, wu1, wd1, shared,
+    layer_out, in_out, act_out, silu_out, slope_out, r_out, prob_out, keep_out, send_out, shared_out,
+    gt, wsem, xsem, nsem, asem, tsem, osem, *scratch,
+):
+    f, c, t = ranks()
+    n_b = n_f * n_c
+    rows, quarter = resid.shape
+    width = rows_all.shape[1]
+    routed = mine * ffe
+    rows_used = routed + srows
+    red = Reducer(n_c, scratch)
+
+    def blocks_phase(wgu, wd, xs, ns, acts):
+        fetches = fetch_experts(
+            n_c, n_f, mine, ffe, srows, hp, (wg0, wu0, wd0, wg1, wu1, wd1), shared, wgu, wd, wsem
         )
-        p_grad = jnp.where(lane == first + k, s, p_grad)
-    p_grad = p_grad * picked[...]
-    pgrad_out[...] = p_grad
-    logit_grad = (prob * (p_grad - jnp.sum(prob * p_grad, axis=1, keepdims=True))).astype(BF)
-    dg = dh * gate
-    da = (dg * b * (sig * (1.0 + a * (1.0 - sig)))).astype(BF)
-    db = (dg * silu).astype(BF)
-    gt_out[:rows_used, :] = da.T[:rows_used, :]
-    gt_out[rows_used : 2 * rows_used, :] = db.T[:rows_used, :]
-    gt_out[2 * rows_used :, :] = actg.T[:rows_used, :]
-    out = dot_nn(actg, wd[...]).astype(BF)
-    rows, quarter = og_b.shape[2], og_b.shape[3]
-    for i in range(og_b.shape[0]):
-        for q in range(og_b.shape[1]):
-            moe_out[i, q] = out[i * rows : (i + 1) * rows, q * quarter : (q + 1) * quarter]
-    back = dot_nn(jnp.concatenate([da, db], axis=1), wgu[...])
-    back = back + dot_nn(logit_grad, router[...])
-    back_out[...] = back.astype(BF)
-
-
-def experts(n_c, n_f, n_t, block, mine, ffe, srows, x, og, picked, gain, router, kept, got, shared):
-    total, width = x.shape
+        for copy in fetches:
+            copy.start()
+
+        def load(i, slot):
+            return pltpu.make_async_copy(
+                rows_all.at[piece(red.row_block(i), rows), :], xs.at[slot], xsem.at[slot]
+            )
+
+        def stores(i, slot):
+            at = piece(red.row_block(i), rows)
+            return [pltpu.make_async_copy(ns.at[slot], in_out.at[at, :], nsem.at[slot])] + [
+                pltpu.make_async_copy(acts.at[slot, k], out.at[at, :], asem.at[slot, k])
+                for k, out in enumerate((act_out, silu_out, slope_out))
+            ]
+
+        load(0, 0).start()
+        blank_rows(rows_used, hp, wgu, wd)
+        greet([{"tp": red.sib}, {"tp": red.far}, {"fsdp": 1 - f}] + line_peers(c, n_c))
+        for copy in fetches:
+            copy.wait()
+
+        def compute(i, between):
+            slot = lax.rem(i, 2)
+            b = red.row_block(i)
+            at = piece(b, rows)
+            load(i, slot).wait()
+
+            @pl.when(i + 1 < n_b)
+            def _():
+                load(i + 1, 1 - slot).start()
+
+            @pl.when(i >= 2)
+            def _():
+                for copy in stores(i - 2, slot):
+                    copy.wait()
+
+            h = xs[slot].astype(F32)
+            r = lax.rsqrt(jnp.sum(h * h, axis=1, keepdims=True) / width + EPS)
+            r_out[at, :] = jnp.broadcast_to(r, (rows, HD))
+            n = (h * r * gain[...]).astype(BF)
+            ns[slot] = n
+            logits = dot_nt(n, router[...])
+            e = jnp.exp(logits - jnp.max(logits, axis=1, keepdims=True))
+            prob = e / jnp.sum(e, axis=1, keepdims=True)
+            prob_out[at, :] = prob
+            gate, _, _ = gates(prob, picked[at, :], (c * n_f + f) * mine, mine, ffe, hp)
+            ab = dot_nt(n, wgu[...])
+            between()
+            a, up = ab[:, :hp], ab[:, hp:]
+            sig = 1.0 / (1.0 + jnp.exp(-a))
+            silu = a * sig
+            act = (silu * up).astype(BF)
+            acts[slot, 0] = act
+            acts[slot, 1] = silu.astype(BF)
+            acts[slot, 2] = (up * (sig * (1.0 + a * (1.0 - sig)))).astype(BF)
+            actg = (act.astype(F32) * gate).astype(BF)
+            gt[:, at] = actg.T[:rows_used, :]
+            for copy in stores(i, slot):
+                copy.start()
+            red.put(i, lambda q: dot_nn(actg, wd[:, piece(q, quarter)]))
+
+        red.loop(n_b, compute)
+        for i in range(n_b - 2, n_b):
+            for copy in stores(i, i % 2):
+                copy.wait()
+
+    pl.run_scoped(
+        blocks_phase,
+        pltpu.VMEM((2 * hp, width), BF),
+        pltpu.VMEM((hp, width), BF),
+        pltpu.VMEM((2, rows, width), BF),
+        pltpu.VMEM((2, rows, width), BF),
+        pltpu.VMEM((2, 3, rows, hp), BF),
+    )
+
+    def grads_phase(tiles, keeps, sends, shs):
+        def tile_of(s):
+            return (1 - f) * 2 + s if s < 2 else f * 2 + s - 2
+
+        def tile_load(s):
+            return pltpu.make_async_copy(og_all.at[:, tile_of(s)], tiles.at[s % 2], tsem.at[s % 2])
+
+        def out_copies(s):
+            cols = pl.ds(s % 2 * quarter, quarter)
+            if s < 2:
+                src, dst = sends.at[s], send_out.at[:, :, cols]
+            else:
+                src, dst = keeps.at[s - 2], keep_out.at[pl.ds(f * mine, mine), :, cols]
+            return [
+                pltpu.make_async_copy(src, dst, osem.at[s, 0]),
+                pltpu.make_async_copy(
+                    shs.at[s], shared_out.at[:, piece(tile_of(s), quarter)], osem.at[s, 1]
+                ),
+            ]
+
+        def work(s):
+            def run():
+                tile_load(s).wait()
+                if s < 3:
+                    tile_load(s + 1).start()
+                g = dot_nn(gt[...], tiles[s % 2].reshape(n_b * rows, quarter))
+                if s < 2:
+                    sends[s] = g[:routed].astype(BF).reshape(mine, ffe, quarter)
+                else:
+                    keeps[s - 2] = g[:routed].reshape(mine, ffe, quarter)
+                shs[s] = g[routed:].astype(BF)
+                for copy in out_copies(s):
+                    copy.start()
+
+            return run
+
+        tile_load(0).start()
+        total = red.drain(n_b, [work(s) for s in range(4)])
+        layer_out[...] = (resid[...] + total).astype(BF)
+        for s in range(4):
+            for copy in out_copies(s):
+                copy.wait()
+
+    pl.run_scoped(
+        grads_phase,
+        pltpu.VMEM((2, n_b, rows, quarter), BF),
+        pltpu.VMEM((2, mine, ffe, quarter), F32),
+        pltpu.VMEM((2, mine, ffe, quarter), BF),
+        pltpu.VMEM((4, srows, quarter), BF),
+    )
+
+
+def expert_sizes(n_c, n_f, n_t, mine, ffe, srows, width):
+    used = mine * ffe + srows
+    return used, -(-used // HD) * HD, 3 * (2 * mine + n_f * n_c)
+
+
+def forward(n_c, n_f, n_t, mine, ffe, srows, rows_all, og_all, resid, picked, gain, router, kept, got, shared):
+    total, width = rows_all.shape
+    rows, quarter = resid.shape
     n_exp = router.shape[0]
-    rows, quarter = og.shape[2], og.shape[3]
-    per = block // rows
-    used = mine * ffe + srows
-    hp = -(-used // HD) * HD
-    row_spec = pl.BlockSpec((block, width), lambda i: (i, 0))
-    blk_spec = pl.BlockSpec((per, n_t, rows, quarter), lambda i: (i, 0, 0, 0))
-    exp_spec = pl.BlockSpec((block, n_exp), lambda i: (i, 0))
+    n_b = n_f * n_c
+    used, hp, n_fetch = expert_sizes(n_c, n_f, n_t, mine, ffe, srows, width)
     sds = jax.ShapeDtypeStruct
     return pl.pallas_call(
-        functools.partial(expert_kernel, n_c, n_f, mine, ffe, srows, hp),
-        grid=(total // block,),
+        functools.partial(forward_kernel, n_c, n_f, mine, ffe, srows, hp),
         out_shape=(
-            sds(og.shape, BF),
+            sds((rows, quarter), BF),
             sds((total, width), BF),
-            sds((total, width), BF),
-            sds((3 * used, total), BF),
+            sds((total, hp), BF),
+            sds((total, hp), BF),
+            sds((total, hp), BF),
             sds((total, HD), F32),
             sds((total, n_exp), F32),
-            sds((total, n_exp), F32),
+            sds((n_f * mine, ffe, width // n_f), F32),
+            sds((mine, ffe, width // n_f), BF),
+            sds((srows, width), BF),
         ),
-        in_specs=[
-            row_spec,
-            blk_spec,
-            exp_spec,
-            pl.BlockSpec((1, width), lambda i: (0, 0)),
-            pl.BlockSpec((n_exp, width), lambda i: (0, 0)),
+        in_specs=[HBM, HBM, VMEM, VMEM, VMEM, VMEM] + [HBM] * 7,
+        out_specs=[VMEM, HBM, HBM, HBM, HBM, VMEM, VMEM, HBM, HBM, HBM],
+        scratch_shapes=[
+            pltpu.VMEM((used, total), BF),
+            DMA((n_fetch,)),
+            DMA((2,)),
+            DMA((2,)),
+            DMA((2, 3)),
+            DMA((2,)),
+            DMA((4, 2)),
         ]
-        + [HBM] * 7,
-        out_specs=[
-            blk_spec,
-            row_spec,
-            row_spec,
-            pl.BlockSpec((3 * used, block), lambda i: (0, i)),
-            pl.BlockSpec((block, HD), lambda i: (i, 0)),
-            exp_spec,
-            exp_spec,
-        ],
+        + reducer_scratch(n_f, n_c, rows, quarter),
+        compiler_params=pltpu.CompilerParams(
+            collective_id=5, has_side_effects=True, vmem_limit_bytes=BIG
+        ),
+        cost_estimate=pl.CostEstimate(
+            flops=8 * total * width * used, bytes_accessed=80 << 20, transcendentals=total * used
+        ),
+        name="forward",
+    )(rows_all, og_all, resid, picked, gain, router, *kept, *got, shared)
+
+
+def backward_kernel(
+    n_c, n_f, mine, ffe, srows, hp, og_all, act, silu, slope, moe_in, r_all, shared_d, prob_in, picked, router,
+    resid, gain, og, wg0, wu0, wd0, wg1, wu1, wd1, shared,
+    mid_out, gain_out, seq_out, shared_out, kg_out, ku_out, gg_out, gu_out,
+    gt, blk, r_own, sends, shs, wsem, xsem, tsem, ksem, ss, sr, rs, es, er, el, ds, dr, dl, *rest,
+):
+    f, c, t = ranks()
+    n_b = n_f * n_c
+    rows, quarter = resid.shape
+    width = shared_d.shape[1]
+    n_exp = router.shape[0]
+    routed = mine * ffe
+    rows_used = routed + srows
+    first = (c * n_f + f) * mine
+    red = Reducer(n_c, rest[:18])
+
+    def blocks_phase(wgu, wd, ogs, acts):
+        fetches = fetch_experts(
+            n_c, n_f, mine, ffe, srows, hp, (wg0, wu0, wd0, wg1, wu1, wd1), shared, wgu, wd, wsem
+        )
+        for copy in fetches:
+            copy.start()
+
+        def loads(i, slot):
+            b = red.row_block(i)
+            return [
+                pltpu.make_async_copy(
+                    og_all.at[b, q], ogs.at[slot, :, pl.ds(q * quarter, quarter)], xsem.at[slot, q]
+                )
+                for q in range(4)
+            ] + [
+                pltpu.make_async_copy(src.at[piece(b, rows), :], acts.at[slot, k], xsem.at[slot, 4 + k])
+                for k, src in enumerate((act, silu, slope))
+            ]
+
+        for copy in loads(0, 0):
+            copy.start()
+        blank_rows(rows_used, hp, wgu, wd)
+        greet([{"tp": red.sib}, {"tp": red.far}, {"tp": opposite(red.sib)}] + each_peers(f, c, n_f, n_c))
+        for copy in fetches:
+            copy.wait()
+
+        def compute(i, between):
+            slot = lax.rem(i, 2)
+            at = piece(red.row_block(i), rows)
+            for copy in loads(i, slot):
+                copy.wait()
+
+            @pl.when(i + 1 < n_b)
+            def _():
+                for copy in loads(i + 1, 1 - slot):
+                    copy.start()
+
+            prob = prob_in[at, :]
+            chosen = picked[at, :]
+            gate, lane, col = gates(prob, chosen, first, mine, ffe, hp)
+            dh = dot_nt(ogs[slot], wd[...])
+            between()
+            ad = acts[slot, 0].astype(F32) * dh
+            p_grad = jnp.zeros(prob.shape, F32)
+            for k in range(mine):
+                s = jnp.sum(
+                    jnp.where((col >= k * ffe) & (col < (k + 1) * ffe), ad, 0.0), axis=1, keepdims=True
+                )
+                p_grad = jnp.where(lane == first + k, s, p_grad)
+            p_grad = p_grad * chosen
+            logit_f = prob * (p_grad - jnp.sum(prob * p_grad, axis=1, keepdims=True))
+            logit_grad = logit_f.astype(BF)
+            dg = dh * gate
+            da = (dg * acts[slot, 2].astype(F32)).astype(BF)
+            db = (dg * acts[slot, 1].astype(F32)).astype(BF)
+            gt[:rows_used, at] = da.T[:rows_used, :]
+            gt[rows_used : 2 * rows_used, at] = db.T[:rows_used, :]
+            gt[2 * rows_used :, at] = logit_f.T.astype(BF)
+            dab = jnp.concatenate([da, db], axis=1)
+
+            def part_of(q):
+                cols = piece(q, quarter)
+                return dot_nn(dab, wgu[:, cols]) + dot_nn(logit_grad, router[:, cols])
+
+            red.put(i, part_of)
+
+        red.loop(n_b, compute)
+
+    pl.run_scoped(
+        blocks_phase,
+        pltpu.VMEM((2 * hp, width), BF),
+        pltpu.VMEM((hp, width), BF),
+        pltpu.VMEM((2, rows, width), BF),
+        pltpu.VMEM((2, 3, rows, hp), BF),
+    )
+
+    def send_copy(s, m):
+        dst = (gg_out, gu_out)[m].at[:, :, pl.ds(s * quarter, quarter)]
+        return remote(sends.at[s, m], dst, ss.at[s, m], sr.at[s, m], {"fsdp": 1 - f})
+
+    def grads_phase(tiles, keeps):
+        def tile_of(s):
+            return (1 - f) * 2 + s if s < 2 else f * 2 + s - 2
+
+        def tile_load(s):
+            return pltpu.make_async_copy(
+                moe_in.at[:, piece(tile_of(s), quarter)], tiles.at[s % 2], tsem.at[s % 2]
+            )
+
+        def keep_copy(s, m):
+            dst = (kg_out, ku_out)[m].at[pl.ds(f * mine, mine), :, pl.ds((s - 2) * quarter, quarter)]
+            return pltpu.make_async_copy(keeps.at[s - 2, m], dst, ksem.at[s - 2, m])
+
+        def work(s):
+            def run():
+                tile_load(s).wait()
+                if s < 3:
+                    tile_load(s + 1).start()
+                g = dot_nn(gt[...], tiles[s % 2])
+                cols = piece(tile_of(s), quarter)
+                for m in range(2):
+                    base = m * rows_used
+                    if s < 2:
+                        sends[s, m] = g[base : base + routed].astype(BF).reshape(mine, ffe, quarter)
+                        send_copy(s, m).start()
+                    else:
+                        keeps[s - 2, m] = g[base : base + routed].reshape(mine, ffe, quarter)
+                        keep_copy(s, m).start()
+                    shs[m * srows : (m + 1) * srows, cols] = g[base + routed : base + rows_used].astype(BF)
+                shs[2 * srows :, cols] = g[2 * rows_used :].astype(BF)
+
+            return run
+
+        tile_load(0).start()
+        blk[...] = red.drain(n_b, [work(s) for s in range(4)])
+        for s in (2, 3):
+            for m in range(2):
+                keep_copy(s, m).wait()
+
+    fetch = pltpu.make_async_copy(r_all.at[piece(f * n_c + c, rows), :], r_own, rs)
+    fetch.start()
+    pl.run_scoped(
+        grads_phase,
+        pltpu.VMEM((2, n_b * rows, quarter), BF),
+        pltpu.VMEM((2, 2, mine, ffe, quarter), F32),
+    )
+    cols = width // n_b
+    n_gu = shs.shape[0]
+
+    def exchange(act):
+        for src, at, sems in (
+            (shs, pl.ds(0, n_gu), (es, er, el)),
+            (shared_d, pl.ds(n_gu, srows), (ds, dr, dl)),
+        ):
+            to_each(lambda b: src.at[:, piece(b, cols)], shared_out.at[:, at, :], n_f, n_c, sems, act)
+
+    fetch.wait()
+    back, gain_part = norm_grad(resid[...], r_own[:, :1], gain[...], blk[...], width, *rest[18:22])
+    gain_out[...] = jnp.broadcast_to(gain_part, gain_out.shape)
+    grad = og[...].astype(F32) + back
+    mid_out[...] = grad
+    own = rest[22]
+    own[...] = grad.astype(BF)
+
+    def place(g, cc, tt):
+        return seq_out.at[piece(cc, rows), piece(tt, quarter)]
+
+    spread(own, place, n_c, False, rest[23:], lambda: exchange("start"))
+    exchange("wait")
+    for s in range(2):
+        for m in range(2):
+            send_copy(s, m).wait()
+
+
+def backward(
+    n_c, n_f, n_t, mine, ffe, srows, og_all, act, silu, slope, moe_in, r_all, shared_d, prob, picked, router,
+    resid, gain, og, kept, got, shared,
+):
+    total, width = moe_in.shape
+    rows, quarter = resid.shape
+    n_exp = router.shape[0]
+    n_b = n_f * n_c
+    used, hp, n_fetch = expert_sizes(n_c, n_f, n_t, mine, ffe, srows, width)
+    sds = jax.ShapeDtypeStruct
+    kept_g = sds((n_f * mine, ffe, width // n_f), F32)
+    sent_g = sds((mine, ffe, width // n_f), BF)
+    return pl.pallas_call(
+        functools.partial(backward_kernel, n_c, n_f, mine, ffe, srows, hp),
+        out_shape=(
+            sds((rows, quarter), F32),
+            sds((8, quarter), F32),
+            sds((rows * n_c, width), BF),
+            sds((n_b, 3 * srows + n_exp, width // n_b), BF),
+            kept_g,
+            kept_g,
+            sent_g,
+            sent_g,
+        ),
+        in_specs=[HBM] * 7 + [VMEM] * 6 + [HBM] * 7,
+        out_specs=[VMEM, VMEM] + [HBM] * 6,
         scratch_shapes=[
-            pltpu.VMEM((2 * hp, width), BF),
-            pltpu.VMEM((hp, width), BF),
-            DMA((3 * (2 * mine + n_f * n_c),)),
-        ],
-        compiler_params=pltpu.CompilerParams(vmem_limit_bytes=BIG),
+            pltpu.VMEM((2 * used + n_exp, total), BF),
+            pltpu.VMEM((rows, quarter), F32),
+            pltpu.VMEM((rows, HD), F32),
+            pltpu.VMEM((2, 2, mine, ffe, quarter), BF),
+            pltpu.VMEM((2 * srows + n_exp, width), BF),
+            DMA((n_fetch,)),
+            DMA((2, 7)),
+            DMA((2,)),
+            DMA((2, 2)),
+            DMA((2, 2)),
+            DMA((2, 2)),
+            DMA(()),
+            DMA((n_b,)),
+            DMA((n_b,)),
+            DMA(()),
+            DMA((n_b,)),
+            DMA((n_b,)),
+            DMA(()),
+        ]
+        + reducer_scratch(n_f, n_c, rows, quarter)
+        + norm_grad_scratch(rows)
+        + [pltpu.VMEM((rows, quarter), BF)]
+        + spread_sems(n_c),
+        compiler_params=pltpu.CompilerParams(
+            collective_id=3, has_side_effects=True, vmem_limit_bytes=BIG
+        ),
         cost_estimate=pl.CostEstimate(
-            flops=12 * total * width * used, bytes_accessed=70 << 20, transcendentals=total * used
+            flops=10 * total * width * used, bytes_accessed=200 << 20, transcendentals=0
         ),
-        name="experts",
-    )(x, og, picked, gain, router, *kept, *got, shared)
-
-
-def expert_grad_kernel(used, mine, ffe, f_ref, gt, x, og, kg, ku, kd, sg, su, sd, shared):
-    del f_ref
-    step = pl.program_id(0)
-    cols = x.shape[1]
-    routed = mine * ffe
-    og_rows = og[...].reshape(-1, cols)
-    for i, (keep, send) in enumerate(((kg, sg), (ku, su), (kd, sd))):
-        rhs = og_rows if i == 2 else x[...]
-        g = dot_nn(gt[i * used : (i + 1) * used, :], rhs)
-        shared[i * (used - routed) : (i + 1) * (used - routed), :] = g[routed:].astype(BF)
-
-        @pl.when(step < 2)
-        def _():
-            send[...] = g[:routed].astype(BF).reshape(mine, ffe, cols)
-
-        @pl.when(step >= 2)
-        def _():
-            keep[...] = g[:routed].reshape(mine, ffe, cols)
-
-
-def expert_grads(f_rank, n_f, used, mine, ffe, gt, x, og):
-    total, width = x.shape
-    n_blocks, n_t, rows, quarter = og.shape
-    half = width // n_f
-    srows = used - mine * ffe
-    sds = jax.ShapeDtypeStruct
-
-    def tile(i, f):
-        other = 1 - f[0]
-        return jnp.where(i < 2, other * 2 + i, f[0] * 2 + i - 2)
-
-    keep_spec = pl.BlockSpec((mine, ffe, quarter), lambda i, f: (f[0], 0, jnp.where(i < 2, 0, i - 2)))
-    send_spec = pl.BlockSpec((mine, ffe, quarter), lambda i, f: (0, 0, jnp.where(i < 2, i, 1)))
-    return pl.pallas_call(
-        functools.partial(expert_grad_kernel, used, mine, ffe),
-        grid_spec=pltpu.PrefetchScalarGridSpec(
-            num_scalar_prefetch=1,
-            grid=(width // quarter,),
-            in_specs=[
-                pl.BlockSpec(gt.shape, lambda i, f: (0, 0)),
-                pl.BlockSpec((total, quarter), lambda i, f: (0, tile(i, f))),
-                pl.BlockSpec((n_blocks, 1, rows, quarter), lambda i, f: (0, tile(i, f), 0, 0)),
-            ],
-            out_specs=[keep_spec] * 3
-            + [send_spec] * 3
-            + [pl.BlockSpec((3 * srows, quarter), lambda i, f: (0, tile(i, f)))],
-        ),
-        out_shape=tuple([sds((n_f * mine, ffe, half), F32)] * 3)
-        + tuple([sds((mine, ffe, half), BF)] * 3)
-        + (sds((3 * srows, width), BF),),
-        compiler_params=pltpu.CompilerParams(vmem_limit_bytes=BIG),
-        cost_estimate=pl.CostEstimate(
-            flops=6 * total * width * used, bytes_accessed=50 << 20, transcendentals=0
-        ),
-        name="expert_grads",
-    )(f_rank, gt, x, og)
+        name="backward",
+    )(
+        og_all, act, silu, slope, moe_in, r_all, shared_d, prob, picked, router, resid, gain, og,
+        *kept, *got, shared,
+    )
 
 
 def fill_kernel(f_ref, a, b, c, _a, _b, _c, oa, ob, oc):
@@ -1105,139 +1527,6 @@
         DMA((3,)),
         DMA((3,)),
     ]
-
-
-def back_kernel(
-    n_c, width, part, resid, r_all, gain, og, mid_out, gain_out, seq_out,
-    blk, r_own, own, in1, out2, in2, out3, in3, acc, out4, in4,
-    ls, rs, s1, r1, s2, r2, s3, r3, s4, r4, *rest,
-):
-    f, c, t = ranks()
-    rows, quarter = og.shape
-    far, sib = opposite(t), sibling(t)
-    to_sib, to_far, to_other = {"tp": sib}, {"tp": far}, {"fsdp": 1 - f}
-    greet([to_sib, to_far, {"tp": opposite(sib)}, to_other] + line_peers(c, n_c))
-    order = [2, 1, 3, 0] if n_c == 4 else list(range(1, n_c)) + [0]
-    blocks = [(g, d) for g in (1, 0) for d in order]
-
-    def part_at(g, d, q):
-        group = 1 - f if g else f
-        return part.at[piece(group * n_c + lax.rem(c + d, n_c), rows), piece(q, quarter)]
-
-    def core(g, d):
-        i = g * n_c + d
-        return [
-            remote(part_at(g, d, q), in1.at[i, k], s1.at[i, k], r1.at[i, k], to_sib)
-            for k, q in enumerate((opposite(sib), sib))
-        ]
-
-    def mine_of(g, d):
-        i = g * n_c + d
-        return [
-            pltpu.make_async_copy(part_at(g, d, q), own.at[i, k], ls.at[i, k])
-            for k, q in enumerate((far, t))
-        ]
-
-    fetch = pltpu.make_async_copy(r_all.at[piece(f * n_c + c, rows), :], r_own, rs)
-    fetch.start()
-    for g, d in blocks:
-        for copy in core(g, d) + mine_of(g, d):
-            copy.start()
-
-    def over(g, d):
-        i = g * n_c + d
-        return remote(out2.at[i], in2.at[i], s2.at[i], r2.at[i], to_far)
-
-    for g, d in blocks:
-        i = g * n_c + d
-        for copy in core(g, d) + mine_of(g, d):
-            copy.wait()
-        out2[i] = (own[i, 0].astype(F32) + in1[i, 0].astype(F32)).astype(BF)
-        over(g, d).start()
-
-    def other(d):
-        return remote(out3.at[d], in3.at[d], s3.at[d], r3.at[d], to_other)
-
-    for g, d in blocks:
-        i = g * n_c + d
-        over(g, d).wait()
-        total = own[i, 1].astype(F32) + in1[i, 1].astype(F32) + in2[i].astype(F32)
-        if g:
-            out3[d] = total.astype(BF)
-            other(d).start()
-        else:
-            acc[d] = total
-
-    def line(d, to):
-        return remote(out4.at[d], in4.at[d], s4.at[d], r4.at[d], {"ctx": to})
-
-    for d in order:
-        other(d).wait()
-        total = acc[d] + in3[d].astype(F32)
-        if d:
-            out4[d] = total.astype(BF)
-            line(d, lax.rem(c + d, n_c)).start()
-    for d in order[:-1]:
-        line(d, c).wait()
-        total = total + in4[d].astype(F32)
-    fetch.wait()
-    back, gain_part = norm_grad(resid[...], r_own[:, :1], gain[...], total, width, *rest[:4])
-    gain_out[...] = jnp.broadcast_to(gain_part, gain_out.shape)
-    grad = og[...].astype(F32) + back
-    mid_out[...] = grad
-    blk[...] = grad.astype(BF)
-
-    def place(g, cc, tt):
-        return seq_out.at[piece(cc, rows), piece(tt, quarter)]
-
-    spread(blk, place, n_c, False, rest[4:])
-
-
-def back(n_c, n_f, n_t, part, resid, r_all, gain, og):
-    rows, quarter = og.shape
-    n_b = n_c * n_f
-    sds = jax.ShapeDtypeStruct
-    blocks = lambda *lead: pltpu.VMEM(lead + (rows, quarter), BF)
-    return pl.pallas_call(
-        functools.partial(back_kernel, n_c, quarter * n_t),
-        out_shape=(
-            sds((rows, quarter), F32),
-            sds((8, quarter), F32),
-            sds((rows * n_c, quarter * n_t), BF),
-        ),
-        in_specs=[HBM, VMEM, HBM, VMEM, VMEM],
-        out_specs=[VMEM, VMEM, HBM],
-        scratch_shapes=[
-            blocks(),
-            pltpu.VMEM((rows, HD), F32),
-            blocks(n_b, 2),
-            blocks(n_b, 2),
-            blocks(n_b),
-            blocks(n_b),
-            blocks(n_c),
-            blocks(n_c),
-            pltpu.VMEM((n_c, rows, quarter), F32),
-            blocks(n_c),
-            blocks(n_c),
-            DMA((n_b, 2)),
-            DMA(()),
-            DMA((n_b, 2)),
-            DMA((n_b, 2)),
-            DMA((n_b,)),
-            DMA((n_b,)),
-            DMA((n_c,)),
-            DMA((n_c,)),
-            DMA((n_c,)),
-            DMA((n_c,)),
-        ]
-        + norm_grad_scratch(rows)
-        + spread_sems(n_c),
-        compiler_params=pltpu.CompilerParams(
-            collective_id=3, has_side_effects=True, vmem_limit_bytes=BIG
-        ),
-        cost_estimate=pl.CostEstimate(flops=1 << 20, bytes_accessed=200 << 20, transcendentals=0),
-        name="back",
-    )(part, resid, r_all, gain, og)
 
 
 def attend_back_kernel(
@@ -1292,9 +1581,9 @@
 
 
 def last_kernel(
-    n_c, n_f, n_t, width, dqkv, wqkv, hidden, r_all, gain, mid_grad, gain2, gattn,
-    in_out, gq, gk, gv, go, gains_out,
-    r_own, outx, inx, own, outz, inz, gsend, gin, rs, sx, rx, lx, sz, rz, gs, gr, *rest,
+    n_c, n_f, n_t, width, dqkv, wqkv, hidden, r_all, gain, mid_grad, gain2, rpart, gattn,
+    in_out, gq, gk, gv, go, gains_out, router_out,
+    rin, rss, rsr, r_own, outx, inx, own, outz, inz, gsend, gin, rs, sx, rx, lx, sz, rz, gs, gr, *rest,
 ):
     f, c, t = ranks()
     rows, quarter = hidden.shape
@@ -1329,6 +1618,12 @@
     def line(d, to):
         return remote(outz.at[d], inz.at[d], sz.at[d], rz.at[d], {"ctx": to})
 
+    router_copies = [
+        remote(rpart, rin.at[i], rss.at[i], rsr.at[i], {"tp": peer})
+        for i, peer in enumerate([sibling(t), opposite(t), opposite(sibling(t))])
+    ]
+    for copy in router_copies:
+        copy.start()
     fetch = pltpu.make_async_copy(r_all.at[piece(c, rows), :], r_own, rs)
     fetch.start()
     for d in order:
@@ -1408,9 +1703,12 @@
         jnp.zeros((8, part), F32),
     )
     gains_out[...] = own_part + jnp.sum(gin[...], axis=0)
-
-
-def last(n_c, n_f, n_t, dqkv, wqkv, hidden, r_all, gain, mid_grad, gain2, gattn):
+    for copy in router_copies:
+        copy.wait()
+    router_out[...] = rpart[...] + jnp.sum(rin[...], axis=0)
+
+
+def last(n_c, n_f, n_t, dqkv, wqkv, hidden, r_all, gain, mid_grad, gain2, rpart, gattn):
     rows, quarter = hidden.shape
     width = quarter * n_t
     part = width // (n_f * n_c)
@@ -1425,10 +1723,14 @@
             sds((part, n_c * HD), F32),
             sds((n_c * HD, part), F32),
             sds((8, part), F32),
+            sds(rpart.shape, F32),
         ),
-        in_specs=[VMEM, VMEM, VMEM, HBM, VMEM, VMEM, VMEM, HBM],
-        out_specs=[VMEM] * 6,
+        in_specs=[VMEM, VMEM, VMEM, HBM, VMEM, VMEM, VMEM, VMEM, HBM],
+        out_specs=[VMEM] * 7,
         scratch_shapes=[
+            pltpu.VMEM((3,) + rpart.shape, F32),
+            DMA((3,)),
+            DMA((3,)),
             pltpu.VMEM((rows, HD), F32),
             slab,
             slab,
@@ -1453,7 +1755,7 @@
         ),
         cost_estimate=pl.CostEstimate(flops=2 << 30, bytes_accessed=150 << 20, transcendentals=0),
         name="last",
-    )(dqkv, wqkv, hidden, r_all, gain, mid_grad, gain2, gattn)
+    )(dqkv, wqkv, hidden, r_all, gain, mid_grad, gain2, rpart, gattn)
 
 
 def per_device_seq(
@@ -1495,12 +1797,12 @@
 
     gate_t, up_t = expert_gate.swapaxes(1, 2), expert_up.swapaxes(1, 2)
     weights = (gate_t, up_t, expert_down)
-    got = tuple(
-        lax.ppermute(
-            lax.dynamic_slice_in_dim(w, (n_f - 1 - f_rank) * mine, mine, 0), "fsdp", swap
-        )
-        for w in weights
-    )
+
+    def swapped(weight):
+        given = lax.dynamic_slice_in_dim(weight, (n_f - 1 - f_rank) * mine, mine, 0)
+        return lax.ppermute(given, "fsdp", swap)
+
+    got_down = swapped(expert_down)
 
     picked_own = jnp.sum(
         (chosen[:, :, None] == jnp.arange(n_exp)[None, None, :]).astype(F32), axis=1
@@ -1521,8 +1823,9 @@
     router_t = small_all[2 : 2 + n_exp].astype(BF)
     picked = small_all[2 + n_exp : 2 + 2 * n_exp].T
     pos_seq = lax.dynamic_slice(small_all, (2 + 2 * n_exp, f_rank * seq), (1, seq))[0]
-    after = lambda x: lax.optimization_barrier((x, hidden_seq))[0]
-    grad_all = lax.all_gather(after(out_grad), every, axis=0, tiled=False)
+    after = lambda x, y: lax.optimization_barrier((x, y))[0]
+    got = (swapped(after(gate_t, hidden_seq)), swapped(after(up_t, hidden_seq)), got_down)
+    grad_all = lax.all_gather(after(out_grad, hidden_seq), every, axis=0, tiled=False)
     grad_all = grad_all.reshape(n_b, n_t, rows, quarter)
 
     def shared_part(weight):
@@ -1533,7 +1836,6 @@
     shared = jnp.concatenate(
         [shared_part(shared_gate.T), shared_part(shared_up.T), shared_part(shared_down)], axis=1
     )
-    shared = lax.all_to_all(after(shared), group, split_axis=0, concat_axis=0, tiled=True)
 
     half = HD // 2
     inverse = 10000.0 ** (-jnp.arange(half, dtype=F32) * 2.0 / HD)
@@ -1542,36 +1844,29 @@
     cosine = jnp.concatenate([cosine, cosine], axis=1)
     sine = jnp.concatenate([-sine, sine], axis=1)
     normed, q, k, v, heads_f, heads_b, lse, r_one = attend(hidden_seq, gain_one, wqkv, cosine, sine)
-    resid_mid, resid_all = mid(n_c, n_f, n_t, heads_b, wo, hidden_in)
-
-    moe_part, back_part, moe_in, g_t, r_two, prob, p_part = experts(
-        n_c, n_f, n_t, rows, mine, ffe, srows, resid_all, grad_all, picked, gain_two, router_t,
-        weights, got, shared,
-    )
-    used = mine * ffe + srows
-    kg, ku, kd, sg, su, sd, shared_g = expert_grads(f_arr, n_f, used, mine, ffe, g_t, moe_in, grad_all)
-    arrived = tuple(lax.ppermute(s, "fsdp", swap) for s in (sg, su, sd))
+    resid_mid, resid_all, shared = mid(n_c, n_f, n_t, heads_b, wo, hidden_in, shared)
+
+    sizes = (n_c, n_f, n_t, mine, ffe, srows)
+    layer_out, moe_in, act, silu, slope, r_two, prob, kd, sd, shared_d = forward(
+        *sizes, resid_all, grad_all, resid_mid, picked, gain_two, router_t, weights, got, shared
+    )
+    arrived_d = lax.ppermute(sd, "fsdp", swap)
     own_cols = lambda x: lax.dynamic_slice_in_dim(x, t_rank * quarter, quarter, 1)
-    mid_grad, gain_two_part, mid_seq = back(
-        n_c, n_f, n_t, back_part, resid_mid, r_two, own_cols(gain_two), out_grad
-    )
-    later = lambda x: lax.optimization_barrier((x, mid_seq))[0]
-    moe_q = lax.psum_scatter(
-        later(moe_part).reshape(n_b * n_t, rows, quarter), every, scatter_dimension=0, tiled=True
-    )[0].astype(F32)
-    layer_out = (resid_mid + moe_q).astype(BF)
-    p_grad = lax.psum(later(p_part), every)
-    logit_grad = (prob * (p_grad - jnp.sum(prob * p_grad, axis=1, keepdims=True))).astype(BF)
-    router_grad = dot_tn(lax.dynamic_slice_in_dim(moe_in, block * part, part, 1), logit_grad)
-    shared_sent = later(shared_g).reshape(3 * srows, n_b, part).swapaxes(0, 1)
-    shared_back = lax.all_to_all(shared_sent, group, split_axis=0, concat_axis=0, tiled=True)
+    mid_grad, gain_two_part, mid_seq, shared_back, kg, ku, gg, gu = backward(
+        *sizes, grad_all, act, silu, slope, moe_in, r_two, shared_d, prob, picked, router_t,
+        resid_mid, own_cols(gain_two), out_grad, weights, got, shared,
+    )
+    n_gu = 2 * srows
+    router_part = jnp.sum(shared_back[:, n_gu : n_gu + n_exp].astype(F32), axis=0)
+    shared_back = jnp.concatenate([shared_back[:, :n_gu], shared_back[:, n_gu + n_exp :]], axis=1)
     shared_back = shared_back.reshape(n_b, 3, srows, part)[:, :, :own_shared].astype(F32)
 
     dqkv, gattn = attend_back(mid_seq, wo, q, k, v, heads_f, lse, cosine, sine, normed)
-    input_grad, gq, gk, gv, go, gains = last(
-        n_c, n_f, n_t, dqkv, wqkv, hidden_in, r_one, own_cols(gain_one), mid_grad, gain_two_part, gattn
-    )
-    eg, eu, ed = fill_experts(f_arr, arrived, (kg, ku, kd))
+    input_grad, gq, gk, gv, go, gains, router_grad = last(
+        n_c, n_f, n_t, dqkv, wqkv, hidden_in, r_one, own_cols(gain_one), mid_grad, gain_two_part,
+        router_part, gattn,
+    )
+    eg, eu, ed = fill_experts(f_arr, (gg, gu, arrived_d), (kg, ku, kd))
 
     def shared_cols(i):
         return shared_back[:, i].reshape(n_b * own_shared, part)
@@ -1585,7 +1880,7 @@
         gv,
         go,
         gains[1],
-        router_grad,
+        router_grad.T,
         shared_cols(0).T,
         shared_cols(1).T,
         shared_cols(2),

time: 773 us -> 599 us (0.77)
  waiting for transfers between devices: 85.3 us -> 0.05 us
  Pallas kernels: 615 us -> 533 us
  starting transfers between devices: 16.1 us -> 2.9 us
  local copies, waits for them, and re-layouts: 18.7 us -> 30.9 us
    reduce_scatter x1 -> x0, waiting for transfers between devices: 84.5 us -> none  [per_device_seq(): lax.psum_scatter(later(moe_part).reshape(n_b * n_t, rows, quarter), every...]
    pallas_call x1, Pallas kernels: 146 us -> 69.1 us  [last(): pl.pallas_call(functools.partial(last_kernel, n_c, n_f, n_t, width), out_...]
    unnamed x27 -> x44, local copies, waits for them, and re-layouts: 4.01 us -> 18.4 us
    pallas_call x1, Pallas kernels: 83.2 us -> 70.4 us  [front(): pl.pallas_call(functools.partial(front_kernel, n_c, part), out_shape=(jax...]
    all_to_all x2 -> x0, starting transfers between devices: 8 us -> none  [the longest x1 4.26 us: per_device_seq(): lax.all_to_all(after(shared), group, split_axis=0, concat_axis=0, tiled=T...]
    pallas_call x4 -> x3, Pallas kernels: 358 us -> 366 us  [the longest x1 143 us: backward(): pl.pallas_call(functools.partial(backward_kernel, n_c, n_f, mine, ffe, sr...]
  transfers between devices with their start and end apart: 11 -> 5, of which waited for: 1 -> 0; matrix products, arithmetic and copies ran while one was open for 3% -> 3% of each run, Pallas kernels for 45% -> 64%
where the time goes in v3:
time: 599 us; the launch traced here: 590 us
  Pallas kernels  533 us (89%)
  local copies, waits for them, and re-layouts  30.9 us (5%)
  between operations  14.4 us (2%)
  other arithmetic  9.57 us (2%)
    pallas_call x1, Pallas kernels, backward(): pl.pallas_call(functools.partial(backward_kernel, n_c, n_f, mine, ffe, sr...  143 us
    pallas_call x1, Pallas kernels, mid(): pl.pallas_call(functools.partial(mid_kernel, n_c, n_f), out_shape=(jax.Sh...  143 us
    pallas_call x1, Pallas kernels, forward(): pl.pallas_call(functools.partial(forward_kernel, n_c, n_f, mine, ffe, sro...  79.5 us
    pallas_call x1, Pallas kernels, front(): pl.pallas_call(functools.partial(front_kernel, n_c, part), out_shape=(jax...  70.4 us
    pallas_call x1, Pallas kernels, last(): pl.pallas_call(functools.partial(last_kernel, n_c, n_f, n_t, width), out_...  69.1 us
    unnamed x44, local copies, waits for them, and re-layouts  18.4 us
  transfers between devices with their start and end apart: 5, of which 0 were waited for; matrix products, arithmetic and copies ran while one was open for 3% of the time, Pallas kernels for 64%

profile of v3, /device:TPU:0, one launch (start us, length us, event | category | flops | bytes accessed | tf_op | source)
XLA Modules:
  0.0 590.4 jit_solution(3383813843271954762)
XLA Ops:
  11.5 70.4 %front.1 = (bf16[1024,2048]{1,0:T(8,128)(2,1)}, bf16[2048,384]{1,0:T(8,128)(2,1)}, bf16[128,2048]{1,0:T(8,128)(2,1)}, f32[40,2048]{1,0:T(8,128)}) custom-call(bf16[256,512]{1,0:T(8,128)(2,1)} %hidden.5, bf16[256,512]{1,0:T(8,128)(2,1)} %wq.1, bf16[256,512]{1,0:T(8,128)(2,1)} %wk.1, bf16[256,512]{1,0:T(8,128)(2,1)} %wv.1, bf16[512,256]{1,0:T(8,128)(2,1)} %wo.1, ...), custom_call_target="tpu_custom_call" | custom-call | bytes 104857600 | tf_op jit(solution)/shard_map/front/pallas_call | solution.py:722
  82.0 1.6 constant_dynamic-slice_fusion.2
  84.3 1.5 constant_dynamic-slice_fusion.3
  85.8 1.6 collective-permute-start.1
  87.3 1.2 constant_dynamic-slice_fusion.4
  89.7 1.3 copy.37
  91.1 1.9 fusion.6
  93.0 1.3 pad_maximum_fusion.1
  95.0 9.4 %attend.1 = (bf16[1024,2048]{1,0:T(8,128)(2,1)}, bf16[1024,128]{1,0:T(8,128)(2,1)}, bf16[1024,128]{1,0:T(8,128)(2,1)}, bf16[1024,128]{1,0:T(8,128)(2,1)}, f32[10...) custom-call(bf16[1024,2048]{1,0:T(8,128)(2,1)} %get-tuple-element.63.hidden, ...), custom_call_target="tpu_custom_call" | custom-call | flops 2147483648 | bytes 12582912 | tf_op jit(solution)/shard_map/attend/pallas_call | solution.py:786
  104.4 2.1 fusion.5.shared
  106.4 142.8 %mid.1 = (f32[256,512]{1,0:T(8,128)}, bf16[2048,2048]{1,0:T(8,128)(2,1)}, bf16[8,288,256]{2,1,0:T(8,128)(2,1)}) custom-call(bf16[1024,128]{1,0:T(8,128)(2,1)} %get-tuple-element.66.heads, bf16[128,2048]{1,0:T(8,128)(2,1)} %get-tuple-element.67.wo, bf16[256,512]{1,0:T(8,128)(2,1)} %hidden.5, bf16[8,288,256]{2,1,0:T(8,128)(2,1)} %fusion.5.shared), custom_call_target="tpu_custom_call" | custom-call | flops 536870912 | bytes 209715200 | tf_op jit(solution)/shard_map/mid/pallas_call | solution.py:870
  249.2 1.3 constant_dynamic-slice_fusion.gain
  251.1 79.5 %forward.1 = (bf16[256,512]{1,0:T(8,128)(2,1)}, bf16[2048,2048]{1,0:T(8,128)(2,1)}, bf16[2048,896]{1,0:T(8,128)(2,1)}, bf16[2048,896]{1,0:T(8,128)(2,1)}, bf16[2...) custom-call(bf16[2048,2048]{1,0:T(8,128)(2,1)} %get-tuple-element.68, ...), custom_call_target="tpu_custom_call" | custom-call | flops 26843545600 | bytes 83886080 | tf_op jit(solution)/shard_map/forward/pallas_call | solution.py:1212
  330.8 143.4 %backward.1 = (f32[256,512]{1,0:T(8,128)}, f32[8,512]{1,0:T(8,128)}, bf16[1024,2048]{1,0:T(8,128)(2,1)}, bf16[8,304,256]{2,1,0:T(8,128)(2,1)}, f32[4,352,1024]{2...) custom-call(bf16[8,4,256,512]{3,2,1,0:T(8,128)(2,1)} %bitcast.60, ...), custom_call_target="tpu_custom_call" | custom-call | flops 33554432000 | bytes 209715200 | tf_op jit(solution)/shard_map/backward/pallas_call | solution.py:1430
  474.2 11.9 %attend_back.1 = (bf16[1024,384]{1,0:T(8,128)(2,1)}, bf16[512,2048]{1,0:T(8,128)(2,1)}) custom-call(bf16[1024,2048]{1,0:T(8,128)(2,1)} %get-tuple-element.82.mid, bf16[128,2048]{1,0:T(8,128)(2,1)} %get-tuple-element.67.wo, bf16[1024,128]{1,0:T(8,128)(2,1)} %get-tuple-element.83.q, bf16[1024,128]{1,0:T(8,128)(2,1)} %get-tuple-element.84.k, ...), custom_call_target="tpu_custom_call" | custom-call | flops 6442450944 | bytes 16777216 | tf_op jit(solution)/shard_map/attend_back/pallas_call | solution.py:1571
  486.8 69.1 %last.1 = (f32[256,512]{1,0:T(8,128)}, f32[256,512]{1,0:T(8,128)}, f32[256,512]{1,0:T(8,128)}, f32[256,512]{1,0:T(8,128)}, f32[512,256]{1,0:T(8,128)}, /*index=5*/f32[8,256]{1,0:T(8,128)}, f32[16,256]{1,0:T(8,128)}) custom-call(bf16[1024,384]{1,0:T(8,128)(2,1)} %get-tuple-element.89.dqkv, bf16[2048,384]{1,0:T(8,128)(2,1)} %get-tuple-element.65.wqkv, ...), custom_call_target="tpu_custom_call" | custom-call | flops 2147483648 | bytes 157286400 | tf_op jit(solution)/shard_map/last/pallas_call | solution.py:1717
  556.0 1.3 fusion.9
  557.5 1.4 fusion.7
  560.0 6.2 %fill_experts.1 = (f32[4,352,1024]{2,1,0:T(8,128)}, f32[4,352,1024]{2,1,0:T(8,128)}, f32[4,352,1024]{2,1,0:T(8,128)}) custom-call(s32[1]{0:T(128)} %bitcast.24.f_ref, bf16[2,352,1024]{2,1,0:T(8,128)(2,1)} %get-tuple-element.102.a, bf16[2,352,1024]{2,1,0:T(8,128)(2,1)} %get-tuple-element.103.b, ...), custom_call_target="tpu_custom_call", output_to_operand_aliasing={{0}: (4, {}), {1}: (5, {}), {2}: (6, {})} | custom-call | tf_op jit(solution)/shard_map/fill_experts/pallas_call | solution.py:1493
  566.2 1.8 copy.51
  572.6 2.9 copy.58
  575.5 1.8 copy-done.1
  577.3 2.8 copy.59
  580.9 2.5 copy.60
  (68 shorter events, 15.1 us)
Async XLA Ops:
  7.2 243.9 %all-gather.3.cloned.1.call-start = ((), (), s32[]{:S(2)}) async-start(), calls=%async_computation | async-start | bytes 8650752 | tf_op jit(solution)/shard_map/all_gather | solution.py:1828
  82.0 5.3 copy-start.4
  83.7 167.4 %collective-permute-start.2 = (bf16[2,352,1024]{2,1,0:T(8,128)(2,1)S(1)}, bf16[2,352,1024]{2,1,0:T(8,128)(2,1)}, u32[]{:S(2)}, u32[]{:S(2)}) collective-permute-start(bf16[2,352,1024]{2,1,0:T(8,128)(2,1)S(1)} %constant_dynamic-slice_fusion.2), channel_id=1, source_target_pairs={{0,16},{16,0},{1,17},{17,1},{2,18},{18,2},{3,19},{19,3},{4,20},{20... | collective-permute-start | bytes 4325384 | tf_op jit(solution)/shard_map/ppermute | solution.py:1803
  84.3 4.8 copy-start.12
  85.8 165.3 %collective-permute-start.1 = (bf16[2,352,1024]{2,1,0:T(8,128)(2,1)S(1)}, bf16[2,352,1024]{2,1,0:T(8,128)(2,1)}, u32[]{:S(2)}, u32[]{:S(2)}) collective-permute-start(bf16[2,352,1024]{2,1,0:T(8,128)(2,1)S(1)} %constant_dynamic-slice_fusion.3), channel_id=1, source_target_pairs={{0,16},{16,0},{1,17},{17,1},{2,18},{18,2},{3,19},{19,3},{4,20},{20... | collective-permute-start | bytes 4325384 | tf_op jit(solution)/shard_map/ppermute | solution.py:1803
  88.5 162.5 %collective-permute-start = (bf16[2,352,1024]{2,1,0:T(8,128)(2,1)}, bf16[2,352,1024]{2,1,0:T(8,128)(2,1)}, u32[]{:S(2)}, u32[]{:S(2)}) collective-permute-start(bf16[2,352,1024]{2,1,0:T(8,128)(2,1)} %constant_dynamic-slice_fusion.4), channel_id=1, source_target_pairs={{0,16},{16,0},{1,17},{17,1},{2,18},{18,2},{3,19},{19,3},{4,20},{20... | collective-permute-start | bytes 4325384 | tf_op jit(solution)/shard_map/ppermute | solution.py:1803
  94.9 155.5 %copy-start.14 = (f32[1,2048]{1,0:T(1,128)}, f32[1,2048]{1,0:T(1,128)S(1)}, u32[]{:S(2)}) copy-start(f32[1,2048]{1,0:T(1,128)S(1)} %get-tuple-element.114.gain) | copy-start | bytes 24580
  94.9 9.4 %copy-start.10 = (bf16[704,256]{1,0:T(8,128)(2,1)S(1)}, bf16[704,256]{1,0:T(8,128)(2,1)}, u32[]{:S(2)}) copy-start(bf16[704,256]{1,0:T(8,128)(2,1)} %param.30) | copy-start | bytes 1081348
  94.9 9.4 %copy-start.11 = (bf16[256,704]{0,1:T(8,128)(2,1)S(1)}, bf16[256,704]{0,1:T(8,128)(2,1)}, u32[]{:S(2)}) copy-start(bf16[256,704]{0,1:T(8,128)(2,1)} %param.29) | copy-start | bytes 1081348
  330.6 228.2 %collective-permute-start.3 = (bf16[2,352,1024]{2,1,0:T(8,128)(2,1)}, bf16[2,352,1024]{2,1,0:T(8,128)(2,1)S(1)}, u32[]{:S(2)}, u32[]{:S(2)}) collective-permute-start(bf16[2,352,1024]{2,1,0:T(8,128)(2,1)} %get-tuple-element.104), channel_id=1, source_target_pairs={{0,16},{16,0},{1,17},{17,1},{2,18},{18,2},{3,19},{19,3},{4,20},{20... | collective-permute-start | bytes 4325384 | tf_op jit(solution)/shard_map/ppermute | solution.py:1853
  474.2 11.9 %copy-start.3 = (bf16[8,304,256]{2,1,0:T(8,128)(2,1)S(1)}, bf16[8,304,256]{2,1,0:T(8,128)(2,1)}, u32[]{:S(2)}) copy-start(bf16[8,304,256]{2,1,0:T(8,128)(2,1)} %get-tuple-element.93) | copy-start | bytes 3735556
  558.9 1.1 copy-start.2
  560.0 8.0 %copy-start.9 = (f32[256,512]{1,0:T(8,128)S(1)}, f32[256,512]{1,0:T(8,128)}, u32[]{:S(2)}) copy-start(f32[256,512]{1,0:T(8,128)} %get-tuple-element.139) | copy-start | bytes 1572868
  560.0 8.8 %copy-start.8 = (f32[256,512]{1,0:T(8,128)S(1)}, f32[256,512]{1,0:T(8,128)}, u32[]{:S(2)}) copy-start(f32[256,512]{1,0:T(8,128)} %get-tuple-element.141) | copy-start | bytes 1572868
  560.0 9.6 %copy-start.7 = (f32[256,512]{1,0:T(8,128)S(1)}, f32[256,512]{1,0:T(8,128)}, u32[]{:S(2)}) copy-start(f32[256,512]{1,0:T(8,128)} %get-tuple-element.142) | copy-start | bytes 1572868
  560.0 10.4 %copy-start.6 = (f32[256,512]{1,0:T(8,128)S(1)}, f32[256,512]{1,0:T(8,128)}, u32[]{:S(2)}) copy-start(f32[256,512]{1,0:T(8,128)} %get-tuple-element.143) | copy-start | bytes 1572868
  560.0 11.2 %copy-start.5 = (f32[512,256]{1,0:T(8,128)S(1)}, f32[512,256]{1,0:T(8,128)}, u32[]{:S(2)}) copy-start(f32[512,256]{1,0:T(8,128)} %get-tuple-element.144) | copy-start | bytes 1572868
  560.0 12.0 %copy-start.13 = (f32[16,256]{1,0:T(8,128)S(1)}, f32[16,256]{1,0:T(8,128)}, u32[]{:S(2)}) copy-start(f32[16,256]{1,0:T(8,128)} %get-tuple-element.101) | copy-start | bytes 49156
  566.1 6.4 %copy-start = (f32[4,352,1024]{2,1,0:T(8,128)S(1)}, f32[4,352,1024]{2,1,0:T(8,128)}, u32[]{:S(2)}) copy-start(f32[4,352,1024]{2,1,0:T(8,128)} %get-tuple-element.108) | copy-start | bytes 17301508
  572.6 4.7 copy-start.1
  572.6 7.5 %slice-start = ((s8[5767168]{0:T(1024)(128)(4,1)}), s8[4194304]{0:T(1024)(128)(4,1)S(1)}, s32[]{:S(2)}) async-start(s8[5767168]{0:T(1024)(128)(4,1)} %bitcast.32), calls=%async_computation.1 | async-start | bytes 8388608
  577.3 3.6 slice-start.1
Sparse Core Ops, SparseCore 0:
  82.1 119.2 all-gather.2

commit v4 on v3

--- a/solution.py
+++ b/solution.py
@@ -514,112 +514,129 @@
     ]
 
 
-def spread(own, place, n_c, both, sems, after_line=None):
-    zs, zr, xs, xr, ys, yr, ks, kr, ls = sems
-    f, c, t = ranks()
-    far = opposite(t)
-    to_sib, to_far, to_other = {"tp": sibling(t)}, {"tp": far}, {"fsdp": 1 - f}
-
-    def far_copy(src, i, g, cc):
-        return remote(src, place(g, cc, t), ys.at[i], yr.at[i], to_far)
-
-    def sib_copy(src, i, which, g, cc, col):
+class Spread:
+    def __init__(self, own, place, n_c, both, sems):
+        self.own, self.place, self.n_c, self.both = own, place, n_c, both
+        self.zs, self.zr, self.xs, self.xr, self.ys, self.yr, self.ks, self.kr, self.ls = sems
+        self.f, self.c, self.t = ranks()
+        self.other_t = opposite(self.t)
+        self.groups = ((self.f, 0), (1 - self.f, n_c))[: 2 if both else 1]
+
+    def local(self):
+        return pltpu.make_async_copy(self.own, self.place(self.f, self.c, self.t), self.ls)
+
+    def far_copy(self, src, i, g, cc, col):
+        return remote(src, self.place(g, cc, col), self.ys.at[i], self.yr.at[i], {"tp": self.other_t})
+
+    def sib_copy(self, src, i, which, g, cc, col):
         at = 2 * i + which
-        return remote(src, place(g, cc, col), ks.at[at], kr.at[at], to_sib)
-
-    def other_copy(src, cc):
-        return remote(src, place(f, cc, t), xs.at[cc], xr.at[cc], to_other)
-
-    def line_copy(src, cc, sem, to):
-        return remote(src, place(f, cc, t), zs.at[sem], zr.at[cc], {"ctx": to})
-
-    def pass_on(src, i, g, cc):
-        far_copy(src, i, g, cc).start()
-        sib_copy(src, i, 0, g, cc, t).start()
-
-    local = pltpu.make_async_copy(own, place(f, c, t), ls)
-    local.start()
-
-    @pl.when(c < n_c - 1)
-    def _():
-        line_copy(own, c, n_c, c + 1).start()
-
-    @pl.when(c > 0)
-    def _():
-        line_copy(own, c, n_c + 1, c - 1).start()
-
-    if both:
-        other_copy(own, c).start()
-    pass_on(own, c, f, c)
-    for step in range(1, n_c):
-        for side in (-1, 1):
-            cc = c + side * step
-            onward = c - side
-
-            @pl.when((cc >= 0) & (cc < n_c))
+        return remote(src, self.place(g, cc, col), self.ks.at[at], self.kr.at[at], {"tp": sibling(self.t)})
+
+    def other_copy(self, src, g, cc):
+        return remote(src, self.place(g, cc, self.t), self.xs.at[cc], self.xr.at[cc], {"fsdp": 1 - self.f})
+
+    def line_copy(self, src, cc, sem, to):
+        return remote(src, self.place(self.f, cc, self.t), self.zs.at[sem], self.zr.at[cc], {"ctx": to})
+
+    def pass_on(self, src, i, g, cc):
+        self.far_copy(src, i, g, cc, self.t).start()
+        self.sib_copy(src, i, 0, g, cc, self.t).start()
+
+    def start(self):
+        self.local().start()
+        n_c, c, own = self.n_c, self.c, self.own
+
+        @pl.when(c < n_c - 1)
+        def _():
+            self.line_copy(own, c, n_c, c + 1).start()
+
+        @pl.when(c > 0)
+        def _():
+            self.line_copy(own, c, n_c + 1, c - 1).start()
+
+        if self.both:
+            self.other_copy(own, self.f, c).start()
+        self.pass_on(own, c, self.f, c)
+
+    def each_other(self, act):
+        for step in range(1, self.n_c):
+            for side in (-1, 1):
+                cc = self.c + side * step
+
+                @pl.when((cc >= 0) & (cc < self.n_c))
+                def _():
+                    act(cc, self.c - side)
+
+    def line(self):
+        n_c = self.n_c
+
+        def arrive(cc, onward):
+            block = self.place(self.f, cc, self.t)
+            self.line_copy(block, cc, cc, self.c).wait_recv()
+
+            @pl.when((onward >= 0) & (onward < n_c))
             def _():
-                block = place(f, cc, t)
-                line_copy(block, cc, cc, c).wait_recv()
-
-                @pl.when((onward >= 0) & (onward < n_c))
-                def _():
-                    line_copy(block, cc, cc, onward).start()
-
-                if both:
-                    other_copy(block, cc).start()
-                pass_on(block, cc, f, cc)
-
-    if after_line is not None:
-        after_line()
-    if both:
-
-        def from_other(cc):
-            block = place(1 - f, cc, t)
-            remote(block, block, xs.at[cc], xr.at[cc], to_other).wait_recv()
-            pass_on(block, n_c + cc, 1 - f, cc)
-
-        nearest(c, n_c, from_other)
-    for g, base in ((f, 0), (1 - f, n_c))[: 2 if both else 1]:
-
-        def from_far(cc):
+                self.line_copy(block, cc, cc, onward).start()
+
+            if self.both:
+                self.other_copy(block, self.f, cc).start()
+            self.pass_on(block, cc, self.f, cc)
+
+        self.each_other(arrive)
+
+    def other(self):
+        def arrive(cc):
+            block = self.place(1 - self.f, cc, self.t)
+            self.other_copy(block, 1 - self.f, cc).wait_recv()
+            self.pass_on(block, self.n_c + cc, 1 - self.f, cc)
+
+        nearest(self.c, self.n_c, arrive)
+
+    def far(self, which):
+        g, base = self.groups[which]
+
+        def arrive(cc):
             i = base + cc
-            block = place(g, cc, far)
-            remote(block, block, ys.at[i], yr.at[i], to_far).wait_recv()
-            sib_copy(block, i, 1, g, cc, far).start()
-
-        nearest(c, n_c, from_far)
-    for g, base in ((f, 0), (1 - f, n_c))[: 2 if both else 1]:
-        for cc in range(n_c):
-            i = base + cc
-            block = place(g, cc, t)
-            for which in range(2):
-                copy = sib_copy(block, i, which, g, cc, t)
-                copy.wait_recv()
-                copy.wait_send()
-            far_copy(block, i, g, cc).wait_send()
-    if both:
-        for cc in range(n_c):
-            other_copy(place(f, cc, t), cc).wait_send()
-    block = place(f, c, t)
-
-    @pl.when(c < n_c - 1)
-    def _():
-        line_copy(own, c, n_c, c).wait_send()
-
-    @pl.when(c > 0)
-    def _():
-        line_copy(own, c, n_c + 1, c).wait_send()
-
-    for step in range(1, n_c):
-        for side in (-1, 1):
-            cc = c + side * step
-            onward = c - side
-
-            @pl.when((cc >= 0) & (cc < n_c) & (onward >= 0) & (onward < n_c))
+            block = self.place(g, cc, self.other_t)
+            self.far_copy(block, i, g, cc, self.other_t).wait_recv()
+            self.sib_copy(block, i, 1, g, cc, self.other_t).start()
+
+        nearest(self.c, self.n_c, arrive)
+
+    def arrived(self, which):
+        g, base = self.groups[which]
+        for cc in range(self.n_c):
+            block = self.place(g, cc, self.t)
+            for half in range(2):
+                self.sib_copy(block, base + cc, half, g, cc, self.t).wait_recv()
+
+    def finish(self):
+        n_c, c, f, t, own = self.n_c, self.c, self.f, self.t, self.own
+        for g, base in self.groups:
+            for cc in range(n_c):
+                block = self.place(g, cc, t)
+                for half in range(2):
+                    self.sib_copy(block, base + cc, half, g, cc, t).wait_send()
+                self.far_copy(block, base + cc, g, cc, t).wait_send()
+        if self.both:
+            for cc in range(n_c):
+                self.other_copy(self.place(f, cc, t), f, cc).wait_send()
+        block = self.place(f, c, t)
+
+        @pl.when(c < n_c - 1)
+        def _():
+            self.line_copy(block, c, n_c, c).wait_send()
+
+        @pl.when(c > 0)
+        def _():
+            self.line_copy(block, c, n_c + 1, c).wait_send()
+
+        def sent(cc, onward):
+            @pl.when((onward >= 0) & (onward < n_c))
             def _():
-                line_copy(block, cc, cc, c).wait_send()
-
-    local.wait()
+                self.line_copy(block, cc, cc, c).wait_send()
+
+        self.each_other(sent)
 
 
 def to_each(src_of, dst, n_f, n_c, sems, act):
@@ -649,151 +666,6 @@
     ]
 
 
-def front_kernel(n_c, part, hidden, wq, wk, wv, wo, small, seq_out, wqkv_out, wo_out, small_out, *sems):
-    ws, wr, ls, xs, xr = sems[:5]
-    f, c, t = ranks()
-    rows, quarter = hidden.shape
-    greet([{"tp": sibling(t)}, {"tp": opposite(t)}, {"fsdp": 1 - f}] + line_peers(c, n_c))
-
-    def targets(g, cc):
-        block = piece(g * n_c + cc, part)
-        return [wqkv_out.at[block, pl.ds(i * HD, HD)] for i in range(3)] + [
-            wo_out.at[:, block],
-            small_out.at[:, block],
-        ]
-
-    def sources(head):
-        cols = piece(head, HD)
-        return [wq.at[:, cols], wk.at[:, cols], wv.at[:, cols], wo.at[cols, :], small]
-
-    for step in range(1, n_c):
-        to = lax.rem(c + step, n_c)
-        for i, (src, dst) in enumerate(zip(sources(to), targets(f, c))):
-            remote(src, dst, ws.at[step, i], wr.at[step, i], {"ctx": to}).start()
-    own = [
-        pltpu.make_async_copy(src, dst, ls.at[i])
-        for i, (src, dst) in enumerate(zip(sources(c), targets(f, c)))
-    ]
-    for copy in own:
-        copy.start()
-    for copy in own:
-        copy.wait()
-
-    def slabs(g, cc):
-        block = piece(g * n_c + cc, part)
-        return [wqkv_out.at[block, :], wo_out.at[:, block], small_out.at[:, block]]
-
-    def across(step, g, cc):
-        return [
-            remote(slab, slab, xs.at[step, i], xr.at[step, i], {"fsdp": 1 - f})
-            for i, slab in enumerate(slabs(g, cc))
-        ]
-
-    for copy in across(0, f, c):
-        copy.start()
-
-    def place(g, cc, tt):
-        return seq_out.at[piece(cc, rows), piece(tt, quarter)]
-
-    def weights_across():
-        for step in range(1, n_c):
-            cc = lax.rem(c - step + n_c, n_c)
-            for i, dst in enumerate(targets(f, cc)):
-                remote(dst, dst, ws.at[step, i], wr.at[step, i], {"ctx": cc}).wait_recv()
-            for copy in across(step, f, cc):
-                copy.start()
-
-    spread(hidden, place, n_c, False, sems[5:], weights_across)
-    for step in range(n_c):
-        cc = lax.rem(c - step + n_c, n_c)
-        for copy in across(step, 1 - f, cc):
-            copy.wait_recv()
-        for copy in across(step, f, cc):
-            copy.wait_send()
-    for step in range(1, n_c):
-        for i, (src, dst) in enumerate(zip(sources(c), targets(f, c))):
-            remote(src, dst, ws.at[step, i], wr.at[step, i], {"ctx": c}).wait_send()
-
-
-def front(n_c, n_f, n_t, hidden, wq, wk, wv, wo, small):
-    rows, quarter = hidden.shape
-    part = wq.shape[0]
-    width = quarter * n_t
-    return pl.pallas_call(
-        functools.partial(front_kernel, n_c, part),
-        out_shape=(
-            jax.ShapeDtypeStruct((rows * n_c, width), BF),
-            jax.ShapeDtypeStruct((width, 3 * HD), BF),
-            jax.ShapeDtypeStruct((HD, width), BF),
-            jax.ShapeDtypeStruct((small.shape[0], width), F32),
-        ),
-        in_specs=[HBM] * 6,
-        out_specs=[HBM] * 4,
-        scratch_shapes=[
-            DMA((n_c, 5)),
-            DMA((n_c, 5)),
-            DMA((5,)),
-            DMA((n_c, 3)),
-            DMA((n_c, 3)),
-        ]
-        + spread_sems(n_c),
-        compiler_params=pltpu.CompilerParams(collective_id=1, has_side_effects=True),
-        cost_estimate=pl.CostEstimate(flops=0, bytes_accessed=100 << 20, transcendentals=0),
-        name="front",
-    )(hidden, wq, wk, wv, wo, small)
-
-
-def attend_kernel(block, hidden, gain, wqkv, cosine, sine, normed, q_out, k_out, v_out, hf_out, hb_out, lse_out, r_out):
-    seq, width = hidden.shape
-    scale_att = HD ** (-0.5)
-    for start in range(0, seq, block):
-        at = pl.ds(start, block)
-        h = hidden[at, :].astype(F32)
-        r = lax.rsqrt(jnp.sum(h * h, axis=1, keepdims=True) / width + EPS)
-        n = (h * r * gain[...]).astype(BF)
-        normed[at, :] = n
-        r_out[at, :] = jnp.broadcast_to(r, (block, HD))
-        qkv = dot_nn(n, wqkv[...])
-        cos, sin = cosine[at, :], sine[at, :]
-
-        def rotate(values):
-            return (values * cos + pltpu.roll(values, HD // 2, 1) * sin).astype(BF)
-
-        q_out[at, :] = rotate(qkv[:, :HD])
-        k_out[at, :] = rotate(qkv[:, HD : 2 * HD])
-        v_out[at, :] = qkv[:, 2 * HD :].astype(BF)
-    for start in range(0, seq, block):
-        at = pl.ds(start, block)
-        seen = start + block
-        s = dot_nt(q_out[at, :], k_out[:seen, :]) * scale_att
-        row = lax.broadcasted_iota(jnp.int32, (block, seen), 0) + start
-        col = lax.broadcasted_iota(jnp.int32, (block, seen), 1)
-        s = jnp.where(col <= row, s, NEG_BIG)
-        top = jnp.max(s, axis=1, keepdims=True)
-        e = jnp.exp(s - top)
-        total = jnp.sum(e, axis=1, keepdims=True)
-        p = (e / total).astype(BF)
-        out = dot_nn(p, v_out[:seen, :])
-        hf_out[at, :] = out
-        hb_out[at, :] = out.astype(BF)
-        lse_out[at, :] = jnp.broadcast_to(top + jnp.log(total), (block, HD))
-
-
-def attend(hidden, gain, wqkv, cosine, sine):
-    seq, width = hidden.shape
-    head = jax.ShapeDtypeStruct((seq, HD), BF)
-    head_f = jax.ShapeDtypeStruct((seq, HD), F32)
-    return pl.pallas_call(
-        functools.partial(attend_kernel, min(256, seq)),
-        out_shape=(jax.ShapeDtypeStruct((seq, width), BF), head, head, head, head_f, head, head_f, head_f),
-        in_specs=[VMEM] * 5,
-        out_specs=[VMEM] * 8,
-        compiler_params=pltpu.CompilerParams(vmem_limit_bytes=BIG),
-        cost_estimate=pl.CostEstimate(flops=2 << 30, bytes_accessed=12 << 20, transcendentals=1 << 20),
-        name="attend",
-    )(hidden, gain, wqkv, cosine, sine)
-
-
 def reduce_seq_scratch(n_c, rows, quarter):
     return [
         pltpu.VMEM((n_c, 2, rows, quarter), BF),
@@ -812,7 +684,7 @@
     ]
 
 
-def reduce_seq(part_of, n_c, scratch, between=None):
+def reduce_seq(part_of, n_c, scratch, between=None, before_last=None):
     out1, in1, own, out2, in2, out3, in3, s1, r1, s2, r2, s3, r3 = scratch
     f, c, t = ranks()
     far, sib = opposite(t), sibling(t)
@@ -838,58 +710,249 @@
             out3[d] = total.astype(BF)
             cc = lax.rem(c + d, n_c)
             remote(out3.at[d], in3.at[d], s3.at[d], r3.at[d], {"ctx": cc}).start()
+    if before_last is not None:
+        before_last()
     for d in order[:-1]:
         remote(out3.at[d], in3.at[d], s3.at[d], r3.at[d], {"ctx": c}).wait()
         total = total + in3[d].astype(F32)
     return total
 
 
-def mid_kernel(n_c, n_f, heads, wo, hidden, shared, resid_out, all_out, shared_out, blk, ss, sr, sl, *scratch):
+def first_kernel(
+    n_c, n_f, n_exp, mine, hidden, wq, wk, wv, wo, small, og, gate_t, up_t, down, shared, angle,
+    normed, q_out, k_out, v_out, hf_out, lse_out, r_out, cos_out, sin_out, resid_out,
+    wqkv_out, wo_out, small_out, all_out, og_out, shared_out, gg_out, gu_out, gd_out,
+    seq, wqkv, wo_all, small_all, hb, blk, own_og,
+    ws, wr, ls, xs, xr, ss, sr, sl, es, er, os, *scratch,
+):
     f, c, t = ranks()
-    rows, quarter = hidden.shape
+    rows, quarter = blk.shape
+    part = wo.shape[1]
+    tokens, width = seq.shape
+    n_s = len(spread_sems(n_c))
     greet([{"tp": sibling(t)}, {"tp": opposite(t)}] + each_peers(f, c, n_f, n_c))
+    seq_place = lambda g, cc, tt: seq.at[piece(cc, rows), piece(tt, quarter)]
+    og_place = lambda g, cc, tt: og_out.at[g * n_c + cc, tt]
+    all_place = lambda g, cc, tt: all_out.at[piece(g * n_c + cc, rows), piece(tt, quarter)]
+    hid = Spread(hidden, seq_place, n_c, False, scratch[:n_s])
+    grad = Spread(og, og_place, n_c, True, scratch[n_s : 2 * n_s])
+    res = Spread(blk, all_place, n_c, True, scratch[2 * n_s : 3 * n_s])
+
+    def targets(g, cc):
+        block = piece(g * n_c + cc, part)
+        return [wqkv.at[block, pl.ds(i * HD, HD)] for i in range(3)] + [
+            wo_all.at[:, block],
+            small_all.at[:, block],
+        ]
+
+    def sources(head):
+        cols = piece(head, HD)
+        return [wq.at[:, cols], wk.at[:, cols], wv.at[:, cols], wo.at[cols, :], small]
+
+    def slabs(g, cc):
+        block = piece(g * n_c + cc, part)
+        return [wqkv.at[block, :], wo_all.at[:, block], small_all.at[:, block]]
+
+    def across(step, g, cc):
+        return [
+            remote(slab, slab, xs.at[step, i], xr.at[step, i], {"fsdp": 1 - f})
+            for i, slab in enumerate(slabs(g, cc))
+        ]
+
+    def swap(weight, out, k):
+        return [
+            remote(weight.at[(1 - f) * mine + e], out.at[e], es.at[k, e], er.at[k, e], {"fsdp": 1 - f})
+            for e in range(mine)
+        ]
+
+    more = swap(down, gd_out, 2)
+    for copy in more:
+        copy.start()
+    hid.start()
+    for step in range(1, n_c):
+        to = lax.rem(c + step, n_c)
+        for i, (src, dst) in enumerate(zip(sources(to), targets(f, c))):
+            remote(src, dst, ws.at[step, i], wr.at[step, i], {"ctx": to}).start()
+    own = [
+        pltpu.make_async_copy(src, dst, ls.at[i])
+        for i, (src, dst) in enumerate(zip(sources(c), targets(f, c)))
+    ]
+    for copy in own:
+        copy.start()
+    for copy in own:
+        copy.wait()
+    for copy in across(0, f, c):
+        copy.start()
+    grad.start()
+    hid.line()
+    for step in range(1, n_c):
+        cc = lax.rem(c - step + n_c, n_c)
+        for i, dst in enumerate(targets(f, cc)):
+            remote(dst, dst, ws.at[step, i], wr.at[step, i], {"ctx": cc}).wait_recv()
+        for copy in across(step, f, cc):
+            copy.start()
+    grad.line()
+    swaps = swap(gate_t, gg_out, 0) + swap(up_t, gu_out, 1)
+    for copy in swaps:
+        copy.start()
+    hid.far(0)
+    hid.arrived(0)
+    hid.local().wait()
+    for step in range(n_c):
+        for copy in across(step, 1 - f, lax.rem(c - step + n_c, n_c)):
+            copy.wait_recv()
+    outs = [
+        pltpu.make_async_copy(src, dst, os.at[i])
+        for i, (src, dst) in enumerate(((wqkv, wqkv_out), (wo_all, wo_out), (small_all, small_out)))
+    ]
+    for copy in outs:
+        copy.start()
+    grad.other()
+
+    scale_att = HD ** (-0.5)
+    gain = small_all[0:1, :].astype(F32)
+    place_row = 2 + 2 * n_exp
+    for start in range(0, tokens, rows):
+        at = pl.ds(start, rows)
+        h = seq[at, :].astype(F32)
+        r = lax.rsqrt(jnp.sum(h * h, axis=1, keepdims=True) / width + EPS)
+        n = (h * r * gain).astype(BF)
+        normed[at, :] = n
+        r_out[at, :] = jnp.broadcast_to(r, (rows, HD))
+        cols = pl.ds(pl.multiple_of(f * tokens + start, rows), rows)
+        pos = small_all[place_row : place_row + 2, cols].astype(F32)
+        pos = pos[0:1] * 64.0 + pos[1:2]
+        turn = jnp.broadcast_to(pos, (HD, rows)).T * angle[0:1, :]
+        cos, sin = jnp.cos(turn), jnp.sin(turn) * angle[1:2, :]
+        cos_out[at, :] = cos
+        sin_out[at, :] = sin
+        qkv = dot_nn(n, wqkv[...])
+
+        def rotate(values):
+            return (values * cos + pltpu.roll(values, HD // 2, 1) * sin).astype(BF)
+
+        q_out[at, :] = rotate(qkv[:, :HD])
+        k_out[at, :] = rotate(qkv[:, HD : 2 * HD])
+        v_out[at, :] = qkv[:, 2 * HD :].astype(BF)
+    for start in range(0, tokens, rows):
+        at = pl.ds(start, rows)
+        seen = start + rows
+        s = dot_nt(q_out[at, :], k_out[:seen, :]) * scale_att
+        row = lax.broadcasted_iota(jnp.int32, (rows, seen), 0) + start
+        col = lax.broadcasted_iota(jnp.int32, (rows, seen), 1)
+        s = jnp.where(col <= row, s, NEG_BIG)
+        top = jnp.max(s, axis=1, keepdims=True)
+        e = jnp.exp(s - top)
+        total = jnp.sum(e, axis=1, keepdims=True)
+        out = dot_nn((e / total).astype(BF), v_out[:seen, :])
+        hf_out[at, :] = out
+        hb[at, :] = out.astype(BF)
+        lse_out[at, :] = jnp.broadcast_to(top + jnp.log(total), (rows, HD))
+
     exchange = lambda act: to_each(lambda b: shared.at[b], shared_out, n_f, n_c, (ss, sr, sl), act)
 
     def part_of(cc, q):
-        return dot_nn(heads[piece(cc, rows), :], wo[:, piece(q, quarter)])
-
-    total = reduce_seq(part_of, n_c, scratch[:13], lambda: exchange("start"))
-    resid = hidden[...].astype(F32) + total
+        return dot_nn(hb[piece(cc, rows), :], wo_all[:, piece(q, quarter)])
+
+    fetch = pltpu.make_async_copy(hidden, own_og, os.at[3])
+    fetch.start()
+    total = reduce_seq(part_of, n_c, scratch[3 * n_s :])
+    fetch.wait()
+    resid = own_og[...].astype(F32) + total
     resid_out[...] = resid
     blk[...] = resid.astype(BF)
-
-    def place(g, cc, tt):
-        return all_out.at[piece(g * n_c + cc, rows), piece(tt, quarter)]
-
-    spread(blk, place, n_c, True, scratch[13:])
+    res.start()
+    res.line()
+    exchange("start")
+    grad.far(0)
+    grad.far(1)
+    res.other()
+    res.far(0)
+    res.far(1)
+    for which in range(2):
+        grad.arrived(which)
+        res.arrived(which)
     exchange("wait")
-
-
-def mid(n_c, n_f, n_t, heads, wo, hidden, shared):
+    for copy in swaps + more:
+        copy.wait()
+    for step in range(1, n_c):
+        for i, (src, dst) in enumerate(zip(sources(c), targets(f, c))):
+            remote(src, dst, ws.at[step, i], wr.at[step, i], {"ctx": c}).wait_send()
+    for step in range(n_c):
+        for copy in across(step, f, lax.rem(c - step + n_c, n_c)):
+            copy.wait_send()
+    for item in (hid, grad, res):
+        item.finish()
+    grad.local().wait()
+    res.local().wait()
+    for copy in outs:
+        copy.wait()
+
+
+def first(n_c, n_f, n_t, mine, hidden, wq, wk, wv, wo, small, og, weights, shared, angle):
     rows, quarter = hidden.shape
+    width = quarter * n_t
+    seq = rows * n_c
+    n_exp = mine * n_f * n_c
+    ffe, half = weights[0].shape[1:]
+    sds = jax.ShapeDtypeStruct
+    head, head_f = sds((seq, HD), BF), sds((seq, HD), F32)
+    got = sds((mine, ffe, half), BF)
     return pl.pallas_call(
-        functools.partial(mid_kernel, n_c, n_f),
+        functools.partial(first_kernel, n_c, n_f, n_exp, mine),
         out_shape=(
-            jax.ShapeDtypeStruct((rows, quarter), F32),
-            jax.ShapeDtypeStruct((rows * n_c * n_f, quarter * n_t), BF),
-            jax.ShapeDtypeStruct(shared.shape, BF),
+            sds((seq, width), BF),
+            head,
+            head,
+            head,
+            head_f,
+            head_f,
+            head_f,
+            head_f,
+            head_f,
+            sds((rows, quarter), F32),
+            sds((width, 3 * HD), BF),
+            sds((HD, width), BF),
+            sds((small.shape[0], width), BF),
+            sds((seq * n_f, width), BF),
+            sds((n_f * n_c, n_t, rows, quarter), BF),
+            sds(shared.shape, BF),
+            got,
+            got,
+            got,
         ),
-        in_specs=[VMEM] * 3 + [HBM],
-        out_specs=[VMEM, HBM, HBM],
+        in_specs=[HBM] * 11 + [VMEM],
+        out_specs=[VMEM] * 10 + [HBM] * 9,
         scratch_shapes=[
+            pltpu.VMEM((seq, width), BF),
+            pltpu.VMEM((width, 3 * HD), BF),
+            pltpu.VMEM((HD, width), BF),
+            pltpu.VMEM((small.shape[0], width), BF),
+            pltpu.VMEM((seq, HD), BF),
             pltpu.VMEM((rows, quarter), BF),
+            pltpu.VMEM((rows, quarter), BF),
+            DMA((n_c, 5)),
+            DMA((n_c, 5)),
+            DMA((5,)),
+            DMA((n_c, 3)),
+            DMA((n_c, 3)),
             DMA((n_f * n_c,)),
             DMA((n_f * n_c,)),
             DMA(()),
+            DMA((3, mine)),
+            DMA((3, mine)),
+            DMA((4,)),
         ]
-        + reduce_seq_scratch(n_c, rows, quarter)
-        + spread_sems(n_c),
+        + spread_sems(n_c) * 3
+        + reduce_seq_scratch(n_c, rows, quarter),
         compiler_params=pltpu.CompilerParams(
-            collective_id=2, has_side_effects=True, vmem_limit_bytes=BIG
+            collective_id=1, has_side_effects=True, vmem_limit_bytes=BIG
         ),
-        cost_estimate=pl.CostEstimate(flops=1 << 29, bytes_accessed=200 << 20, transcendentals=0),
-        name="mid",
-    )(heads, wo, hidden, shared)
+        cost_estimate=pl.CostEstimate(
+            flops=5 << 30, bytes_accessed=300 << 20, transcendentals=1 << 20
+        ),
+        name="first",
+    )(hidden, wq, wk, wv, wo, small, og, *weights, shared, angle)
 
 
 def fetch_experts(n_c, n_f, mine, ffe, srows, hp, weights, shared, wgu, wd, sems):
@@ -1041,12 +1104,13 @@
     def drain(self, n_b, works):
         works = list(works)
         self.over(n_b - 1)
-        for i in range(n_b - 3, n_b):
+        for i in range(n_b - 4, n_b):
+            if i > n_b - 4:
+                self.after_own(i) if i >= self.n_c else self.after_other(i)
+            if i >= self.n_c:
+                total = self.along(i - self.n_c)
             if works:
                 works.pop(0)()
-            self.after_own(i) if i >= self.n_c else self.after_other(i)
-        for j in range(self.n_c):
-            total = self.along(j)
         for work in works:
             work()
         return self.total(total)
@@ -1157,7 +1221,7 @@
             if s < 2:
                 src, dst = sends.at[s], send_out.at[:, :, cols]
             else:
-                src, dst = keeps.at[s - 2], keep_out.at[pl.ds(f * mine, mine), :, cols]
+                src, dst = keeps.at[s - 2], keep_out.at[:, :, cols]
             return [
                 pltpu.make_async_copy(src, dst, osem.at[s, 0]),
                 pltpu.make_async_copy(
@@ -1219,7 +1283,7 @@
             sds((total, hp), BF),
             sds((total, HD), F32),
             sds((total, n_exp), F32),
-            sds((n_f * mine, ffe, width // n_f), F32),
+            sds((mine, ffe, width // n_f), F32),
             sds((mine, ffe, width // n_f), BF),
             sds((srows, width), BF),
         ),
@@ -1248,7 +1312,7 @@
 def backward_kernel(
     n_c, n_f, mine, ffe, srows, hp, og_all, act, silu, slope, moe_in, r_all, shared_d, prob_in, picked, router,
     resid, gain, og, wg0, wu0, wd0, wg1, wu1, wd1, shared,
-    mid_out, gain_out, seq_out, shared_out, kg_out, ku_out, gg_out, gu_out,
+    mid_out, gain_out, seq_out, shared_out, kg_out, ku_out, gg_out, gu_out, lg_out, lu_out,
     gt, blk, r_own, sends, shs, wsem, xsem, tsem, ksem, ss, sr, rs, es, er, el, ds, dr, dl, *rest,
 ):
     f, c, t = ranks()
@@ -1261,6 +1325,16 @@
     first = (c * n_f + f) * mine
     red = Reducer(n_c, rest[:18])
 
+    cols = width // n_b
+    n_gu = shs.shape[0]
+
+    def exchange(act, which):
+        src, at, sems = (
+            (shs, pl.ds(0, n_gu), (es, er, el)),
+            (shared_d, pl.ds(n_gu, srows), (ds, dr, dl)),
+        )[which]
+        to_each(lambda b: src.at[:, piece(b, cols)], shared_out.at[:, at, :], n_f, n_c, sems, act)
+
     def blocks_phase(wgu, wd, ogs, acts):
         fetches = fetch_experts(
             n_c, n_f, mine, ffe, srows, hp, (wg0, wu0, wd0, wg1, wu1, wd1), shared, wgu, wd, wsem
@@ -1284,6 +1358,7 @@
             copy.start()
         blank_rows(rows_used, hp, wgu, wd)
         greet([{"tp": red.sib}, {"tp": red.far}, {"tp": opposite(red.sib)}] + each_peers(f, c, n_f, n_c))
+        exchange("start", 1)
         for copy in fetches:
             copy.wait()
 
@@ -1338,8 +1413,9 @@
     )
 
     def send_copy(s, m):
-        dst = (gg_out, gu_out)[m].at[:, :, pl.ds(s * quarter, quarter)]
-        return remote(sends.at[s, m], dst, ss.at[s, m], sr.at[s, m], {"fsdp": 1 - f})
+        if s:
+            return pltpu.make_async_copy(sends.at[s, m], (lg_out, lu_out)[m], ss.at[s, m])
+        return remote(sends.at[s, m], (gg_out, gu_out)[m], ss.at[s, m], sr.at[m], {"fsdp": 1 - f})
 
     def grads_phase(tiles, keeps):
         def tile_of(s):
@@ -1351,7 +1427,7 @@
             )
 
         def keep_copy(s, m):
-            dst = (kg_out, ku_out)[m].at[pl.ds(f * mine, mine), :, pl.ds((s - 2) * quarter, quarter)]
+            dst = (kg_out, ku_out)[m].at[:, :, pl.ds((s - 2) * quarter, quarter)]
             return pltpu.make_async_copy(keeps.at[s - 2, m], dst, ksem.at[s - 2, m])
 
         def work(s):
@@ -1387,16 +1463,6 @@
         pltpu.VMEM((2, n_b * rows, quarter), BF),
         pltpu.VMEM((2, 2, mine, ffe, quarter), F32),
     )
-    cols = width // n_b
-    n_gu = shs.shape[0]
-
-    def exchange(act):
-        for src, at, sems in (
-            (shs, pl.ds(0, n_gu), (es, er, el)),
-            (shared_d, pl.ds(n_gu, srows), (ds, dr, dl)),
-        ):
-            to_each(lambda b: src.at[:, piece(b, cols)], shared_out.at[:, at, :], n_f, n_c, sems, act)
-
     fetch.wait()
     back, gain_part = norm_grad(resid[...], r_own[:, :1], gain[...], blk[...], width, *rest[18:22])
     gain_out[...] = jnp.broadcast_to(gain_part, gain_out.shape)
@@ -1408,8 +1474,16 @@
     def place(g, cc, tt):
         return seq_out.at[piece(cc, rows), piece(tt, quarter)]
 
-    spread(own, place, n_c, False, rest[23:], lambda: exchange("start"))
-    exchange("wait")
+    sequence = Spread(own, place, n_c, False, rest[23:])
+    sequence.start()
+    sequence.line()
+    exchange("start", 0)
+    sequence.far(0)
+    sequence.arrived(0)
+    sequence.finish()
+    sequence.local().wait()
+    exchange("wait", 0)
+    exchange("wait", 1)
     for s in range(2):
         for m in range(2):
             send_copy(s, m).wait()
@@ -1425,8 +1499,8 @@
     n_b = n_f * n_c
     used, hp, n_fetch = expert_sizes(n_c, n_f, n_t, mine, ffe, srows, width)
     sds = jax.ShapeDtypeStruct
-    kept_g = sds((n_f * mine, ffe, width // n_f), F32)
-    sent_g = sds((mine, ffe, width // n_f), BF)
+    kept_g = sds((mine, ffe, width // n_f), F32)
+    sent_g = sds((mine, ffe, quarter), BF)
     return pl.pallas_call(
         functools.partial(backward_kernel, n_c, n_f, mine, ffe, srows, hp),
         out_shape=(
@@ -1438,9 +1512,11 @@
             kept_g,
             sent_g,
             sent_g,
+            sent_g,
+            sent_g,
         ),
         in_specs=[HBM] * 7 + [VMEM] * 6 + [HBM] * 7,
-        out_specs=[VMEM, VMEM] + [HBM] * 6,
+        out_specs=[VMEM, VMEM] + [HBM] * 8,
         scratch_shapes=[
             pltpu.VMEM((2 * used + n_exp, total), BF),
             pltpu.VMEM((rows, quarter), F32),
@@ -1452,7 +1528,7 @@
             DMA((2,)),
             DMA((2, 2)),
             DMA((2, 2)),
-            DMA((2, 2)),
+            DMA((2,)),
             DMA(()),
             DMA((n_b,)),
             DMA((n_b,)),
@@ -1478,25 +1554,51 @@
     )
 
 
-def fill_kernel(f_ref, a, b, c, _a, _b, _c, oa, ob, oc):
-    del f_ref, _a, _b, _c
-    oa[...] = a[...].astype(F32)
-    ob[...] = b[...].astype(F32)
-    oc[...] = c[...].astype(F32)
+def fill_kernel(f_ref, ga, gb, ua, ub, d, kg, ku, kd, og, ou, od):
+    step = pl.program_id(0)
+    f = f_ref[0]
+    n_e = kg.shape[0]
+
+    def put(own, at):
+        for keep, out in ((kg, og), (ku, ou), (kd, od)):
+            out[at : at + n_e] = keep[...]
+        for out, halves in ((og, (ga, gb)), (ou, (ua, ub))):
+            @pl.when(step < 2)
+            def _():
+                out[n_e - at : 2 * n_e - at] = halves[0][...].astype(F32)
+
+            @pl.when(step >= 2)
+            def _():
+                out[n_e - at : 2 * n_e - at] = halves[1][...].astype(F32)
+
+        od[n_e - at : 2 * n_e - at] = d[...].astype(F32)
+
+    @pl.when(f == 0)
+    def _():
+        put(0, 0)
+
+    @pl.when(f != 0)
+    def _():
+        put(1, n_e)
 
 
 def fill_experts(f_rank, arrived, kept):
-    mine, ffe, half = arrived[0].shape
+    mine, ffe, quarter = arrived[0].shape
+    half = kept[0].shape[2]
     tile = half // 4
-    src = pl.BlockSpec((mine, ffe, tile), lambda i, f: (0, 0, i))
-    dst = pl.BlockSpec((mine, ffe, tile), lambda i, f: (1 - f[0], 0, i))
+    first = pl.BlockSpec((mine, ffe, tile), lambda i, f: (0, 0, jnp.minimum(i, 1)))
+    second = pl.BlockSpec((mine, ffe, tile), lambda i, f: (0, 0, jnp.maximum(i - 2, 0)))
+    every = pl.BlockSpec((mine, ffe, tile), lambda i, f: (0, 0, i))
+    out = pl.BlockSpec((2 * mine, ffe, tile), lambda i, f: (0, 0, i))
     return pl.pallas_call(
         fill_kernel,
         grid_spec=pltpu.PrefetchScalarGridSpec(
-            num_scalar_prefetch=1, grid=(4,), in_specs=[src] * 3 + [HBM] * 3, out_specs=[dst] * 3
+            num_scalar_prefetch=1,
+            grid=(4,),
+            in_specs=[first, second, first, second, every] + [every] * 3,
+            out_specs=[out] * 3,
         ),
-        out_shape=tuple(jax.ShapeDtypeStruct(k.shape, k.dtype) for k in kept),
-        input_output_aliases={4: 0, 5: 1, 6: 2},
+        out_shape=tuple(jax.ShapeDtypeStruct((2 * mine, ffe, half), F32) for k in kept),
         compiler_params=pltpu.CompilerParams(vmem_limit_bytes=BIG),
         name="fill_experts",
     )(f_rank, *arrived, *kept)
@@ -1504,8 +1606,9 @@
 
 def norm_grad(values, r, gain, grad, width, out, into, send, recv):
     f, c, t = ranks()
+    rows = values.shape[0]
     local = jnp.sum(grad * gain * values, axis=1, keepdims=True)
-    out[...] = jnp.broadcast_to(local, out.shape)
+    out[...] = jnp.broadcast_to(local, (rows, HD)).T[:8, :]
     peers = [sibling(t), opposite(t), opposite(sibling(t))]
     copies = [
         remote(out, into.at[i], send.at[i], recv.at[i], {"tp": peer}) for i, peer in enumerate(peers)
@@ -1513,17 +1616,18 @@
     for copy in copies:
         copy.start()
     gain_part = jnp.sum(grad * values * r, axis=0, keepdims=True)
-    total = local
+    total = out[...]
     for i, copy in enumerate(copies):
         copy.wait()
-        total = total + into[i][:, :1]
+        total = total + into[i]
+    total = jnp.broadcast_to(total[0:1, :], (HD, rows)).T[:, :1]
     return r * gain * grad - values * (r * r * r * (total / width)), gain_part
 
 
 def norm_grad_scratch(rows):
     return [
-        pltpu.VMEM((rows, HD), F32),
-        pltpu.VMEM((3, rows, HD), F32),
+        pltpu.VMEM((8, rows), F32),
+        pltpu.VMEM((3, 8, rows), F32),
         DMA((3,)),
         DMA((3,)),
     ]
@@ -1581,9 +1685,9 @@
 
 
 def last_kernel(
-    n_c, n_f, n_t, width, dqkv, wqkv, hidden, r_all, gain, mid_grad, gain2, rpart, gattn,
-    in_out, gq, gk, gv, go, gains_out, router_out,
-    rin, rss, rsr, r_own, outx, inx, own, outz, inz, gsend, gin, rs, sx, rx, lx, sz, rz, gs, gr, *rest,
+    n_c, n_f, n_t, width, dqkv, wqkv, hidden, r_all, gain, mid_grad, gain2, rpart, gattn, lg, lu,
+    in_out, gq, gk, gv, go, gains_out, router_out, lg_out, lu_out,
+    es, er, rin, rss, rsr, r_own, mine, inx, own, outz, inz, gsend, gin, rs, sx, rx, lx, sz, rz, gs, gr, *rest,
 ):
     f, c, t = ranks()
     rows, quarter = hidden.shape
@@ -1622,6 +1726,10 @@
         remote(rpart, rin.at[i], rss.at[i], rsr.at[i], {"tp": peer})
         for i, peer in enumerate([sibling(t), opposite(t), opposite(sibling(t))])
     ]
+    late = [
+        remote(src, dst, es.at[i], er.at[i], {"fsdp": 1 - f})
+        for i, (src, dst) in enumerate(((lg, lg_out), (lu, lu_out)))
+    ]
     for copy in router_copies:
         copy.start()
     fetch = pltpu.make_async_copy(r_all.at[piece(c, rows), :], r_own, rs)
@@ -1629,20 +1737,24 @@
     for d in order:
         cross(d).start()
         keep(d).start()
+    for copy in late:
+        copy.start()
 
     def part_of(cc, q):
         return dot_nt(dqkv[piece(cc, rows), :], wqkv[piece(q, quarter), :])
 
-    total = reduce_seq(part_of, n_c, rest[:13])
-    for d in order:
-        cross(d).wait()
-        keep(d).wait()
-        both = own[d].astype(F32) + inx[d].astype(F32)
-        if d:
-            outz[d] = both.astype(BF)
-            line(d, lax.rem(c + d, n_c)).start()
-        else:
-            mine = both
+    def pass_weights():
+        for d in order:
+            cross(d).wait()
+            keep(d).wait()
+            both = own[d].astype(F32) + inx[d].astype(F32)
+            if d:
+                outz[d] = both.astype(BF)
+                line(d, lax.rem(c + d, n_c)).start()
+            else:
+                mine[...] = both
+
+    total = reduce_seq(part_of, n_c, rest[:13], None, pass_weights)
     fetch.wait()
     back, gain_part = norm_grad(
         hidden[...].astype(F32), r_own[:, :1], gain[...], total, width, *rest[13:17]
@@ -1680,7 +1792,7 @@
             ref[:, at] = block[i * HD : (i + 1) * HD, :].T
         go[at, :] = block[3 * HD :, :]
 
-    put(c, mine)
+    put(c, mine[...])
     for d in order[:-1]:
         line(d, c).wait()
         put(lax.rem(c - d + n_c, n_c), inz[d].astype(F32))
@@ -1703,12 +1815,12 @@
         jnp.zeros((8, part), F32),
     )
     gains_out[...] = own_part + jnp.sum(gin[...], axis=0)
-    for copy in router_copies:
+    for copy in router_copies + late:
         copy.wait()
     router_out[...] = rpart[...] + jnp.sum(rin[...], axis=0)
 
 
-def last(n_c, n_f, n_t, dqkv, wqkv, hidden, r_all, gain, mid_grad, gain2, rpart, gattn):
+def last(n_c, n_f, n_t, dqkv, wqkv, hidden, r_all, gain, mid_grad, gain2, rpart, gattn, lg, lu):
     rows, quarter = hidden.shape
     width = quarter * n_t
     part = width // (n_f * n_c)
@@ -1724,15 +1836,19 @@
             sds((n_c * HD, part), F32),
             sds((8, part), F32),
             sds(rpart.shape, F32),
+            sds(lg.shape, BF),
+            sds(lu.shape, BF),
         ),
-        in_specs=[VMEM, VMEM, VMEM, HBM, VMEM, VMEM, VMEM, VMEM, HBM],
-        out_specs=[VMEM] * 7,
+        in_specs=[VMEM, VMEM, VMEM, HBM, VMEM, VMEM, VMEM, VMEM, HBM, HBM, HBM],
+        out_specs=[VMEM] * 7 + [HBM] * 2,
         scratch_shapes=[
+            DMA((2,)),
+            DMA((2,)),
             pltpu.VMEM((3,) + rpart.shape, F32),
             DMA((3,)),
             DMA((3,)),
             pltpu.VMEM((rows, HD), F32),
-            slab,
+            pltpu.VMEM((4 * HD, part), F32),
             slab,
             slab,
             slab,
@@ -1755,7 +1871,7 @@
         ),
         cost_estimate=pl.CostEstimate(flops=2 << 30, bytes_accessed=150 << 20, transcendentals=0),
         name="last",
-    )(dqkv, wqkv, hidden, r_all, gain, mid_grad, gain2, rpart, gattn)
+    )(dqkv, wqkv, hidden, r_all, gain, mid_grad, gain2, rpart, gattn, lg, lu)
 
 
 def per_device_seq(
@@ -1794,39 +1910,21 @@
     block = f_rank * n_c + c_rank
     f_arr = f_rank.astype(jnp.int32).reshape(1)
     swap = [(i, n_f - 1 - i) for i in range(n_f)]
-
-    gate_t, up_t = expert_gate.swapaxes(1, 2), expert_up.swapaxes(1, 2)
-    weights = (gate_t, up_t, expert_down)
-
-    def swapped(weight):
-        given = lax.dynamic_slice_in_dim(weight, (n_f - 1 - f_rank) * mine, mine, 0)
-        return lax.ppermute(given, "fsdp", swap)
-
-    got_down = swapped(expert_down)
+    weights = (expert_gate.swapaxes(1, 2), expert_up.swapaxes(1, 2), expert_down)
 
     picked_own = jnp.sum(
         (chosen[:, :, None] == jnp.arange(n_exp)[None, None, :]).astype(F32), axis=1
     )
     small = [
-        attn_gain.astype(F32)[None],
-        moe_gain.astype(F32)[None],
-        router.T.astype(F32),
-        picked_own.T,
-        positions.astype(F32)[None],
+        attn_gain[None],
+        moe_gain[None],
+        router.T,
+        picked_own.T.astype(BF),
+        (positions // 64).astype(BF)[None],
+        (positions % 64).astype(BF)[None],
     ]
     small = jnp.concatenate(small, axis=0)
-    small = jnp.pad(small, ((0, -small.shape[0] % 8), (0, 0)))
-    hidden_seq, wqkv, wo, small_all = front(
-        n_c, n_f, n_t, hidden_in, w_query, w_key, w_value, w_out, small
-    )
-    gain_one, gain_two = small_all[0:1], small_all[1:2]
-    router_t = small_all[2 : 2 + n_exp].astype(BF)
-    picked = small_all[2 + n_exp : 2 + 2 * n_exp].T
-    pos_seq = lax.dynamic_slice(small_all, (2 + 2 * n_exp, f_rank * seq), (1, seq))[0]
-    after = lambda x, y: lax.optimization_barrier((x, y))[0]
-    got = (swapped(after(gate_t, hidden_seq)), swapped(after(up_t, hidden_seq)), got_down)
-    grad_all = lax.all_gather(after(out_grad, hidden_seq), every, axis=0, tiled=False)
-    grad_all = grad_all.reshape(n_b, n_t, rows, quarter)
+    small = jnp.pad(small, ((0, -small.shape[0] % 16), (0, 0)))
 
     def shared_part(weight):
         return jnp.pad(
@@ -1836,23 +1934,25 @@
     shared = jnp.concatenate(
         [shared_part(shared_gate.T), shared_part(shared_up.T), shared_part(shared_down)], axis=1
     )
-
     half = HD // 2
     inverse = 10000.0 ** (-jnp.arange(half, dtype=F32) * 2.0 / HD)
-    angles = pos_seq[:, None] * inverse[None, :]
-    cosine, sine = jnp.cos(angles), jnp.sin(angles)
-    cosine = jnp.concatenate([cosine, cosine], axis=1)
-    sine = jnp.concatenate([-sine, sine], axis=1)
-    normed, q, k, v, heads_f, heads_b, lse, r_one = attend(hidden_seq, gain_one, wqkv, cosine, sine)
-    resid_mid, resid_all, shared = mid(n_c, n_f, n_t, heads_b, wo, hidden_in, shared)
-
+    angle = jnp.stack([jnp.tile(inverse, 2), jnp.where(jnp.arange(HD) < half, -1.0, 1.0)])
+    (
+        normed, q, k, v, heads_f, lse, r_one, cosine, sine, resid_mid,
+        wqkv, wo, small_all, resid_all, grad_all, shared, *got,
+    ) = first(
+        n_c, n_f, n_t, mine, hidden_in, w_query, w_key, w_value, w_out, small, out_grad, weights, shared, angle
+    )
+    gain_one, gain_two = small_all[0:1].astype(F32), small_all[1:2].astype(F32)
+    router_t = small_all[2 : 2 + n_exp]
+    picked = small_all[2 + n_exp : 2 + 2 * n_exp].astype(F32).T
     sizes = (n_c, n_f, n_t, mine, ffe, srows)
     layer_out, moe_in, act, silu, slope, r_two, prob, kd, sd, shared_d = forward(
         *sizes, resid_all, grad_all, resid_mid, picked, gain_two, router_t, weights, got, shared
     )
     arrived_d = lax.ppermute(sd, "fsdp", swap)
     own_cols = lambda x: lax.dynamic_slice_in_dim(x, t_rank * quarter, quarter, 1)
-    mid_grad, gain_two_part, mid_seq, shared_back, kg, ku, gg, gu = backward(
+    mid_grad, gain_two_part, mid_seq, shared_back, kg, ku, gg, gu, lg, lu = backward(
         *sizes, grad_all, act, silu, slope, moe_in, r_two, shared_d, prob, picked, router_t,
         resid_mid, own_cols(gain_two), out_grad, weights, got, shared,
     )
@@ -1862,11 +1962,11 @@
     shared_back = shared_back.reshape(n_b, 3, srows, part)[:, :, :own_shared].astype(F32)
 
     dqkv, gattn = attend_back(mid_seq, wo, q, k, v, heads_f, lse, cosine, sine, normed)
-    input_grad, gq, gk, gv, go, gains, router_grad = last(
+    input_grad, gq, gk, gv, go, gains, router_grad, lg, lu = last(
         n_c, n_f, n_t, dqkv, wqkv, hidden_in, r_one, own_cols(gain_one), mid_grad, gain_two_part,
-        router_part, gattn,
-    )
-    eg, eu, ed = fill_experts(f_arr, (gg, gu, arrived_d), (kg, ku, kd))
+        router_part, gattn, lg, lu,
+    )
+    eg, eu, ed = fill_experts(f_arr, (gg, lg, gu, lu, arrived_d), (kg, ku, kd))
 
     def shared_cols(i):
         return shared_back[:, i].reshape(n_b * own_shared, part)

time: 599 us -> 519 us (0.87)
  Pallas kernels: 533 us -> 482 us
  local copies, waits for them, and re-layouts: 30.9 us -> 16.9 us
  between operations: 14.4 us -> 0.96 us
    pallas_call x3 -> x1, Pallas kernels: 223 us -> 200 us  [first(): pl.pallas_call(functools.partial(first_kernel, n_c, n_f, n_exp, mine), ou...]
    pallas_call x1, Pallas kernels: 143 us -> 122 us  [backward(): pl.pallas_call(functools.partial(backward_kernel, n_c, n_f, mine, ffe, sr...]
    unnamed x44 -> x23, local copies, waits for them, and re-layouts: 18.4 us -> 6.42 us
    pallas_call x1, Pallas kernels: 79.5 us -> 68.6 us  [forward(): pl.pallas_call(functools.partial(forward_kernel, n_c, n_f, mine, ffe, sro...]
  transfers between devices with their start and end apart: 5 -> 1, of which waited for: 0 -> 0; matrix products, arithmetic and copies ran while one was open for 3% -> 2% of each run, Pallas kernels for 64% -> 39%
where the time goes in v4:
time: 519 us; the launch traced here: 511 us
  Pallas kernels  482 us (93%)
  local copies, waits for them, and re-layouts  16.9 us (3%)
  other arithmetic  9.64 us (2%)
    pallas_call x1, Pallas kernels, first(): pl.pallas_call(functools.partial(first_kernel, n_c, n_f, n_exp, mine), ou...  200 us
    pallas_call x1, Pallas kernels, backward(): pl.pallas_call(functools.partial(backward_kernel, n_c, n_f, mine, ffe, sr...  122 us
    pallas_call x1, Pallas kernels, forward(): pl.pallas_call(functools.partial(forward_kernel, n_c, n_f, mine, ffe, sro...  68.6 us
    pallas_call x1, Pallas kernels, last(): pl.pallas_call(functools.partial(last_kernel, n_c, n_f, n_t, width), out_...  67.7 us
    pallas_call x1, Pallas kernels, fill_experts(): pl.pallas_call(fill_kernel, grid_spec=pltpu.PrefetchScalarGridSpec(num_sc...  12.1 us
    pallas_call x1, Pallas kernels, attend_back(): pl.pallas_call(functools.partial(attend_back_kernel, min(256, seq)), out_...  11.8 us
  transfers between devices with their start and end apart: 1, of which 0 were waited for; matrix products, arithmetic and copies ran while one was open for 2% of the time, Pallas kernels for 39%

profile of v4, /device:TPU:0, one launch (start us, length us, event | category | flops | bytes accessed | tf_op | source)
XLA Modules:
  0.0 510.9 jit_solution(15488466151153019570)
XLA Ops:
  4.1 1.0 concatenate.9
  5.7 2.3 fusion.5.shared
  8.0 199.9 %first.1 = (bf16[1024,2048]{1,0:T(8,128)(2,1)}, bf16[1024,128]{1,0:T(8,128)(2,1)}, bf16[1024,128]{1,0:T(8,128)(2,1)}, bf16[1024,128]{1,0:T(8,128)(2,1)}, f32[102...) custom-call(bf16[256,512]{1,0:T(8,128)(2,1)} %hidden.3, ...), custom_call_target="tpu_custom_call" | custom-call | flops 5368709120 | bytes 314572800 | tf_op jit(solution)/shard_map/first/pallas_call | solution.py:901
  207.8 1.4 fusion.9
  209.3 1.6 fusion.10
  210.9 1.3 copy.34
  212.2 68.6 %forward.1 = (bf16[256,512]{1,0:T(8,128)(2,1)}, bf16[2048,2048]{1,0:T(8,128)(2,1)}, bf16[2048,896]{1,0:T(8,128)(2,1)}, bf16[2048,896]{1,0:T(8,128)(2,1)}, bf16[2...) custom-call(bf16[2048,2048]{1,0:T(8,128)(2,1)} %get-tuple-element.68, ...), custom_call_target="tpu_custom_call" | custom-call | flops 26843545600 | bytes 83886080 | tf_op jit(solution)/shard_map/forward/pallas_call | solution.py:1276
  280.8 1.5 collective-permute-start
  282.3 1.3 constant_dynamic-slice_fusion.gain
  283.6 121.8 %backward.1 = (f32[256,512]{1,0:T(8,128)}, f32[8,512]{1,0:T(8,128)}, bf16[1024,2048]{1,0:T(8,128)(2,1)}, bf16[8,304,256]{2,1,0:T(8,128)(2,1)}, f32[2,352,1024]{2...) custom-call(bf16[8,4,256,512]{3,2,1,0:T(8,128)(2,1)} %get-tuple-elem, ...), custom_call_target="tpu_custom_call" | custom-call | flops 33554432000 | bytes 209715200 | tf_op jit(solution)/shard_map/backward/pallas_call | solution.py:1504
  405.4 11.8 %attend_back.1 = (bf16[1024,384]{1,0:T(8,128)(2,1)}, bf16[512,2048]{1,0:T(8,128)(2,1)}) custom-call(bf16[1024,2048]{1,0:T(8,128)(2,1)} %get-tuple-element.84.mid, bf16[128,2048]{1,0:T(8,128)(2,1)} %get-tuple-element.85.wo, bf16[1024,128]{1,0:T(8,128)(2,1)} %get-tuple-element.86.q, bf16[1024,128]{1,0:T(8,128)(2,1)} %get-tuple-element.87.k, ...), custom_call_target="tpu_custom_call" | custom-call | flops 6442450944 | bytes 16777216 | tf_op jit(solution)/shard_map/attend_back/pallas_call | solution.py:1675
  417.2 1.0 slice.47
  418.2 1.2 slice.46
  420.0 1.5 convert_reduce_fusion.rpart
  421.5 67.7 %last.1 = (f32[256,512]{1,0:T(8,128)}, f32[256,512]{1,0:T(8,128)}, f32[256,512]{1,0:T(8,128)}, f32[256,512]{1,0:T(8,128)}, f32[512,256]{1,0:T(8,128)}, /*index=5...) custom-call(bf16[1024,384]{1,0:T(8,128)(2,1)} %get-tuple-element.94.dqkv, ...), custom_call_target="tpu_custom_call" | custom-call | flops 2147483648 | bytes 157286400 | tf_op jit(solution)/shard_map/last/pallas_call | solution.py:1829
  489.3 1.3 fusion.11
  490.8 1.4 fusion.8
  492.2 1.1 copy-done
  493.3 12.1 %fill_experts.1 = (f32[4,352,1024]{2,1,0:T(8,128)}, f32[4,352,1024]{2,1,0:T(8,128)}, f32[4,352,1024]{2,1,0:T(8,128)}) custom-call(s32[1]{0:T(128)} %bitcast.19.f_ref, bf16[2,352,512]{2,1,0:T(8,128)(2,1)} %get-tuple-element.110.ga, bf16[2,352,512]{2,1,0:T(8,128)(2,1)} %get-tuple-element.111.gb, bf16[2,352,512]{2,1,0:T(8,128)(2,1)} %get-tuple-element.112.ua, ...), custom_call_target="tpu_custom_call" | custom-call | tf_op jit(solution)/shard_map/fill_experts/pallas_call | solution.py:1593
  506.1 0.8 copy.43
  506.9 0.8 copy.44
  507.7 0.8 copy.45
  508.5 0.8 copy.46
  509.3 0.8 copy.47
  (33 shorter events, 6.2 us)
Async XLA Ops:
  280.8 211.4 %collective-permute-start = (bf16[2,352,1024]{2,1,0:T(8,128)(2,1)}, bf16[2,352,1024]{2,1,0:T(8,128)(2,1)S(1)}, u32[]{:S(2)}, u32[]{:S(2)}) collective-permute-start(bf16[2,352,1024]{2,1,0:T(8,128)(2,1)} %get-tuple-element.114), channel_id=1, source_target_pairs={{0,16},{16,0},{1,17},{17,1},{2,18},{18,2},{3,19},{19,3},{4,20},{20... | collective-permute-start | bytes 4325384 | tf_op jit(solution)/shard_map/ppermute | solution.py:1953
  492.2 1.1 copy-start
  493.3 12.1 %copy-start.6 = (bf16[256,512]{1,0:T(8,128)(2,1)S(1)}, bf16[256,512]{1,0:T(8,128)(2,1)}, u32[]{:S(2)}) copy-start(bf16[256,512]{1,0:T(8,128)(2,1)} %get-tuple-element.147) | copy-start | bytes 786436
  493.3 12.8 %copy-start.5 = (f32[256,512]{1,0:T(8,128)S(1)}, f32[256,512]{1,0:T(8,128)}, u32[]{:S(2)}) copy-start(f32[256,512]{1,0:T(8,128)} %get-tuple-element.148) | copy-start | bytes 1572868
  493.3 13.6 %copy-start.4 = (f32[256,512]{1,0:T(8,128)S(1)}, f32[256,512]{1,0:T(8,128)}, u32[]{:S(2)}) copy-start(f32[256,512]{1,0:T(8,128)} %get-tuple-element.150) | copy-start | bytes 1572868
  505.4 2.3 copy-start.3
  505.4 3.1 copy-start.2
  505.4 3.9 copy-start.1
  506.9 3.2 copy-start.7

commit v5 on v4

--- a/solution.py
+++ b/solution.py
@@ -2,6 +2,7 @@
 
 import jax
 import jax.numpy as jnp
+import numpy as np
 from jax import lax
 from jax.experimental import pallas as pl
 from jax.experimental.pallas import tpu as pltpu
@@ -684,7 +685,7 @@
     ]
 
 
-def reduce_seq(part_of, n_c, scratch, between=None, before_last=None):
+def reduce_seq(part_of, n_c, scratch, middle=None, before_last=None):
     out1, in1, own, out2, in2, out3, in3, s1, r1, s2, r2, s3, r3 = scratch
     f, c, t = ranks()
     far, sib = opposite(t), sibling(t)
@@ -697,12 +698,12 @@
         remote(out1.at[d], in1.at[d], s1.at[d], r1.at[d], to_sib).start()
         own[d, 0] = part_of(cc, t)
         own[d, 1] = part_of(cc, far)
-    if between is not None:
-        between()
     for d in order:
         remote(out1.at[d], in1.at[d], s1.at[d], r1.at[d], to_sib).wait()
         out2[d] = (own[d, 1] + in1[d, 1].astype(F32)).astype(BF)
         remote(out2.at[d], in2.at[d], s2.at[d], r2.at[d], to_far).start()
+    if middle is not None:
+        middle()
     for d in order:
         remote(out2.at[d], in2.at[d], s2.at[d], r2.at[d], to_far).wait()
         total = own[d, 0] + in1[d, 0].astype(F32) + in2[d].astype(F32)
@@ -719,10 +720,10 @@
 
 
 def first_kernel(
-    n_c, n_f, n_exp, mine, hidden, wq, wk, wv, wo, small, og, gate_t, up_t, down, shared, angle,
+    n_c, n_f, n_exp, mine, hidden, wq, wk, wv, wo, og, gate_t, up_t, down, router_in, chosen, lines, sg, su, sd, angle,
     normed, q_out, k_out, v_out, hf_out, lse_out, r_out, cos_out, sin_out, resid_out,
     wqkv_out, wo_out, small_out, all_out, og_out, shared_out, gg_out, gu_out, gd_out,
-    seq, wqkv, wo_all, small_all, hb, blk, own_og,
+    seq, wqkv, wo_all, small_all, hb, blk, own_og, small, shared,
     ws, wr, ls, xs, xr, ss, sr, sl, es, er, os, *scratch,
 ):
     f, c, t = ranks()
@@ -730,6 +731,20 @@
     part = wo.shape[1]
     tokens, width = seq.shape
     n_s = len(spread_sems(n_c))
+    named = lax.broadcasted_iota(jnp.int32, (n_exp, part), 0)
+    mask = jnp.zeros((n_exp, part), F32)
+    for k in range(chosen.shape[0]):
+        mask = mask + jnp.where(chosen[k : k + 1, :] == named, 1.0, 0.0)
+    small[:n_exp, :] = router_in[...]
+    small[n_exp : 2 * n_exp, :] = mask.astype(BF)
+    small[2 * n_exp :, :] = lines[...]
+    n_b = n_f * n_c
+    own_rows, srows = sg.shape[0] // n_b, shared.shape[1] // 3
+    for i, src in enumerate((sg, su, sd)):
+        for b in range(n_b):
+            shared[b, i * srows : i * srows + own_rows, :] = src[b * own_rows : (b + 1) * own_rows, :]
+            if srows > own_rows:
+                shared[b, i * srows + own_rows : (i + 1) * srows, :] = jnp.zeros((srows - own_rows, part), BF)
     greet([{"tp": sibling(t)}, {"tp": opposite(t)}] + each_peers(f, c, n_f, n_c))
     seq_place = lambda g, cc, tt: seq.at[piece(cc, rows), piece(tt, quarter)]
     og_place = lambda g, cc, tt: og_out.at[g * n_c + cc, tt]
@@ -810,8 +825,8 @@
     grad.other()
 
     scale_att = HD ** (-0.5)
-    gain = small_all[0:1, :].astype(F32)
-    place_row = 2 + 2 * n_exp
+    gain = small_all[2 * n_exp : 2 * n_exp + 1, :].astype(F32)
+    place_row = 2 * n_exp + 2
     for start in range(0, tokens, rows):
         at = pl.ds(start, rows)
         h = seq[at, :].astype(F32)
@@ -889,13 +904,15 @@
         copy.wait()
 
 
-def first(n_c, n_f, n_t, mine, hidden, wq, wk, wv, wo, small, og, weights, shared, angle):
+def first(n_c, n_f, n_t, mine, srows, hidden, wq, wk, wv, wo, og, weights, router, chosen, lines, shared, angle):
     rows, quarter = hidden.shape
     width = quarter * n_t
     seq = rows * n_c
     n_exp = mine * n_f * n_c
     ffe, half = weights[0].shape[1:]
     sds = jax.ShapeDtypeStruct
+    part = wo.shape[1]
+    n_small = 2 * n_exp + lines.shape[0]
     head, head_f = sds((seq, HD), BF), sds((seq, HD), F32)
     got = sds((mine, ffe, half), BF)
     return pl.pallas_call(
@@ -913,24 +930,26 @@
             sds((rows, quarter), F32),
             sds((width, 3 * HD), BF),
             sds((HD, width), BF),
-            sds((small.shape[0], width), BF),
+            sds((n_small, width), BF),
             sds((seq * n_f, width), BF),
             sds((n_f * n_c, n_t, rows, quarter), BF),
-            sds(shared.shape, BF),
+            sds((n_f * n_c, 3 * srows, part), BF),
             got,
             got,
             got,
         ),
-        in_specs=[HBM] * 11 + [VMEM],
+        in_specs=[HBM] * 9 + [VMEM] * 7,
         out_specs=[VMEM] * 10 + [HBM] * 9,
         scratch_shapes=[
             pltpu.VMEM((seq, width), BF),
             pltpu.VMEM((width, 3 * HD), BF),
             pltpu.VMEM((HD, width), BF),
-            pltpu.VMEM((small.shape[0], width), BF),
+            pltpu.VMEM((n_small, width), BF),
             pltpu.VMEM((seq, HD), BF),
             pltpu.VMEM((rows, quarter), BF),
             pltpu.VMEM((rows, quarter), BF),
+            pltpu.VMEM((n_small, part), BF),
+            pltpu.VMEM((n_f * n_c, 3 * srows, part), BF),
             DMA((n_c, 5)),
             DMA((n_c, 5)),
             DMA((5,)),
@@ -952,7 +971,7 @@
             flops=5 << 30, bytes_accessed=300 << 20, transcendentals=1 << 20
         ),
         name="first",
-    )(hidden, wq, wk, wv, wo, small, og, *weights, shared, angle)
+    )(hidden, wq, wk, wv, wo, og, *weights, router, chosen, lines, *shared, angle)
 
 
 def fetch_experts(n_c, n_f, mine, ffe, srows, hp, weights, shared, wgu, wd, sems):
@@ -1117,7 +1136,7 @@
 
 
 def forward_kernel(
-    n_c, n_f, mine, ffe, srows, hp, rows_all, og_all, resid, picked, gain, router,
+    n_c, n_f, mine, ffe, srows, hp, rows_all, og_all, resid, small,
     wg0, wu0, wd0, wg1, wu1, wd1, shared,
     layer_out, in_out, act_out, silu_out, slope_out, r_out, prob_out, keep_out, send_out, shared_out,
     gt, wsem, xsem, nsem, asem, tsem, osem, *scratch,
@@ -1128,6 +1147,7 @@
     width = rows_all.shape[1]
     routed = mine * ffe
     rows_used = routed + srows
+    n_exp = mine * n_b
     red = Reducer(n_c, scratch)
 
     def blocks_phase(wgu, wd, xs, ns, acts):
@@ -1173,13 +1193,14 @@
             h = xs[slot].astype(F32)
             r = lax.rsqrt(jnp.sum(h * h, axis=1, keepdims=True) / width + EPS)
             r_out[at, :] = jnp.broadcast_to(r, (rows, HD))
-            n = (h * r * gain[...]).astype(BF)
+            gain = small[2 * n_exp + 1 : 2 * n_exp + 2, :].astype(F32)
+            n = (h * r * gain).astype(BF)
             ns[slot] = n
-            logits = dot_nt(n, router[...])
+            logits = dot_nt(n, small[:n_exp, :])
             e = jnp.exp(logits - jnp.max(logits, axis=1, keepdims=True))
             prob = e / jnp.sum(e, axis=1, keepdims=True)
             prob_out[at, :] = prob
-            gate, _, _ = gates(prob, picked[at, :], (c * n_f + f) * mine, mine, ffe, hp)
+            gate, _, _ = gates(prob, small[n_exp : 2 * n_exp, at].astype(F32).T, (c * n_f + f) * mine, mine, ffe, hp)
             ab = dot_nt(n, wgu[...])
             between()
             a, up = ab[:, :hp], ab[:, hp:]
@@ -1238,7 +1259,7 @@
                 if s < 2:
                     sends[s] = g[:routed].astype(BF).reshape(mine, ffe, quarter)
                 else:
-                    keeps[s - 2] = g[:routed].reshape(mine, ffe, quarter)
+                    keeps[s - 2] = g[:routed].astype(BF).reshape(mine, ffe, quarter)
                 shs[s] = g[routed:].astype(BF)
                 for copy in out_copies(s):
                     copy.start()
@@ -1255,7 +1276,7 @@
     pl.run_scoped(
         grads_phase,
         pltpu.VMEM((2, n_b, rows, quarter), BF),
-        pltpu.VMEM((2, mine, ffe, quarter), F32),
+        pltpu.VMEM((2, mine, ffe, quarter), BF),
         pltpu.VMEM((2, mine, ffe, quarter), BF),
         pltpu.VMEM((4, srows, quarter), BF),
     )
@@ -1266,11 +1287,11 @@
     return used, -(-used // HD) * HD, 3 * (2 * mine + n_f * n_c)
 
 
-def forward(n_c, n_f, n_t, mine, ffe, srows, rows_all, og_all, resid, picked, gain, router, kept, got, shared):
+def forward(n_c, n_f, n_t, mine, ffe, srows, rows_all, og_all, resid, small, kept, got, shared):
     total, width = rows_all.shape
     rows, quarter = resid.shape
-    n_exp = router.shape[0]
     n_b = n_f * n_c
+    n_exp = mine * n_b
     used, hp, n_fetch = expert_sizes(n_c, n_f, n_t, mine, ffe, srows, width)
     sds = jax.ShapeDtypeStruct
     return pl.pallas_call(
@@ -1283,11 +1304,11 @@
             sds((total, hp), BF),
             sds((total, HD), F32),
             sds((total, n_exp), F32),
-            sds((mine, ffe, width // n_f), F32),
+            sds((mine, ffe, width // n_f), BF),
             sds((mine, ffe, width // n_f), BF),
             sds((srows, width), BF),
         ),
-        in_specs=[HBM, HBM, VMEM, VMEM, VMEM, VMEM] + [HBM] * 7,
+        in_specs=[HBM, HBM, VMEM, VMEM] + [HBM] * 7,
         out_specs=[VMEM, HBM, HBM, HBM, HBM, VMEM, VMEM, HBM, HBM, HBM],
         scratch_shapes=[
             pltpu.VMEM((used, total), BF),
@@ -1306,34 +1327,29 @@
             flops=8 * total * width * used, bytes_accessed=80 << 20, transcendentals=total * used
         ),
         name="forward",
-    )(rows_all, og_all, resid, picked, gain, router, *kept, *got, shared)
+    )(rows_all, og_all, resid, small, *kept, *got, shared)
 
 
 def backward_kernel(
-    n_c, n_f, mine, ffe, srows, hp, og_all, act, silu, slope, moe_in, r_all, shared_d, prob_in, picked, router,
-    resid, gain, og, wg0, wu0, wd0, wg1, wu1, wd1, shared,
-    mid_out, gain_out, seq_out, shared_out, kg_out, ku_out, gg_out, gu_out, lg_out, lu_out,
-    gt, blk, r_own, sends, shs, wsem, xsem, tsem, ksem, ss, sr, rs, es, er, el, ds, dr, dl, *rest,
+    n_c, n_f, mine, ffe, srows, hp, og_all, act, silu, slope, moe_in, r_all, shared_d, prob_in, small,
+    resid, og, wg0, wu0, wd0, wg1, wu1, wd1, shared,
+    mid_out, gain_out, seq_out, shared_out, shs_out, kg_out, ku_out, gg_out, gu_out, lg_out, lu_out,
+    gt, blk, r_own, sends, shs, wsem, xsem, tsem, ksem, ss, sr, rs, es, ds, dr, dl, *rest,
 ):
     f, c, t = ranks()
     n_b = n_f * n_c
     rows, quarter = resid.shape
     width = shared_d.shape[1]
-    n_exp = router.shape[0]
+    n_exp = mine * n_b
     routed = mine * ffe
     rows_used = routed + srows
     first = (c * n_f + f) * mine
     red = Reducer(n_c, rest[:18])
 
     cols = width // n_b
-    n_gu = shs.shape[0]
-
-    def exchange(act, which):
-        src, at, sems = (
-            (shs, pl.ds(0, n_gu), (es, er, el)),
-            (shared_d, pl.ds(n_gu, srows), (ds, dr, dl)),
-        )[which]
-        to_each(lambda b: src.at[:, piece(b, cols)], shared_out.at[:, at, :], n_f, n_c, sems, act)
+
+    def exchange(act):
+        to_each(lambda b: shared_d.at[:, piece(b, cols)], shared_out, n_f, n_c, (ds, dr, dl), act)
 
     def blocks_phase(wgu, wd, ogs, acts):
         fetches = fetch_experts(
@@ -1358,7 +1374,7 @@
             copy.start()
         blank_rows(rows_used, hp, wgu, wd)
         greet([{"tp": red.sib}, {"tp": red.far}, {"tp": opposite(red.sib)}] + each_peers(f, c, n_f, n_c))
-        exchange("start", 1)
+        exchange("start")
         for copy in fetches:
             copy.wait()
 
@@ -1374,7 +1390,7 @@
                     copy.start()
 
             prob = prob_in[at, :]
-            chosen = picked[at, :]
+            chosen = small[n_exp : 2 * n_exp, at].astype(F32).T
             gate, lane, col = gates(prob, chosen, first, mine, ffe, hp)
             dh = dot_nt(ogs[slot], wd[...])
             between()
@@ -1398,7 +1414,7 @@
 
             def part_of(q):
                 cols = piece(q, quarter)
-                return dot_nn(dab, wgu[:, cols]) + dot_nn(logit_grad, router[:, cols])
+                return dot_nn(dab, wgu[:, cols]) + dot_nn(logit_grad, small[:n_exp, cols])
 
             red.put(i, part_of)
 
@@ -1443,7 +1459,7 @@
                         sends[s, m] = g[base : base + routed].astype(BF).reshape(mine, ffe, quarter)
                         send_copy(s, m).start()
                     else:
-                        keeps[s - 2, m] = g[base : base + routed].reshape(mine, ffe, quarter)
+                        keeps[s - 2, m] = g[base : base + routed].astype(BF).reshape(mine, ffe, quarter)
                         keep_copy(s, m).start()
                     shs[m * srows : (m + 1) * srows, cols] = g[base + routed : base + rows_used].astype(BF)
                 shs[2 * srows :, cols] = g[2 * rows_used :].astype(BF)
@@ -1461,10 +1477,13 @@
     pl.run_scoped(
         grads_phase,
         pltpu.VMEM((2, n_b * rows, quarter), BF),
-        pltpu.VMEM((2, 2, mine, ffe, quarter), F32),
-    )
+        pltpu.VMEM((2, 2, mine, ffe, quarter), BF),
+    )
+    shs_copy = pltpu.make_async_copy(shs, shs_out, es)
+    shs_copy.start()
     fetch.wait()
-    back, gain_part = norm_grad(resid[...], r_own[:, :1], gain[...], blk[...], width, *rest[18:22])
+    gain = small[2 * n_exp + 1 : 2 * n_exp + 2, piece(t, quarter)].astype(F32)
+    back, gain_part = norm_grad(resid[...], r_own[:, :1], gain, blk[...], width, *rest[18:22])
     gain_out[...] = jnp.broadcast_to(gain_part, gain_out.shape)
     grad = og[...].astype(F32) + back
     mid_out[...] = grad
@@ -1477,29 +1496,28 @@
     sequence = Spread(own, place, n_c, False, rest[23:])
     sequence.start()
     sequence.line()
-    exchange("start", 0)
     sequence.far(0)
     sequence.arrived(0)
     sequence.finish()
     sequence.local().wait()
-    exchange("wait", 0)
-    exchange("wait", 1)
+    exchange("wait")
+    shs_copy.wait()
     for s in range(2):
         for m in range(2):
             send_copy(s, m).wait()
 
 
 def backward(
-    n_c, n_f, n_t, mine, ffe, srows, og_all, act, silu, slope, moe_in, r_all, shared_d, prob, picked, router,
-    resid, gain, og, kept, got, shared,
+    n_c, n_f, n_t, mine, ffe, srows, og_all, act, silu, slope, moe_in, r_all, shared_d, prob, small,
+    resid, og, kept, got, shared,
 ):
     total, width = moe_in.shape
     rows, quarter = resid.shape
-    n_exp = router.shape[0]
     n_b = n_f * n_c
+    n_exp = mine * n_b
     used, hp, n_fetch = expert_sizes(n_c, n_f, n_t, mine, ffe, srows, width)
     sds = jax.ShapeDtypeStruct
-    kept_g = sds((mine, ffe, width // n_f), F32)
+    kept_g = sds((mine, ffe, width // n_f), BF)
     sent_g = sds((mine, ffe, quarter), BF)
     return pl.pallas_call(
         functools.partial(backward_kernel, n_c, n_f, mine, ffe, srows, hp),
@@ -1507,7 +1525,8 @@
             sds((rows, quarter), F32),
             sds((8, quarter), F32),
             sds((rows * n_c, width), BF),
-            sds((n_b, 3 * srows + n_exp, width // n_b), BF),
+            sds((n_b, srows, width // n_b), BF),
+            sds((2 * srows + n_exp, width), BF),
             kept_g,
             kept_g,
             sent_g,
@@ -1515,8 +1534,8 @@
             sent_g,
             sent_g,
         ),
-        in_specs=[HBM] * 7 + [VMEM] * 6 + [HBM] * 7,
-        out_specs=[VMEM, VMEM] + [HBM] * 8,
+        in_specs=[HBM] * 7 + [VMEM] * 4 + [HBM] * 7,
+        out_specs=[VMEM, VMEM] + [HBM] * 9,
         scratch_shapes=[
             pltpu.VMEM((2 * used + n_exp, total), BF),
             pltpu.VMEM((rows, quarter), F32),
@@ -1530,8 +1549,6 @@
             DMA((2, 2)),
             DMA((2,)),
             DMA(()),
-            DMA((n_b,)),
-            DMA((n_b,)),
             DMA(()),
             DMA((n_b,)),
             DMA((n_b,)),
@@ -1549,19 +1566,22 @@
         ),
         name="backward",
     )(
-        og_all, act, silu, slope, moe_in, r_all, shared_d, prob, picked, router, resid, gain, og,
+        og_all, act, silu, slope, moe_in, r_all, shared_d, prob, small, resid, og,
         *kept, *got, shared,
     )
 
 
-def fill_kernel(f_ref, ga, gb, ua, ub, d, kg, ku, kd, og, ou, od):
+def finish_kernel(n_plain, f_ref, *refs):
+    ga, gb, ua, ub, d, kg, ku, kd, shared = refs[:9]
+    plain = refs[9 : 9 + n_plain]
+    og, ou, od, shared_out = refs[9 + n_plain : 13 + n_plain]
     step = pl.program_id(0)
     f = f_ref[0]
     n_e = kg.shape[0]
 
-    def put(own, at):
+    def put(at):
         for keep, out in ((kg, og), (ku, ou), (kd, od)):
-            out[at : at + n_e] = keep[...]
+            out[at : at + n_e] = keep[...].astype(F32)
         for out, halves in ((og, (ga, gb)), (ou, (ua, ub))):
             @pl.when(step < 2)
             def _():
@@ -1575,33 +1595,52 @@
 
     @pl.when(f == 0)
     def _():
-        put(0, 0)
+        put(0)
 
     @pl.when(f != 0)
     def _():
-        put(1, n_e)
-
-
-def fill_experts(f_rank, arrived, kept):
+        put(n_e)
+
+    own = shared_out.shape[0] // shared.shape[0]
+    for b in range(shared.shape[0]):
+        shared_out[b * own : (b + 1) * own, :] = shared[b, :own, :].astype(F32)
+    for src, dst in zip(plain, refs[13 + n_plain :]):
+        dst[...] = src[...]
+
+
+def finish(f_rank, own_shared, arrived, kept, shared, plain):
     mine, ffe, quarter = arrived[0].shape
     half = kept[0].shape[2]
     tile = half // 4
+    n_b, srows, part = shared.shape
     first = pl.BlockSpec((mine, ffe, tile), lambda i, f: (0, 0, jnp.minimum(i, 1)))
     second = pl.BlockSpec((mine, ffe, tile), lambda i, f: (0, 0, jnp.maximum(i - 2, 0)))
     every = pl.BlockSpec((mine, ffe, tile), lambda i, f: (0, 0, i))
     out = pl.BlockSpec((2 * mine, ffe, tile), lambda i, f: (0, 0, i))
+
+    def rows_of(x):
+        if x.shape[0] % 64:
+            return pl.BlockSpec(x.shape, lambda i, f: (0, 0))
+        return pl.BlockSpec((x.shape[0] // 4, x.shape[1]), lambda i, f: (i, 0))
+
+    shared_grad = jax.ShapeDtypeStruct((n_b * own_shared, part), F32)
     return pl.pallas_call(
-        fill_kernel,
+        functools.partial(finish_kernel, len(plain)),
         grid_spec=pltpu.PrefetchScalarGridSpec(
             num_scalar_prefetch=1,
             grid=(4,),
-            in_specs=[first, second, first, second, every] + [every] * 3,
-            out_specs=[out] * 3,
+            in_specs=[first, second, first, second, every]
+            + [every] * 3
+            + [pl.BlockSpec((n_b // 4, srows, part), lambda i, f: (i, 0, 0))]
+            + [rows_of(x) for x in plain],
+            out_specs=[out] * 3 + [rows_of(shared_grad)] + [rows_of(x) for x in plain],
         ),
-        out_shape=tuple(jax.ShapeDtypeStruct((2 * mine, ffe, half), F32) for k in kept),
+        out_shape=tuple(jax.ShapeDtypeStruct((2 * mine, ffe, half), F32) for k in kept)
+        + (shared_grad,)
+        + tuple(jax.ShapeDtypeStruct(x.shape, x.dtype) for x in plain),
         compiler_params=pltpu.CompilerParams(vmem_limit_bytes=BIG),
-        name="fill_experts",
-    )(f_rank, *arrived, *kept)
+        name="finish",
+    )(f_rank, *arrived, *kept, shared, *plain)
 
 
 def norm_grad(values, r, gain, grad, width, out, into, send, recv):
@@ -1633,9 +1672,7 @@
     ]
 
 
-def attend_back_kernel(
-    block, mid, wo, q, k, v, hf, lse, cosine, sine, normed, dqkv, gattn, hg, dq, dk, dv
-):
+def attend_back(block, mid, wo, q, k, v, hf, lse, cosine, sine, dqkv, hg, dq, dk, dv):
     seq = mid.shape[0]
     scale_att = HD ** (-0.5)
     for start in range(0, seq, block):
@@ -1665,34 +1702,20 @@
         dqkv[at, :HD] = rotate(dq[at, :], at)
         dqkv[at, HD : 2 * HD] = rotate(dk[at, :], at)
         dqkv[at, 2 * HD :] = dv[at, :].astype(BF)
-    gattn[: 3 * HD, :] = dot_tn(dqkv[...], normed[...]).astype(BF)
-    gattn[3 * HD :, :] = dot_tn(hf[...].astype(BF), mid[...]).astype(BF)
-
-
-def attend_back(mid_seq, wo, q, k, v, hf, lse, cosine, sine, normed):
-    seq, width = mid_seq.shape
-    sds = jax.ShapeDtypeStruct
-    return pl.pallas_call(
-        functools.partial(attend_back_kernel, min(256, seq)),
-        out_shape=(sds((seq, 3 * HD), BF), sds((4 * HD, width), BF)),
-        in_specs=[VMEM] * 10,
-        out_specs=[VMEM] * 2,
-        scratch_shapes=[pltpu.VMEM((seq, HD), BF)] + [pltpu.VMEM((seq, HD), F32)] * 3,
-        compiler_params=pltpu.CompilerParams(vmem_limit_bytes=BIG),
-        cost_estimate=pl.CostEstimate(flops=6 << 30, bytes_accessed=16 << 20, transcendentals=1 << 20),
-        name="attend_back",
-    )(mid_seq, wo, q, k, v, hf, lse, cosine, sine, normed)
 
 
 def last_kernel(
-    n_c, n_f, n_t, width, dqkv, wqkv, hidden, r_all, gain, mid_grad, gain2, rpart, gattn, lg, lu,
-    in_out, gq, gk, gv, go, gains_out, router_out, lg_out, lu_out,
-    es, er, rin, rss, rsr, r_own, mine, inx, own, outz, inz, gsend, gin, rs, sx, rx, lx, sz, rz, gs, gr, *rest,
+    n_c, n_f, n_t, n_exp, own_shared, mid_seq, wo, q, k, v, hf, lse, cosine, sine, normed, wqkv, hidden, r_all,
+    small, mid_grad, gain2, shs, lg, lu,
+    in_out, gq, gk, gv, go, gains_out, router_out, sg_out, su_out, lg_out, lu_out,
+    dqkv, hg, dq, dk, dv, gattn, shs_in, rpart, hs, hr, hl, es, er, rin, rss, rsr, r_own, mine, inx, own, outz, inz, gsend, gin, rs, sx, rx, lx, sz, rz, gs, gr, *rest,
 ):
     f, c, t = ranks()
     rows, quarter = hidden.shape
+    tokens, width = normed.shape
     part = width // (n_f * n_c)
     here = f * n_c + c
+    srows = (shs.shape[0] - n_exp) // 2
     others = []
     for df in range(n_f):
         for dc in range(n_c):
@@ -1726,19 +1749,25 @@
         remote(rpart, rin.at[i], rss.at[i], rsr.at[i], {"tp": peer})
         for i, peer in enumerate([sibling(t), opposite(t), opposite(sibling(t))])
     ]
+    shared = lambda act: to_each(lambda b: shs.at[:, piece(b, part)], shs_in, n_f, n_c, (hs, hr, hl), act)
     late = [
         remote(src, dst, es.at[i], er.at[i], {"fsdp": 1 - f})
         for i, (src, dst) in enumerate(((lg, lg_out), (lu, lu_out)))
     ]
-    for copy in router_copies:
-        copy.start()
+    shared("start")
     fetch = pltpu.make_async_copy(r_all.at[piece(c, rows), :], r_own, rs)
     fetch.start()
-    for d in order:
-        cross(d).start()
-        keep(d).start()
     for copy in late:
         copy.start()
+    attend_back(rows, mid_seq, wo, q, k, v, hf, lse, cosine, sine, dqkv, hg, dq, dk, dv)
+    gattn[3 * HD :, :] = dot_tn(hf[...].astype(BF), mid_seq[...]).astype(BF)
+
+    def weights():
+        gattn[: 3 * HD, :] = dot_tn(dqkv[...], normed[...]).astype(BF)
+        for d in order:
+            cross(d).start()
+            keep(d).start()
+
 
     def part_of(cc, q):
         return dot_nt(dqkv[piece(cc, rows), :], wqkv[piece(q, quarter), :])
@@ -1754,10 +1783,11 @@
             else:
                 mine[...] = both
 
-    total = reduce_seq(part_of, n_c, rest[:13], None, pass_weights)
+    total = reduce_seq(part_of, n_c, rest[:13], weights, pass_weights)
     fetch.wait()
+    gain = small[2 * n_exp : 2 * n_exp + 1, piece(t, quarter)].astype(F32)
     back, gain_part = norm_grad(
-        hidden[...].astype(F32), r_own[:, :1], gain[...], total, width, *rest[13:17]
+        hidden[...].astype(F32), r_own[:, :1], gain, total, width, *rest[13:17]
     )
     in_out[...] = mid_grad[...] + back
 
@@ -1792,6 +1822,14 @@
             ref[:, at] = block[i * HD : (i + 1) * HD, :].T
         go[at, :] = block[3 * HD :, :]
 
+    shared("wait")
+    rpart[...] = jnp.sum(shs_in[:, 2 * srows :, :].astype(F32), axis=0)
+    for copy in router_copies:
+        copy.start()
+    for b in range(n_f * n_c):
+        at = pl.ds(b * own_shared, own_shared)
+        sg_out[at, :] = shs_in[b, :own_shared, :].astype(F32)
+        su_out[at, :] = shs_in[b, srows : srows + own_shared, :].astype(F32)
     put(c, mine[...])
     for d in order[:-1]:
         line(d, c).wait()
@@ -1820,14 +1858,19 @@
     router_out[...] = rpart[...] + jnp.sum(rin[...], axis=0)
 
 
-def last(n_c, n_f, n_t, dqkv, wqkv, hidden, r_all, gain, mid_grad, gain2, rpart, gattn, lg, lu):
+def last(
+    n_c, n_f, n_t, n_exp, own_shared, mid_seq, wo, q, k, v, hf, lse, cosine, sine, normed, wqkv, hidden, r_all,
+    small, mid_grad, gain2, shs, lg, lu,
+):
     rows, quarter = hidden.shape
-    width = quarter * n_t
+    seq, width = normed.shape
     part = width // (n_f * n_c)
     sds = jax.ShapeDtypeStruct
     slab = pltpu.VMEM((n_c, 4 * HD, part), BF)
+    head_f = pltpu.VMEM((seq, HD), F32)
+    shared_grad = sds((n_f * n_c * own_shared, part), F32)
     return pl.pallas_call(
-        functools.partial(last_kernel, n_c, n_f, n_t, width),
+        functools.partial(last_kernel, n_c, n_f, n_t, n_exp, own_shared),
         out_shape=(
             sds((rows, quarter), F32),
             sds((part, n_c * HD), F32),
@@ -1835,16 +1878,29 @@
             sds((part, n_c * HD), F32),
             sds((n_c * HD, part), F32),
             sds((8, part), F32),
-            sds(rpart.shape, F32),
+            sds((n_exp, part), F32),
+            shared_grad,
+            shared_grad,
             sds(lg.shape, BF),
             sds(lu.shape, BF),
         ),
-        in_specs=[VMEM, VMEM, VMEM, HBM, VMEM, VMEM, VMEM, VMEM, HBM, HBM, HBM],
-        out_specs=[VMEM] * 7 + [HBM] * 2,
+        in_specs=[VMEM] * 12 + [HBM] + [VMEM] * 3 + [HBM] * 3,
+        out_specs=[VMEM] * 9 + [HBM] * 2,
         scratch_shapes=[
+            pltpu.VMEM((seq, 3 * HD), BF),
+            pltpu.VMEM((seq, HD), BF),
+            head_f,
+            head_f,
+            head_f,
+            pltpu.VMEM((4 * HD, width), BF),
+            pltpu.VMEM((n_f * n_c, shs.shape[0], part), BF),
+            pltpu.VMEM((n_exp, part), F32),
+            DMA((n_f * n_c,)),
+            DMA((n_f * n_c,)),
+            DMA(()),
             DMA((2,)),
             DMA((2,)),
-            pltpu.VMEM((3,) + rpart.shape, F32),
+            pltpu.VMEM((3, n_exp, part), F32),
             DMA((3,)),
             DMA((3,)),
             pltpu.VMEM((rows, HD), F32),
@@ -1869,9 +1925,12 @@
         compiler_params=pltpu.CompilerParams(
             collective_id=4, has_side_effects=True, vmem_limit_bytes=BIG
         ),
-        cost_estimate=pl.CostEstimate(flops=2 << 30, bytes_accessed=150 << 20, transcendentals=0),
+        cost_estimate=pl.CostEstimate(flops=8 << 30, bytes_accessed=150 << 20, transcendentals=1 << 20),
         name="last",
-    )(dqkv, wqkv, hidden, r_all, gain, mid_grad, gain2, rpart, gattn, lg, lu)
+    )(
+        mid_seq, wo, q, k, v, hf, lse, cosine, sine, normed, wqkv, hidden, r_all, small, mid_grad, gain2,
+        shs, lg, lu,
+    )
 
 
 def per_device_seq(
@@ -1907,69 +1966,42 @@
     n_b = n_f * n_c
     own_shared = shared_gate.shape[1] // n_b
     srows = -(-own_shared // 16) * 16
-    block = f_rank * n_c + c_rank
     f_arr = f_rank.astype(jnp.int32).reshape(1)
     swap = [(i, n_f - 1 - i) for i in range(n_f)]
     weights = (expert_gate.swapaxes(1, 2), expert_up.swapaxes(1, 2), expert_down)
 
-    picked_own = jnp.sum(
-        (chosen[:, :, None] == jnp.arange(n_exp)[None, None, :]).astype(F32), axis=1
-    )
-    small = [
-        attn_gain[None],
-        moe_gain[None],
-        router.T,
-        picked_own.T.astype(BF),
-        (positions // 64).astype(BF)[None],
-        (positions % 64).astype(BF)[None],
-    ]
-    small = jnp.concatenate(small, axis=0)
-    small = jnp.pad(small, ((0, -small.shape[0] % 16), (0, 0)))
-
-    def shared_part(weight):
-        return jnp.pad(
-            weight.reshape(n_b, own_shared, part), ((0, 0), (0, srows - own_shared), (0, 0))
-        )
-
-    shared = jnp.concatenate(
-        [shared_part(shared_gate.T), shared_part(shared_up.T), shared_part(shared_down)], axis=1
-    )
-    half = HD // 2
-    inverse = 10000.0 ** (-jnp.arange(half, dtype=F32) * 2.0 / HD)
-    angle = jnp.stack([jnp.tile(inverse, 2), jnp.where(jnp.arange(HD) < half, -1.0, 1.0)])
+    line = jnp.arange(16)[:, None]
+    lines = jnp.where(line == 0, attn_gain[None], jnp.zeros((), BF))
+    lines = jnp.where(line == 1, moe_gain[None], lines)
+    lines = jnp.where(line == 2, (positions // 64).astype(BF)[None], lines)
+    lines = jnp.where(line == 3, (positions % 64).astype(BF)[None], lines)
+    lane = np.arange(HD)
+    inverse = 10000.0 ** (-(lane % (HD // 2)) * 2.0 / HD)
+    angle = jnp.asarray(np.stack([inverse, np.where(lane < HD // 2, -1.0, 1.0)]).astype(np.float32))
     (
         normed, q, k, v, heads_f, lse, r_one, cosine, sine, resid_mid,
-        wqkv, wo, small_all, resid_all, grad_all, shared, *got,
+        wqkv, wo, small, resid_all, grad_all, shared, *got,
     ) = first(
-        n_c, n_f, n_t, mine, hidden_in, w_query, w_key, w_value, w_out, small, out_grad, weights, shared, angle
-    )
-    gain_one, gain_two = small_all[0:1].astype(F32), small_all[1:2].astype(F32)
-    router_t = small_all[2 : 2 + n_exp]
-    picked = small_all[2 + n_exp : 2 + 2 * n_exp].astype(F32).T
+        n_c, n_f, n_t, mine, srows, hidden_in, w_query, w_key, w_value, w_out, out_grad, weights,
+        router.T, chosen.T, lines, (shared_gate.T, shared_up.T, shared_down), angle,
+    )
     sizes = (n_c, n_f, n_t, mine, ffe, srows)
     layer_out, moe_in, act, silu, slope, r_two, prob, kd, sd, shared_d = forward(
-        *sizes, resid_all, grad_all, resid_mid, picked, gain_two, router_t, weights, got, shared
+        *sizes, resid_all, grad_all, resid_mid, small, weights, got, shared
     )
     arrived_d = lax.ppermute(sd, "fsdp", swap)
-    own_cols = lambda x: lax.dynamic_slice_in_dim(x, t_rank * quarter, quarter, 1)
-    mid_grad, gain_two_part, mid_seq, shared_back, kg, ku, gg, gu, lg, lu = backward(
-        *sizes, grad_all, act, silu, slope, moe_in, r_two, shared_d, prob, picked, router_t,
-        resid_mid, own_cols(gain_two), out_grad, weights, got, shared,
-    )
-    n_gu = 2 * srows
-    router_part = jnp.sum(shared_back[:, n_gu : n_gu + n_exp].astype(F32), axis=0)
-    shared_back = jnp.concatenate([shared_back[:, :n_gu], shared_back[:, n_gu + n_exp :]], axis=1)
-    shared_back = shared_back.reshape(n_b, 3, srows, part)[:, :, :own_shared].astype(F32)
-
-    dqkv, gattn = attend_back(mid_seq, wo, q, k, v, heads_f, lse, cosine, sine, normed)
-    input_grad, gq, gk, gv, go, gains, router_grad, lg, lu = last(
-        n_c, n_f, n_t, dqkv, wqkv, hidden_in, r_one, own_cols(gain_one), mid_grad, gain_two_part,
-        router_part, gattn, lg, lu,
-    )
-    eg, eu, ed = fill_experts(f_arr, (gg, lg, gu, lu, arrived_d), (kg, ku, kd))
-
-    def shared_cols(i):
-        return shared_back[:, i].reshape(n_b * own_shared, part)
+    mid_grad, gain_two_part, mid_seq, shared_back, shs, kg, ku, gg, gu, lg, lu = backward(
+        *sizes, grad_all, act, silu, slope, moe_in, r_two, shared_d, prob, small,
+        resid_mid, out_grad, weights, got, shared,
+    )
+    input_grad, gq, gk, gv, go, gains, router_grad, shared_g, shared_u, lg, lu = last(
+        n_c, n_f, n_t, n_exp, own_shared, mid_seq, wo, q, k, v, heads_f, lse, cosine, sine, normed, wqkv,
+        hidden_in, r_one, small, mid_grad, gain_two_part, shs, lg, lu,
+    )
+    plain = (layer_out, input_grad, gq, gk, gv, go, router_grad, shared_g, shared_u)
+    eg, eu, ed, shared_d, layer_out, input_grad, gq, gk, gv, go, router_grad, shared_g, shared_u = finish(
+        f_arr, own_shared, (gg, lg, gu, lu, arrived_d), (kg, ku, kd), shared_back, plain
+    )
 
     return (
         layer_out,
@@ -1981,9 +2013,9 @@
         go,
         gains[1],
         router_grad.T,
-        shared_cols(0).T,
-        shared_cols(1).T,
-        shared_cols(2),
+        shared_g.T,
+        shared_u.T,
+        shared_d,
         eg.swapaxes(1, 2),
         eu.swapaxes(1, 2),
         ed,

time: 519 us -> 491 us (0.946)
  local copies, waits for them, and re-layouts: 16.9 us -> 2.49 us
  other arithmetic: 9.64 us -> 2.05 us
  Pallas kernels: 482 us -> 476 us
    pallas_call x1, Pallas kernels: 122 us -> 111 us  [backward(): pl.pallas_call(functools.partial(backward_kernel, n_c, n_f, mine, ffe, sr...]
    unnamed x23 -> x2, local copies, waits for them, and re-layouts: 6.42 us -> 1.14 us
    pallas_call x3 -> x2, Pallas kernels: 91.6 us -> 95.3 us  [the longest x1 82.8 us: last(): pl.pallas_call(functools.partial(last_kernel, n_c, n_f, n_t, n_exp, own_s...]
  transfers between devices with their start and end apart: 1 -> 1, of which waited for: 0 -> 0; matrix products, arithmetic and copies ran while one was open for 2% -> 0% of each run, Pallas kernels for 39% -> 40%
where the time goes in v5:
time: 491 us; the launch traced here: 483 us
  Pallas kernels  476 us (97%)
    pallas_call x1, Pallas kernels, first(): pl.pallas_call(functools.partial(first_kernel, n_c, n_f, n_exp, mine), ou...  201 us
    pallas_call x1, Pallas kernels, backward(): pl.pallas_call(functools.partial(backward_kernel, n_c, n_f, mine, ffe, sr...  111 us
    pallas_call x1, Pallas kernels, last(): pl.pallas_call(functools.partial(last_kernel, n_c, n_f, n_t, n_exp, own_s...  82.8 us
    pallas_call x1, Pallas kernels, forward(): pl.pallas_call(functools.partial(forward_kernel, n_c, n_f, mine, ffe, sro...  68.2 us
    pallas_call x1, Pallas kernels, finish(): pl.pallas_call(functools.partial(finish_kernel, len(plain)), grid_spec=pl...  12.5 us
  transfers between devices with their start and end apart: 1, of which 0 were waited for; matrix products, arithmetic and copies ran while one was open for 0% of the time, Pallas kernels for 40%

profile of v5, /device:TPU:0, one launch (start us, length us, event | category | flops | bytes accessed | tf_op | source)
XLA Modules:
  0.0 482.6 jit_solution(11061176984965709693)
XLA Ops:
  0.7 0.7 fusion
  1.4 1.3 select_select_fusion.lines
  2.7 200.6 %first.1 = (bf16[1024,2048]{1,0:T(8,128)(2,1)}, bf16[1024,128]{1,0:T(8,128)(2,1)}, bf16[1024,128]{1,0:T(8,128)(2,1)}, bf16[1024,128]{1,0:T(8,128)(2,1)}, f32[102...) custom-call(bf16[256,512]{1,0:T(8,128)(2,1)} %hidden.3, ...), custom_call_target="tpu_custom_call" | custom-call | flops 5368709120 | bytes 314572800 | tf_op jit(solution)/shard_map/first/pallas_call | solution.py:918
  203.3 68.2 %forward.1 = (bf16[256,512]{1,0:T(8,128)(2,1)}, bf16[2048,2048]{1,0:T(8,128)(2,1)}, bf16[2048,896]{1,0:T(8,128)(2,1)}, bf16[2048,896]{1,0:T(8,128)(2,1)}, bf16[2...) custom-call(bf16[2048,2048]{1,0:T(8,128)(2,1)} %get-tuple-element.80, ...), custom_call_target="tpu_custom_call" | custom-call | flops 26843545600 | bytes 83886080 | tf_op jit(solution)/shard_map/forward/pallas_call | solution.py:1297
  271.5 1.6 collective-permute-start
  273.1 111.5 %backward.1 = (f32[256,512]{1,0:T(8,128)}, f32[8,512]{1,0:T(8,128)}, bf16[1024,2048]{1,0:T(8,128)(2,1)}, bf16[8,96,256]{2,1,0:T(8,128)(2,1)}, bf16[208,2048]{1,0...) custom-call(bf16[8,4,256,512]{3,2,1,0:T(8,128)(2,1)} %get-tuple-elem, ...), custom_call_target="tpu_custom_call" | custom-call | flops 33554432000 | bytes 209715200 | tf_op jit(solution)/shard_map/backward/pallas_call | solution.py:1522
  384.6 82.8 %last.1 = (f32[256,512]{1,0:T(8,128)}, f32[256,512]{1,0:T(8,128)}, f32[256,512]{1,0:T(8,128)}, f32[256,512]{1,0:T(8,128)}, f32[512,256]{1,0:T(8,128)}, /*index=5...) custom-call(bf16[1024,2048]{1,0:T(8,128)(2,1)} %get-tuple-element.95, ...), custom_call_target="tpu_custom_call" | custom-call | flops 8589934592 | bytes 157286400 | tf_op jit(solution)/shard_map/last/pallas_call | solution.py:1872
  467.4 1.3 fusion.2
  468.7 0.0 collective-permute-done.refs_4_
  468.7 0.0 copy-start
  468.7 1.1 copy-done
  469.9 12.5 %finish.1 = (f32[4,352,1024]{2,1,0:T(8,128)}, f32[4,352,1024]{2,1,0:T(8,128)}, f32[4,352,1024]{2,1,0:T(8,128)}, f32[704,256]{1,0:T(8,128)}, bf16[256,512]{1,0:T(...) custom-call(s32[1]{0:T(128)} %bitcast.f_ref, ...), custom_call_target="tpu_custom_call" | custom-call | tf_op jit(solution)/shard_map/finish/pallas_call | solution.py:1627
  (2 shorter events, 0.0 us)
Async XLA Ops:
  271.5 197.2 %collective-permute-start = (bf16[2,352,1024]{2,1,0:T(8,128)(2,1)}, bf16[2,352,1024]{2,1,0:T(8,128)(2,1)S(1)}, u32[]{:S(2)}, u32[]{:S(2)}) collective-permute-start(bf16[2,352,1024]{2,1,0:T(8,128)(2,1)} %get-tuple-element.115), channel_id=1, source_target_pairs={{0,16},{16,0},{1,17},{17,1},{2,18},{18,2},{3,19},{19,3},{4,20},{20... | collective-permute-start | bytes 4325384 | tf_op jit(solution)/shard_map/ppermute | solution.py:1992
  468.7 1.1 copy-start

commit v6 on v5

--- a/solution.py
+++ b/solution.py
@@ -721,9 +721,9 @@
 
 def first_kernel(
     n_c, n_f, n_exp, mine, hidden, wq, wk, wv, wo, og, gate_t, up_t, down, router_in, chosen, lines, sg, su, sd, angle,
-    normed, q_out, k_out, v_out, hf_out, lse_out, r_out, cos_out, sin_out, resid_out,
+    normed_out, q_out, k_out, v_out, hf_out, lse_out, r_out, cos_out, sin_out, resid_out,
     wqkv_out, wo_out, small_out, all_out, og_out, shared_out, gg_out, gu_out, gd_out,
-    seq, wqkv, wo_all, small_all, hb, blk, own_og, small, shared,
+    seq, wqkv, wo_all, small_all, hb, blk, own_og, small, shared, normed,
     ws, wr, ls, xs, xr, ss, sr, sl, es, er, os, *scratch,
 ):
     f, c, t = ranks()
@@ -784,10 +784,20 @@
     for copy in more:
         copy.start()
     hid.start()
-    for step in range(1, n_c):
+    def weights_out(step):
         to = lax.rem(c + step, n_c)
         for i, (src, dst) in enumerate(zip(sources(to), targets(f, c))):
             remote(src, dst, ws.at[step, i], wr.at[step, i], {"ctx": to}).start()
+
+    def weights_on(step):
+        cc = lax.rem(c - step + n_c, n_c)
+        for i, dst in enumerate(targets(f, cc)):
+            remote(dst, dst, ws.at[step, i], wr.at[step, i], {"ctx": cc}).wait_recv()
+        for copy in across(step, f, cc):
+            copy.start()
+
+    steps = ([2, 1, 3] if n_c == 4 else list(range(1, n_c))) + [None]
+    weights_out(steps[0])
     own = [
         pltpu.make_async_copy(src, dst, ls.at[i])
         for i, (src, dst) in enumerate(zip(sources(c), targets(f, c)))
@@ -800,15 +810,13 @@
         copy.start()
     grad.start()
     hid.line()
-    for step in range(1, n_c):
-        cc = lax.rem(c - step + n_c, n_c)
-        for i, dst in enumerate(targets(f, cc)):
-            remote(dst, dst, ws.at[step, i], wr.at[step, i], {"ctx": cc}).wait_recv()
-        for copy in across(step, f, cc):
-            copy.start()
+    for step, following in zip(steps, steps[1:]):
+        if following is not None:
+            weights_out(following)
+        weights_on(step)
     grad.line()
     swaps = swap(gate_t, gg_out, 0) + swap(up_t, gu_out, 1)
-    for copy in swaps:
+    for copy in swaps[: mine + 1]:
         copy.start()
     hid.far(0)
     hid.arrived(0)
@@ -822,7 +830,6 @@
     ]
     for copy in outs:
         copy.start()
-    grad.other()
 
     scale_att = HD ** (-0.5)
     gain = small_all[2 * n_exp : 2 * n_exp + 1, :].astype(F32)
@@ -849,6 +856,8 @@
         q_out[at, :] = rotate(qkv[:, :HD])
         k_out[at, :] = rotate(qkv[:, HD : 2 * HD])
         v_out[at, :] = qkv[:, 2 * HD :].astype(BF)
+    outs.append(pltpu.make_async_copy(normed, normed_out, os.at[4]))
+    outs[-1].start()
     for start in range(0, tokens, rows):
         at = pl.ds(start, rows)
         seen = start + rows
@@ -859,7 +868,7 @@
         top = jnp.max(s, axis=1, keepdims=True)
         e = jnp.exp(s - top)
         total = jnp.sum(e, axis=1, keepdims=True)
-        out = dot_nn((e / total).astype(BF), v_out[:seen, :])
+        out = dot_nn((e * (1.0 / total)).astype(BF), v_out[:seen, :])
         hf_out[at, :] = out
         hb[at, :] = out.astype(BF)
         lse_out[at, :] = jnp.broadcast_to(top + jnp.log(total), (rows, HD))
@@ -869,6 +878,7 @@
     def part_of(cc, q):
         return dot_nn(hb[piece(cc, rows), :], wo_all[:, piece(q, quarter)])
 
+    grad.other()
     fetch = pltpu.make_async_copy(hidden, own_og, os.at[3])
     fetch.start()
     total = reduce_seq(part_of, n_c, scratch[3 * n_s :])
@@ -878,6 +888,8 @@
     blk[...] = resid.astype(BF)
     res.start()
     res.line()
+    for copy in swaps[mine + 1 :]:
+        copy.start()
     exchange("start")
     grad.far(0)
     grad.far(1)
@@ -939,7 +951,7 @@
             got,
         ),
         in_specs=[HBM] * 9 + [VMEM] * 7,
-        out_specs=[VMEM] * 10 + [HBM] * 9,
+        out_specs=[HBM] + [VMEM] * 9 + [HBM] * 9,
         scratch_shapes=[
             pltpu.VMEM((seq, width), BF),
             pltpu.VMEM((width, 3 * HD), BF),
@@ -950,6 +962,7 @@
             pltpu.VMEM((rows, quarter), BF),
             pltpu.VMEM((n_small, part), BF),
             pltpu.VMEM((n_f * n_c, 3 * srows, part), BF),
+            pltpu.VMEM((seq, width), BF),
             DMA((n_c, 5)),
             DMA((n_c, 5)),
             DMA((5,)),
@@ -960,7 +973,7 @@
             DMA(()),
             DMA((3, mine)),
             DMA((3, mine)),
-            DMA((4,)),
+            DMA((5,)),
         ]
         + spread_sems(n_c) * 3
         + reduce_seq_scratch(n_c, rows, quarter),
@@ -986,6 +999,7 @@
     def add(src, dst):
         copies.append(pltpu.make_async_copy(src, dst, sems.at[len(copies)]))
 
+    groups = []
     for i, (kept, got) in enumerate(((wg0, wg1), (wu0, wu1), (wd0, wd1))):
         dst, base = ((wgu, 0), (wgu, hp), (wd, 0))[i]
         for e in range(mine):
@@ -997,7 +1011,8 @@
                 shared.at[b, pl.ds(i * srows, srows), :],
                 dst.at[pl.ds(base + used, srows), pl.ds(b * part, part)],
             )
-    return copies
+        groups.append(copies[sum(map(len, groups)) :])
+    return groups[0] + groups[1], groups[2]
 
 
 def blank_rows(rows_used, hp, wgu, wd):
@@ -1019,8 +1034,10 @@
     return gate, lane, col
 
 
-def reducer_scratch(n_f, n_c, rows, quarter):
+def reducer_scratch(n_f, n_c, rows, quarter, split):
     n_b = n_f * n_c
+    upper = rows // 2 if split else rows
+    lower = rows // 2 if split else 16
     blocks = lambda *lead: pltpu.VMEM(lead + (rows, quarter), BF)
     return [
         blocks(n_b, 2),
@@ -1028,19 +1045,35 @@
         blocks(n_b, 2),
         blocks(n_b),
         blocks(n_b),
-        blocks(n_c),
-        blocks(n_c),
+        pltpu.VMEM((n_c, upper, quarter), BF),
+        pltpu.VMEM((n_c, upper, quarter), BF),
         pltpu.VMEM((n_c, rows, quarter), F32),
         blocks(n_c),
         blocks(n_c),
-    ] + [DMA((n_b,))] * 4 + [DMA((n_c,))] * 4
+        pltpu.VMEM((n_c, 2, lower, quarter), BF),
+        pltpu.VMEM((n_c, 2, lower, quarter), BF),
+    ] + [DMA((n_b,))] * 4 + [DMA((n_c,))] * 6
+
+
+N_REDUCER = 22
+
+
+def when(condition, act):
+    if isinstance(condition, bool):
+        if condition:
+            act()
+    else:
+        pl.when(condition)(act)
 
 
 class Reducer:
     def __init__(self, n_c, scratch):
         self.n_c = n_c
         (self.out1, self.in1, self.own, self.out2, self.in2, self.out3, self.in3, self.acc,
-         self.out4, self.in4, self.s1, self.r1, self.s2, self.r2, self.s3, self.r3, self.s4, self.r4) = scratch
+         self.out4, self.in4, self.out5, self.in5, self.s1, self.r1, self.s2, self.r2, self.s3, self.r3,
+         self.s4, self.r4, self.s5, self.r5) = scratch
+        self.half = self.out3.shape[1]
+        self.split = self.half < self.out4.shape[1]
         self.f, self.c, self.t = ranks()
         self.far, self.sib = opposite(self.t), sibling(self.t)
 
@@ -1052,11 +1085,17 @@
     def core_copy(self, i):
         return remote(self.out1.at[i], self.in1.at[i], self.s1.at[i], self.r1.at[i], {"tp": self.sib})
 
-    def far_copy(self, i):
-        return remote(self.out2.at[i], self.in2.at[i], self.s2.at[i], self.r2.at[i], {"tp": self.far})
+    def far_copy(self, i, upper=False):
+        src, dst = self.out2.at[i], self.in2.at[i]
+        if upper:
+            src, dst = src.at[pl.ds(0, self.half)], dst.at[pl.ds(0, self.half)]
+        return remote(src, dst, self.s2.at[i], self.r2.at[i], {"tp": self.far})
 
     def other_copy(self, j):
         return remote(self.out3.at[j], self.in3.at[j], self.s3.at[j], self.r3.at[j], {"fsdp": 1 - self.f})
+
+    def lower_copy(self, j):
+        return remote(self.out5.at[j], self.in5.at[j], self.s5.at[j], self.r5.at[j], {"fsdp": 1 - self.f})
 
     def line_copy(self, j, to):
         return remote(self.out4.at[j], self.in4.at[j], self.s4.at[j], self.r4.at[j], {"ctx": to})
@@ -1068,25 +1107,56 @@
         self.own[i, 0] = part_of(self.far).astype(BF)
         self.own[i, 1] = part_of(self.t).astype(BF)
 
+    def core_sum(self, i, which):
+        return self.own[i, which].astype(F32) + self.in1[i, which].astype(F32)
+
     def over(self, i):
         self.core_copy(i).wait()
-        self.out2[i] = (self.own[i, 0].astype(F32) + self.in1[i, 0].astype(F32)).astype(BF)
-        self.far_copy(i).start()
-
-    def _sum(self, i):
+        half, n_c = self.half, self.n_c
+
+        def of_other():
+            far = self.core_sum(i, 0)
+            if self.split:
+                self.out5[i, 0] = far[half:].astype(BF)
+                self.out5[i, 1] = self.core_sum(i, 1)[half:].astype(BF)
+                self.lower_copy(i).start()
+            self.out2[i, :half] = far[:half].astype(BF)
+            self.far_copy(i, True).start()
+
+        def of_own():
+            j = i - n_c
+            if self.split:
+                self.lower_copy(j).wait_recv()
+            far = self.core_sum(i, 0)
+            self.out2[i, :half] = far[:half].astype(BF)
+            if self.split:
+                self.out2[i, half:] = (far[half:] + self.in5[j, 0].astype(F32)).astype(BF)
+            self.far_copy(i).start()
+
+        when(i < n_c, of_other)
+        when(i >= n_c, of_own)
+
+    def after_other(self, i):
+        half = self.half
+        self.far_copy(i, True).wait()
+        self.out3[i] = (self.core_sum(i, 1)[:half] + self.in2[i, :half].astype(F32)).astype(BF)
+        self.other_copy(i).start()
+
+    def after_own(self, i):
+        j, half = i - self.n_c, self.half
         self.far_copy(i).wait()
-        return self.own[i, 1].astype(F32) + self.in1[i, 1].astype(F32) + self.in2[i].astype(F32)
-
-    def after_other(self, i):
-        self.out3[i] = self._sum(i).astype(BF)
-        self.other_copy(i).start()
-
-    def after_own(self, i):
-        self.acc[i - self.n_c] = self._sum(i)
+        total = self.core_sum(i, 1) + self.in2[i].astype(F32)
+        self.acc[j, :half] = total[:half]
+        if self.split:
+            self.acc[j, half:] = total[half:] + self.in5[j, 1].astype(F32)
 
     def along(self, j):
+        half = self.half
+        if self.split:
+            self.lower_copy(j).wait_send()
         self.other_copy(j).wait()
-        total = self.acc[j] + self.in3[j].astype(F32)
+        self.acc[j, :half] = self.acc[j, :half] + self.in3[j].astype(F32)
+        total = self.acc[j]
         if j < self.n_c - 1:
             self.out4[j] = total.astype(BF)
             self.line_copy(j, lax.rem(self.c + j + 1, self.n_c)).start()
@@ -1151,10 +1221,10 @@
     red = Reducer(n_c, scratch)
 
     def blocks_phase(wgu, wd, xs, ns, acts):
-        fetches = fetch_experts(
+        gate_up, down = fetch_experts(
             n_c, n_f, mine, ffe, srows, hp, (wg0, wu0, wd0, wg1, wu1, wd1), shared, wgu, wd, wsem
         )
-        for copy in fetches:
+        for copy in gate_up + down:
             copy.start()
 
         def load(i, slot):
@@ -1172,7 +1242,7 @@
         load(0, 0).start()
         blank_rows(rows_used, hp, wgu, wd)
         greet([{"tp": red.sib}, {"tp": red.far}, {"fsdp": 1 - f}] + line_peers(c, n_c))
-        for copy in fetches:
+        for copy in gate_up:
             copy.wait()
 
         def compute(i, between):
@@ -1214,6 +1284,12 @@
             gt[:, at] = actg.T[:rows_used, :]
             for copy in stores(i, slot):
                 copy.start()
+
+            @pl.when(i == 0)
+            def _():
+                for copy in down:
+                    copy.wait()
+
             red.put(i, lambda q: dot_nn(actg, wd[:, piece(q, quarter)]))
 
         red.loop(n_b, compute)
@@ -1319,7 +1395,7 @@
             DMA((2,)),
             DMA((4, 2)),
         ]
-        + reducer_scratch(n_f, n_c, rows, quarter),
+        + reducer_scratch(n_f, n_c, rows, quarter, True),
         compiler_params=pltpu.CompilerParams(
             collective_id=5, has_side_effects=True, vmem_limit_bytes=BIG
         ),
@@ -1344,7 +1420,8 @@
     routed = mine * ffe
     rows_used = routed + srows
     first = (c * n_f + f) * mine
-    red = Reducer(n_c, rest[:18])
+    reduce_scratch, rest = rest[:N_REDUCER], rest[N_REDUCER:]
+    red = Reducer(n_c, reduce_scratch)
 
     cols = width // n_b
 
@@ -1352,10 +1429,10 @@
         to_each(lambda b: shared_d.at[:, piece(b, cols)], shared_out, n_f, n_c, (ds, dr, dl), act)
 
     def blocks_phase(wgu, wd, ogs, acts):
-        fetches = fetch_experts(
+        gate_up, down = fetch_experts(
             n_c, n_f, mine, ffe, srows, hp, (wg0, wu0, wd0, wg1, wu1, wd1), shared, wgu, wd, wsem
         )
-        for copy in fetches:
+        for copy in down + gate_up:
             copy.start()
 
         def loads(i, slot):
@@ -1375,7 +1452,7 @@
         blank_rows(rows_used, hp, wgu, wd)
         greet([{"tp": red.sib}, {"tp": red.far}, {"tp": opposite(red.sib)}] + each_peers(f, c, n_f, n_c))
         exchange("start")
-        for copy in fetches:
+        for copy in down:
             copy.wait()
 
         def compute(i, between):
@@ -1412,6 +1489,11 @@
             gt[2 * rows_used :, at] = logit_f.T.astype(BF)
             dab = jnp.concatenate([da, db], axis=1)
 
+            @pl.when(i == 0)
+            def _():
+                for copy in gate_up:
+                    copy.wait()
+
             def part_of(q):
                 cols = piece(q, quarter)
                 return dot_nn(dab, wgu[:, cols]) + dot_nn(logit_grad, small[:n_exp, cols])
@@ -1483,17 +1565,17 @@
     shs_copy.start()
     fetch.wait()
     gain = small[2 * n_exp + 1 : 2 * n_exp + 2, piece(t, quarter)].astype(F32)
-    back, gain_part = norm_grad(resid[...], r_own[:, :1], gain, blk[...], width, *rest[18:22])
+    back, gain_part = norm_grad(resid[...], r_own[:, :1], gain, blk[...], width, *rest[:4])
     gain_out[...] = jnp.broadcast_to(gain_part, gain_out.shape)
     grad = og[...].astype(F32) + back
     mid_out[...] = grad
-    own = rest[22]
+    own = rest[4]
     own[...] = grad.astype(BF)
 
     def place(g, cc, tt):
         return seq_out.at[piece(cc, rows), piece(tt, quarter)]
 
-    sequence = Spread(own, place, n_c, False, rest[23:])
+    sequence = Spread(own, place, n_c, False, rest[5:])
     sequence.start()
     sequence.line()
     sequence.far(0)
@@ -1554,7 +1636,7 @@
             DMA((n_b,)),
             DMA(()),
         ]
-        + reducer_scratch(n_f, n_c, rows, quarter)
+        + reducer_scratch(n_f, n_c, rows, quarter, False)
         + norm_grad_scratch(rows)
         + [pltpu.VMEM((rows, quarter), BF)]
         + spread_sems(n_c),
@@ -1705,10 +1787,10 @@
 
 
 def last_kernel(
-    n_c, n_f, n_t, n_exp, own_shared, mid_seq, wo, q, k, v, hf, lse, cosine, sine, normed, wqkv, hidden, r_all,
+    n_c, n_f, n_t, n_exp, own_shared, mid_in, wo, q, k, v, hf, lse, cosine, sine, normed_in, wqkv_in, hidden, r_all,
     small, mid_grad, gain2, shs, lg, lu,
     in_out, gq, gk, gv, go, gains_out, router_out, sg_out, su_out, lg_out, lu_out,
-    dqkv, hg, dq, dk, dv, gattn, shs_in, rpart, hs, hr, hl, es, er, rin, rss, rsr, r_own, mine, inx, own, outz, inz, gsend, gin, rs, sx, rx, lx, sz, rz, gs, gr, *rest,
+    mid_seq, normed, wqkv, big, dqkv, hg, dq, dk, dv, gattn, shs_in, rpart, hs, hr, hl, es, er, rin, rss, rsr, r_own, mine, inx, own, outz, inz, gsend, gin, rs, sx, rx, lx, sz, rz, gs, gr, *rest,
 ):
     f, c, t = ranks()
     rows, quarter = hidden.shape
@@ -1728,6 +1810,12 @@
                             "tp": lax.rem(t + dt, n_t),
                         }
                     )
+    large = [
+        pltpu.make_async_copy(src, dst, big.at[i])
+        for i, (src, dst) in enumerate(((mid_in, mid_seq), (wqkv_in, wqkv), (normed_in, normed)))
+    ]
+    for copy in large:
+        copy.start()
     gin[...] = jnp.zeros_like(gin)
     greet(others)
     order = [2, 1, 3, 0] if n_c == 4 else list(range(1, n_c)) + [0]
@@ -1757,16 +1845,20 @@
     shared("start")
     fetch = pltpu.make_async_copy(r_all.at[piece(c, rows), :], r_own, rs)
     fetch.start()
-    for copy in late:
-        copy.start()
+    late[0].start()
+    large[0].wait()
     attend_back(rows, mid_seq, wo, q, k, v, hf, lse, cosine, sine, dqkv, hg, dq, dk, dv)
     gattn[3 * HD :, :] = dot_tn(hf[...].astype(BF), mid_seq[...]).astype(BF)
 
+    large[1].wait()
+
     def weights():
+        large[2].wait()
         gattn[: 3 * HD, :] = dot_tn(dqkv[...], normed[...]).astype(BF)
         for d in order:
             cross(d).start()
             keep(d).start()
+        late[1].start()
 
 
     def part_of(cc, q):
@@ -1884,9 +1976,13 @@
             sds(lg.shape, BF),
             sds(lu.shape, BF),
         ),
-        in_specs=[VMEM] * 12 + [HBM] + [VMEM] * 3 + [HBM] * 3,
+        in_specs=[HBM] + [VMEM] * 8 + [HBM] * 2 + [VMEM, HBM] + [VMEM] * 3 + [HBM] * 3,
         out_specs=[VMEM] * 9 + [HBM] * 2,
         scratch_shapes=[
+            pltpu.VMEM((seq, width), BF),
+            pltpu.VMEM((seq, width), BF),
+            pltpu.VMEM((width, 3 * HD), BF),
+            DMA((3,)),
             pltpu.VMEM((seq, 3 * HD), BF),
             pltpu.VMEM((seq, HD), BF),
             head_f,

time: 491 us -> 473 us (0.963)
  Pallas kernels: 476 us -> 459 us
    pallas_call x1, Pallas kernels: 201 us -> 191 us  [first(): pl.pallas_call(functools.partial(first_kernel, n_c, n_f, n_exp, mine), ou...]
    pallas_call x1, Pallas kernels: 82.8 us -> 74.5 us  [last(): pl.pallas_call(functools.partial(last_kernel, n_c, n_f, n_t, n_exp, own_s...]
where the time goes in v6:
time: 473 us; the launch traced here: 464 us
  Pallas kernels  459 us (97%)
    pallas_call x1, Pallas kernels, first(): pl.pallas_call(functools.partial(first_kernel, n_c, n_f, n_exp, mine), ou...  191 us
    pallas_call x1, Pallas kernels, backward(): pl.pallas_call(functools.partial(backward_kernel, n_c, n_f, mine, ffe, sr...  113 us
    pallas_call x1, Pallas kernels, last(): pl.pallas_call(functools.partial(last_kernel, n_c, n_f, n_t, n_exp, own_s...  74.5 us
    pallas_call x1, Pallas kernels, forward(): pl.pallas_call(functools.partial(forward_kernel, n_c, n_f, mine, ffe, sro...  67 us
    pallas_call x1, Pallas kernels, finish(): pl.pallas_call(functools.partial(finish_kernel, len(plain)), grid_spec=pl...  12.5 us
  transfers between devices with their start and end apart: 1, of which 0 were waited for; matrix products, arithmetic and copies ran while one was open for 0% of the time, Pallas kernels for 40%

profile of v6, /device:TPU:0, one launch (start us, length us, event | category | flops | bytes accessed | tf_op | source)
XLA Modules:
  0.0 464.3 jit_solution(10198784588021564988)
XLA Ops:
  0.7 0.7 fusion
  1.4 1.3 select_select_fusion.lines
  2.7 191.2 %first.1 = (bf16[1024,2048]{1,0:T(8,128)(2,1)}, bf16[1024,128]{1,0:T(8,128)(2,1)}, bf16[1024,128]{1,0:T(8,128)(2,1)}, bf16[1024,128]{1,0:T(8,128)(2,1)}, f32[102...) custom-call(bf16[256,512]{1,0:T(8,128)(2,1)} %hidden.3, ...), custom_call_target="tpu_custom_call" | custom-call | flops 5368709120 | bytes 314572800 | tf_op jit(solution)/shard_map/first/pallas_call | solution.py:930
  193.9 67.0 %forward.1 = (bf16[256,512]{1,0:T(8,128)(2,1)}, bf16[2048,2048]{1,0:T(8,128)(2,1)}, bf16[2048,896]{1,0:T(8,128)(2,1)}, bf16[2048,896]{1,0:T(8,128)(2,1)}, bf16[2...) custom-call(bf16[2048,2048]{1,0:T(8,128)(2,1)} %get-tuple-element.80, ...), custom_call_target="tpu_custom_call" | custom-call | flops 26843545600 | bytes 83886080 | tf_op jit(solution)/shard_map/forward/pallas_call | solution.py:1373
  260.9 0.2 collective-permute-start
  261.1 113.4 %backward.1 = (f32[256,512]{1,0:T(8,128)}, f32[8,512]{1,0:T(8,128)}, bf16[1024,2048]{1,0:T(8,128)(2,1)}, bf16[8,96,256]{2,1,0:T(8,128)(2,1)}, bf16[208,2048]{1,0...) custom-call(bf16[8,4,256,512]{3,2,1,0:T(8,128)(2,1)} %get-tuple-elem, ...), custom_call_target="tpu_custom_call" | custom-call | flops 33554432000 | bytes 209715200 | tf_op jit(solution)/shard_map/backward/pallas_call | solution.py:1604
  374.5 74.5 %last.1 = (f32[256,512]{1,0:T(8,128)}, f32[256,512]{1,0:T(8,128)}, f32[256,512]{1,0:T(8,128)}, f32[256,512]{1,0:T(8,128)}, f32[512,256]{1,0:T(8,128)}, /*index=5...) custom-call(bf16[1024,2048]{1,0:T(8,128)(2,1)} %get-tuple-element.95, ...), custom_call_target="tpu_custom_call" | custom-call | flops 8589934592 | bytes 157286400 | tf_op jit(solution)/shard_map/last/pallas_call | solution.py:1964
  449.0 1.3 fusion.2
  450.4 0.0 collective-permute-done.refs_4_
  450.4 0.0 copy-start
  450.4 1.1 copy-done
  451.5 12.5 %finish.1 = (f32[4,352,1024]{2,1,0:T(8,128)}, f32[4,352,1024]{2,1,0:T(8,128)}, f32[4,352,1024]{2,1,0:T(8,128)}, f32[704,256]{1,0:T(8,128)}, bf16[256,512]{1,0:T(...) custom-call(s32[1]{0:T(128)} %bitcast.f_ref, ...), custom_call_target="tpu_custom_call" | custom-call | tf_op jit(solution)/shard_map/finish/pallas_call | solution.py:1709
  (2 shorter events, 0.0 us)
Async XLA Ops:
  260.9 189.5 %collective-permute-start = (bf16[2,352,1024]{2,1,0:T(8,128)(2,1)}, bf16[2,352,1024]{2,1,0:T(8,128)(2,1)S(1)}, u32[]{:S(2)}, u32[]{:S(2)}) collective-permute-start(bf16[2,352,1024]{2,1,0:T(8,128)(2,1)} %get-tuple-element.115), channel_id=1, source_target_pairs={{0,16},{16,0},{1,17},{17,1},{2,18},{18,2},{3,19},{19,3},{4,20},{20... | collective-permute-start | bytes 4325384 | tf_op jit(solution)/shard_map/ppermute | solution.py:2088
  450.4 1.1 copy-start

commit v7 on v6

--- a/solution.py
+++ b/solution.py
@@ -831,6 +831,9 @@
     for copy in outs:
         copy.start()
 
+    exchange = lambda act: to_each(lambda b: shared.at[b], shared_out, n_f, n_c, (ss, sr, sl), act)
+    exchange("start")
+
     scale_att = HD ** (-0.5)
     gain = small_all[2 * n_exp : 2 * n_exp + 1, :].astype(F32)
     place_row = 2 * n_exp + 2
@@ -873,15 +876,12 @@
         hb[at, :] = out.astype(BF)
         lse_out[at, :] = jnp.broadcast_to(top + jnp.log(total), (rows, HD))
 
-    exchange = lambda act: to_each(lambda b: shared.at[b], shared_out, n_f, n_c, (ss, sr, sl), act)
-
     def part_of(cc, q):
         return dot_nn(hb[piece(cc, rows), :], wo_all[:, piece(q, quarter)])
 
-    grad.other()
     fetch = pltpu.make_async_copy(hidden, own_og, os.at[3])
     fetch.start()
-    total = reduce_seq(part_of, n_c, scratch[3 * n_s :])
+    total = reduce_seq(part_of, n_c, scratch[3 * n_s :], grad.other)
     fetch.wait()
     resid = own_og[...].astype(F32) + total
     resid_out[...] = resid
@@ -890,7 +890,6 @@
     res.line()
     for copy in swaps[mine + 1 :]:
         copy.start()
-    exchange("start")
     grad.far(0)
     grad.far(1)
     res.other()
@@ -1028,9 +1027,9 @@
     gated = prob * picked
     col = lax.broadcasted_iota(jnp.int32, (block, hp), 1)
     gate = jnp.ones((block, hp), F32)
-    for k in range(mine):
+    for k in reversed(range(mine)):
         g = jnp.sum(jnp.where(lane == first + k, gated, 0.0), axis=1, keepdims=True)
-        gate = jnp.where((col >= k * ffe) & (col < (k + 1) * ffe), g, gate)
+        gate = jnp.where(col < (k + 1) * ffe, g, gate)
     return gate, lane, col
 
 
@@ -1274,7 +1273,7 @@
             ab = dot_nt(n, wgu[...])
             between()
             a, up = ab[:, :hp], ab[:, hp:]
-            sig = 1.0 / (1.0 + jnp.exp(-a))
+            sig = 0.5 * jnp.tanh(0.5 * a) + 0.5
             silu = a * sig
             act = (silu * up).astype(BF)
             acts[slot, 0] = act
@@ -1473,11 +1472,12 @@
             between()
             ad = acts[slot, 0].astype(F32) * dh
             p_grad = jnp.zeros(prob.shape, F32)
-            for k in range(mine):
-                s = jnp.sum(
-                    jnp.where((col >= k * ffe) & (col < (k + 1) * ffe), ad, 0.0), axis=1, keepdims=True
-                )
+            for k in reversed(range(mine)):
+                below = jnp.where(col < k * ffe, ad, 0.0) if k else jnp.zeros_like(ad)
+                ad = jnp.where(col < (k + 1) * ffe, ad, 0.0)
+                s = jnp.sum(ad - below, axis=1, keepdims=True)
                 p_grad = jnp.where(lane == first + k, s, p_grad)
+                ad = below
             p_grad = p_grad * chosen
             logit_f = prob * (p_grad - jnp.sum(prob * p_grad, axis=1, keepdims=True))
             logit_grad = logit_f.astype(BF)
@@ -1655,7 +1655,7 @@
 
 def finish_kernel(n_plain, f_ref, *refs):
     ga, gb, ua, ub, d, kg, ku, kd, shared = refs[:9]
-    plain = refs[9 : 9 + n_plain]
+    plain, gains, refs = refs[9 : 9 + n_plain], refs[9 + n_plain], refs[:9] + refs[10:]
     og, ou, od, shared_out = refs[9 + n_plain : 13 + n_plain]
     step = pl.program_id(0)
     f = f_ref[0]
@@ -1688,9 +1688,11 @@
         shared_out[b * own : (b + 1) * own, :] = shared[b, :own, :].astype(F32)
     for src, dst in zip(plain, refs[13 + n_plain :]):
         dst[...] = src[...]
-
-
-def finish(f_rank, own_shared, arrived, kept, shared, plain):
+    for i, dst in enumerate(refs[13 + 2 * n_plain :]):
+        dst[...] = gains[i : i + 1, :]
+
+
+def finish(f_rank, own_shared, arrived, kept, shared, plain, gains):
     mine, ffe, quarter = arrived[0].shape
     half = kept[0].shape[2]
     tile = half // 4
@@ -1714,15 +1716,20 @@
             in_specs=[first, second, first, second, every]
             + [every] * 3
             + [pl.BlockSpec((n_b // 4, srows, part), lambda i, f: (i, 0, 0))]
-            + [rows_of(x) for x in plain],
-            out_specs=[out] * 3 + [rows_of(shared_grad)] + [rows_of(x) for x in plain],
+            + [rows_of(x) for x in plain]
+            + [rows_of(gains)],
+            out_specs=[out] * 3
+            + [rows_of(shared_grad)]
+            + [rows_of(x) for x in plain]
+            + [pl.BlockSpec((1, part), lambda i, f: (0, 0))] * 2,
         ),
         out_shape=tuple(jax.ShapeDtypeStruct((2 * mine, ffe, half), F32) for k in kept)
         + (shared_grad,)
-        + tuple(jax.ShapeDtypeStruct(x.shape, x.dtype) for x in plain),
+        + tuple(jax.ShapeDtypeStruct(x.shape, x.dtype) for x in plain)
+        + (jax.ShapeDtypeStruct((1, part), F32),) * 2,
         compiler_params=pltpu.CompilerParams(vmem_limit_bytes=BIG),
         name="finish",
-    )(f_rank, *arrived, *kept, shared, *plain)
+    )(f_rank, *arrived, *kept, shared, *plain, gains)
 
 
 def norm_grad(values, r, gain, grad, width, out, into, send, recv):
@@ -2095,19 +2102,19 @@
         hidden_in, r_one, small, mid_grad, gain_two_part, shs, lg, lu,
     )
     plain = (layer_out, input_grad, gq, gk, gv, go, router_grad, shared_g, shared_u)
-    eg, eu, ed, shared_d, layer_out, input_grad, gq, gk, gv, go, router_grad, shared_g, shared_u = finish(
-        f_arr, own_shared, (gg, lg, gu, lu, arrived_d), (kg, ku, kd), shared_back, plain
-    )
+    (
+        eg, eu, ed, shared_d, layer_out, input_grad, gq, gk, gv, go, router_grad, shared_g, shared_u, gain_1, gain_2,
+    ) = finish(f_arr, own_shared, (gg, lg, gu, lu, arrived_d), (kg, ku, kd), shared_back, plain, gains)
 
     return (
         layer_out,
         input_grad,
-        gains[0],
+        gain_1[0],
         gq,
         gk,
         gv,
         go,
-        gains[1],
+        gain_2[0],
         router_grad.T,
         shared_g.T,
         shared_u.T,

time: 473 us -> 467 us (0.987)
  transfers between devices with their start and end apart: 1 -> 1, of which waited for: 0 -> 0; matrix products, arithmetic and copies ran while one was open for 0% -> 0% of each run, Pallas kernels for 40% -> 41%
where the time goes in v7:
time: 467 us; the launch traced here: 460 us
  Pallas kernels  455 us (97%)
    pallas_call x1, Pallas kernels, first(): pl.pallas_call(functools.partial(first_kernel, n_c, n_f, n_exp, mine), ou...  189 us
    pallas_call x1, Pallas kernels, backward(): pl.pallas_call(functools.partial(backward_kernel, n_c, n_f, mine, ffe, sr...  113 us
    pallas_call x1, Pallas kernels, last(): pl.pallas_call(functools.partial(last_kernel, n_c, n_f, n_t, n_exp, own_s...  74.5 us
    pallas_call x1, Pallas kernels, forward(): pl.pallas_call(functools.partial(forward_kernel, n_c, n_f, mine, ffe, sro...  66.1 us
    pallas_call x1, Pallas kernels, finish(): pl.pallas_call(functools.partial(finish_kernel, len(plain)), grid_spec=pl...  12.6 us
  transfers between devices with their start and end apart: 1, of which 0 were waited for; matrix products, arithmetic and copies ran while one was open for 0% of the time, Pallas kernels for 41%

profile of v7, /device:TPU:0, one launch (start us, length us, event | category | flops | bytes accessed | tf_op | source)
XLA Modules:
  0.0 459.6 jit_solution(3166795072265888290)
XLA Ops:
  0.7 0.7 fusion
  1.4 1.3 select_select_fusion.lines
  2.7 188.5 %first.1 = (bf16[1024,2048]{1,0:T(8,128)(2,1)}, bf16[1024,128]{1,0:T(8,128)(2,1)}, bf16[1024,128]{1,0:T(8,128)(2,1)}, bf16[1024,128]{1,0:T(8,128)(2,1)}, f32[102...) custom-call(bf16[256,512]{1,0:T(8,128)(2,1)} %hidden.3, ...), custom_call_target="tpu_custom_call" | custom-call | flops 5368709120 | bytes 314572800 | tf_op jit(solution)/shard_map/first/pallas_call | solution.py:929
  191.2 66.1 %forward.1 = (bf16[256,512]{1,0:T(8,128)(2,1)}, bf16[2048,2048]{1,0:T(8,128)(2,1)}, bf16[2048,896]{1,0:T(8,128)(2,1)}, bf16[2048,896]{1,0:T(8,128)(2,1)}, bf16[2...) custom-call(bf16[2048,2048]{1,0:T(8,128)(2,1)} %get-tuple-element.82, ...), custom_call_target="tpu_custom_call" | custom-call | flops 26843545600 | bytes 83886080 | tf_op jit(solution)/shard_map/forward/pallas_call | solution.py:1372
  257.3 0.6 collective-permute-start
  257.9 113.3 %backward.1 = (f32[256,512]{1,0:T(8,128)}, f32[8,512]{1,0:T(8,128)}, bf16[1024,2048]{1,0:T(8,128)(2,1)}, bf16[8,96,256]{2,1,0:T(8,128)(2,1)}, bf16[208,2048]{1,0...) custom-call(bf16[8,4,256,512]{3,2,1,0:T(8,128)(2,1)} %get-tuple-elem, ...), custom_call_target="tpu_custom_call" | custom-call | flops 33554432000 | bytes 209715200 | tf_op jit(solution)/shard_map/backward/pallas_call | solution.py:1604
  371.2 74.5 %last.1 = (f32[256,512]{1,0:T(8,128)}, f32[256,512]{1,0:T(8,128)}, f32[256,512]{1,0:T(8,128)}, f32[256,512]{1,0:T(8,128)}, f32[512,256]{1,0:T(8,128)}, /*index=5...) custom-call(bf16[1024,2048]{1,0:T(8,128)(2,1)} %get-tuple-element.97, ...), custom_call_target="tpu_custom_call" | custom-call | flops 8589934592 | bytes 157286400 | tf_op jit(solution)/shard_map/last/pallas_call | solution.py:1971
  445.7 0.0 collective-permute-done.refs_4_
  445.7 0.0 copy-start
  445.7 1.1 copy-done
  446.8 12.6 %finish.1 = (f32[4,352,1024]{2,1,0:T(8,128)}, f32[4,352,1024]{2,1,0:T(8,128)}, f32[4,352,1024]{2,1,0:T(8,128)}, f32[704,256]{1,0:T(8,128)}, bf16[256,512]{1,0:T(...) custom-call(s32[1]{0:T(128)} %bitcast.f_ref, ...), custom_call_target="tpu_custom_call" | custom-call | tf_op jit(solution)/shard_map/finish/pallas_call | solution.py:1711
  (2 shorter events, 0.0 us)
Async XLA Ops:
  257.3 188.4 %collective-permute-start = (bf16[2,352,1024]{2,1,0:T(8,128)(2,1)}, bf16[2,352,1024]{2,1,0:T(8,128)(2,1)S(1)}, u32[]{:S(2)}, u32[]{:S(2)}) collective-permute-start(bf16[2,352,1024]{2,1,0:T(8,128)(2,1)} %get-tuple-element.117), channel_id=1, source_target_pairs={{0,16},{16,0},{1,17},{17,1},{2,18},{18,2},{3,19},{19,3},{4,20},{20... | collective-permute-start | bytes 4325384 | tf_op jit(solution)/shard_map/ppermute | solution.py:2095
  445.7 1.1 copy-start

commit v8 on v7

--- a/solution.py
+++ b/solution.py
@@ -1167,8 +1167,9 @@
             total = total + self.in4[j].astype(F32)
         return total
 
-    def loop(self, n_b, compute):
+    def loop(self, n_b, lag, compute):
         n_c = self.n_c
+        assert lag >= n_b - n_c
 
         def step(i, carry):
             def between():
@@ -1176,27 +1177,24 @@
                 def _():
                     self.over(i - 1)
 
-                @pl.when((i >= 3) & (i < 3 + n_c))
+                @pl.when((i >= lag) & (i < lag + n_c))
                 def _():
-                    self.after_other(i - 3)
-
-                @pl.when(i >= 3 + n_c)
-                def _():
-                    self.after_own(i - 3)
+                    self.after_other(i - lag)
 
             compute(i, between)
             return carry
 
         lax.fori_loop(0, n_b, step, 0)
 
-    def drain(self, n_b, works):
+    def drain(self, n_b, lag, works):
         works = list(works)
         self.over(n_b - 1)
-        for i in range(n_b - 4, n_b):
-            if i > n_b - 4:
-                self.after_own(i) if i >= self.n_c else self.after_other(i)
-            if i >= self.n_c:
-                total = self.along(i - self.n_c)
+        for i in range(n_b - lag, n_b):
+            if i < self.n_c:
+                self.after_other(i)
+                continue
+            self.after_own(i)
+            total = self.along(i - self.n_c)
             if works:
                 works.pop(0)()
         for work in works:
@@ -1291,7 +1289,7 @@
 
             red.put(i, lambda q: dot_nn(actg, wd[:, piece(q, quarter)]))
 
-        red.loop(n_b, compute)
+        red.loop(n_b, n_c, compute)
         for i in range(n_b - 2, n_b):
             for copy in stores(i, i % 2):
                 copy.wait()
@@ -1342,7 +1340,7 @@
             return run
 
         tile_load(0).start()
-        total = red.drain(n_b, [work(s) for s in range(4)])
+        total = red.drain(n_b, n_c, [work(s) for s in range(4)])
         layer_out[...] = (resid[...] + total).astype(BF)
         for s in range(4):
             for copy in out_copies(s):
@@ -1500,7 +1498,7 @@
 
             red.put(i, part_of)
 
-        red.loop(n_b, compute)
+        red.loop(n_b, n_c + 1, compute)
 
     pl.run_scoped(
         blocks_phase,
@@ -1549,7 +1547,7 @@
             return run
 
         tile_load(0).start()
-        blk[...] = red.drain(n_b, [work(s) for s in range(4)])
+        blk[...] = red.drain(n_b, n_c + 1, [work(s) for s in range(4)])
         for s in (2, 3):
             for m in range(2):
                 keep_copy(s, m).wait()

time: 467 us -> 464 us (level)
  transfers between devices with their start and end apart: 1 -> 1, of which waited for: 0 -> 0; matrix products, arithmetic and copies ran while one was open for 0% -> 0% of each run, Pallas kernels for 41% -> 40%
where the time goes in v8:
time: 464 us; the launch traced here: 456 us
  Pallas kernels  452 us (97%)
    pallas_call x1, Pallas kernels, first(): pl.pallas_call(functools.partial(first_kernel, n_c, n_f, n_exp, mine), ou...  189 us
    pallas_call x1, Pallas kernels, backward(): pl.pallas_call(functools.partial(backward_kernel, n_c, n_f, mine, ffe, sr...  110 us
    pallas_call x1, Pallas kernels, last(): pl.pallas_call(functools.partial(last_kernel, n_c, n_f, n_t, n_exp, own_s...  74.8 us
    pallas_call x1, Pallas kernels, forward(): pl.pallas_call(functools.partial(forward_kernel, n_c, n_f, mine, ffe, sro...  66 us
    pallas_call x1, Pallas kernels, finish(): pl.pallas_call(functools.partial(finish_kernel, len(plain)), grid_spec=pl...  12.6 us
  transfers between devices with their start and end apart: 1, of which 0 were waited for; matrix products, arithmetic and copies ran while one was open for 0% of the time, Pallas kernels for 40%

profile of v8, /device:TPU:0, one launch (start us, length us, event | category | flops | bytes accessed | tf_op | source)
XLA Modules:
  0.0 456.5 jit_solution(9576779098462230509)
XLA Ops:
  0.7 0.7 fusion
  1.4 1.3 select_select_fusion.lines
  2.7 188.5 %first.1 = (bf16[1024,2048]{1,0:T(8,128)(2,1)}, bf16[1024,128]{1,0:T(8,128)(2,1)}, bf16[1024,128]{1,0:T(8,128)(2,1)}, bf16[1024,128]{1,0:T(8,128)(2,1)}, f32[102...) custom-call(bf16[256,512]{1,0:T(8,128)(2,1)} %hidden.3, ...), custom_call_target="tpu_custom_call" | custom-call | flops 5368709120 | bytes 314572800 | tf_op jit(solution)/shard_map/first/pallas_call | solution.py:929
  191.2 66.0 %forward.1 = (bf16[256,512]{1,0:T(8,128)(2,1)}, bf16[2048,2048]{1,0:T(8,128)(2,1)}, bf16[2048,896]{1,0:T(8,128)(2,1)}, bf16[2048,896]{1,0:T(8,128)(2,1)}, bf16[2...) custom-call(bf16[2048,2048]{1,0:T(8,128)(2,1)} %get-tuple-element.82, ...), custom_call_target="tpu_custom_call" | custom-call | flops 26843545600 | bytes 83886080 | tf_op jit(solution)/shard_map/forward/pallas_call | solution.py:1370
  257.3 0.6 collective-permute-start
  257.9 109.9 %backward.1 = (f32[256,512]{1,0:T(8,128)}, f32[8,512]{1,0:T(8,128)}, bf16[1024,2048]{1,0:T(8,128)(2,1)}, bf16[8,96,256]{2,1,0:T(8,128)(2,1)}, bf16[208,2048]{1,0...) custom-call(bf16[8,4,256,512]{3,2,1,0:T(8,128)(2,1)} %get-tuple-elem, ...), custom_call_target="tpu_custom_call" | custom-call | flops 33554432000 | bytes 209715200 | tf_op jit(solution)/shard_map/backward/pallas_call | solution.py:1602
  367.7 74.8 %last.1 = (f32[256,512]{1,0:T(8,128)}, f32[256,512]{1,0:T(8,128)}, f32[256,512]{1,0:T(8,128)}, f32[256,512]{1,0:T(8,128)}, f32[512,256]{1,0:T(8,128)}, /*index=5...) custom-call(bf16[1024,2048]{1,0:T(8,128)(2,1)} %get-tuple-element.97, ...), custom_call_target="tpu_custom_call" | custom-call | flops 8589934592 | bytes 157286400 | tf_op jit(solution)/shard_map/last/pallas_call | solution.py:1969
  442.5 0.0 collective-permute-done.refs_4_
  442.6 0.0 copy-start
  442.6 1.1 copy-done
  443.7 12.6 %finish.1 = (f32[4,352,1024]{2,1,0:T(8,128)}, f32[4,352,1024]{2,1,0:T(8,128)}, f32[4,352,1024]{2,1,0:T(8,128)}, f32[704,256]{1,0:T(8,128)}, bf16[256,512]{1,0:T(...) custom-call(s32[1]{0:T(128)} %bitcast.f_ref, ...), custom_call_target="tpu_custom_call" | custom-call | tf_op jit(solution)/shard_map/finish/pallas_call | solution.py:1709
  (2 shorter events, 0.0 us)
Async XLA Ops:
  257.3 185.3 %collective-permute-start = (bf16[2,352,1024]{2,1,0:T(8,128)(2,1)}, bf16[2,352,1024]{2,1,0:T(8,128)(2,1)S(1)}, u32[]{:S(2)}, u32[]{:S(2)}) collective-permute-start(bf16[2,352,1024]{2,1,0:T(8,128)(2,1)} %get-tuple-element.117), channel_id=1, source_target_pairs={{0,16},{16,0},{1,17},{17,1},{2,18},{18,2},{3,19},{19,3},{4,20},{20... | collective-permute-start | bytes 4325384 | tf_op jit(solution)/shard_map/ppermute | solution.py:2093
  442.6 1.1 copy-start

commit v9 on v8

--- a/solution.py
+++ b/solution.py
@@ -8,6 +8,7 @@
 from jax.experimental.pallas import tpu as pltpu
 from jax.sharding import PartitionSpec as P
 
+FSDP, CTX, TP = "fsdp", "ctx", "tp"
 HD = 128
 TOPK = 6
 
@@ -21,27 +22,27 @@
 
 
 def features(local_part):
-    return lax.all_gather(local_part, "tp", axis=1, tiled=True)
+    return lax.all_gather(local_part, TP, axis=1, tiled=True)
 
 
 def row_stats(partial_terms):
-    return lax.psum(partial_terms, "tp")
+    return lax.psum(partial_terms, TP)
 
 
 def partial_sums(partial_terms):
     return jax.tree.map(
         lambda part: part.astype(jnp.float32),
-        lax.psum_scatter(as_sent(partial_terms), "tp", scatter_dimension=1, tiled=True),
+        lax.psum_scatter(as_sent(partial_terms), TP, scatter_dimension=1, tiled=True),
     )
 
 
 def to_owners(slot_rows):
-    return lax.all_to_all(slot_rows, "ctx", split_axis=0, concat_axis=2, tiled=True)
+    return lax.all_to_all(slot_rows, CTX, split_axis=0, concat_axis=2, tiled=True)
 
 
 def to_sources(slot_rows):
     return lax.all_to_all(
-        slot_rows.astype(jnp.bfloat16), "ctx", split_axis=2, concat_axis=0, tiled=True
+        slot_rows.astype(jnp.bfloat16), CTX, split_axis=2, concat_axis=0, tiled=True
     ).astype(slot_rows.dtype)
 
 
@@ -113,27 +114,27 @@
     expert_up,
     expert_down,
 ):
-    tp_rank = lax.axis_index("tp")
-    ctx_rank = lax.axis_index("ctx")
-    n_ctx = lax.axis_size("ctx")
+    tp_rank = lax.axis_index(TP)
+    ctx_rank = lax.axis_index(CTX)
+    n_ctx = lax.axis_size(CTX)
     tok_rows, quarter = hidden_in.shape
-    model_width = quarter * lax.axis_size("tp")
+    model_width = quarter * lax.axis_size(TP)
     gain_one, wq_all, wk_all, wv_all, gain_two, router_all, gate_all, up_all, wo_all, down_all = (
-        lax.all_gather(attn_gain, ("fsdp", "ctx"), axis=0, tiled=True),
-        lax.all_gather(w_query, ("fsdp", "ctx"), axis=0, tiled=True),
-        lax.all_gather(w_key, ("fsdp", "ctx"), axis=0, tiled=True),
-        lax.all_gather(w_value, ("fsdp", "ctx"), axis=0, tiled=True),
-        lax.all_gather(moe_gain, ("fsdp", "ctx"), axis=0, tiled=True),
-        lax.all_gather(router, ("fsdp", "ctx"), axis=0, tiled=True),
-        lax.all_gather(shared_gate, ("fsdp", "ctx"), axis=0, tiled=True),
-        lax.all_gather(shared_up, ("fsdp", "ctx"), axis=0, tiled=True),
-        lax.all_gather(w_out, ("fsdp", "ctx"), axis=1, tiled=True),
-        lax.all_gather(shared_down, ("fsdp", "ctx"), axis=1, tiled=True),
+        lax.all_gather(attn_gain, (FSDP, CTX), axis=0, tiled=True),
+        lax.all_gather(w_query, (FSDP, CTX), axis=0, tiled=True),
+        lax.all_gather(w_key, (FSDP, CTX), axis=0, tiled=True),
+        lax.all_gather(w_value, (FSDP, CTX), axis=0, tiled=True),
+        lax.all_gather(moe_gain, (FSDP, CTX), axis=0, tiled=True),
+        lax.all_gather(router, (FSDP, CTX), axis=0, tiled=True),
+        lax.all_gather(shared_gate, (FSDP, CTX), axis=0, tiled=True),
+        lax.all_gather(shared_up, (FSDP, CTX), axis=0, tiled=True),
+        lax.all_gather(w_out, (FSDP, CTX), axis=1, tiled=True),
+        lax.all_gather(shared_down, (FSDP, CTX), axis=1, tiled=True),
     )
     expert_gate_weights, expert_up_weights, expert_down_weights = (
-        lax.all_gather(expert_gate, "fsdp", axis=1, tiled=True),
-        lax.all_gather(expert_up, "fsdp", axis=1, tiled=True),
-        lax.all_gather(expert_down, "fsdp", axis=2, tiled=True),
+        lax.all_gather(expert_gate, FSDP, axis=1, tiled=True),
+        lax.all_gather(expert_up, FSDP, axis=1, tiled=True),
+        lax.all_gather(expert_down, FSDP, axis=2, tiled=True),
     )
     gain_q1 = lax.dynamic_slice_in_dim(gain_one, tp_rank * quarter, quarter).astype(jnp.float32)
     gain_q2 = lax.dynamic_slice_in_dim(gain_two, tp_rank * quarter, quarter).astype(jnp.float32)
@@ -163,8 +164,8 @@
         jnp.zeros((tok_rows, head_count), jnp.float32),
         jnp.zeros((tok_rows, head_count, HD), jnp.float32),
     )
-    keys_blk = lax.all_gather(key_b, "ctx", axis=0, tiled=True)
-    vals_blk = lax.all_gather(value_b, "ctx", axis=0, tiled=True)
+    keys_blk = lax.all_gather(key_b, CTX, axis=0, tiled=True)
+    vals_blk = lax.all_gather(value_b, CTX, axis=0, tiled=True)
     key_count = keys_blk.shape[0]
 
     def compute(state_in):
@@ -310,8 +311,8 @@
         jnp.zeros((seq_len, head_count, HD), jnp.float32),
         jnp.zeros((seq_len, head_count, HD), jnp.float32),
     )
-    attend_keys_blk = lax.all_gather(key_b, "ctx", axis=0, tiled=True)
-    attend_vals_blk = lax.all_gather(value_b, "ctx", axis=0, tiled=True)
+    attend_keys_blk = lax.all_gather(key_b, CTX, axis=0, tiled=True)
+    attend_vals_blk = lax.all_gather(value_b, CTX, axis=0, tiled=True)
     attend_key_count = attend_keys_blk.shape[0]
 
     def compute(state_in):
@@ -348,10 +349,10 @@
     )
     key_grad, value_grad = (
         lax.psum_scatter(
-            key_grad_all.astype(jnp.bfloat16), "ctx", scatter_dimension=0, tiled=True
+            key_grad_all.astype(jnp.bfloat16), CTX, scatter_dimension=0, tiled=True
         ).astype(jnp.float32),
         lax.psum_scatter(
-            value_grad_all.astype(jnp.bfloat16), "ctx", scatter_dimension=0, tiled=True
+            value_grad_all.astype(jnp.bfloat16), CTX, scatter_dimension=0, tiled=True
         ).astype(jnp.float32),
     )
     query_pre_grad = (
@@ -377,45 +378,45 @@
     input_grad = mid_grad + first_back
     dense = (
         lax.psum_scatter(
-            gain_one_grad.astype(jnp.bfloat16), ("fsdp", "ctx"), scatter_dimension=0, tiled=True
+            gain_one_grad.astype(jnp.bfloat16), (FSDP, CTX), scatter_dimension=0, tiled=True
         ).astype(jnp.float32),
         lax.psum_scatter(
-            wq_grad.astype(jnp.bfloat16), ("fsdp", "ctx"), scatter_dimension=0, tiled=True
+            wq_grad.astype(jnp.bfloat16), (FSDP, CTX), scatter_dimension=0, tiled=True
         ).astype(jnp.float32),
         lax.psum_scatter(
-            wk_grad.astype(jnp.bfloat16), ("fsdp", "ctx"), scatter_dimension=0, tiled=True
+            wk_grad.astype(jnp.bfloat16), (FSDP, CTX), scatter_dimension=0, tiled=True
         ).astype(jnp.float32),
         lax.psum_scatter(
-            wv_grad.astype(jnp.bfloat16), ("fsdp", "ctx"), scatter_dimension=0, tiled=True
+            wv_grad.astype(jnp.bfloat16), (FSDP, CTX), scatter_dimension=0, tiled=True
         ).astype(jnp.float32),
         lax.psum_scatter(
-            gain_two_grad.astype(jnp.bfloat16), ("fsdp", "ctx"), scatter_dimension=0, tiled=True
+            gain_two_grad.astype(jnp.bfloat16), (FSDP, CTX), scatter_dimension=0, tiled=True
         ).astype(jnp.float32),
         lax.psum_scatter(
-            router_grad.astype(jnp.bfloat16), ("fsdp", "ctx"), scatter_dimension=0, tiled=True
+            router_grad.astype(jnp.bfloat16), (FSDP, CTX), scatter_dimension=0, tiled=True
         ).astype(jnp.float32),
         lax.psum_scatter(
-            shared_gate_grad.astype(jnp.bfloat16), ("fsdp", "ctx"), scatter_dimension=0, tiled=True
+            shared_gate_grad.astype(jnp.bfloat16), (FSDP, CTX), scatter_dimension=0, tiled=True
         ).astype(jnp.float32),
         lax.psum_scatter(
-            shared_up_grad.astype(jnp.bfloat16), ("fsdp", "ctx"), scatter_dimension=0, tiled=True
+            shared_up_grad.astype(jnp.bfloat16), (FSDP, CTX), scatter_dimension=0, tiled=True
         ).astype(jnp.float32),
         lax.psum_scatter(
-            wo_grad.astype(jnp.bfloat16), ("fsdp", "ctx"), scatter_dimension=1, tiled=True
+            wo_grad.astype(jnp.bfloat16), (FSDP, CTX), scatter_dimension=1, tiled=True
         ).astype(jnp.float32),
         lax.psum_scatter(
-            shared_down_grad.astype(jnp.bfloat16), ("fsdp", "ctx"), scatter_dimension=1, tiled=True
+            shared_down_grad.astype(jnp.bfloat16), (FSDP, CTX), scatter_dimension=1, tiled=True
         ).astype(jnp.float32),
     )
     experts_done = (
         lax.psum_scatter(
-            egate_grad.astype(jnp.bfloat16), "fsdp", scatter_dimension=1, tiled=True
+            egate_grad.astype(jnp.bfloat16), FSDP, scatter_dimension=1, tiled=True
         ).astype(jnp.float32),
         lax.psum_scatter(
-            expert_up_weight_grad.astype(jnp.bfloat16), "fsdp", scatter_dimension=1, tiled=True
+            expert_up_weight_grad.astype(jnp.bfloat16), FSDP, scatter_dimension=1, tiled=True
         ).astype(jnp.float32),
         lax.psum_scatter(
-            edown_grad.astype(jnp.bfloat16), "fsdp", scatter_dimension=2, tiled=True
+            edown_grad.astype(jnp.bfloat16), FSDP, scatter_dimension=2, tiled=True
         ).astype(jnp.float32),
     )
     return (
@@ -458,7 +459,7 @@
 
 
 def ranks():
-    return lax.axis_index("fsdp"), lax.axis_index("ctx"), lax.axis_index("tp")
+    return lax.axis_index(FSDP), lax.axis_index(CTX), lax.axis_index(TP)
 
 
 def sibling(t):
@@ -483,7 +484,7 @@
 
 
 def line_peers(c, n_c):
-    return [{"ctx": lax.rem(c + step, n_c)} for step in range(1, n_c)]
+    return [{CTX: lax.rem(c + step, n_c)} for step in range(1, n_c)]
 
 
 def piece(index, size):
@@ -527,17 +528,17 @@
         return pltpu.make_async_copy(self.own, self.place(self.f, self.c, self.t), self.ls)
 
     def far_copy(self, src, i, g, cc, col):
-        return remote(src, self.place(g, cc, col), self.ys.at[i], self.yr.at[i], {"tp": self.other_t})
+        return remote(src, self.place(g, cc, col), self.ys.at[i], self.yr.at[i], {TP: self.other_t})
 
     def sib_copy(self, src, i, which, g, cc, col):
         at = 2 * i + which
-        return remote(src, self.place(g, cc, col), self.ks.at[at], self.kr.at[at], {"tp": sibling(self.t)})
+        return remote(src, self.place(g, cc, col), self.ks.at[at], self.kr.at[at], {TP: sibling(self.t)})
 
     def other_copy(self, src, g, cc):
-        return remote(src, self.place(g, cc, self.t), self.xs.at[cc], self.xr.at[cc], {"fsdp": 1 - self.f})
+        return remote(src, self.place(g, cc, self.t), self.xs.at[cc], self.xr.at[cc], {FSDP: 1 - self.f})
 
     def line_copy(self, src, cc, sem, to):
-        return remote(src, self.place(self.f, cc, self.t), self.zs.at[sem], self.zr.at[cc], {"ctx": to})
+        return remote(src, self.place(self.f, cc, self.t), self.zs.at[sem], self.zr.at[cc], {CTX: to})
 
     def pass_on(self, src, i, g, cc):
         self.far_copy(src, i, g, cc, self.t).start()
@@ -653,14 +654,14 @@
                 continue
             to_f, to_c = lax.rem(f + df, n_f), lax.rem(c + dc, n_c)
             copy = remote(
-                src_of(to_f * n_c + to_c), dst.at[here], send.at[i], recv.at[i], {"fsdp": to_f, "ctx": to_c}
+                src_of(to_f * n_c + to_c), dst.at[here], send.at[i], recv.at[i], {FSDP: to_f, CTX: to_c}
             )
             copy.start() if act == "start" else copy.wait()
 
 
 def each_peers(f, c, n_f, n_c):
     return [
-        {"fsdp": lax.rem(f + df, n_f), "ctx": lax.rem(c + dc, n_c)}
+        {FSDP: lax.rem(f + df, n_f), CTX: lax.rem(c + dc, n_c)}
         for df in range(n_f)
         for dc in range(n_c)
         if df or dc
@@ -689,7 +690,7 @@
     out1, in1, own, out2, in2, out3, in3, s1, r1, s2, r2, s3, r3 = scratch
     f, c, t = ranks()
     far, sib = opposite(t), sibling(t)
-    to_sib, to_far = {"tp": sib}, {"tp": far}
+    to_sib, to_far = {TP: sib}, {TP: far}
     order = [2, 1, 3, 0] if n_c == 4 else list(range(1, n_c)) + [0]
     for d in order:
         cc = lax.rem(c + d, n_c)
@@ -710,11 +711,11 @@
         if d:
             out3[d] = total.astype(BF)
             cc = lax.rem(c + d, n_c)
-            remote(out3.at[d], in3.at[d], s3.at[d], r3.at[d], {"ctx": cc}).start()
+            remote(out3.at[d], in3.at[d], s3.at[d], r3.at[d], {CTX: cc}).start()
     if before_last is not None:
         before_last()
     for d in order[:-1]:
-        remote(out3.at[d], in3.at[d], s3.at[d], r3.at[d], {"ctx": c}).wait()
+        remote(out3.at[d], in3.at[d], s3.at[d], r3.at[d], {CTX: c}).wait()
         total = total + in3[d].astype(F32)
     return total
 
@@ -745,7 +746,7 @@
             shared[b, i * srows : i * srows + own_rows, :] = src[b * own_rows : (b + 1) * own_rows, :]
             if srows > own_rows:
                 shared[b, i * srows + own_rows : (i + 1) * srows, :] = jnp.zeros((srows - own_rows, part), BF)
-    greet([{"tp": sibling(t)}, {"tp": opposite(t)}] + each_peers(f, c, n_f, n_c))
+    greet([{TP: sibling(t)}, {TP: opposite(t)}] + each_peers(f, c, n_f, n_c))
     seq_place = lambda g, cc, tt: seq.at[piece(cc, rows), piece(tt, quarter)]
     og_place = lambda g, cc, tt: og_out.at[g * n_c + cc, tt]
     all_place = lambda g, cc, tt: all_out.at[piece(g * n_c + cc, rows), piece(tt, quarter)]
@@ -770,13 +771,13 @@
 
     def across(step, g, cc):
         return [
-            remote(slab, slab, xs.at[step, i], xr.at[step, i], {"fsdp": 1 - f})
+            remote(slab, slab, xs.at[step, i], xr.at[step, i], {FSDP: 1 - f})
             for i, slab in enumerate(slabs(g, cc))
         ]
 
     def swap(weight, out, k):
         return [
-            remote(weight.at[(1 - f) * mine + e], out.at[e], es.at[k, e], er.at[k, e], {"fsdp": 1 - f})
+            remote(weight.at[(1 - f) * mine + e], out.at[e], es.at[k, e], er.at[k, e], {FSDP: 1 - f})
             for e in range(mine)
         ]
 
@@ -787,12 +788,12 @@
     def weights_out(step):
         to = lax.rem(c + step, n_c)
         for i, (src, dst) in enumerate(zip(sources(to), targets(f, c))):
-            remote(src, dst, ws.at[step, i], wr.at[step, i], {"ctx": to}).start()
+            remote(src, dst, ws.at[step, i], wr.at[step, i], {CTX: to}).start()
 
     def weights_on(step):
         cc = lax.rem(c - step + n_c, n_c)
         for i, dst in enumerate(targets(f, cc)):
-            remote(dst, dst, ws.at[step, i], wr.at[step, i], {"ctx": cc}).wait_recv()
+            remote(dst, dst, ws.at[step, i], wr.at[step, i], {CTX: cc}).wait_recv()
         for copy in across(step, f, cc):
             copy.start()
 
@@ -903,7 +904,7 @@
         copy.wait()
     for step in range(1, n_c):
         for i, (src, dst) in enumerate(zip(sources(c), targets(f, c))):
-            remote(src, dst, ws.at[step, i], wr.at[step, i], {"ctx": c}).wait_send()
+            remote(src, dst, ws.at[step, i], wr.at[step, i], {CTX: c}).wait_send()
     for step in range(n_c):
         for copy in across(step, f, lax.rem(c - step + n_c, n_c)):
             copy.wait_send()
@@ -987,7 +988,7 @@
 
 
 def fetch_experts(n_c, n_f, mine, ffe, srows, hp, weights, shared, wgu, wd, sems):
-    f = lax.axis_index("fsdp")
+    f = lax.axis_index(FSDP)
     wg0, wu0, wd0, wg1, wu1, wd1 = weights
     width = wd.shape[1]
     used = mine * ffe
@@ -1082,22 +1083,22 @@
         return group * n_c + lax.rem(self.c + lax.rem(i, n_c) + 1, n_c)
 
     def core_copy(self, i):
-        return remote(self.out1.at[i], self.in1.at[i], self.s1.at[i], self.r1.at[i], {"tp": self.sib})
+        return remote(self.out1.at[i], self.in1.at[i], self.s1.at[i], self.r1.at[i], {TP: self.sib})
 
     def far_copy(self, i, upper=False):
         src, dst = self.out2.at[i], self.in2.at[i]
         if upper:
             src, dst = src.at[pl.ds(0, self.half)], dst.at[pl.ds(0, self.half)]
-        return remote(src, dst, self.s2.at[i], self.r2.at[i], {"tp": self.far})
+        return remote(src, dst, self.s2.at[i], self.r2.at[i], {TP: self.far})
 
     def other_copy(self, j):
-        return remote(self.out3.at[j], self.in3.at[j], self.s3.at[j], self.r3.at[j], {"fsdp": 1 - self.f})
+        return remote(self.out3.at[j], self.in3.at[j], self.s3.at[j], self.r3.at[j], {FSDP: 1 - self.f})
 
     def lower_copy(self, j):
-        return remote(self.out5.at[j], self.in5.at[j], self.s5.at[j], self.r5.at[j], {"fsdp": 1 - self.f})
+        return remote(self.out5.at[j], self.in5.at[j], self.s5.at[j], self.r5.at[j], {FSDP: 1 - self.f})
 
     def line_copy(self, j, to):
-        return remote(self.out4.at[j], self.in4.at[j], self.s4.at[j], self.r4.at[j], {"ctx": to})
+        return remote(self.out4.at[j], self.in4.at[j], self.s4.at[j], self.r4.at[j], {CTX: to})
 
     def put(self, i, part_of):
         self.out1[i, 0] = part_of(opposite(self.sib)).astype(BF)
@@ -1238,7 +1239,7 @@
 
         load(0, 0).start()
         blank_rows(rows_used, hp, wgu, wd)
-        greet([{"tp": red.sib}, {"tp": red.far}, {"fsdp": 1 - f}] + line_peers(c, n_c))
+        greet([{TP: red.sib}, {TP: red.far}, {FSDP: 1 - f}] + line_peers(c, n_c))
         for copy in gate_up:
             copy.wait()
 
@@ -1447,7 +1448,7 @@
         for copy in loads(0, 0):
             copy.start()
         blank_rows(rows_used, hp, wgu, wd)
-        greet([{"tp": red.sib}, {"tp": red.far}, {"tp": opposite(red.sib)}] + each_peers(f, c, n_f, n_c))
+        greet([{TP: red.sib}, {TP: red.far}, {TP: opposite(red.sib)}] + each_peers(f, c, n_f, n_c))
         exchange("start")
         for copy in down:
             copy.wait()
@@ -1511,7 +1512,7 @@
     def send_copy(s, m):
         if s:
             return pltpu.make_async_copy(sends.at[s, m], (lg_out, lu_out)[m], ss.at[s, m])
-        return remote(sends.at[s, m], (gg_out, gu_out)[m], ss.at[s, m], sr.at[m], {"fsdp": 1 - f})
+        return remote(sends.at[s, m], (gg_out, gu_out)[m], ss.at[s, m], sr.at[m], {FSDP: 1 - f})
 
     def grads_phase(tiles, keeps):
         def tile_of(s):
@@ -1737,7 +1738,7 @@
     out[...] = jnp.broadcast_to(local, (rows, HD)).T[:8, :]
     peers = [sibling(t), opposite(t), opposite(sibling(t))]
     copies = [
-        remote(out, into.at[i], send.at[i], recv.at[i], {"tp": peer}) for i, peer in enumerate(peers)
+        remote(out, into.at[i], send.at[i], recv.at[i], {TP: peer}) for i, peer in enumerate(peers)
     ]
     for copy in copies:
         copy.start()
@@ -1810,9 +1811,9 @@
                 if df or dc or dt:
                     others.append(
                         {
-                            "fsdp": lax.rem(f + df, n_f),
-                            "ctx": lax.rem(c + dc, n_c),
-                            "tp": lax.rem(t + dt, n_t),
+                            FSDP: lax.rem(f + df, n_f),
+                            CTX: lax.rem(c + dc, n_c),
+                            TP: lax.rem(t + dt, n_t),
                         }
                     )
     large = [
@@ -1828,7 +1829,7 @@
     def cross(d):
         cc = lax.rem(c + d, n_c)
         return remote(
-            gattn.at[:, piece((1 - f) * n_c + cc, part)], inx.at[d], sx.at[d], rx.at[d], {"fsdp": 1 - f}
+            gattn.at[:, piece((1 - f) * n_c + cc, part)], inx.at[d], sx.at[d], rx.at[d], {FSDP: 1 - f}
         )
 
     def keep(d):
@@ -1836,15 +1837,15 @@
         return pltpu.make_async_copy(gattn.at[:, piece(f * n_c + cc, part)], own.at[d], lx.at[d])
 
     def line(d, to):
-        return remote(outz.at[d], inz.at[d], sz.at[d], rz.at[d], {"ctx": to})
+        return remote(outz.at[d], inz.at[d], sz.at[d], rz.at[d], {CTX: to})
 
     router_copies = [
-        remote(rpart, rin.at[i], rss.at[i], rsr.at[i], {"tp": peer})
+        remote(rpart, rin.at[i], rss.at[i], rsr.at[i], {TP: peer})
         for i, peer in enumerate([sibling(t), opposite(t), opposite(sibling(t))])
     ]
     shared = lambda act: to_each(lambda b: shs.at[:, piece(b, part)], shs_in, n_f, n_c, (hs, hr, hl), act)
     late = [
-        remote(src, dst, es.at[i], er.at[i], {"fsdp": 1 - f})
+        remote(src, dst, es.at[i], er.at[i], {FSDP: 1 - f})
         for i, (src, dst) in enumerate(((lg, lg_out), (lu, lu_out)))
     ]
     shared("start")
@@ -1900,7 +1901,7 @@
             gin.at[here],
             gs.at[h * n_t + tt],
             gr.at[here],
-            {"fsdp": b // n_c, "ctx": lax.rem(b, n_c), "tp": jnp.int32(tt)},
+            {FSDP: b // n_c, CTX: lax.rem(b, n_c), TP: jnp.int32(tt)},
         )
 
     def is_me(h, tt):
@@ -1942,7 +1943,7 @@
 
         @pl.when((b != here) | (holder != t))
         def _():
-            remote(gin.at[b], gin.at[b], gs.at[0], gr.at[b], {"tp": sibling(t)}).wait_recv()
+            remote(gin.at[b], gin.at[b], gs.at[0], gr.at[b], {TP: sibling(t)}).wait_recv()
 
     own_part = jnp.where(
         holder == t,
@@ -2054,7 +2055,7 @@
     expert_down,
 ):
     f_rank, c_rank, t_rank = ranks()
-    n_f, n_c, n_t = (lax.axis_size(name) for name in ("fsdp", "ctx", "tp"))
+    n_f, n_c, n_t = (lax.axis_size(name) for name in (FSDP, CTX, TP))
     rows, quarter = hidden_in.shape
     width = quarter * n_t
     part = w_query.shape[0]
@@ -2062,8 +2063,8 @@
     n_exp = router.shape[1]
     mine = n_exp // n_c // n_f
     ffe = expert_gate.shape[2]
-    group = ("fsdp", "ctx")
-    every = ("fsdp", "ctx", "tp")
+    group = (FSDP, CTX)
+    every = (FSDP, CTX, TP)
     n_b = n_f * n_c
     own_shared = shared_gate.shape[1] // n_b
     srows = -(-own_shared // 16) * 16
@@ -2090,7 +2091,7 @@
     layer_out, moe_in, act, silu, slope, r_two, prob, kd, sd, shared_d = forward(
         *sizes, resid_all, grad_all, resid_mid, small, weights, got, shared
     )
-    arrived_d = lax.ppermute(sd, "fsdp", swap)
+    arrived_d = lax.ppermute(sd, FSDP, swap)
     mid_grad, gain_two_part, mid_seq, shared_back, shs, kg, ku, gg, gu, lg, lu = backward(
         *sizes, grad_all, act, silu, slope, moe_in, r_two, shared_d, prob, small,
         resid_mid, out_grad, weights, got, shared,
@@ -2124,7 +2125,7 @@
 
 
 def one_head_each(mesh, args):
-    n_f, n_c, n_t = (mesh.shape[name] for name in ("fsdp", "ctx", "tp"))
+    n_f, n_c, n_t = (mesh.shape[name] for name in (FSDP, CTX, TP))
     heads = args[5].shape[1] // HD
     experts = args[10].shape[1]
     return (
@@ -2138,23 +2139,23 @@
 
 def solution(mesh):
     placed = (
-        P(("fsdp", "ctx"), "tp"),
-        P(("fsdp", "ctx")),
-        P(("fsdp", "ctx"), None),
-        P(("fsdp", "ctx"), "tp"),
-        P(("fsdp", "ctx")),
-        P(("fsdp", "ctx"), "tp"),
-        P(("fsdp", "ctx"), "tp"),
-        P(("fsdp", "ctx"), "tp"),
-        P("tp", ("fsdp", "ctx")),
-        P(("fsdp", "ctx")),
-        P(("fsdp", "ctx"), None),
-        P(("fsdp", "ctx"), "tp"),
-        P(("fsdp", "ctx"), "tp"),
-        P("tp", ("fsdp", "ctx")),
-        P("ctx", "fsdp", "tp"),
-        P("ctx", "fsdp", "tp"),
-        P("ctx", "tp", "fsdp"),
+        P((FSDP, CTX), TP),
+        P((FSDP, CTX)),
+        P((FSDP, CTX), None),
+        P((FSDP, CTX), TP),
+        P((FSDP, CTX)),
+        P((FSDP, CTX), TP),
+        P((FSDP, CTX), TP),
+        P((FSDP, CTX), TP),
+        P(TP, (FSDP, CTX)),
+        P((FSDP, CTX)),
+        P((FSDP, CTX), None),
+        P((FSDP, CTX), TP),
+        P((FSDP, CTX), TP),
+        P(TP, (FSDP, CTX)),
+        P(CTX, FSDP, TP),
+        P(CTX, FSDP, TP),
+        P(CTX, TP, FSDP),
     )
     def run(*args):
         body = per_device_seq if one_head_each(mesh, args) else per_device
@@ -2163,21 +2164,21 @@
         mesh=mesh,
         in_specs=placed,
         out_specs=(
-            P(("fsdp", "ctx"), "tp"),
-            P(("fsdp", "ctx"), "tp"),
-            P(("fsdp", "ctx")),
-            P(("fsdp", "ctx"), "tp"),
-            P(("fsdp", "ctx"), "tp"),
-            P(("fsdp", "ctx"), "tp"),
-            P("tp", ("fsdp", "ctx")),
-            P(("fsdp", "ctx")),
-            P(("fsdp", "ctx"), None),
-            P(("fsdp", "ctx"), "tp"),
-            P(("fsdp", "ctx"), "tp"),
-            P("tp", ("fsdp", "ctx")),
-            P("ctx", "fsdp", "tp"),
-            P("ctx", "fsdp", "tp"),
-            P("ctx", "tp", "fsdp"),
+            P((FSDP, CTX), TP),
+            P((FSDP, CTX), TP),
+            P((FSDP, CTX)),
+            P((FSDP, CTX), TP),
+            P((FSDP, CTX), TP),
+            P((FSDP, CTX), TP),
+            P(TP, (FSDP, CTX)),
+            P((FSDP, CTX)),
+            P((FSDP, CTX), None),
+            P((FSDP, CTX), TP),
+            P((FSDP, CTX), TP),
+            P(TP, (FSDP, CTX)),
+            P(CTX, FSDP, TP),
+            P(CTX, FSDP, TP),
+            P(CTX, TP, FSDP),
         ),
         check_vma=False,
     )(*args)

time: 464 us -> 464 us (level)
  no operation moved by 1% of the time
where the time goes in v9:
time: 464 us; the launch traced here: 456 us
  Pallas kernels  452 us (97%)
    pallas_call x1, Pallas kernels, first(): pl.pallas_call(functools.partial(first_kernel, n_c, n_f, n_exp, mine), ou...  189 us
    pallas_call x1, Pallas kernels, backward(): pl.pallas_call(functools.partial(backward_kernel, n_c, n_f, mine, ffe, sr...  110 us
    pallas_call x1, Pallas kernels, last(): pl.pallas_call(functools.partial(last_kernel, n_c, n_f, n_t, n_exp, own_s...  74.8 us
    pallas_call x1, Pallas kernels, forward(): pl.pallas_call(functools.partial(forward_kernel, n_c, n_f, mine, ffe, sro...  66 us
    pallas_call x1, Pallas kernels, finish(): pl.pallas_call(functools.partial(finish_kernel, len(plain)), grid_spec=pl...  12.6 us
  transfers between devices with their start and end apart: 1, of which 0 were waited for; matrix products, arithmetic and copies ran while one was open for 0% of the time, Pallas kernels for 40%

profile of v9, /device:TPU:0, one launch (start us, length us, event | category | flops | bytes accessed | tf_op | source)
XLA Modules:
  0.0 456.5 jit_solution(9576779098462230509)
XLA Ops:
  0.7 0.7 fusion
  1.4 1.3 select_select_fusion.lines
  2.7 188.5 %first.1 = (bf16[1024,2048]{1,0:T(8,128)(2,1)}, bf16[1024,128]{1,0:T(8,128)(2,1)}, bf16[1024,128]{1,0:T(8,128)(2,1)}, bf16[1024,128]{1,0:T(8,128)(2,1)}, f32[102...) custom-call(bf16[256,512]{1,0:T(8,128)(2,1)} %hidden.3, ...), custom_call_target="tpu_custom_call" | custom-call | flops 5368709120 | bytes 314572800 | tf_op jit(solution)/shard_map/first/pallas_call | solution.py:930
  191.2 66.0 %forward.1 = (bf16[256,512]{1,0:T(8,128)(2,1)}, bf16[2048,2048]{1,0:T(8,128)(2,1)}, bf16[2048,896]{1,0:T(8,128)(2,1)}, bf16[2048,896]{1,0:T(8,128)(2,1)}, bf16[2...) custom-call(bf16[2048,2048]{1,0:T(8,128)(2,1)} %get-tuple-element.82, ...), custom_call_target="tpu_custom_call" | custom-call | flops 26843545600 | bytes 83886080 | tf_op jit(solution)/shard_map/forward/pallas_call | solution.py:1371
  257.3 0.6 collective-permute-start
  257.9 109.9 %backward.1 = (f32[256,512]{1,0:T(8,128)}, f32[8,512]{1,0:T(8,128)}, bf16[1024,2048]{1,0:T(8,128)(2,1)}, bf16[8,96,256]{2,1,0:T(8,128)(2,1)}, bf16[208,2048]{1,0...) custom-call(bf16[8,4,256,512]{3,2,1,0:T(8,128)(2,1)} %get-tuple-elem, ...), custom_call_target="tpu_custom_call" | custom-call | flops 33554432000 | bytes 209715200 | tf_op jit(solution)/shard_map/backward/pallas_call | solution.py:1603
  367.7 74.8 %last.1 = (f32[256,512]{1,0:T(8,128)}, f32[256,512]{1,0:T(8,128)}, f32[256,512]{1,0:T(8,128)}, f32[256,512]{1,0:T(8,128)}, f32[512,256]{1,0:T(8,128)}, /*index=5...) custom-call(bf16[1024,2048]{1,0:T(8,128)(2,1)} %get-tuple-element.97, ...), custom_call_target="tpu_custom_call" | custom-call | flops 8589934592 | bytes 157286400 | tf_op jit(solution)/shard_map/last/pallas_call | solution.py:1970
  442.5 0.0 collective-permute-done.refs_4_
  442.6 0.0 copy-start
  442.6 1.1 copy-done
  443.7 12.6 %finish.1 = (f32[4,352,1024]{2,1,0:T(8,128)}, f32[4,352,1024]{2,1,0:T(8,128)}, f32[4,352,1024]{2,1,0:T(8,128)}, f32[704,256]{1,0:T(8,128)}, bf16[256,512]{1,0:T(...) custom-call(s32[1]{0:T(128)} %bitcast.f_ref, ...), custom_call_target="tpu_custom_call" | custom-call | tf_op jit(solution)/shard_map/finish/pallas_call | solution.py:1710
  (2 shorter events, 0.0 us)
Async XLA Ops:
  257.3 185.3 %collective-permute-start = (bf16[2,352,1024]{2,1,0:T(8,128)(2,1)}, bf16[2,352,1024]{2,1,0:T(8,128)(2,1)S(1)}, u32[]{:S(2)}, u32[]{:S(2)}) collective-permute-start(bf16[2,352,1024]{2,1,0:T(8,128)(2,1)} %get-tuple-element.117), channel_id=1, source_target_pairs={{0,16},{16,0},{1,17},{17,1},{2,18},{18,2},{3,19},{19,3},{4,20},{20... | collective-permute-start | bytes 4325384 | tf_op jit(solution)/shard_map/ppermute | solution.py:2094
  442.6 1.1 copy-start
